TPU v7x, 32 devices: a whole 2x2x4 slice. The times are simulated.
32 devices in a mesh: batch: 4 (over z), seq: 8 (over y, x, core).
Axes of the slice: x: 2, y: 2, z: 4, core: 2. Of those that a mesh axis runs over, the one named last changes fastest.
Arguments:
- hidden: bfloat16 [16, 1024, 768], P('batch', 'seq'), may hold values from -6 to 6
- char_ids: int32 [16, 4096], P('batch', 'seq'), may hold values from 0 to 255
- group_ids: int32 [16], P('batch'), may hold values from 0 to 3
- word_lengths: int32 [16, 8, 128], P('batch', 'seq'), may hold values from 1 to 8, 512 in all within a row
- qkv_weight: bfloat16 [768, 2304], P('seq'), may hold values from -0.21875 to 0.21875
- out_weight: bfloat16 [768, 768], P('seq'), may hold values from -6 to 6
- up_weight: bfloat16 [768, 3072], P('seq'), may hold values from -0.21875 to 0.21875
- ffn_bias: bfloat16 [3072], P('seq'), may hold values from -3 to 3
- down_weight: bfloat16 [3072, 768], P('seq'), may hold values from -0.109375 to 0.109375
- gru_weight: bfloat16 [768, 1536], P('seq'), may hold values from -0.21875 to 0.21875
- gate_bias: bfloat16 [768], P('seq'), may hold values from -14 to -3
- candidate_bias: bfloat16 [768], P('seq'), may hold values from -3 to 3
- char_weight: bfloat16 [768, 768], P('seq'), may hold values from -1.25 to 1.25
- conv_weight: bfloat16 [3, 1536, 1536], P(None, 'seq'), may hold values from -0.09375 to 0.09375
- char_table: bfloat16 [1024, 768], P('seq'), may hold values from -6 to 6
- norm_gain: bfloat16 [768, 4], P('seq'), may hold values from 0.099609375 to 1.8984375
- norm_shift: bfloat16 [768, 4], P('seq'), may hold values from -3 to 3
- tok_grad: bfloat16 [16, 1024, 768], P('batch', 'seq'), may hold values from -6 to 6
- char_grad: bfloat16 [16, 1024, 768], P('batch', 'seq'), may hold values from -6 to 6
Outputs:
- tok_out: float32 [16, 1024, 768], P('batch', 'seq')
- char_out: float32 [16, 1024, 768], P('batch', 'seq')
- hidden_grad: float32 [16, 1024, 768], P('batch', 'seq')
- qkv_weight_grad: float32 [768, 2304], P('seq')
- out_weight_grad: float32 [768, 768], P('seq')
- up_weight_grad: float32 [768, 3072], P('seq')
- ffn_bias_grad: float32 [3072], P('seq')
- down_weight_grad: float32 [3072, 768], P('seq')
- gru_weight_grad: float32 [768, 1536], P('seq')
- gate_bias_grad: float32 [768], P('seq')
- candidate_bias_grad: float32 [768], P('seq')
- char_weight_grad: float32 [768, 768], P('seq')
- conv_weight_grad: float32 [3, 1536, 1536], P(None, 'seq')
- char_table_grad: float32 [1024, 768], P('seq')
- norm_gain_grad: float32 [768, 4], P('seq')
- norm_shift_grad: float32 [768, 4], P('seq')
Inputs may be any that keep to these rules, and one draw needn't show every extreme that they name: `word_lengths`: within each block of 128 tokens (one sequence on one device) the lengths sum to exactly 512.
All inputs are finite; a program needn't handle non-finite values.
Results may differ from a plain program's by a relative error of at most 0.02.
Values may be sent and summed in bfloat16 or wider, within the bound.
No kernel may reach another device: no remote copies, remote signals or barrier semaphores. Data moves between devices by JAX's collectives and lax.ppermute only.
A program may use at most 320 MiB of HBM per device.

v0:
```python
import jax
import jax.numpy as jnp
from jax import lax
from jax.sharding import PartitionSpec as P

HEADS = 12
NCHAR = 256
MICRO = 2


NORM_EPS = 1e-06


def prefix(part, axis, combine, identity, reverse):
    count = lax.axis_size(axis)
    place = lax.axis_index(axis)
    ahead = count - 1 - place if reverse else place
    gathered = jax.tree.map(lambda a: lax.all_gather(a, axis), part)
    state = jax.tree.map(lambda a, e: jnp.zeros_like(a) + jnp.asarray(e, a.dtype), part, identity)

    def one(lap, state):
        source = count - 1 - lap if reverse else lap
        return combine(
            state, jax.tree.map(lambda a: lax.dynamic_index_in_dim(a, source, 0, False), gathered)
        )

    return lax.fori_loop(0, ahead, one, state)


def extended(block, sides, width):
    for axis, dim in sides:
        count = lax.axis_size(axis)
        forward = [(i, i + 1) for i in range(count - 1)]
        backward = [(target, source) for source, target in forward]
        low = lax.ppermute(
            lax.slice_in_dim(block, block.shape[dim] - width, None, axis=dim), axis, forward
        )
        high = lax.ppermute(lax.slice_in_dim(block, 0, width, axis=dim), axis, backward)
        block = jnp.concatenate([low, block, high], axis=dim)
    return block


def matmul(left, right):
    return jnp.dot(left, right, preferred_element_type=jnp.float32)


def layer_norm(values, gains, shifts):
    center = values - jnp.mean(values, -1, keepdims=True)
    spread = jnp.mean(center * center, -1, keepdims=True)
    return center * lax.rsqrt(spread + NORM_EPS) * gains + shifts


def norm_back(values, gains, shifts, gradient):
    result, pullback = jax.vjp(layer_norm, values, gains, shifts)
    return pullback(gradient)


def affine(earlier, latter):
    return (earlier[0] * latter[0], latter[0] * earlier[1] + latter[1])


def local_scan(decays, drives, backwards):
    return lax.associative_scan(affine, (decays, drives), axis=1, reverse=backwards)


def gate_terms(gate_input):
    quarter = gate_input.shape[-1] // 4
    update_fwd = jax.nn.sigmoid(gate_input[..., :quarter])
    cand_fwd = jnp.tanh(gate_input[..., quarter : 2 * quarter])
    update_rev = jax.nn.sigmoid(gate_input[..., 2 * quarter : 3 * quarter])
    cand_rev = jnp.tanh(gate_input[..., 3 * quarter :])
    return (1.0 - update_fwd, update_fwd * cand_fwd, 1.0 - update_rev, update_rev * cand_rev)


def gelu_exact(values):
    return jax.nn.gelu(values, approximate=False)


def reduce_grads(gradients):
    rows_part = (
        lax.psum_scatter(
            gradients[0].astype(jnp.bfloat16), "seq", scatter_dimension=0, tiled=True
        ).astype(jnp.float32),
        lax.psum_scatter(
            gradients[1].astype(jnp.bfloat16), "seq", scatter_dimension=0, tiled=True
        ).astype(jnp.float32),
        lax.psum_scatter(
            gradients[2].astype(jnp.bfloat16), "seq", scatter_dimension=0, tiled=True
        ).astype(jnp.float32),
        lax.psum_scatter(
            gradients[3].astype(jnp.bfloat16), "seq", scatter_dimension=0, tiled=True
        ).astype(jnp.float32),
        lax.psum_scatter(
            gradients[4].astype(jnp.bfloat16), "seq", scatter_dimension=0, tiled=True
        ).astype(jnp.float32),
        lax.psum_scatter(
            gradients[5].astype(jnp.bfloat16), "seq", scatter_dimension=0, tiled=True
        ).astype(jnp.float32),
        lax.psum_scatter(
            gradients[6].astype(jnp.bfloat16), "seq", scatter_dimension=0, tiled=True
        ).astype(jnp.float32),
        lax.psum_scatter(
            gradients[7].astype(jnp.bfloat16), "seq", scatter_dimension=0, tiled=True
        ).astype(jnp.float32),
        lax.psum_scatter(
            gradients[8].astype(jnp.bfloat16), "seq", scatter_dimension=0, tiled=True
        ).astype(jnp.float32),
        lax.psum_scatter(
            gradients[9].astype(jnp.bfloat16), "seq", scatter_dimension=1, tiled=True
        ).astype(jnp.float32),
        lax.psum_scatter(
            gradients[10].astype(jnp.bfloat16), "seq", scatter_dimension=0, tiled=True
        ).astype(jnp.float32),
        lax.psum_scatter(
            gradients[11].astype(jnp.bfloat16), "seq", scatter_dimension=0, tiled=True
        ).astype(jnp.float32),
        lax.psum_scatter(
            gradients[12].astype(jnp.bfloat16), "seq", scatter_dimension=0, tiled=True
        ).astype(jnp.float32),
    )
    return (
        lax.psum(rows_part[0].astype(jnp.bfloat16), "batch").astype(jnp.float32),
        lax.psum(rows_part[1].astype(jnp.bfloat16), "batch").astype(jnp.float32),
        lax.psum(rows_part[2].astype(jnp.bfloat16), "batch").astype(jnp.float32),
        lax.psum(rows_part[3].astype(jnp.bfloat16), "batch").astype(jnp.float32),
        lax.psum(rows_part[4].astype(jnp.bfloat16), "batch").astype(jnp.float32),
        lax.psum(rows_part[5].astype(jnp.bfloat16), "batch").astype(jnp.float32),
        lax.psum(rows_part[6].astype(jnp.bfloat16), "batch").astype(jnp.float32),
        lax.psum(rows_part[7].astype(jnp.bfloat16), "batch").astype(jnp.float32),
        lax.psum(rows_part[8].astype(jnp.bfloat16), "batch").astype(jnp.float32),
        lax.psum(rows_part[9].astype(jnp.bfloat16), "batch").astype(jnp.float32),
        lax.psum(rows_part[10].astype(jnp.bfloat16), "batch").astype(jnp.float32),
        lax.psum(rows_part[11].astype(jnp.bfloat16), "batch").astype(jnp.float32),
        lax.psum(rows_part[12].astype(jnp.bfloat16), "batch").astype(jnp.float32),
    )


def micro_step(weights, hidden, char_ids, group_ids, word_lengths, tok_grad, char_grad):
    (
        w_qkv,
        w_out,
        w_up,
        b_ffn,
        w_down,
        w_gru,
        b_gate,
        b_cand,
        w_char,
        w_conv,
        table,
        gains,
        shifts,
    ) = weights
    seq_count, tok_count, model_width = hidden.shape
    char_count = char_ids.shape[1]
    half_width = model_width // 2
    head_width = model_width // HEADS
    score_scale = head_width ** (-0.5)
    row_count = seq_count * tok_count
    gains32 = gains.astype(jnp.float32)
    shifts32 = shifts.astype(jnp.float32)
    rows_flat = hidden.reshape(row_count, model_width)
    hidden32 = rows_flat.astype(jnp.float32)
    projected = matmul(rows_flat, w_qkv).astype(jnp.bfloat16)
    queries = projected[:, :model_width].reshape(seq_count, tok_count, HEADS, head_width)
    key_part = projected[:, model_width : 2 * model_width].reshape(
        seq_count, tok_count, model_width
    )
    value_part = projected[:, 2 * model_width :].reshape(seq_count, tok_count, model_width)
    keys_all, values_all = (
        lax.all_gather(key_part, "seq", axis=1, tiled=True),
        lax.all_gather(value_part, "seq", axis=1, tiled=True),
    )

    def attend(record):
        query_one, key_one, value_one = record
        key_heads = key_one.reshape(-1, HEADS, head_width)
        value_heads = value_one.reshape(-1, HEADS, head_width)
        scores = (
            jnp.einsum("qhe,khe->hqk", query_one, key_heads, preferred_element_type=jnp.float32)
            * score_scale
        )
        highest = jnp.max(scores, -1, keepdims=True)
        expo_part = jnp.exp(scores - highest)
        totals = jnp.sum(expo_part, -1, keepdims=True)
        probability = (expo_part / totals).astype(jnp.bfloat16)
        mixture = jnp.einsum(
            "hqk,khe->qhe", probability, value_heads, preferred_element_type=jnp.float32
        )
        return (mixture, (highest + jnp.log(totals))[..., 0])

    mixture, log_total = lax.map(attend, (queries, keys_all, values_all))
    mixture_b = mixture.reshape(row_count, model_width).astype(jnp.bfloat16)
    attn_sum = hidden32 + matmul(mixture_b, w_out)
    normed_a = layer_norm(attn_sum, gains32[:, 0], shifts32[:, 0])
    normed_b = normed_a.astype(jnp.bfloat16)
    up_proj = matmul(normed_b, w_up) + b_ffn.astype(jnp.float32)
    activated, gelu_pull = jax.vjp(gelu_exact, up_proj)
    activated_b = activated.astype(jnp.bfloat16)
    ffn_sum = normed_a + matmul(activated_b, w_down)
    ffn_norm = layer_norm(ffn_sum, gains32[:, 1], shifts32[:, 1])
    table_rows = (group_ids[:, None] * NCHAR + char_ids).reshape(seq_count * char_count)
    onehot = (table_rows[:, None] == jnp.arange(table.shape[0], dtype=jnp.int32)[None, :]).astype(
        jnp.bfloat16
    )
    embedded = matmul(onehot, table).astype(jnp.bfloat16)
    bias_all = jnp.concatenate(
        [b_gate[:half_width], b_cand[:half_width], b_gate[half_width:], b_cand[half_width:]]
    ).astype(jnp.float32)
    gate_input = (matmul(embedded, w_gru) + bias_all).reshape(
        seq_count, char_count, 2 * model_width
    )
    terms, gate_pull = jax.vjp(gate_terms, gate_input)
    decay_fwd, drive_fwd, decay_rev, drive_rev = terms
    cum_fwd, local_fwd = local_scan(decay_fwd, drive_fwd, False)
    start_fwd = prefix(
        (cum_fwd[:, -1], local_fwd[:, -1]),
        "seq",
        affine,
        (jnp.ones_like(cum_fwd[:, -1]), jnp.zeros_like(local_fwd[:, -1])),
        False,
    )[1]
    state_fwd = local_fwd + cum_fwd * start_fwd[:, None]
    cum_rev, local_rev = local_scan(decay_rev, drive_rev, True)
    start_rev = prefix(
        (cum_rev[:, 0], local_rev[:, 0]),
        "seq",
        affine,
        (jnp.ones_like(cum_rev[:, 0]), jnp.zeros_like(local_rev[:, 0])),
        True,
    )[1]
    state_rev = local_rev + cum_rev * start_rev[:, None]
    states = jnp.concatenate([state_fwd, state_rev], -1).astype(jnp.bfloat16)
    word_lens = word_lengths.reshape(seq_count, tok_count)
    word_ends = jnp.cumsum(word_lens, axis=1)
    char_place = jnp.arange(char_count, dtype=jnp.int32)
    owner_token = jnp.sum(
        (word_ends[:, None, :] <= char_place[None, :, None]).astype(jnp.int32), -1
    )
    members = (
        owner_token[:, None, :] == jnp.arange(tok_count, dtype=jnp.int32)[None, :, None]
    ).astype(jnp.bfloat16)
    summed = jnp.einsum("mtc,mcd->mtd", members, states, preferred_element_type=jnp.float32)
    lens_float = word_lens.astype(jnp.float32)[..., None]
    pooled_b = (summed / lens_float).astype(jnp.bfloat16).reshape(row_count, model_width)
    char_proj = matmul(pooled_b, w_char)
    joined = (
        jnp.concatenate([ffn_norm, char_proj], -1)
        .astype(jnp.bfloat16)
        .reshape(seq_count, tok_count, 2 * model_width)
    )
    padded = extended(joined, (("seq", 1),), 1)
    merged = jnp.einsum(
        "mtc,co->mto", padded[:, 0:tok_count], w_conv[0], preferred_element_type=jnp.float32
    )
    merged = merged + jnp.einsum(
        "mtc,co->mto", padded[:, 1 : tok_count + 1], w_conv[1], preferred_element_type=jnp.float32
    )
    merged = merged + jnp.einsum(
        "mtc,co->mto", padded[:, 2 : tok_count + 2], w_conv[2], preferred_element_type=jnp.float32
    )
    merged = merged.reshape(row_count, 2 * model_width)
    tok_sum = ffn_norm + merged[:, :model_width]
    char_sum = char_proj + merged[:, model_width:]
    tok_out = layer_norm(tok_sum, gains32[:, 2], shifts32[:, 2])
    char_out = layer_norm(char_sum, gains32[:, 3], shifts32[:, 3])
    d_tok_sum, gain_two, shift_two = norm_back(
        tok_sum,
        gains32[:, 2],
        shifts32[:, 2],
        tok_grad.reshape(row_count, model_width).astype(jnp.float32),
    )
    d_char_sum, gain_three, shift_three = norm_back(
        char_sum,
        gains32[:, 3],
        shifts32[:, 3],
        char_grad.reshape(row_count, model_width).astype(jnp.float32),
    )
    d_merged = (
        jnp.concatenate([d_tok_sum, d_char_sum], -1)
        .astype(jnp.bfloat16)
        .reshape(seq_count, tok_count, 2 * model_width)
    )
    merged_pad = extended(d_merged, (("seq", 1),), 1)
    d_conv = jnp.stack(
        [
            jnp.einsum(
                "mtc,mto->co",
                padded[:, offset : offset + tok_count],
                d_merged,
                preferred_element_type=jnp.float32,
            )
            for offset in range(3)
        ]
    )
    d_joined = jnp.einsum(
        "mto,co->mtc",
        merged_pad[:, 2 : tok_count + 2],
        w_conv[0],
        preferred_element_type=jnp.float32,
    )
    d_joined = d_joined + jnp.einsum(
        "mto,co->mtc",
        merged_pad[:, 1 : tok_count + 1],
        w_conv[1],
        preferred_element_type=jnp.float32,
    )
    d_joined = d_joined + jnp.einsum(
        "mto,co->mtc", merged_pad[:, 0:tok_count], w_conv[2], preferred_element_type=jnp.float32
    )
    d_joined = d_joined.reshape(row_count, 2 * model_width)
    d_ffn_norm = d_tok_sum + d_joined[:, :model_width]
    d_char_proj = (d_char_sum + d_joined[:, model_width:]).astype(jnp.bfloat16)
    d_char_w = jnp.einsum("rd,re->de", pooled_b, d_char_proj, preferred_element_type=jnp.float32)
    d_pooled = jnp.einsum("re,de->rd", d_char_proj, w_char, preferred_element_type=jnp.float32)
    d_summed = (d_pooled.reshape(seq_count, tok_count, model_width) / lens_float).astype(
        jnp.bfloat16
    )
    d_states = jnp.einsum("mtc,mtd->mcd", members, d_summed, preferred_element_type=jnp.float32)
    d_state_fwd = d_states[..., :half_width]
    d_state_rev = d_states[..., half_width:]
    cum_grad_f, local_grad_f = local_scan(decay_fwd, decay_fwd * d_state_fwd, True)
    carry_fwd = prefix(
        (cum_grad_f[:, 0], local_grad_f[:, 0]),
        "seq",
        affine,
        (jnp.ones_like(cum_grad_f[:, 0]), jnp.zeros_like(local_grad_f[:, 0])),
        True,
    )[1]
    whole_grad_f = local_grad_f + cum_grad_f * carry_fwd[:, None]
    next_grad_f = jnp.concatenate([whole_grad_f[:, 1:], carry_fwd[:, None]], 1)
    total_fwd = d_state_fwd + next_grad_f
    prior_fwd = jnp.concatenate([start_fwd[:, None], state_fwd[:, :-1]], 1)
    cum_grad_r, local_grad_r = local_scan(decay_rev, decay_rev * d_state_rev, False)
    carry_rev = prefix(
        (cum_grad_r[:, -1], local_grad_r[:, -1]),
        "seq",
        affine,
        (jnp.ones_like(cum_grad_r[:, -1]), jnp.zeros_like(local_grad_r[:, -1])),
        False,
    )[1]
    whole_grad_r = local_grad_r + cum_grad_r * carry_rev[:, None]
    prior_grad_r = jnp.concatenate([carry_rev[:, None], whole_grad_r[:, :-1]], 1)
    total_rev = d_state_rev + prior_grad_r
    later_rev = jnp.concatenate([state_rev[:, 1:], start_rev[:, None]], 1)
    d_gate_input = gate_pull((total_fwd * prior_fwd, total_fwd, total_rev * later_rev, total_rev))[
        0
    ]
    d_gate_input = d_gate_input.astype(jnp.bfloat16).reshape(
        seq_count * char_count, 2 * model_width
    )
    d_gru_w = jnp.einsum("cd,ce->de", embedded, d_gate_input, preferred_element_type=jnp.float32)
    d_bias_all = jnp.sum(d_gate_input.astype(jnp.float32), 0)
    d_gate_b = jnp.concatenate(
        [d_bias_all[:half_width], d_bias_all[2 * half_width : 3 * half_width]]
    )
    d_cand_b = jnp.concatenate(
        [d_bias_all[half_width : 2 * half_width], d_bias_all[3 * half_width :]]
    )
    d_embedded = jnp.einsum(
        "ce,de->cd", d_gate_input, w_gru, preferred_element_type=jnp.float32
    ).astype(jnp.bfloat16)
    d_table = jnp.einsum("cv,cd->vd", onehot, d_embedded, preferred_element_type=jnp.float32)
    d_ffn_sum, gain_one, shift_one = norm_back(ffn_sum, gains32[:, 1], shifts32[:, 1], d_ffn_norm)
    d_ffn_out = d_ffn_sum.astype(jnp.bfloat16)
    d_down_w = jnp.einsum("rf,rd->fd", activated_b, d_ffn_out, preferred_element_type=jnp.float32)
    d_activated = jnp.einsum("rd,fd->rf", d_ffn_out, w_down, preferred_element_type=jnp.float32)
    d_up_proj = gelu_pull(d_activated)[0].astype(jnp.bfloat16)
    d_up_w = jnp.einsum("rd,rf->df", normed_b, d_up_proj, preferred_element_type=jnp.float32)
    d_ffn_b = jnp.sum(d_up_proj.astype(jnp.float32), 0)
    d_normed = d_ffn_sum + jnp.einsum(
        "rf,df->rd", d_up_proj, w_up, preferred_element_type=jnp.float32
    )
    d_attn_sum, gain_zero, shift_zero = norm_back(attn_sum, gains32[:, 0], shifts32[:, 0], d_normed)
    d_attended = d_attn_sum.astype(jnp.bfloat16)
    d_out_w = jnp.einsum("rd,re->de", mixture_b, d_attended, preferred_element_type=jnp.float32)
    d_mixture = jnp.einsum(
        "re,de->rd", d_attended, w_out, preferred_element_type=jnp.float32
    ).astype(jnp.bfloat16)
    d_mixture = d_mixture.reshape(seq_count, tok_count, HEADS, head_width)

    def attend_back(record):
        query_one, key_one, value_one, total_one, d_mix_one = record
        key_heads = key_one.reshape(-1, HEADS, head_width)
        value_heads = value_one.reshape(-1, HEADS, head_width)
        scores = (
            jnp.einsum("qhe,khe->hqk", query_one, key_heads, preferred_element_type=jnp.float32)
            * score_scale
        )
        probability = jnp.exp(scores - total_one[..., None])
        d_prob = jnp.einsum(
            "qhe,khe->hqk", d_mix_one, value_heads, preferred_element_type=jnp.float32
        )
        d_values = jnp.einsum(
            "hqk,qhe->khe",
            probability.astype(jnp.bfloat16),
            d_mix_one,
            preferred_element_type=jnp.float32,
        )
        centered = jnp.sum(probability * d_prob, -1, keepdims=True)
        d_scores = (probability * (d_prob - centered)).astype(jnp.bfloat16)
        d_queries = (
            jnp.einsum("hqk,khe->qhe", d_scores, key_heads, preferred_element_type=jnp.float32)
            * score_scale
        )
        d_keys = (
            jnp.einsum("hqk,qhe->khe", d_scores, query_one, preferred_element_type=jnp.float32)
            * score_scale
        )
        return (
            d_queries.reshape(query_one.shape[0], model_width),
            d_keys.reshape(key_one.shape[0], model_width),
            d_values.reshape(key_one.shape[0], model_width),
        )

    d_queries, d_keys_all, d_values_all = lax.map(
        attend_back, (queries, keys_all, values_all, log_total, d_mixture)
    )
    d_keys, d_values = (
        lax.psum_scatter(
            d_keys_all.astype(jnp.bfloat16), "seq", scatter_dimension=1, tiled=True
        ).astype(jnp.float32),
        lax.psum_scatter(
            d_values_all.astype(jnp.bfloat16), "seq", scatter_dimension=1, tiled=True
        ).astype(jnp.float32),
    )
    d_projected = (
        jnp.concatenate([d_queries, d_keys, d_values], -1)
        .astype(jnp.bfloat16)
        .reshape(row_count, 3 * model_width)
    )
    d_qkv_w = jnp.einsum("rd,re->de", rows_flat, d_projected, preferred_element_type=jnp.float32)
    hidden_grad = d_attn_sum + jnp.einsum(
        "re,de->rd", d_projected, w_qkv, preferred_element_type=jnp.float32
    )
    d_gains = jnp.stack([gain_zero, gain_one, gain_two, gain_three], 1)
    d_shifts = jnp.stack([shift_zero, shift_one, shift_two, shift_three], 1)
    gradients = (
        d_qkv_w,
        d_out_w,
        d_up_w,
        d_ffn_b,
        d_down_w,
        d_gru_w,
        d_gate_b,
        d_cand_b,
        d_char_w,
        d_conv,
        d_table,
        d_gains,
        d_shifts,
    )
    shape_out = (seq_count, tok_count, model_width)
    return (
        tok_out.reshape(shape_out),
        char_out.reshape(shape_out),
        hidden_grad.reshape(shape_out),
        gradients,
    )


def local(
    hidden,
    char_ids,
    group_ids,
    word_lengths,
    qkv_weight,
    out_weight,
    up_weight,
    ffn_bias,
    down_weight,
    gru_weight,
    gate_bias,
    candidate_bias,
    char_weight,
    conv_weight,
    char_table,
    norm_gain,
    norm_shift,
    tok_grad,
    char_grad,
):
    weights = (
        lax.all_gather(qkv_weight, "seq", axis=0, tiled=True),
        lax.all_gather(out_weight, "seq", axis=0, tiled=True),
        lax.all_gather(up_weight, "seq", axis=0, tiled=True),
        lax.all_gather(ffn_bias, "seq", axis=0, tiled=True),
        lax.all_gather(down_weight, "seq", axis=0, tiled=True),
        lax.all_gather(gru_weight, "seq", axis=0, tiled=True),
        lax.all_gather(gate_bias, "seq", axis=0, tiled=True),
        lax.all_gather(candidate_bias, "seq", axis=0, tiled=True),
        lax.all_gather(char_weight, "seq", axis=0, tiled=True),
        lax.all_gather(conv_weight, "seq", axis=1, tiled=True),
        lax.all_gather(char_table, "seq", axis=0, tiled=True),
        lax.all_gather(norm_gain, "seq", axis=0, tiled=True),
        lax.all_gather(norm_shift, "seq", axis=0, tiled=True),
    )
    per_micro = hidden.shape[0] // MICRO
    tok_parts = []
    char_parts = []
    grad_parts = []
    shards = None
    for micro_index in range(MICRO):
        begin = micro_index * per_micro
        finish = begin + per_micro
        tok_out, char_out, hidden_grad, gradients = micro_step(
            weights,
            hidden[begin:finish],
            char_ids[begin:finish],
            group_ids[begin:finish],
            word_lengths[begin:finish],
            tok_grad[begin:finish],
            char_grad[begin:finish],
        )
        tok_parts.append(tok_out)
        char_parts.append(char_out)
        grad_parts.append(hidden_grad)
        reduced = reduce_grads(gradients)
        shards = reduced if shards is None else jax.tree.map(jnp.add, shards, reduced)
    outputs = (
        jnp.concatenate(tok_parts, 0),
        jnp.concatenate(char_parts, 0),
        jnp.concatenate(grad_parts, 0),
    )
    return outputs + tuple(shards)


def solution(mesh):
    return jax.shard_map(
        local,
        mesh=mesh,
        in_specs=(
            P("batch", "seq", None),
            P("batch", "seq"),
            P("batch"),
            P("batch", "seq", None),
            P("seq", None),
            P("seq", None),
            P("seq", None),
            P("seq"),
            P("seq", None),
            P("seq", None),
            P("seq"),
            P("seq"),
            P("seq", None),
            P(None, "seq", None),
            P("seq", None),
            P("seq", None),
            P("seq", None),
            P("batch", "seq", None),
            P("batch", "seq", None),
        ),
        out_specs=(
            P("batch", "seq", None),
            P("batch", "seq", None),
            P("batch", "seq", None),
            P("seq", None),
            P("seq", None),
            P("seq", None),
            P("seq"),
            P("seq", None),
            P("seq", None),
            P("seq"),
            P("seq"),
            P("seq", None),
            P(None, "seq", None),
            P("seq", None),
            P("seq", None),
            P("seq", None),
        ),
        check_vma=False,
    )
```

profile of v0, /device:TPU:0, one launch (start us, length us, event | category | flops | bytes accessed | tf_op | source)
XLA Modules:
  0.0 3213.6 jit_solution(370712940568718629)
XLA Ops:
  10.1 36.5 %all-gather.32.cloned.1.call-done = bf16[768,2304]{1,0:T(8,128)(2,1)} async-done(((bf16[96,2304]{1,0:T(8,128)(2,1)}), bf16[768,2304]{1,0:T(8,128)(2,1)}) %all-gather.32.cloned.1.call-update) | async-done | bytes 3538960 | tf_op jit(solution)/shard_map/all_gather | solution.py:484
  63.5 8.9 all-gather.16
  73.1 7.9 all-gather.17
  81.7 8.8 all-gather.18
  93.7 13.6 all-reduce.305
  239.2 12.7 reverse.45
  264.8 6.8 slice.2785
  271.6 6.8 slice.2787
  373.7 7.0 slice.2850
  525.5 12.7 reverse.44
  557.9 7.2 slice.2591
  681.8 9.9 all-gather.5
  702.2 8.2 all-gather.4
  711.0 8.9 all-gather.7
  720.6 8.2 all-gather.6
  729.4 12.9 rev.45
  742.3 7.8 rev.44
  772.2 9.9 all-gather.1
  793.0 8.1 all-gather
  801.8 7.0 slice.2654
  824.1 9.1 all-gather.3
  838.3 8.1 all-gather.2
  846.5 10.3 rev.42
  856.7 10.3 rev.41
  893.8 13.4 while.159
  908.6 13.2 while.156
  927.1 11.9 multiply_convert_fusion.2
  950.6 11.5 multiply_convert_fusion.3
  1186.3 29.4 while.162
  1215.7 7.6 copy.182
  1240.4 14.0 all-gather.9
  1262.2 7.8 all-gather.8
  1285.7 10.2 reverse.46
  1307.4 7.0 slice.2988
  1356.8 29.5 while.163
  1386.3 7.6 copy.186
  1529.6 8.7 copy.188
  1662.8 10.3 all-gather.13
  1685.6 9.0 all-gather.12
  1740.7 10.3 reverse.47
  1762.5 7.0 slice.3170
  1959.3 12.5 all-gather.11
  1972.5 8.5 all-gather.10
  2014.3 12.9 rev.48
  2027.2 7.8 rev.47
  2046.7 7.3 all-gather.15
  2063.8 9.9 all-gather.14
  2085.1 10.9 fusion.107
  2102.5 10.3 rev.50
  2120.3 10.8 fusion.109
  2200.2 45.9 %reduce-scatter.57.cloned.1.call-done = bf16[96,1536]{1,0:T(8,128)(2,1)} async-done(((bf16[768,1536]{1,0:T(8,128)(2,1)}), bf16[96,1536]{1,0:T(8,128)(2,1)}) %reduce-scatter.57.cloned.1.call-update) | async-done | bytes 294928 | tf_op jit(solution)/shard_map/reduce_scatter | solution.py:96
  2246.1 46.1 %reduce-scatter.59.cloned.1.call-done = bf16[96,1536]{1,0:T(8,128)(2,1)} async-done(((bf16[768,1536]{1,0:T(8,128)(2,1)}), bf16[96,1536]{1,0:T(8,128)(2,1)}) %reduce-scatter.59.cloned.1.call-update) | async-done | bytes 294928 | tf_op jit(solution)/shard_map/reduce_scatter | solution.py:96
  2292.2 57.2 %reduce-scatter.53.cloned.1.call-done = bf16[384,768]{1,0:T(8,128)(2,1)} async-done(((bf16[3072,768]{1,0:T(8,128)(2,1)}), bf16[384,768]{1,0:T(8,128)(2,1)}) %reduce-scatter.53.cloned.1.call-update) | async-done | bytes 589840 | tf_op jit(solution)/shard_map/reduce_scatter | solution.py:93
  2349.3 57.7 %reduce-scatter.55.cloned.1.call-done = bf16[384,768]{1,0:T(8,128)(2,1)} async-done(((bf16[3072,768]{1,0:T(8,128)(2,1)}), bf16[384,768]{1,0:T(8,128)(2,1)}) %reduce-scatter.55.cloned.1.call-update) | async-done | bytes 589840 | tf_op jit(solution)/shard_map/reduce_scatter | solution.py:93
  2407.1 57.4 %reduce-scatter.49.cloned.1.call-done = bf16[96,3072]{1,0:T(8,128)(2,1)} async-done(((bf16[768,3072]{1,0:T(8,128)(2,1)}), bf16[96,3072]{1,0:T(8,128)(2,1)}) %reduce-scatter.49.cloned.1.call-update) | async-done | bytes 589840 | tf_op jit(solution)/shard_map/reduce_scatter | solution.py:87
  2464.5 57.6 %reduce-scatter.51.cloned.1.call-done = bf16[96,3072]{1,0:T(8,128)(2,1)} async-done(((bf16[768,3072]{1,0:T(8,128)(2,1)}), bf16[96,3072]{1,0:T(8,128)(2,1)}) %reduce-scatter.51.cloned.1.call-update) | async-done | bytes 589840 | tf_op jit(solution)/shard_map/reduce_scatter | solution.py:87
  2522.1 104.4 %reduce-scatter.65.cloned.1.call-done = bf16[3,192,1536]{2,1,0:T(8,128)(2,1)} async-done(((bf16[3,1536,1536]{2,1,0:T(8,128)(2,1)}), bf16[3,192,1536]{2,1,0:T(8,128)(2,1)}) %reduce-scatter.65.cloned.1.call-update) | async-done | bytes 1769488 | tf_op jit(solution)/shard_map/reduce_scatter | solution.py:108
  2626.5 104.3 %reduce-scatter.67.cloned.1.call-done = bf16[3,192,1536]{2,1,0:T(8,128)(2,1)} async-done(((bf16[3,1536,1536]{2,1,0:T(8,128)(2,1)}), bf16[3,192,1536]{2,1,0:T(8,128)(2,1)}) %reduce-scatter.67.cloned.1.call-update) | async-done | bytes 1769488 | tf_op jit(solution)/shard_map/reduce_scatter | solution.py:108
  2738.1 23.1 all-reduce.304
  2768.6 36.7 %reduce-scatter.87.cloned.1.call-done = bf16[96,4]{1,0:T(8,128)(2,1)} async-done(((bf16[768,4]{1,0:T(8,128)(2,1)}), bf16[96,4]{1,0:T(8,128)(2,1)}) %reduce-scatter.87.cloned.1.call-update) | async-done | bytes 784
  2806.1 36.3 %reduce-scatter.91.cloned.1.call-done = bf16[96,4]{1,0:T(8,128)(2,1)} async-done(((bf16[768,4]{1,0:T(8,128)(2,1)}), bf16[96,4]{1,0:T(8,128)(2,1)}) %reduce-scatter.91.cloned.1.call-update) | async-done | bytes 784
  2843.2 36.5 %reduce-scatter.89.cloned.1.call-done = bf16[96,4]{1,0:T(8,128)(2,1)} async-done(((bf16[768,4]{1,0:T(8,128)(2,1)}), bf16[96,4]{1,0:T(8,128)(2,1)}) %reduce-scatter.89.cloned.1.call-update) | async-done | bytes 784
  2880.5 11.9 all-reduce.306
  2902.1 292.4 %all-reduce.310.cloned.1.call-done = (bf16[96,2304]{0,1:T(8,128)(2,1)}, bf16[96,2304]{0,1:T(8,128)(2,1)}, bf16[96,768]{1,0:T(8,128)(2,1)}, bf16[96,768]{1,0:T(8,...) async-done(((bf16[96,2304]{0,1:T(8,128)(2,1)}, ...) | async-done | bytes 8355856 | tf_op jit(solution)/shard_map/psum | solution.py:122
  (2895 shorter events, 1767.9 us)
Async XLA Ops:
  7.2 39.4 %all-gather.32.cloned.1.call-start = ((), (), s32[]{:S(2)}) async-start(), calls=%async_computation.24 | async-start | bytes 3981312 | tf_op jit(solution)/shard_map/all_gather | solution.py:484
  7.9 101.3 %all-gather.44.cloned.1.call-start = ((), (), s32[]{:S(2)}) async-start(), calls=%async_computation.30 | async-start | bytes 1769472 | tf_op jit(solution)/shard_map/all_gather | solution.py:494
  8.7 107.2 %all-gather.46.cloned.1.call-start = ((), (), s32[]{:S(2)}) async-start(), calls=%async_computation.31 | async-start | bytes 2654208 | tf_op jit(solution)/shard_map/all_gather | solution.py:489
  9.4 878.5 %all-gather.48.cloned.1.call-start = ((), (), s32[]{:S(2)}) async-start(), calls=%async_computation.32 | async-start | bytes 1327104 | tf_op jit(solution)/shard_map/all_gather | solution.py:492
  10.0 883.7 %all-gather.52.cloned.1.call-start = ((), (), s32[]{:S(2)}) async-start(), calls=%async_computation.34 | async-start | bytes 3538944 | tf_op jit(solution)/shard_map/all_gather | solution.py:172
  10.1 39.6 %copy-start.170 = (bf16[2,128,768]{2,1,0:T(8,128)(2,1)}, bf16[2,128,768]{2,1,0:T(8,128)(2,1)S(1)}, u32[]{:S(2)}) copy-start(bf16[2,128,768]{2,1,0:T(8,128)(2,1)S(1)} %get-tuple-element.1271) | copy-start | bytes 1179652
  10.1 42.4 %copy-start.168 = (bf16[2,128,768]{2,1,0:T(8,128)(2,1)}, bf16[2,128,768]{2,1,0:T(8,128)(2,1)S(1)}, u32[]{:S(2)}) copy-start(bf16[2,128,768]{2,1,0:T(8,128)(2,1)S(1)} %get-tuple-element.1270) | copy-start | bytes 1179652
  51.5 842.2 %all-gather.54.cloned.1.call-start = ((), (), s32[]{:S(2)}) async-start(), calls=%async_computation.35 | async-start | bytes 3538944 | tf_op jit(solution)/shard_map/all_gather | solution.py:171
  52.5 855.8 %all-gather.34.cloned.1.call-start = ((), (), s32[]{:S(2)}) async-start(), calls=%async_computation.25 | async-start | bytes 3538944 | tf_op jit(solution)/shard_map/all_gather | solution.py:172
  57.4 850.9 %all-gather.36.cloned.1.call-start = ((), (), s32[]{:S(2)}) async-start(), calls=%async_computation.26 | async-start | bytes 3538944 | tf_op jit(solution)/shard_map/all_gather | solution.py:171
  58.5 863.8 %all-gather.38.cloned.1.call-start = ((), (), s32[]{:S(2)}) async-start(), calls=%async_computation.27 | async-start | bytes 1327104 | tf_op jit(solution)/shard_map/all_gather | solution.py:485
  59.3 32.7 %copy-start.547 = (u32[32]{0:T(128)S(1)}, u32[32]{0:T(128)}, u32[]{:S(2)}) copy-start(u32[32]{0:T(128)} %constant.963) | copy-start | bytes 388
  59.3 34.0 %copy-start.565 = (bf16[96]{0:T(256)(128)(2,1)S(1)}, bf16[96]{0:T(256)(128)(2,1)}, u32[]{:S(2)}) copy-start(bf16[96]{0:T(256)(128)(2,1)} %param.53) | copy-start | bytes 580
  59.3 34.2 %copy-start.566 = (bf16[96]{0:T(256)(128)(2,1)S(1)}, bf16[96]{0:T(256)(128)(2,1)}, u32[]{:S(2)}) copy-start(bf16[96]{0:T(256)(128)(2,1)} %param.54) | copy-start | bytes 580
  59.3 48.0 %copy-start.237 = (bf16[4,128,768]{2,1,0:T(8,128)(2,1)S(1)}, bf16[4,128,768]{2,1,0:T(8,128)(2,1)}, u32[]{:S(2)}) copy-start(bf16[4,128,768]{2,1,0:T(8,128)(2,1)} %param.61) | copy-start | bytes 2359300
  59.3 48.0 %copy-start.238 = (bf16[4,128,768]{2,1,0:T(8,128)(2,1)S(1)}, bf16[4,128,768]{2,1,0:T(8,128)(2,1)}, u32[]{:S(2)}) copy-start(bf16[4,128,768]{2,1,0:T(8,128)(2,1)} %param.60) | copy-start | bytes 2359300
  59.3 867.8 %all-gather.40.cloned.1.call-start = ((), (), s32[]{:S(2)}) async-start(), calls=%async_computation.28 | async-start | bytes 5308416 | tf_op jit(solution)/shard_map/all_gather | solution.py:486
  59.9 879.1 %all-gather.42.cloned.1.call-start = ((), (), s32[]{:S(2)}) async-start(), calls=%async_computation.29 | async-start | bytes 5308416 | tf_op jit(solution)/shard_map/all_gather | solution.py:488
  60.6 904.5 %all-gather.50.cloned.1.call-start = ((), (), s32[]{:S(2)}) async-start(), calls=%async_computation.33 | async-start | bytes 15925248 | tf_op jit(solution)/shard_map/all_gather | solution.py:493
  61.2 1636.1 %reduce-scatter.73.cloned.1.call-start = ((), (), s32[]{:S(2)}) async-start(), calls=%async_computation.50 | async-start | bytes 3538944
  63.2 46.0 %copy-start.537 = (s32[1,4,2,128]{3,1,2,0:T(4,128)}, s32[1,4,2,128]{3,1,2,0:T(4,128)S(1)}, u32[]{:S(2)}) copy-start(s32[1,4,2,128]{3,1,2,0:T(4,128)S(1)} %copy.224) | copy-start | bytes 12292
  63.5 820.0 %copy-start.376 = (s32[2,512]{1,0:T(2,128)}, s32[2,512]{1,0:T(2,128)S(1)}, u32[]{:S(2)}) copy-start(s32[2,512]{1,0:T(2,128)S(1)} %convert_reduce_fusion) | copy-start | bytes 12292
  701.4 40.9 %copy-start.59 = (f32[2,512,384]{2,1,0:T(8,128)}, f32[2,512,384]{2,1,0:T(8,128)S(1)}, u32[]{:S(2)}) copy-start(f32[2,512,384]{2,1,0:T(8,128)S(1)} %pad.1011) | copy-start | bytes 4718596
  944.1 29.2 copy-start.185
  945.1 20.0 collective-permute-start.3
  946.6 26.7 collective-permute-start.2
  976.6 7.0 collective-permute-start.1
  977.9 7.7 collective-permute-start
  995.2 16.5 collective-permute-start.5
  998.8 14.3 collective-permute-start.4
  1001.1 100.4 %collective-permute-start.7 = (bf16[2,1,1536]{2,1,0:T(2,128)(2,1)}, bf16[2,1,1536]{2,1,0:T(2,128)(2,1)}, u32[]{:S(2)}, u32[]{:S(2)}) collective-permute-start(bf16[2,1,1536]{2,1,0:T(2,128)(2,1)} %get-tuple-element.1267), channel_id=1, source_target_pairs={{0,1},{1,2},{2,3},{3,4},{4,5},{5,6},{6,7},{8,9},{9,10},{10,11},{11... | collective-permute-start | bytes 18440 | tf_op jit(solution)/shard_map/ppermute | solution.py:35
  1006.1 147.9 %collective-permute-start.6 = (bf16[2,1,1536]{2,1,0:T(2,128)(2,1)}, bf16[2,1,1536]{2,1,0:T(2,128)(2,1)}, u32[]{:S(2)}, u32[]{:S(2)}) collective-permute-start(bf16[2,1,1536]{2,1,0:T(2,128)(2,1)} %get-tuple-element.1266), channel_id=1, source_target_pairs={{1,0},{2,1},{3,2},{4,3},{5,4},{6,5},{7,6},{9,8},{10,9},{11,10},{12... | collective-permute-start | bytes 18440 | tf_op jit(solution)/shard_map/ppermute | solution.py:38
  1063.0 34.6 %copy-start.509 = (f32[256]{0:T(256)S(1)}, f32[256]{0:T(256)}, u32[]{:S(2)}) copy-start(f32[256]{0:T(256)} %copy-done.508) | copy-start | bytes 3076
  1225.7 475.4 %reduce-scatter.75.cloned.1.call-start = ((), (), s32[]{:S(2)}) async-start(), calls=%async_computation.51 | async-start | bytes 3538944
  1351.5 432.7 %reduce-scatter.77.cloned.1.call-start = ((), (), s32[]{:S(2)}) async-start(), calls=%async_computation.52 | async-start | bytes 3538944
  1396.2 389.7 %reduce-scatter.79.cloned.1.call-start = ((), (), s32[]{:S(2)}) async-start(), calls=%async_computation.53 | async-start | bytes 3538944
  1401.3 334.6 %copy-start.9 = (f32[2,512,768]{2,1,0:T(8,128)}, f32[2,512,768]{2,1,0:T(8,128)S(1)}, u32[]{:S(2)}) copy-start(f32[2,512,768]{2,1,0:T(8,128)S(1)} %fusion.222) | copy-start | bytes 9437188
  1568.6 626.6 %reduce-scatter.81.cloned.1.call-start = ((), (), s32[]{:S(2)}) async-start(), calls=%async_computation.54 | async-start | bytes 3981312
  1714.9 482.4 %reduce-scatter.83.cloned.1.call-start = ((), (), s32[]{:S(2)}) async-start(), calls=%async_computation.55 | async-start | bytes 3981312
  1797.3 402.0 %reduce-scatter.63.cloned.1.call-start = ((), (), s32[]{:S(2)}) async-start(), calls=%async_computation.45 | async-start | bytes 1327104 | tf_op jit(solution)/shard_map/reduce_scatter | solution.py:105
  1822.6 31.6 copy-start.137
  1827.1 31.4 copy-start.332
  1920.0 279.4 %reduce-scatter.61.cloned.1.call-start = ((), (), s32[]{:S(2)}) async-start(), calls=%async_computation.44 | async-start | bytes 1327104 | tf_op jit(solution)/shard_map/reduce_scatter | solution.py:105
  1948.9 250.4 %reduce-scatter.45.cloned.1.call-start = ((), (), s32[]{:S(2)}) async-start(), calls=%async_computation.36 | async-start | bytes 1327104 | tf_op jit(solution)/shard_map/reduce_scatter | solution.py:84
  2001.4 198.0 %reduce-scatter.47.cloned.1.call-start = ((), (), s32[]{:S(2)}) async-start(), calls=%async_computation.37 | async-start | bytes 1327104 | tf_op jit(solution)/shard_map/reduce_scatter | solution.py:84
  2079.0 120.4 %reduce-scatter.69.cloned.1.call-start = ((), (), s32[]{:S(2)}) async-start(), calls=%async_computation.48 | async-start | bytes 1769472 | tf_op jit(solution)/shard_map/reduce_scatter | solution.py:111
  2096.0 104.2 %reduce-scatter.71.cloned.1.call-start = ((), (), s32[]{:S(2)}) async-start(), calls=%async_computation.49 | async-start | bytes 1769472 | tf_op jit(solution)/shard_map/reduce_scatter | solution.py:111
  2131.1 115.0 %reduce-scatter.57.cloned.1.call-start = ((), (), s32[]{:S(2)}) async-start(), calls=%async_computation.42 | async-start | bytes 2654208 | tf_op jit(solution)/shard_map/reduce_scatter | solution.py:96
  2136.6 155.6 %reduce-scatter.59.cloned.1.call-start = ((), (), s32[]{:S(2)}) async-start(), calls=%async_computation.43 | async-start | bytes 2654208 | tf_op jit(solution)/shard_map/reduce_scatter | solution.py:96
  2143.8 205.6 %reduce-scatter.53.cloned.1.call-start = ((), (), s32[]{:S(2)}) async-start(), calls=%async_computation.40 | async-start | bytes 5308416 | tf_op jit(solution)/shard_map/reduce_scatter | solution.py:93
  2149.1 258.0 %reduce-scatter.55.cloned.1.call-start = ((), (), s32[]{:S(2)}) async-start(), calls=%async_computation.41 | async-start | bytes 5308416 | tf_op jit(solution)/shard_map/reduce_scatter | solution.py:93
  2154.4 310.0 %reduce-scatter.49.cloned.1.call-start = ((), (), s32[]{:S(2)}) async-start(), calls=%async_computation.38 | async-start | bytes 5308416 | tf_op jit(solution)/shard_map/reduce_scatter | solution.py:87
  2159.7 362.3 %reduce-scatter.51.cloned.1.call-start = ((), (), s32[]{:S(2)}) async-start(), calls=%async_computation.39 | async-start | bytes 5308416 | tf_op jit(solution)/shard_map/reduce_scatter | solution.py:87
  2165.1 461.4 %reduce-scatter.65.cloned.1.call-start = ((), (), s32[]{:S(2)}) async-start(), calls=%async_computation.46 | async-start | bytes 15925248 | tf_op jit(solution)/shard_map/reduce_scatter | solution.py:108
  2177.0 553.8 %reduce-scatter.67.cloned.1.call-start = ((), (), s32[]{:S(2)}) async-start(), calls=%async_computation.47 | async-start | bytes 15925248 | tf_op jit(solution)/shard_map/reduce_scatter | solution.py:108
  2190.6 577.2 %reduce-scatter.85.cloned.1.call-start = ((), (), s32[]{:S(2)}) async-start(), calls=%async_computation.56 | async-start | bytes 221184
  2192.2 613.1 %reduce-scatter.87.cloned.1.call-start = ((), (), s32[]{:S(2)}) async-start(), calls=%async_computation.57 | async-start | bytes 221184
  2193.2 649.2 %reduce-scatter.91.cloned.1.call-start = ((), (), s32[]{:S(2)}) async-start(), calls=%async_computation.59 | async-start | bytes 221184
  2194.2 685.6 %reduce-scatter.89.cloned.1.call-start = ((), (), s32[]{:S(2)}) async-start(), calls=%async_computation.58 | async-start | bytes 221184
  2195.1 999.4 %all-reduce.310.cloned.1.call-start = ((), (), s32[]{:S(2)}) async-start(), calls=%async_computation.60 | async-start | bytes 17301504 | tf_op jit(solution)/shard_map/psum | solution.py:122
  2735.5 159.8 %copy-start.94 = (bf16[128,2,768]{2,1,0:T(2,128)(2,1)S(1)}, bf16[128,2,768]{2,1,0:T(2,128)(2,1)}, u32[]{:S(2)}) copy-start(bf16[128,2,768]{2,1,0:T(2,128)(2,1)} %reshape.667) | copy-start | bytes 1179652
  2735.5 159.8 %copy-start.95 = (bf16[128,2,768]{2,1,0:T(2,128)(2,1)S(1)}, bf16[128,2,768]{2,1,0:T(2,128)(2,1)}, u32[]{:S(2)}) copy-start(bf16[128,2,768]{2,1,0:T(2,128)(2,1)} %reshape.669) | copy-start | bytes 1179652
  2735.5 159.9 %copy-start.97 = (bf16[128,2,768]{2,1,0:T(2,128)(2,1)S(1)}, bf16[128,2,768]{2,1,0:T(2,128)(2,1)}, u32[]{:S(2)}) copy-start(bf16[128,2,768]{2,1,0:T(2,128)(2,1)} %copy-done.96) | copy-start | bytes 1179652
  2736.8 158.7 %copy-start.99 = (bf16[128,2,768]{2,1,0:T(2,128)(2,1)S(1)}, bf16[128,2,768]{2,1,0:T(2,128)(2,1)}, u32[]{:S(2)}) copy-start(bf16[128,2,768]{2,1,0:T(2,128)(2,1)} %copy-done.98) | copy-start | bytes 1179652
  (575 other events, 2725.3 us)
Sparse Core Ops, SparseCore 0:
  9.9 36.6 all-gather.31
  48.5 25.6 all-gather.43
  76.1 29.2 all-gather.45
  107.1 24.0 all-gather.47
  132.9 32.8 all-gather.51
  167.5 32.8 all-gather.53
  202.3 32.8 all-gather.33
  237.0 32.8 all-gather.35
  271.7 24.0 all-gather.37
  297.5 38.9 all-gather.39
  338.4 38.9 all-gather.41
  379.1 78.7 all-gather.49
  1225.8 51.3 reduce-scatter.72
  1351.6 46.8 reduce-scatter.74
  1401.8 46.2 reduce-scatter.76
  1568.8 46.8 reduce-scatter.78
  1715.0 53.3 reduce-scatter.80
  1797.5 53.0 reduce-scatter.82
  1920.1 41.6 reduce-scatter.62
  1965.2 36.7 reduce-scatter.60
  2005.8 36.7 reduce-scatter.44
  2079.1 37.0 reduce-scatter.46
  2119.5 38.4 reduce-scatter.68
  2161.7 38.4 reduce-scatter.70
  2203.6 42.4 reduce-scatter.56
  2249.6 42.4 reduce-scatter.58
  2295.4 53.8 reduce-scatter.52
  2353.2 53.8 reduce-scatter.54
  2410.5 53.8 reduce-scatter.48
  2468.2 53.8 reduce-scatter.50
  2525.7 100.7 reduce-scatter.64
  2630.0 100.7 reduce-scatter.66
  2734.2 33.5 reduce-scatter.84
  2771.7 33.5 reduce-scatter.86
  2808.9 33.4 reduce-scatter.90
  2846.2 33.5 reduce-scatter.88
  2884.6 309.8 all-reduce.309
where the time goes:
time: 3260 us; the launch traced here: 3210 us
  local copies, waits for them, and re-layouts  1310 us (40%)
  waiting for transfers between devices  982 us (30%)
  other arithmetic  425 us (13%)
  blocking collectives  224 us (7%)
  matrix products  219 us (7%)
    slice x492, local copies, waits for them, and re-layouts, local_scan(): lax.associative_scan(affine, (decays, drives), axis=1, reverse=backwards)  787 us
    psum x1, waiting for transfers between devices, reduce_grads(): lax.psum(rows_part[0].astype(jnp.bfloat16), 'batch').astype(jnp.float32)  292 us
    reduce_scatter x2, waiting for transfers between devices, reduce_grads(): lax.psum_scatter(gradients[9].astype(jnp.bfloat16), 'seq', scatter_dimens...  209 us
    pad x252, local copies, waits for them, and re-layouts, local_scan(): lax.associative_scan(affine, (decays, drives), axis=1, reverse=backwards)  172 us
    all_gather x16, blocking collectives, prefix(): gathered = jax.tree.map(lambda a: lax.all_gather(a, axis), part)  150 us
    unnamed x1195, local copies, waits for them, and re-layouts  150 us
    unnamed x47, waiting for transfers between devices  121 us
    reduce_scatter x2, waiting for transfers between devices, reduce_grads(): lax.psum_scatter(gradients[2].astype(jnp.bfloat16), 'seq', scatter_dimens...  115 us
  transfers between devices with their start and end apart: 45, of which 15 were waited for; matrix products, arithmetic and copies ran while one was open for 56% of the time, Pallas kernels for 0%

commit v1 on v0

v1 whole, which is shorter than its diff:
```python
import functools

import jax
import jax.numpy as jnp
from jax import lax
from jax.experimental import pallas as pl
from jax.experimental.pallas import tpu as pltpu
from jax.sharding import PartitionSpec as P

HEADS = 12
NCHAR = 256
NORM_EPS = 1e-06
LANES = 128
SMALL_ROWS = 16
RIDE = 32
SCALE = 1000
F32 = jnp.float32
BF16 = jnp.bfloat16
VMEM_BYTES = 60 << 20


def dot(left, right, left_dim, right_dim):
    return lax.dot_general(
        left, right, (((left_dim,), (right_dim,)), ((), ())), preferred_element_type=F32
    )


def params(grid_rank):
    return pltpu.CompilerParams(
        dimension_semantics=("arbitrary",) * grid_rank, vmem_limit_bytes=VMEM_BYTES
    )


def shape(dims, dtype):
    return jax.ShapeDtypeStruct(dims, dtype)


def whole(dims):
    return pl.BlockSpec(dims, lambda *_: (0,) * len(dims))


def cost(flops, nbytes):
    return pl.CostEstimate(flops=int(flops) * SCALE, bytes_accessed=int(nbytes) * SCALE, transcendentals=0)


LATEST = []


def launch(
    body, grid, prefetch, inputs, in_specs, out_specs, out_shape, scratch, price, name, carry=()
):
    deps = LATEST[-1:]
    single = not isinstance(out_shape, (list, tuple))
    outs = [out_shape] if single else list(out_shape)
    specs = [out_specs] if single else list(out_specs)
    lead = len(prefetch) + len(inputs)
    extra = len(carry) + len(deps)
    anywhere = pl.BlockSpec(memory_space=pl.ANY)

    def kernel(*refs):
        own = refs[lead + extra :]
        body(*refs[:lead], *own[: len(outs)], *own[len(outs) + len(carry) :])

    results = pl.pallas_call(
        kernel,
        grid_spec=pltpu.PrefetchScalarGridSpec(
            num_scalar_prefetch=len(prefetch),
            grid=grid,
            in_specs=list(in_specs) + [anywhere] * extra,
            out_specs=specs + [anywhere] * len(carry),
            scratch_shapes=scratch,
        ),
        out_shape=outs + [shape(v.shape, v.dtype) for v in carry],
        input_output_aliases={lead + i: len(outs) + i for i in range(len(carry))},
        compiler_params=params(len(grid)),
        cost_estimate=price,
        name=name,
    )(*prefetch, *inputs, *carry, *deps)
    LATEST[:] = results[len(outs) - 1 : len(outs)]
    return results[0] if len(results) == 1 else results


def flat_block(ref):
    block = ref[...]
    return block.reshape(block.shape[0] * block.shape[1], block.shape[2])


def norm_forward(values):
    center = values - jnp.mean(values, -1, keepdims=True)
    rstd = lax.rsqrt(jnp.mean(center * center, -1, keepdims=True) + NORM_EPS)
    return center * rstd, rstd


def norm_backward(normal, rstd, gain, gradient):
    scaled = gradient * gain
    first = jnp.mean(scaled, -1, keepdims=True)
    second = jnp.mean(scaled * normal, -1, keepdims=True)
    return rstd * (scaled - first - normal * second)


def column_sum(values):
    return jnp.sum(values, 0, keepdims=True)


def gelu_parts(values):
    size = jnp.abs(values) * 0.7071067811865476
    bell = jnp.exp(-size * size)
    t = 1.0 / (1.0 + 0.3275911 * size)
    series = t * (
        0.254829592
        + t * (-0.284496736 + t * (1.421413741 + t * (-1.453152027 + t * 1.061405429)))
    )
    tail = 0.5 * series * bell
    phi_sum = jnp.where(values < 0, tail, 1.0 - tail)
    return values * phi_sum, phi_sum + values * (bell * 0.3989422804014327)


def qkv_kernel(seqs, toks, per, x_ref, w_ref, o_ref):
    acc = dot(x_ref[...], flat_block(w_ref), 1, 0)
    turned = acc.T.astype(BF16)
    width = turned.shape[0] // HEADS
    for s in range(seqs):
        for h in range(HEADS):
            pair = s * HEADS + h
            o_ref[pair // per, pair % per, 0] = turned[
                h * width : (h + 1) * width, s * toks : (s + 1) * toks
            ]


def qkv_call(rows, packed, base, seqs, count):
    total, width = rows.shape
    toks = total // seqs
    per = seqs * HEADS // count
    head = width // HEADS
    blk = width // count
    return launch(
        functools.partial(qkv_kernel, seqs, toks, per),
        (3,),
        [],
        [rows, packed],
        [ whole(rows.shape), pl.BlockSpec((count, blk, width), lambda j: (0, base + j, 0)), ],
        pl.BlockSpec((count, per, 1, head, toks), lambda j: (0, 0, j, 0, 0)),
        shape((count, per, 3, head, toks), BF16),
        [],
        cost(6 * total * width * width, 6 * width * width + 8 * total * width),
        "qkv",
    )


def spread(ref, index):
    return jnp.concatenate([ref[(i, *index)] for i in range(ref.shape[0])], axis=1)


def attend_kernel(step, scale, x_ref, o_ref, total_ref):
    queries = spread(x_ref, (0, 0)) * scale
    keys = spread(x_ref, (0, 1)).T
    values = spread(x_ref, (0, 2))
    toks = x_ref.shape[-1]
    for begin in range(0, queries.shape[1], step):
        scores = dot(keys, queries[:, begin : begin + step], 1, 0)
        highest = jnp.max(scores, 0, keepdims=True)
        expo = jnp.exp(scores - highest)
        totals = jnp.sum(expo, 0, keepdims=True)
        mixture = (dot(values, expo.astype(BF16), 1, 0) / totals).astype(BF16)
        total_ref[0, :, begin : begin + step] = highest + jnp.log(totals)
        for at in range(0, step, toks):
            o_ref[(begin + at) // toks, 0] = mixture[:, at : at + toks]


def attend_call(qkv, step):
    count, per, _, head, toks = qkv.shape
    length = count * toks
    scale = head**-0.5
    return launch(
        functools.partial(attend_kernel, step, scale),
        (per,),
        [],
        [qkv],
        [pl.BlockSpec((count, 1, 3, head, toks), lambda p: (0, p, 0, 0, 0))],
        [ pl.BlockSpec((count, 1, head, toks), lambda p: (0, p, 0, 0)), pl.BlockSpec((1, 1, length), lambda p: (p, 0, 0)), ],
        [shape((count, per, head, toks), BF16), shape((per, 1, length), F32)],
        [],
        cost(16 * per * length * length * head, 8 * per * length * head),
        "attend",
    )


def attend_back_kernel(step, scale, x_ref, g_ref, total_ref, o_ref):
    queries = spread(x_ref, (0, 0)) * scale
    keys_t = spread(x_ref, (0, 1))
    keys = keys_t.T
    values = spread(x_ref, (0, 2)).T
    grads = spread(g_ref, ())
    toks = x_ref.shape[-1]
    length = queries.shape[1]
    d_keys = jnp.zeros(queries.shape, F32)
    d_values = jnp.zeros(queries.shape, F32)
    for begin in range(0, length, step):
        query = queries[:, begin : begin + step]
        grad = grads[:, begin : begin + step]
        scores = dot(keys, query, 1, 0)
        probability = jnp.exp(scores - total_ref[0, :, begin : begin + step])
        d_prob = dot(values, grad, 1, 0)
        centered = jnp.sum(probability * d_prob, 0, keepdims=True)
        d_scores = (probability * (d_prob - centered)).astype(BF16)
        d_values += dot(grad, probability.astype(BF16), 1, 1)
        d_keys += dot(query, d_scores, 1, 1)
        d_query = (dot(keys_t, d_scores, 1, 0) * scale).astype(BF16)
        for at in range(0, step, toks):
            o_ref[(begin + at) // toks, 0, 0] = d_query[:, at : at + toks]
    d_keys = d_keys.astype(BF16)
    d_values = d_values.astype(BF16)
    for i in range(length // toks):
        o_ref[i, 0, 1] = d_keys[:, i * toks : (i + 1) * toks]
        o_ref[i, 0, 2] = d_values[:, i * toks : (i + 1) * toks]


def attend_back_call(qkv, grads, totals, step):
    count, per, _, head, toks = qkv.shape
    length = count * toks
    scale = head**-0.5
    return launch(
        functools.partial(attend_back_kernel, step, scale),
        (per,),
        [],
        [qkv, grads, totals],
        [ pl.BlockSpec((count, 1, 3, head, toks), lambda p: (0, p, 0, 0, 0)), pl.BlockSpec((count, head, toks), lambda p: (0, p, 0)), pl.BlockSpec((1, 1, length), lambda p: (p, 0, 0)), ],
        pl.BlockSpec((count, 1, 3, head, toks), lambda p: (0, p, 0, 0, 0)),
        shape(qkv.shape, BF16),
        [],
        cost(40 * per * length * length * head, 14 * per * length * head),
        "attend_back",
    )


def ffn_kernel(
    seqs,
    o_ref,
    x_ref,
    w_out_ref,
    w_up_ref,
    w_down_ref,
    bias_ref,
    norms_ref,
    mix_ref,
    normal0_ref,
    rstd0_ref,
    a_ref,
    g_ref,
    slope_ref,
    normal1_ref,
    rstd1_ref,
    f_ref,
    acc_ref,
):
    j = pl.program_id(0)
    per = o_ref.shape[1]
    head, toks = o_ref.shape[2:]

    @pl.when(j == 0)
    def _():
        for s in range(seqs):
            for h in range(HEADS):
                pair = s * HEADS + h
                mix_ref[h * head : (h + 1) * head, s * toks : (s + 1) * toks] = o_ref[
                    pair // per, pair % per
                ]
        attended = dot(mix_ref[...].T, flat_block(w_out_ref), 1, 0)
        normal, rstd = norm_forward(x_ref[...].astype(F32) + attended)
        normal0_ref[...] = normal
        rstd0_ref[...] = rstd
        normed = normal * norms_ref[0:1] + norms_ref[4:5]
        a_ref[...] = normed.astype(BF16)
        acc_ref[...] = normed

    up = dot(a_ref[...], flat_block(w_up_ref), 1, 0) + bias_ref[...]
    active, slope = gelu_parts(up)
    active = active.astype(BF16)
    g_ref[...] = active
    slope_ref[...] = slope
    acc_ref[...] += dot(active, flat_block(w_down_ref), 1, 0)

    @pl.when(j == pl.num_programs(0) - 1)
    def _():
        normal, rstd = norm_forward(acc_ref[...])
        normal1_ref[...] = normal
        rstd1_ref[...] = rstd
        f_ref[...] = (normal * norms_ref[1:2] + norms_ref[5:6]).astype(BF16)


def ffn_call(mixture, rows, packed, at_out, at_up, at_down, bias, norms, seqs):
    count, per, head, toks = mixture.shape
    total, width = rows.shape
    hidden = bias.shape[1]
    chunks = hidden // width
    blk = width // count
    owners = count // chunks
    return launch(
        functools.partial(ffn_kernel, seqs),
        (chunks,),
        [],
        [mixture, rows, packed, packed, packed, bias, norms],
        [ whole(mixture.shape), whole(rows.shape), pl.BlockSpec((count, blk, width), lambda j: (0, at_out, 0)), pl.BlockSpec((count, blk, width), lambda j: (0, at_up + j, 0)), pl.BlockSpec((owners, hidden // count, width), lambda j: (j, at_down, 0)), pl.BlockSpec((1, width), lambda j: (0, j)), whole(norms.shape), ],
        [ whole((width, total)), whole((total, width)), whole((total, 1)), whole((total, width)), pl.BlockSpec((total, width), lambda j: (0, j)), pl.BlockSpec((total, width), lambda j: (0, j)), whole((total, width)), whole((total, 1)), whole((total, width)), ],
        [ shape((width, total), BF16), shape((total, width), F32), shape((total, 1), F32), shape((total, width), BF16), shape((total, hidden), BF16), shape((total, hidden), F32), shape((total, width), F32), shape((total, 1), F32), shape((total, width), BF16), ],
        [pltpu.VMEM((total, width), F32)],
        cost( 2 * total * width * (width + 2 * hidden), 4 * hidden * width + 10 * total * hidden ),
        "ffn",
    )


def ffn_back_kernel(
    seqs,
    slot_ref,
    order_ref,
    d_ref,
    g_ref,
    slope_ref,
    a_ref,
    normal_ref,
    rstd_ref,
    norms_ref,
    w_out_ref,
    w_up_ref,
    w_down_ref,
    total_ref,
    *refs,
):
    j = pl.program_id(0)
    count, blk, width = w_up_ref.shape
    owners, share, _ = w_down_ref.shape
    half = count // 2
    send_refs, refs = refs[:half], refs[half:]
    keep_ref, bias_ref, d_attn_ref, d_attended_ref, sums_ref, d_mix_ref = refs[:6]
    db_ref, at_ref, acc_ref, part_ref = refs[6:]

    @pl.when(j == 0)
    def _():
        db_ref[...] = d_ref[...].astype(BF16)
        at_ref[...] = a_ref[...].T
        acc_ref[...] = d_ref[...]

    part_ref[...] = dot(g_ref[...].T, db_ref[...], 1, 0)
    for i in range(owners):
        slot = slot_ref[j * owners + i]
        piece = part_ref[i * share : (i + 1) * share, :].astype(BF16)

        @pl.when(slot < half)
        def _():
            keep_ref[slot, 0:share, :] = piece

        for at, send_ref in enumerate(send_refs):

            @pl.when(slot == half + at)
            def _():
                send_ref[0:share, :] = piece

    d_up = (dot(db_ref[...], flat_block(w_down_ref), 1, 1) * slope_ref[...]).astype(BF16)
    bias_ref[...] = column_sum(d_up.astype(F32))
    part_ref[...] = dot(at_ref[...], d_up, 1, 0)
    place = pl.ds(pl.multiple_of(share + j * blk, 16), blk)
    for pos in range(count):
        piece = part_ref[pl.ds(pl.multiple_of(order_ref[pos] * blk, 16), blk), :].astype(BF16)
        if pos < half:
            keep_ref[pos, place, :] = piece
        else:
            send_refs[pos - half][place, :] = piece
    acc_ref[...] += dot(d_up, flat_block(w_up_ref), 1, 1)

    @pl.when(j == pl.num_programs(0) - 1)
    def _():
        gradient = acc_ref[...]
        normal = normal_ref[...]
        sums_ref[0:1, :] = column_sum(gradient * normal)
        sums_ref[1:2, :] = column_sum(gradient)
        d_sum = norm_backward(normal, rstd_ref[...], norms_ref[0:1], gradient)
        d_attn_ref[...] = d_sum
        low = d_sum.astype(BF16)
        d_attended_ref[...] = low
        turned = dot(flat_block(w_out_ref), low, 1, 1).astype(BF16)
        per = seqs * HEADS // count
        head, toks = width // HEADS, d_mix_ref.shape[2]
        for s in range(seqs):
            for h in range(HEADS):
                pair = s * HEADS + h
                row = pair % per * head
                d_mix_ref[pair // per, row : row + head] = turned[
                    h * head : (h + 1) * head, s * toks : (s + 1) * toks
                ]
        rest = jnp.concatenate([total_ref[j] for j in range(total_ref.shape[0])], 0)
        rest = jnp.concatenate([rest, jnp.zeros((RIDE - rest.shape[0], LANES), F32)], 0)
        for part in range(3):
            low = rest.astype(BF16)
            rest = rest - low.astype(F32)
            row = per * head + part * RIDE
            for device in range(count):
                d_mix_ref[device, row : row + RIDE] = low


def ffn_back_call(
    slot, order, d_ffn, active, slope, normed, normal, rstd, norms, packed, at_out, at_up, at_down, totals, seqs):
    total, width = d_ffn.shape
    hidden = active.shape[1]
    count = packed.shape[0]
    chunks = hidden // width
    blk = width // count
    share = hidden // count
    owners = count // chunks
    per = seqs * HEADS // count
    head = width // HEADS
    toks = total // seqs
    rows_out = share + chunks * blk
    wide = pl.BlockSpec((total, width), lambda j, *_: (0, j))
    results = launch(
        functools.partial(ffn_back_kernel, seqs),
        (chunks,),
        [slot, order],
        [d_ffn, active, slope, normed, normal, rstd, norms, packed, packed, packed, totals],
        [ whole(d_ffn.shape), wide, wide, whole(normed.shape), whole(normal.shape), whole(rstd.shape), whole(norms.shape), pl.BlockSpec((count, blk, width), lambda j, *_: (0, at_out, 0)), pl.BlockSpec((count, blk, width), lambda j, *_: (0, at_up + j, 0)), pl.BlockSpec((owners, share, width), lambda j, *_: (j, at_down, 0)), whole(totals.shape), ],
        [ *[whole((rows_out, width))] * (count // 2), whole((count // 2, rows_out, width)), pl.BlockSpec((1, width), lambda j, *_: (0, j)), whole((total, width)), whole((total, width)), whole((2, width)), whole((count, per * head + 3 * RIDE, toks)), ],
        [ *[shape((rows_out, width), BF16)] * (count // 2), shape((count // 2, rows_out, width), BF16), shape((1, hidden), F32), shape((total, width), F32), shape((total, width), BF16), shape((2, width), F32), shape((count, per * head + 3 * RIDE, toks), BF16), ],
        [ pltpu.VMEM((total, width), BF16), pltpu.VMEM((width, total), BF16), pltpu.VMEM((total, width), F32), pltpu.VMEM((width, width), F32), ],
        cost( 8 * total * width * hidden + 2 * total * width * width, 8 * hidden * width + 10 * total * hidden, ),
        "ffn_back",
    )
    return results[: count // 2], *results[count // 2 :]


def gates_kernel(
    seqs, groups_ref, ids_ref, back_ids_ref, table_ref, w_fwd_ref, w_rev_ref, bias_ref,
    z_ref, c_ref, totals_ref,
):
    s = pl.program_id(0)
    steps = ids_ref.shape[1]
    rows = 2 * seqs
    table = flat_block(table_ref)
    vocabulary = lax.broadcasted_iota(jnp.int32, (steps, NCHAR), 1)
    chunks = z_ref.shape[0]
    half = chunks * LANES
    for direction, (source, weight) in enumerate(((ids_ref, w_fwd_ref), (back_ids_ref, w_rev_ref))):
        onehot = jnp.where(source[0] == vocabulary, 1.0, 0.0).astype(BF16)
        embedded = dot(onehot, table, 1, 0).astype(BF16)
        gate_input = dot(embedded, flat_block(weight), 1, 0)
        own = slice(direction * half, (direction + 1) * half)
        update = jax.nn.sigmoid(gate_input[:, :half] + bias_ref[8:9, own])
        candidate = jnp.tanh(gate_input[:, half:] + bias_ref[9:10, own])
        place = pl.ds(s + direction * seqs, steps, stride=rows)
        for j in range(chunks):
            z_ref[j, place, :] = update[:, j * LANES : (j + 1) * LANES]
            c_ref[j, place, :] = candidate[:, j * LANES : (j + 1) * LANES]

    @pl.when(s == pl.num_programs(0) - 1)
    def _():
        def one(t, carry):
            states, products = carry
            place = pl.ds(pl.multiple_of(t * rows, rows), rows)
            new_states, new_products = [], []
            for j in range(chunks):
                update = z_ref[j, place, :]
                decay = 1.0 - update
                new_states.append(decay * states[j] + update * c_ref[j, place, :])
                new_products.append(products[j] * decay)
            return tuple(new_states), tuple(new_products)

        zero = jnp.zeros((rows, LANES), F32)
        states, products = lax.fori_loop(
            0, steps, one, ((zero,) * chunks, (zero + 1.0,) * chunks), unroll=8
        )
        for j in range(chunks):
            totals_ref[0, j] = products[j]
            totals_ref[1, j] = states[j]


def gates_call(groups, ids, packed, at_gru, at_table, bias):
    seqs, steps = ids.shape
    count, _, width = packed.shape
    blk = width // count
    table_rows = 4 * NCHAR // count
    per_group = NCHAR // table_rows
    chunks = width // 2 // LANES
    laid = (chunks, steps * 2 * seqs, LANES)
    return launch(
        functools.partial(gates_kernel, seqs),
        (seqs,),
        [groups],
        [ids[..., None], ids[:, ::-1, None], packed, packed, packed, bias],
        [ pl.BlockSpec((1, steps, 1), lambda s, g: (s, 0, 0)), pl.BlockSpec((1, steps, 1), lambda s, g: (s, 0, 0)), pl.BlockSpec((per_group, table_rows, width), lambda s, g: (g[s], at_table, 0)), pl.BlockSpec((count, blk, width), lambda s, g: (0, at_gru, 0)), pl.BlockSpec((count, blk, width), lambda s, g: (0, at_gru + 1, 0)), whole(bias.shape), ],
        [whole(laid), whole(laid), whole((2, chunks, 2 * seqs, LANES))],
        [shape(laid, F32), shape(laid, F32), shape((2, chunks, 2 * seqs, LANES), F32)],
        [],
        cost( 2 * seqs * steps * width * (2 * NCHAR + 2 * width), 16 * seqs * steps * width ),
        "gates",
    )


def entry_state(me, totals, products, rows, seqs, forward):
    count, chunks = products.shape[0], products.shape[1]
    first = lax.broadcasted_iota(jnp.int32, (rows, LANES), 0) < seqs
    result = []
    for j in range(chunks):
        state = jnp.zeros((rows, LANES), F32)
        for lap in range(count):
            up, down = lap, count - 1 - lap
            one, other = (up, down) if forward else (down, up)
            product = jnp.where(first, products[one, j], products[other, j])
            total = jnp.where(first, totals[one, j], totals[other, j])
            up_in, down_in = (up < me).astype(F32), (down > me).astype(F32)
            ahead = jnp.where(first, up_in, down_in) if forward else jnp.where(first, down_in, up_in)
            state = jnp.where(ahead > 0.5, product * state + total, state)
        result.append(state)
    return result


def states_kernel(
    seqs, me_ref, z_ref, c_ref, all_ref, starts_ref, ends_ref, lens_ref, w_ref,
    prior_ref, pooled_ref, proj_ref, proj_low_ref, hold_ref, state_ref, acc_ref,
):
    i = pl.program_id(0)
    last = pl.num_programs(0) - 1
    rows = 2 * seqs
    chunks = z_ref.shape[0]
    span = z_ref.shape[1] // rows
    toks = starts_ref.shape[1]
    half = chunks * LANES

    @pl.when(i == 0)
    def _():
        entry = entry_state(me_ref[0], all_ref[:, 1], all_ref[:, 0], rows, seqs, True)
        for j in range(chunks):
            state_ref[j] = entry[j]
        acc_ref[...] = jnp.zeros_like(acc_ref)

    def one(t, states):
        place = pl.ds(pl.multiple_of(t * rows, rows), rows)
        result = []
        for j in range(chunks):
            prior_ref[j, place, :] = states[j]
            update = z_ref[j, place, :]
            state = (1.0 - update) * states[j] + update * c_ref[j, place, :]
            hold_ref[j, place, :] = state
            result.append(state)
        return tuple(result)

    states = lax.fori_loop(0, span, one, tuple(state_ref[j] for j in range(chunks)), unroll=8)
    for j in range(chunks):
        state_ref[j] = states[j]
    count = lax.broadcasted_iota(jnp.int32, (toks, span), 1) + i * span
    for direction in range(2):
        place_of = count if direction == 0 else (last + 1) * span - 1 - count
        for s in range(seqs):
            member = jnp.where(
                (place_of >= starts_ref[s]) & (place_of < ends_ref[s]), 1.0, 0.0
            ).astype(BF16)
            held = jnp.concatenate(
                [
                    hold_ref[j, pl.ds(s + direction * seqs, span, stride=rows), :]
                    for j in range(chunks)
                ],
                axis=1,
            ).astype(BF16)
            acc_ref[s * toks : (s + 1) * toks, direction * half : (direction + 1) * half] += dot(
                member, held, 1, 0
            )

    @pl.when(i == last)
    def _():
        for s in range(seqs):
            rows_of = slice(s * toks, (s + 1) * toks)
            pooled_ref[rows_of, :] = (acc_ref[rows_of, :] / lens_ref[s]).astype(BF16)
        proj = dot(pooled_ref[...], flat_block(w_ref), 1, 0)
        proj_ref[...] = proj
        proj_low_ref[...] = proj.astype(BF16)


def collect_kernel(me_ref, *refs):
    for mask, ref in enumerate(refs[:-1]):
        refs[-1][me_ref[0] ^ mask] = ref[...]


def collect(me, parts):
    out = (len(parts), *parts[0].shape)
    return launch(
        collect_kernel,
        (1,),
        [me],
        parts,
        [whole(v.shape) for v in parts],
        whole(out),
        shape(out, parts[0].dtype),
        [],
        cost(0, 8 * len(parts) * parts[0].size),
        "collect",
    )


def states_call(me, z, c, gathered, starts, ends, lens, packed, at_char, parts):
    chunks, length, _ = z.shape
    seqs, toks, _ = starts.shape
    count, _, width = packed.shape
    blk = width // count
    span = length // parts
    total = seqs * toks
    stream = pl.BlockSpec((chunks, span, LANES), lambda i, *_: (0, i, 0))
    return launch(
        functools.partial(states_kernel, seqs),
        (parts,),
        [me],
        [z, c, gathered, starts, ends, lens, packed],
        [ stream, stream, whole(gathered.shape), whole(starts.shape), whole(ends.shape), whole(lens.shape), pl.BlockSpec((count, blk, width), lambda i, *_: (0, at_char, 0)), ],
        [stream] + [whole((total, width))] * 3,
        [shape(z.shape, F32), shape((total, width), BF16), shape((total, width), F32), shape((total, width), BF16), ],
        [ pltpu.VMEM((chunks, span, LANES), F32), pltpu.VMEM((chunks, 2 * seqs, LANES), F32), pltpu.VMEM((total, width), F32), ],
        cost(2 * total * width * (width + length // 8), 12 * chunks * length * LANES),
        "states",
    )


def states_back_kernel(
    seqs, d_ref, w_ref, lens_ref, starts_ref, ends_ref, z_ref, ds_ref, total_ref,
):
    rows = 2 * seqs
    chunks = z_ref.shape[0]
    steps = z_ref.shape[1] // rows
    toks = starts_ref.shape[2]
    half = chunks * LANES
    d_pooled = dot(d_ref[...], flat_block(w_ref), 1, 1)
    count = lax.broadcasted_iota(jnp.int32, (steps, toks), 0)
    for s in range(seqs):
        d_summed = (d_pooled[s * toks : (s + 1) * toks] / lens_ref[s]).astype(BF16)
        for direction in range(2):
            place_of = count if direction == 0 else steps - 1 - count
            member = jnp.where(
                (place_of >= starts_ref[s]) & (place_of < ends_ref[s]), 1.0, 0.0
            ).astype(BF16)
            d_states = dot(member, d_summed[:, direction * half : (direction + 1) * half], 1, 0)
            for j in range(chunks):
                ds_ref[j, pl.ds(s + direction * seqs, steps, stride=rows), :] = d_states[
                    :, j * LANES : (j + 1) * LANES
                ]

    def one(lap, carried):
        place = pl.ds(pl.multiple_of((steps - 1 - lap) * rows, rows), rows)
        return tuple(
            (1.0 - z_ref[j, place, :]) * (ds_ref[j, place, :] + carried[j]) for j in range(chunks)
        )

    zero = jnp.zeros((rows, LANES), F32)
    carried = lax.fori_loop(0, steps, one, (zero,) * chunks, unroll=8)
    for j in range(chunks):
        total_ref[j] = carried[j]


def states_back_call(d_proj, packed, at_char, lens, starts, ends, z):
    chunks, length, _ = z.shape
    seqs = starts.shape[0]
    count, _, width = packed.shape
    blk = width // count
    return launch(
        functools.partial(states_back_kernel, seqs),
        (1,),
        [],
        [d_proj, packed, lens, starts, ends, z],
        [ whole(d_proj.shape), pl.BlockSpec((count, blk, width), lambda i: (0, at_char, 0)), whole(lens.shape), whole(starts.shape), whole(ends.shape), whole(z.shape), ],
        [whole(z.shape), whole((chunks, 2 * seqs, LANES))],
        [shape(z.shape, F32), shape((chunks, 2 * seqs, LANES), F32)],
        [],
        cost( 2 * d_proj.shape[0] * width * (width + length // 8), 8 * chunks * length * LANES ),
        "states_back",
    )


def gates_back_kernel(
    seqs, me_ref, groups_ref, z_ref, c_ref, prior_ref, ds_ref, all_ref, back_ref, ids_ref,
    back_ids_ref, s_ref, bias_ref, du_ref, dc_ref, carried_ref, acc_ref,
):
    i = pl.program_id(0)
    rows = 2 * seqs
    chunks = z_ref.shape[0]
    span = z_ref.shape[1] // rows
    half = chunks * LANES

    @pl.when(i == 0)
    def _():
        parts = back_ref[...].astype(F32)
        summed = parts[:, :RIDE] + parts[:, RIDE : 2 * RIDE] + parts[:, 2 * RIDE :]
        totals = summed[:, : chunks * rows].reshape(-1, chunks, rows, LANES)
        entry = entry_state(me_ref[0], totals, all_ref[:, 0], rows, seqs, False)
        for j in range(chunks):
            carried_ref[j] = entry[j]
        acc_ref[...] = jnp.zeros_like(acc_ref)

    def one(lap, carried):
        place = pl.ds(pl.multiple_of((span - 1 - lap) * rows, rows), rows)
        result = []
        for j in range(chunks):
            update = z_ref[j, place, :]
            candidate = c_ref[j, place, :]
            total = ds_ref[j, place, :] + carried[j]
            decay = 1.0 - update
            gated = total * update
            du_ref[j, place, :] = gated * decay * (candidate - prior_ref[j, place, :])
            dc_ref[j, place, :] = gated * (1.0 - candidate * candidate)
            result.append(decay * total)
        return tuple(result)

    carried = lax.fori_loop(0, span, one, tuple(carried_ref[j] for j in range(chunks)), unroll=8)
    for j in range(chunks):
        carried_ref[j] = carried[j]
    vocabulary = lax.broadcasted_iota(jnp.int32, (NCHAR, span), 0)
    for direction in range(2):
        source = ids_ref if direction == 0 else back_ids_ref
        for s in range(seqs):
            place = pl.ds(s + direction * seqs, span, stride=rows)
            gradient = jnp.concatenate(
                [part[j, place, :] for part in (du_ref, dc_ref) for j in range(chunks)], axis=1
            ).astype(BF16)
            onehot = jnp.where(source[s] == vocabulary, 1.0, 0.0).astype(BF16)
            acc_ref[groups_ref[s], :, direction * 2 * half : (direction + 1) * 2 * half] += dot(
                onehot, gradient, 1, 0
            )

    @pl.when(i == pl.num_programs(0) - 1)
    def _():
        total = jnp.zeros((1, 4 * half), F32)
        for g in range(acc_ref.shape[0]):
            total += column_sum(acc_ref[g])
            s_ref[g] = acc_ref[g].astype(BF16)
        bias_ref[...] = total


def gates_back_call(me, groups, z, c, prior, ds, gathered, gathered_back, ids, n_groups, parts):
    chunks, length, _ = z.shape
    seqs, steps = ids.shape
    span = length // parts
    width = 2 * chunks * LANES
    stream = pl.BlockSpec((chunks, span, LANES), lambda i, *_: (0, parts - 1 - i, 0))
    lanes = pl.BlockSpec((seqs, 1, steps // parts), lambda i, *_: (0, 0, parts - 1 - i))
    return launch(
        functools.partial(gates_back_kernel, seqs),
        (parts,),
        [me, groups],
        [z, c, prior, ds, gathered, gathered_back, ids[:, None, :], ids[:, None, ::-1]],
        [stream] * 4 + [whole(gathered.shape), pl.BlockSpec((gathered_back.shape[0], 3 * RIDE, LANES), lambda i, *_: (0, gathered_back.shape[1] // (3 * RIDE) - 1, 0)), lanes, lanes],
        [whole((n_groups, NCHAR, 2 * width)), whole((1, 2 * width))],
        [shape((n_groups, NCHAR, 2 * width), BF16), shape((1, 2 * width), F32)],
        [ pltpu.VMEM((chunks, span, LANES), F32), pltpu.VMEM((chunks, span, LANES), F32), pltpu.VMEM((chunks, 2 * seqs, LANES), F32), pltpu.VMEM((n_groups, NCHAR, 2 * width), F32), ],
        cost(4 * seqs * steps * NCHAR * width, 16 * chunks * length * LANES),
        "gates_back",
    )


def shifted(values, toks, low, high):
    total = values.shape[0]
    row = lax.broadcasted_iota(jnp.int32, (total, 1), 0)
    before = pltpu.roll(values, 1, 0)
    after = pltpu.roll(values, total - 1, 0)
    for s in range(total // toks):
        before = jnp.where(row == s * toks, low[s], before)
        after = jnp.where(row == (s + 1) * toks - 1, high[s], after)
    return before.astype(BF16), after.astype(BF16)


def conv_kernel(
    toks, f_ref, p_ref, normal_ref, proj_ref, norms_ref, low_ref, high_ref, w_ref, tok_g_ref,
    char_g_ref, tok_ref, char_ref, d_tok_ref, d_char_ref, dm_ref, sums_ref, begin_ref, end_ref,
    acc_ref, x_ref,
):
    half, k = pl.program_id(0), pl.program_id(1)
    width = f_ref.shape[1]

    @pl.when((half == 0) & (k == 0))
    def _():
        for part, source in enumerate((f_ref, p_ref)):
            columns = slice(part * width, (part + 1) * width)
            before, after = shifted(
                source[...].astype(F32),
                toks,
                low_ref[:, :, columns].astype(F32),
                high_ref[:, :, columns].astype(F32),
            )
            x_ref[0, :, columns] = before
            x_ref[1, :, columns] = source[...]
            x_ref[2, :, columns] = after

    product = dot(x_ref[k], flat_block(w_ref), 1, 0)

    @pl.when(k == 0)
    def _():
        acc_ref[...] = product

    @pl.when(k > 0)
    def _():
        acc_ref[...] += product

    def finish(which, base, grad_ref, out_ref, d_ref):
        normal, rstd = norm_forward(base + acc_ref[...])
        gain = norms_ref[2 + which : 3 + which]
        out_ref[...] = normal * gain + norms_ref[6 + which : 7 + which]
        gradient = grad_ref[...].astype(F32)
        sums_ref[0, 0:1, :] = column_sum(gradient * normal)
        sums_ref[0, 1:2, :] = column_sum(gradient)
        d_sum = norm_backward(normal, rstd, gain, gradient)
        d_ref[...] = d_sum
        low_sum = d_sum.astype(BF16)
        dm_ref[...] = low_sum
        for s in range(begin_ref.shape[0]):
            begin_ref[s] = low_sum[s * toks : s * toks + 1]
            end_ref[s] = low_sum[(s + 1) * toks - 1 : (s + 1) * toks]

    @pl.when((half == 0) & (k == 2))
    def _():
        finish(
            0, normal_ref[...] * norms_ref[1:2] + norms_ref[5:6], tok_g_ref, tok_ref, d_tok_ref
        )

    @pl.when((half == 1) & (k == 2))
    def _():
        finish(1, proj_ref[...], char_g_ref, char_ref, d_char_ref)


def conv_call(f_low, proj_low, normal1, proj, norms, low, high, packed, tok_grad, char_grad, seqs, carry):
    total, width = f_low.shape
    count = packed.shape[0]
    blk = 2 * width // count
    rows = (total, width)
    return launch(
        functools.partial(conv_kernel, total // seqs),
        (2, 3),
        [],
        [f_low, proj_low, normal1, proj, norms, low, high, packed, tok_grad, char_grad],
        [ whole(rows), whole(rows), whole(rows), whole(rows), whole(norms.shape), whole(low.shape), whole(high.shape), pl.BlockSpec((count, blk, width), lambda h, k: (0, 2 * k + h, 0)), whole(rows), whole(rows), ],
        [ whole(rows), whole(rows), whole(rows), whole(rows), pl.BlockSpec(rows, lambda h, k: (0, h)), pl.BlockSpec((1, 2, width), lambda h, k: (h, 0, 0)), pl.BlockSpec((seqs, 1, width), lambda h, k: (0, 0, h)), pl.BlockSpec((seqs, 1, width), lambda h, k: (0, 0, h)), ],
        [ shape(rows, F32), shape(rows, F32), shape(rows, F32), shape(rows, F32), shape((total, 2 * width), BF16), shape((2, 2, width), F32), shape((seqs, 1, 2 * width), BF16), shape((seqs, 1, 2 * width), BF16), ],
        [pltpu.VMEM(rows, F32), pltpu.VMEM((3, total, 2 * width), BF16)],
        cost(24 * total * width * width, 24 * width * width + 40 * total * width),
        "conv",
        carry,
    )


def place_blocks(part_ref, order_ref, send_ref, keep_ref, blk, row=0):
    count = part_ref.shape[0] // blk
    for pos in range(count):
        start = pl.multiple_of(order_ref[pos] * blk, 16)
        piece = part_ref[pl.ds(start, blk), :].astype(BF16)
        if pos < count // 2:
            keep_ref[pos, row : row + blk, :] = piece
        else:
            send_ref[pos - count // 2, row : row + blk, :] = piece


def conv_weight_kernel(
    toks, order_ref, f_ref, p_ref, other_f_ref, other_p_ref, dm_ref, low_ref, high_ref,
    other_dm_ref, begin_ref, end_ref, far_low_ref, far_high_ref, keep_a_ref, sent_a_ref, keep_b_ref, sent_b_ref,
    turned_ref, whole_ref, shift_ref, part_ref,
):
    k, half = pl.program_id(0), pl.program_id(1)
    total, width = f_ref.shape
    pieces = 2 * keep_a_ref.shape[0]
    blk = keep_a_ref.shape[1]

    @pl.when((k == 0) & (half == 0))
    def _():
        for core, pair in enumerate(((f_ref, p_ref), (other_f_ref, other_p_ref))):
            for part, source in enumerate(pair):
                whole_ref[part * width : (part + 1) * width, :] = source[...].T
            for pos in range(pieces):
                start = pl.multiple_of(order_ref[pos] * blk, 16)
                turned_ref[pos * blk : (pos + 1) * blk, core * total : (core + 1) * total] = (
                    whole_ref[pl.ds(start, blk), :]
                )
        odd = (order_ref[0] & 1) == 1
        edges = (
            (low_ref[...], high_ref[...]),
            (
                jnp.where(odd, far_low_ref[...], end_ref[...]),
                jnp.where(odd, begin_ref[...], far_high_ref[...]),
            ),
        )
        for core, (source, (low, high)) in enumerate(zip((dm_ref, other_dm_ref), edges)):
            rows = slice(core * total, (core + 1) * total)
            for part in range(2):
                columns = slice(part * width, (part + 1) * width)
                middle = source[:, columns]
                before, after = shifted(
                    middle.astype(F32),
                    toks,
                    low[:, :, columns].astype(F32),
                    high[:, :, columns].astype(F32),
                )
                shift_ref[part, rows, :] = after
                shift_ref[2 + part, rows, :] = middle
                shift_ref[4 + part, rows, :] = before

    at = 2 * k + half
    part_ref[...] = dot(turned_ref[...], shift_ref[at], 1, 0)

    def put(keep_ref, sent_ref, kept, sent):
        for index, (one, other) in enumerate(zip(kept, sent)):
            keep_ref[index] = part_ref[one * blk : (one + 1) * blk, :].astype(BF16)
            sent_ref[index] = part_ref[other * blk : (other + 1) * blk, :].astype(BF16)

    @pl.when(at < 3)
    def _():
        put(keep_a_ref, sent_a_ref, range(pieces // 2), range(pieces // 2, pieces))

    @pl.when(at >= 3)
    def _():
        put(keep_b_ref, sent_b_ref, range(0, pieces, 2), range(1, pieces, 2))


def conv_weight_call(order, own, other, dm, low, high, other_dm, begin, end, far_low, far_high, count):
    total, width = own[0].shape
    toks = total // low.shape[0]
    blk = 2 * width // count
    out = (count // 4, 3 * blk, width)
    first = pl.BlockSpec((count // 4, blk, width), lambda k, h, *_: (0, jnp.minimum(2 * k + h, 2), 0))
    second = pl.BlockSpec(
        (count // 4, blk, width), lambda k, h, *_: (0, jnp.maximum(2 * k + h - 3, 0), 0)
    )
    inputs = [*own, *other, dm, low, high, other_dm, begin, end, far_low, far_high]
    keep_a, sent_a, keep_b, sent_b = launch(
        functools.partial(conv_weight_kernel, toks),
        (3, 2),
        [order],
        inputs,
        [whole(v.shape) for v in inputs],
        [first, first, second, second],
        [shape(out, BF16)] * 4,
        [
            pltpu.VMEM((width, 2 * total), BF16),
            pltpu.VMEM((2 * width, total), BF16),
            pltpu.VMEM((6, 2 * total, width), BF16),
            pltpu.VMEM((width, width), F32),
        ],
        cost(24 * total * width * width, 12 * width * width),
        "conv_weight",
    )
    return [[keep_a, sent_a], [keep_b, sent_b]]


def conv_back_kernel(
    toks, dm_ref, low_ref, high_ref, w_ref, d_tok_ref, d_char_ref, normal_ref, rstd_ref,
    norms_ref, d_proj_ref, d_ffn_ref, sums_ref, shift_ref, acc_ref,
):
    k, half = pl.program_id(0), pl.program_id(1)
    width = d_tok_ref.shape[1]

    @pl.when((half == 0) & (k == 0))
    def _():
        for part in range(2):
            columns = slice(part * width, (part + 1) * width)
            source = dm_ref[:, columns]
            before, after = shifted(
                source.astype(F32),
                toks,
                low_ref[:, :, columns].astype(F32),
                high_ref[:, :, columns].astype(F32),
            )
            shift_ref[part] = after
            shift_ref[2 + part] = source
            shift_ref[4 + part] = before

    product = dot(shift_ref[2 * k + half], flat_block(w_ref), 1, 1)

    @pl.when((k == 0) & (half == 0))
    def _():
        acc_ref[...] = product

    @pl.when((k > 0) | (half > 0))
    def _():
        acc_ref[...] += product

    @pl.when((k == 2) & (half == 1))
    def _():
        d_proj_ref[...] = (d_char_ref[...] + acc_ref[:, width:]).astype(BF16)
        gradient = d_tok_ref[...] + acc_ref[:, :width]
        normal = normal_ref[...]
        sums_ref[0:1, :] = column_sum(gradient * normal)
        sums_ref[1:2, :] = column_sum(gradient)
        d_ffn_ref[...] = norm_backward(normal, rstd_ref[...], norms_ref[1:2], gradient)


def conv_back_call(d_merged, low, high, packed, d_tok, d_char, normal1, rstd1, norms, seqs, carry):
    total, width = d_tok.shape
    count = packed.shape[0]
    blk = 2 * width // count
    rows = (total, width)
    return launch(
        functools.partial(conv_back_kernel, total // seqs),
        (3, 2),
        [],
        [d_merged, low, high, packed, d_tok, d_char, normal1, rstd1, norms],
        [ whole(d_merged.shape), whole(low.shape), whole(high.shape), pl.BlockSpec((count, blk, width), lambda k, h: (0, 2 * k + h, 0)), whole(rows), whole(rows), whole(rows), whole(rstd1.shape), whole(norms.shape), ],
        [whole(rows), whole(rows), whole((2, width))],
        [shape(rows, BF16), shape(rows, F32), shape((2, width), F32)],
        [ pltpu.VMEM((6, total, width), BF16), pltpu.VMEM((total, 2 * width), F32), ],
        cost(24 * total * width * width, 24 * width * width + 20 * total * width),
        "conv_back",
        carry,
    )


def rest_kernel(
    order_ref, table_ref, s_ref, w0_ref, w1_ref, mix_ref, d_att_ref, send_ref, keep_ref, part_ref,
):
    count, blk, width = w0_ref.shape
    rows = part_ref.shape[0]
    turned = flat_block(table_ref).T
    sums = s_ref[...].reshape(rows, 2 * width)
    for part in range(2):
        part_ref[0:width, :] = dot(turned, sums[:, part * width : (part + 1) * width], 1, 0)
        place_blocks(part_ref.at[0:width], order_ref, send_ref, keep_ref, blk, part * blk)
    part_ref[...] = dot(sums[:, :width], flat_block(w0_ref), 1, 1) + dot(
        sums[:, width:], flat_block(w1_ref), 1, 1
    )
    place_blocks(part_ref, order_ref, send_ref, keep_ref, rows // count, 2 * blk)
    part_ref[0:width, :] = dot(mix_ref[...], d_att_ref[...], 1, 0)
    place_blocks(
        part_ref.at[0:width], order_ref, send_ref, keep_ref, blk, 2 * blk + rows // count
    )


def rest_call(order, packed, at_table, at_gru, sums, mixture, d_att, height):
    count, _, width = packed.shape
    blk = width // count
    rows = sums.shape[0] * sums.shape[1]
    table_rows = rows // count
    out = (count // 2, height, width)
    return launch(
        rest_kernel,
        (1,),
        [order],
        [packed, sums, packed, packed, mixture, d_att],
        [
            pl.BlockSpec((count, table_rows, width), lambda i, *_: (0, at_table, 0)),
            whole(sums.shape),
            pl.BlockSpec((count, blk, width), lambda i, *_: (0, at_gru, 0)),
            pl.BlockSpec((count, blk, width), lambda i, *_: (0, at_gru + 1, 0)),
            whole(mixture.shape),
            whole(d_att.shape),
        ],
        [whole(out), whole(out)],
        [shape(out, BF16), shape(out, BF16)],
        [pltpu.VMEM((rows, width), F32)],
        cost(8 * rows * width * width, 20 * width * width),
        "rest",
    )


def qkv_back_kernel(
    seqs, order_ref, d_ref, x_ref, w_ref, d_attn_ref, pooled_ref, d_proj_ref,
    sums0_ref, sums1_ref, sums23_ref, bias_ref, bias_up_ref, out_ref, send_ref, keep_ref, xt_ref,
    dt_ref, part_ref, small_ref,
):
    j = pl.program_id(0)
    per = d_ref.shape[1]
    head, toks = d_ref.shape[3:]
    pieces, _, width = send_ref.shape
    blk = width // (2 * pieces)
    half = width // 2

    def put(row):
        for pos in range(2 * pieces):
            start = pl.multiple_of(order_ref[pos] * blk, 16)
            piece = part_ref[pl.ds(start, blk), :].astype(BF16)
            if pos < pieces:
                keep_ref[pos, row, :] = piece
            else:
                send_ref[pos - pieces, row, :] = piece

    @pl.when(j == 0)
    def _():
        xt_ref[...] = x_ref[...].T
        out_ref[...] = d_attn_ref[...]
        small_ref[...] = jnp.zeros_like(small_ref)
        for row, ref in enumerate((sums0_ref, sums1_ref)):
            small_ref[row : row + 1] = ref[0:1]
            small_ref[4 + row : 5 + row] = ref[1:2]
        for which in range(2):
            small_ref[2 + which : 3 + which] = sums23_ref[which, 0:1]
            small_ref[6 + which : 7 + which] = sums23_ref[which, 1:2]
        for part in range(2):
            own = slice(part * half, (part + 1) * half)
            small_ref[8:9, own] = bias_ref[:, part * width : part * width + half]
            small_ref[9:10, own] = bias_ref[:, part * width + half : (part + 1) * width]
        for part in range(bias_up_ref.shape[1] // width):
            small_ref[10 + part : 11 + part] = bias_up_ref[:, part * width : (part + 1) * width]
        small = small_ref[...].astype(BF16)
        for pos in range(pieces):
            keep_ref[pos, 4 * blk : 4 * blk + SMALL_ROWS, :] = small
            send_ref[pos, 4 * blk : 4 * blk + SMALL_ROWS, :] = small
        part_ref[...] = dot(pooled_ref[...].T, d_proj_ref[...], 1, 0)
        put(slice(3 * blk, 4 * blk))

    for s in range(seqs):
        for h in range(HEADS):
            pair = s * HEADS + h
            dt_ref[h * head : (h + 1) * head, s * toks : (s + 1) * toks] = d_ref[
                pair // per, pair % per, 0
            ]
    gradient = dt_ref[...].T
    part_ref[...] = dot(xt_ref[...], gradient, 1, 0)
    put(pl.ds(pl.multiple_of(j * blk, 16), blk))
    out_ref[...] += dot(gradient, flat_block(w_ref), 1, 1)


def qkv_back_call(
    order, d_qkv, rows, packed, base, d_attn, pooled, d_proj, small, seqs, height
):
    count, per, _, head, toks = d_qkv.shape
    total, width = rows.shape
    blk = width // count
    out = (count // 2, height, width)
    rest = [d_attn, pooled, d_proj, *small]
    return launch(
        functools.partial(qkv_back_kernel, seqs),
        (3,),
        [order],
        [d_qkv, rows, packed, *rest],
        [
            pl.BlockSpec((count, per, 1, head, toks), lambda j, *_: (0, 0, j, 0, 0)),
            whole(rows.shape),
            pl.BlockSpec((count, blk, width), lambda j, *_: (0, base + j, 0)),
            *[whole(v.shape) for v in rest],
        ],
        [whole((total, width)), whole(out), whole(out)],
        [shape((total, width), F32), shape(out, BF16), shape(out, BF16)],
        [
            pltpu.VMEM((width, total), BF16),
            pltpu.VMEM((width, total), BF16),
            pltpu.VMEM((width, width), F32),
            pltpu.VMEM((SMALL_ROWS, width), F32),
        ],
        cost(16 * total * width * width, 20 * width * width + 16 * total * width),
        "qkv_back",
    )


def pack_kernel(layout, *refs):
    ins, out_ref = refs[:-1], refs[-1]
    at = 0
    out_ref[...] = jnp.zeros_like(out_ref)
    width = out_ref.shape[1]
    for ref, row in zip(ins, layout):
        height, columns = ref.shape
        if columns < width:
            out_ref[row : row + height, :columns] = ref[...]
        else:
            for block in range(columns // width):
                out_ref[row + block * height : row + (block + 1) * height, :] = ref[
                    :, block * width : (block + 1) * width
                ]


def pack(arrays, layout, rows, width):
    return launch(
        functools.partial(pack_kernel, layout),
        (1,),
        [],
        arrays,
        [whole(v.shape) for v in arrays],
        whole((rows, width)),
        shape((rows, width), BF16),
        [],
        cost(0, 4 * rows * width),
        "pack",
    )


def swap(value, axis, bit):
    size = lax.axis_size(axis)
    return lax.ppermute(value, axis, [(i, i ^ (1 << bit)) for i in range(size)])


def add_low(kept, arrived):
    return (kept.astype(F32) + arrived.astype(F32)).astype(BF16)


def fold_kernel(keep_top, keep_bottom, came_top, came_bottom, ka_ref, sa_ref, kb_ref, sb_ref):
    half = ka_ref.shape[0]
    for index in range(half):
        ka_ref[index] = add_low(keep_top[index], came_top[index])
        sa_ref[index] = add_low(keep_top[half + index], came_top[half + index])
        kb_ref[index] = add_low(keep_bottom[2 * index], came_bottom[2 * index])
        sb_ref[index] = add_low(keep_bottom[2 * index + 1], came_bottom[2 * index + 1])


def tiles(rows):
    return 3 if rows % 48 == 0 else 1


def fold_pieces_kernel(keep_top, keep_bottom, *refs):
    pieces = keep_top.shape[0]
    top, bottom, outs = refs[:pieces], refs[pieces : 2 * pieces], refs[2 * pieces :]
    ka_ref, sa_ref, kb_ref, sb_ref = outs
    half = pieces // 2
    for index in range(half):
        ka_ref[index] = add_low(keep_top[index], top[index][...])
        sa_ref[index] = add_low(keep_top[half + index], top[half + index][...])
        kb_ref[index] = add_low(keep_bottom[2 * index], bottom[2 * index][...])
        sb_ref[index] = add_low(keep_bottom[2 * index + 1], bottom[2 * index + 1][...])


def fold(keep, arrived):
    pieces, rows, width = keep.shape
    steps = tiles(rows // 2)
    tile = rows // 2 // steps
    top = pl.BlockSpec((pieces, tile, width), lambda i: (0, i, 0))
    bottom = pl.BlockSpec((pieces, tile, width), lambda i: (0, steps + i, 0))
    one_top = pl.BlockSpec((tile, width), lambda i: (i, 0))
    one_bottom = pl.BlockSpec((tile, width), lambda i: (steps + i, 0))
    ka, sa, kb, sb = launch(
        fold_pieces_kernel,
        (steps,),
        [],
        [keep, keep, *arrived, *arrived],
        [top, bottom] + [one_top] * pieces + [one_bottom] * pieces,
        [pl.BlockSpec((pieces // 2, tile, width), lambda i: (0, i, 0))] * 4,
        [shape((pieces // 2, rows // 2, width), BF16)] * 4,
        [],
        cost(pieces * rows * width, 6 * pieces * rows * width),
        "fold",
    )
    return [[ka, sa], [kb, sb]]


def send_links(state, step):
    bits = lax.axis_size("seq").bit_length() - 1
    return [
        [kept, swap(sent, "seq", bit)] for (kept, sent), bit in zip(state, (step, bits - step))
    ]


def split(state, carry=()):
    pieces, rows, width = state[0][0].shape
    steps = tiles(rows)
    spec = pl.BlockSpec((pieces, rows // steps, width), lambda i: (0, i, 0))
    out = pl.BlockSpec((pieces // 2, rows // steps, width), lambda i: (0, i, 0))
    ka, sa, kb, sb, *carried = launch(
        fold_kernel,
        (steps,),
        [],
        [state[0][0], state[1][0], state[0][1], state[1][1]],
        [spec] * 4,
        [out] * 4,
        [shape((pieces // 2, rows, width), BF16)] * 4,
        [],
        cost(pieces * rows * width, 12 * pieces * rows * width),
        "split",
        carry,
    )
    return [[ka, sa], [kb, sb]], carried


def cross_kernel(place_ref, ka_ref, kb_ref, ca_ref, cb_ref, kept_ref, sent_ref):
    high = (place_ref[0] & 1) == 1
    first = add_low(ka_ref[0], ca_ref[0])
    second = add_low(kb_ref[0], cb_ref[0])
    kept_ref[...] = jnp.where(high, second, first)
    sent_ref[...] = jnp.where(high, first, second)


def cross(place, state, carry=()):
    _, rows, width = state[0][0].shape
    steps = tiles(rows)
    spec = pl.BlockSpec((1, rows // steps, width), lambda i, *_: (0, i, 0))
    return launch(
        cross_kernel,
        (steps,),
        [place],
        [state[0][0], state[1][0], state[0][1], state[1][1]],
        [spec] * 4,
        [pl.BlockSpec((rows // steps, width), lambda i, *_: (i, 0))] * 2,
        [shape((rows, width), BF16)] * 2,
        [],
        cost(rows * width, 12 * rows * width),
        "cross",
        carry,
    )


def halve_kernel(bit, place_ref, kept_ref, came_ref, next_ref, sent_ref):
    high = ((place_ref[0] >> bit) & 1) == 1
    rows = next_ref.shape[0]
    first = add_low(kept_ref[:rows], came_ref[:rows])
    second = add_low(kept_ref[rows:], came_ref[rows:])
    next_ref[...] = jnp.where(high, second, first)
    sent_ref[...] = jnp.where(high, first, second)


def halve(place, bit, kept, came, carry):
    rows, width = kept.shape
    return launch(
        functools.partial(halve_kernel, bit),
        (1,),
        [place],
        [kept, came],
        [whole(kept.shape)] * 2,
        [whole((rows // 2, width))] * 2,
        [shape((rows // 2, width), BF16)] * 2,
        [],
        cost(rows * width, 6 * rows * width),
        "halve",
        carry,
    )


def add_kernel(kept_ref, came_ref, out_ref):
    out_ref[...] = add_low(kept_ref[...], came_ref[...])


def add(kept, came):
    return launch(
        add_kernel,
        (1,),
        [],
        [kept, came],
        [whole(kept.shape)] * 2,
        whole(kept.shape),
        shape(kept.shape, BF16),
        [],
        cost(kept.size, 6 * kept.size),
        "add",
    )


def assemble_kernel(bit, place_ref, held_ref, came_ref, out_ref):
    high = ((place_ref[0] >> bit) & 1) == 1
    rows = held_ref.shape[0]
    held, came = held_ref[...], came_ref[...]
    out_ref[:rows] = jnp.where(high, came, held)
    out_ref[rows:] = jnp.where(high, held, came)


def assemble(place, bit, held, came):
    rows, width = held.shape
    return launch(
        functools.partial(assemble_kernel, bit),
        (1,),
        [place],
        [held, came],
        [whole(held.shape)] * 2,
        whole((2 * rows, width)),
        shape((2 * rows, width), BF16),
        [],
        cost(rows * width, 8 * rows * width),
        "assemble",
    )


def finish_kernel(layout, place_ref, held_ref, came_ref, *out_refs):
    high = (place_ref[0] & 1) == 1
    rows = held_ref.shape[0]
    for begin, size, out, index in layout:
        part = slice(begin % rows, begin % rows + size)
        held, came = held_ref[part].astype(F32), came_ref[part].astype(F32)
        out_refs[out][index] = jnp.where(high == (begin < rows), came, held)


def cut(layout, rows):
    for begin, size, out, index in layout:
        edges = [begin, begin + size]
        if begin < rows < begin + size:
            edges.insert(1, rows)
        for low, high in zip(edges, edges[1:]):
            yield low, high - low, out, index[:-2] + (slice(low - begin, high - begin), index[-1])


def finish(place, held, came, layout, outs):
    layout = list(cut(layout, held.shape[0]))
    return launch(
        functools.partial(finish_kernel, layout),
        (1,),
        [place],
        [held, came],
        [whole(held.shape)] * 2,
        [whole(dims) for dims in outs],
        [shape(dims, F32) for dims in outs],
        [],
        cost(held.size, 16 * held.size),
        "finish",
    )


def across_halves(place, kept, sent, layout, outs):
    bits = lax.axis_size("batch").bit_length() - 1
    came = swap(sent, "batch", 0)
    carry = yield
    for bit in range(1, bits):
        kept, sent, *carry = halve(place, bit, kept, came, carry or ())
        came = swap(sent, "batch", bit)
        carry = yield carry
    held = add(kept, came)
    for bit in reversed(range(bits)):
        came = swap(held, "batch", bit)
        yield
        if bit:
            held = assemble(place, bit, held, came)
    yield finish(place, held, came, layout, outs)


def deal_kernel(place_ref, ka_ref, kb_ref, ca_ref, cb_ref, *refs):
    outs, sum_ref = refs[:-1], refs[-1]
    rows, part = ka_ref.shape[1], outs[0].shape[0]
    sum_ref[:rows] = add_low(ka_ref[0], ca_ref[0])
    sum_ref[rows:] = add_low(kb_ref[0], cb_ref[0])
    for mask, out_ref in enumerate(outs):
        start = pl.multiple_of((place_ref[0] ^ mask) * part, 16)
        out_ref[...] = sum_ref[pl.ds(start, part), :]


def total_kernel(*refs):
    total = refs[0][...].astype(F32)
    for ref in refs[1:-1]:
        total += ref[...].astype(F32)
    refs[-1][...] = total.astype(BF16)


def spread_kernel(layout, parts, place_ref, *refs):
    ins, outs, all_ref = refs[:parts], refs[parts:-1], refs[-1]
    rows = ins[0].shape[0]
    for mask, ref in enumerate(ins):
        start = pl.multiple_of((place_ref[0] ^ mask) * rows, 16)
        all_ref[pl.ds(start, rows), :] = ref[...]
    for begin, size, out, index in layout:
        outs[out][index] = all_ref[begin : begin + size].astype(F32)


def across_direct(place, state, layout, outs):
    parts = lax.axis_size("batch")
    _, rows, width = state[0][0].shape
    part = (2 * rows // parts, width)
    ends = [(mask, [(i, i ^ mask) for i in range(parts)]) for mask in range(1, parts)]
    pieces = launch(
        deal_kernel,
        (1,),
        [place],
        [state[0][0], state[1][0], state[0][1], state[1][1]],
        [whole(state[0][0].shape)] * 4,
        [whole(part)] * parts,
        [shape(part, BF16)] * parts,
        [pltpu.VMEM((2 * rows, width), BF16)],
        cost(rows * width, 12 * rows * width),
        "deal",
    )
    came = [lax.ppermute(pieces[mask], "batch", pairs) for mask, pairs in ends]
    yield
    held = launch(
        total_kernel,
        (1,),
        [],
        [pieces[0], *came],
        [whole(part)] * parts,
        whole(part),
        shape(part, BF16),
        [],
        cost(rows * width, 5 * rows * width),
        "total",
    )
    came = [lax.ppermute(held, "batch", pairs) for _, pairs in ends]
    yield
    yield launch(
        functools.partial(spread_kernel, layout, parts),
        (1,),
        [place],
        [held, *came],
        [whole(part)] * parts,
        [whole(dims) for dims in outs],
        [shape(dims, F32) for dims in outs],
        [pltpu.VMEM((2 * rows, width), BF16)],
        cost(rows * width, 12 * rows * width),
        "spread",
    )


def last(steps):
    result = None
    for result in steps:
        pass
    return result if isinstance(result, (list, tuple)) else [result]


def neighbours(first, last):
    count = lax.axis_size("seq")
    up = [(i, i + 1) for i in range(count - 1)]
    down = [(target, source) for source, target in up]
    return lax.ppermute(last, "seq", up), lax.ppermute(first, "seq", down)


def local(
    hidden, char_ids, group_ids, word_lengths, qkv_weight, out_weight, up_weight, ffn_bias,
    down_weight, gru_weight, gate_bias, candidate_bias, char_weight, conv_weight, char_table,
    norm_gain, norm_shift, tok_grad, char_grad,
):
    count = lax.axis_size("seq")
    bits = count.bit_length() - 1
    me = lax.axis_index("seq").astype(jnp.int32)
    seqs, toks, width = hidden.shape
    total = seqs * toks
    half = width // 2
    blk = width // count
    share = ffn_bias.shape[0]
    table_rows = char_table.shape[0]
    chars = char_ids.shape[1]
    reverse = [int(format(i, f"0{bits}b")[::-1], 2) for i in range(count)]
    order = jnp.asarray(reverse, jnp.int32) ^ me
    slot = sum(
        (((jnp.arange(count, dtype=jnp.int32) ^ me) >> b) & 1) << (bits - 1 - b) for b in range(bits)
    )
    me_one = me.reshape(1)

    place = lax.axis_index("batch").astype(jnp.int32).reshape(1)
    LATEST.clear()

    table_at = share
    small_at = table_at + table_rows
    block_at = small_at + 16
    block_at += -block_at % blk
    pack_rows = block_at + 11 * blk
    small = jnp.concatenate(
        [norm_gain.T, norm_shift.T, gate_bias[None], candidate_bias[None]], 0
    )
    small = jnp.pad(small, ((0, 6), (0, width - blk)))
    small = small.at[10, :share].set(ffn_bias)
    arrays = [
        down_weight, char_table, small, gru_weight, qkv_weight, char_weight, out_weight, up_weight
    ]
    at_block = block_at // blk
    at_gru, at_qkv, at_char, at_out, at_up = (at_block + i for i in (0, 2, 5, 6, 7))
    layout = [0, table_at, small_at] + [i * blk for i in (at_gru, at_qkv, at_char, at_out, at_up)]
    at_table, at_down = table_at // table_rows, 0
    first = pack(arrays, layout, pack_rows, width)
    third = pack(
        [conv_weight[k] for k in range(3)], [k * 4 * blk for k in range(3)], 12 * blk, width
    )
    first = lax.all_gather(first, "seq", axis=0)
    third = lax.all_gather(third, "seq", axis=0)
    vectors = (
        first[:, small_at : small_at + 10, :blk].astype(F32).transpose(1, 0, 2).reshape(10, width)
    )
    bias_up = first[:, small_at + 10, :share].astype(F32).reshape(1, -1)
    norms = vectors

    rows = hidden.reshape(total, width)
    words = word_lengths.reshape(seqs, toks)
    ends = jnp.cumsum(words, axis=1)
    starts = ends - words
    lens = words.astype(F32)[..., None]

    qkv = qkv_call(rows, first, at_qkv, seqs, count)
    qkv = lax.all_to_all(qkv, "seq", 0, 0, tiled=True)
    z, c, block_totals = gates_call(group_ids, char_ids, first, at_gru, at_table, vectors)
    gathered = [block_totals] + [
        lax.ppermute(block_totals, "seq", [(i, i ^ mask) for i in range(count)])
        for mask in range(1, count)
    ]
    step = 512
    mixture, totals = attend_call(qkv, step)
    mixture = lax.all_to_all(mixture, "seq", 0, 0, tiled=True)
    gathered = collect(me_one, gathered)
    prior, pooled, proj, proj_low = states_call(
        me_one, z, c, gathered, starts[..., None], ends[..., None], lens, first, at_char, 2
    )
    mix_t, normal0, rstd0, normed, active, slope, normal1, rstd1, f_low = ffn_call(
        mixture, rows, first, at_out, at_up, at_down, bias_up, norms, seqs
    )

    def edges(left, right):
        joined = [v.reshape(seqs, toks, width) for v in (left, right)]
        return (
            jnp.concatenate([v[:, :1] for v in joined], -1),
            jnp.concatenate([v[:, -1:] for v in joined], -1),
        )

    low, high = neighbours(*edges(f_low, proj_low))
    other = [swap(v, "seq", 0) for v in (f_low, proj_low)]
    tok_out, char_out, d_tok, d_char, d_merged, sums23, begin, end, *other = conv_call(
        f_low, proj_low, normal1, proj, norms, low, high, third,
        tok_grad.reshape(total, width), char_grad.reshape(total, width), seqs, other,
    )

    low, high = neighbours(begin, end)
    other_dm = swap(d_merged, "seq", 0)

    def onward(state, first_link, carry=()):
        for link in range(first_link + 1, bits):
            state, carry = split(state, carry)
            state = send_links(state, link)
        return state, carry

    def columns_of(begin, blocks, out):
        return [
            (begin + j * blk, blk, out, (slice(None), slice(j * width, (j + 1) * width)))
            for j in range(blocks)
        ]

    everything = (slice(None), slice(None))
    double = 2 * blk
    unit = 8 * lax.axis_size("batch")
    height = max(3 * blk + table_rows, 4 * blk + SMALL_ROWS)
    height += -height % unit
    d_proj, d_ffn, sums1, begin, end = conv_back_call(
        d_merged, low, high, third, d_tok, d_char, normal1, rstd1, norms, seqs, [begin, end]
    )
    far_high = lax.ppermute(begin, "seq", [(i, i - 2) for i in range(2, count)])
    far_low = lax.ppermute(end, "seq", [(i, i + 2) for i in range(count - 2)])
    conv_state = conv_weight_call(
        order, (f_low, proj_low), other, d_merged, low, high, other_dm, begin, end, far_low,
        far_high, count,
    )
    conv_state = send_links(conv_state, 1)
    ds, back_totals = states_back_call(
        d_proj, first, at_char, lens, starts[:, None, :], ends[:, None, :], z
    )
    send, keep, d_bias_up, d_attn, d_attended, sums0, d_mix = ffn_back_call(
        slot, order, d_ffn, active, slope, normed, normal0, rstd0, norms, first, at_out, at_up,
        at_down, back_totals, seqs,
    )
    d_mix = lax.all_to_all(d_mix, "seq", 0, 0, tiled=True)
    ffn_came = [swap(piece, "seq", 0) for piece in send]
    conv_state, _ = onward(conv_state, 1)
    ffn_state = fold(keep, ffn_came)
    ffn_state = send_links(ffn_state, 1)
    d_qkv = attend_back_call(qkv, d_mix, totals, step)
    d_qkv = lax.all_to_all(d_qkv, "seq", 0, 0, tiled=True)
    conv_steps = across_halves(
        place, *cross(place, conv_state),
        [
            (r * double, double, 0, (r // 2, slice(None), slice(r % 2 * width, (r % 2 + 1) * width)))
            for r in range(6)
        ],
        [(3, double, 2 * width)],
    )
    next(conv_steps)
    sums, d_bias = gates_back_call(
        me_one, group_ids, z, c, prior, ds, gathered, d_mix, char_ids,
        count * table_rows // NCHAR, 2,
    )
    ffn_state, _ = onward(ffn_state, 1)
    rest_send, rest_keep = rest_call(
        order, first, at_table, at_gru, sums, mix_t, d_attended, height
    )
    next(conv_steps)
    hidden_grad, qkv_send, qkv_keep = qkv_back_call(
        order, d_qkv, rows, first, at_qkv, d_attn, pooled, d_proj,
        [sums0, sums1, sums23, d_bias, d_bias_up], seqs, height,
    )
    kept, sent, *both = cross(place, ffn_state, (rest_send, qkv_send))
    rest_came, qkv_came = (swap(send, "seq", 0) for send in both)
    ffn_steps = across_halves(
        place, kept, sent,
        [(0, share, 0, everything), *columns_of(share, 4, 1)],
        [(share, width), (blk, 4 * width)],
    )
    next(ffn_steps)
    next(conv_steps)
    last_state, _ = split([[rest_keep, rest_came], [qkv_keep, qkv_came]])
    last_state = send_links(last_state, 1)
    next(ffn_steps)
    next(conv_steps)
    last_state, _ = onward(last_state, 1)
    next(ffn_steps)
    (conv_grad,) = last(conv_steps)
    last_steps = across_direct(
        place, last_state,
        [
            *columns_of(0, 2, 0),
            (2 * blk, table_rows, 1, everything),
            (2 * blk + table_rows, blk, 2, everything),
            *columns_of(height, 3, 3),
            (height + 3 * blk, blk, 4, everything),
            (height + 4 * blk, SMALL_ROWS, 5, everything),
        ],
        [
            (blk, 2 * width), (table_rows, width), (blk, width), (blk, 3 * width), (blk, width),
            (SMALL_ROWS, width),
        ],
    )
    next(last_steps)
    next(ffn_steps)
    next(last_steps)
    down_grad, up_grad = last(ffn_steps)
    gru_grad, table_grad, out_grad, qkv_grad, char_grad_w, small_sum = last(last_steps)

    mine = lax.dynamic_slice(small_sum, (0, me * blk), (10, blk))
    d_gain, d_shift, d_gate_b, d_cand_b = mine[:4].T, mine[4:8].T, mine[8], mine[9]
    d_ffn_b = lax.dynamic_slice(small_sum[10:14].reshape(-1), (me * share,), (share,))
    shape_out = (seqs, toks, width)
    return (
        tok_out.reshape(shape_out),
        char_out.reshape(shape_out),
        hidden_grad.reshape(shape_out),
        qkv_grad,
        out_grad,
        up_grad,
        d_ffn_b,
        down_grad,
        gru_grad,
        d_gate_b,
        d_cand_b,
        char_grad_w,
        conv_grad,
        table_grad,
        d_gain,
        d_shift,
    )


def solution(mesh):
    rows, columns = P("seq", None), P("batch", "seq", None)
    return jax.shard_map(
        local,
        mesh=mesh,
        in_specs=(
            columns, P("batch", "seq"), P("batch"), columns, rows, rows, rows, P("seq"), rows,
            rows, P("seq"), P("seq"), rows, P(None, "seq", None), rows, rows, rows, columns,
            columns,
        ),
        out_specs=(
            columns, columns, columns, rows, rows, rows, P("seq"), rows, rows, P("seq"), P("seq"),
            rows, P(None, "seq", None), rows, rows, rows,
        ),
        check_vma=False,
    )
```

time: 3260 us -> 660 us (0.20); the launches traced: 3210 us -> 651 us
  local copies, waits for them, and re-layouts: 1310 us -> 34.4 us
  waiting for transfers between devices: 982 us -> 222 us
  other arithmetic: 425 us -> 6.02 us
  Pallas kernels: 0 us -> 291 us
  blocking collectives: 224 us -> 0 us
  matrix products: 219 us -> 0 us
  starting transfers between devices: 24.2 us -> 83.2 us
    slice x509 -> x4, local copies, waits for them, and re-layouts: 806 us -> 3.25 us  [the longest x2 1.69 us: edges(): v[:, :1]]
    reduce_scatter x14 -> x0, waiting for transfers between devices: 531 us -> none  [the longest x2 209 us: reduce_grads(): lax.psum_scatter(gradients[9].astype(jnp.bfloat16), 'seq', scatter_dimens...]
    psum x1 -> x0, waiting for transfers between devices: 292 us -> none  [reduce_grads(): lax.psum(rows_part[0].astype(jnp.bfloat16), 'batch').astype(jnp.float32)]
    pallas_call x0 -> x35, Pallas kernels: none -> 291 us  [launch(): pl.pallas_call(kernel, grid_spec=pltpu.PrefetchScalarGridSpec(num_scalar_...]
    dot_general x88 -> x0, matrix products: 219 us -> none  [the longest x14 56.1 us: matmul(): return jnp.dot(left, right, preferred_element_type=jnp.float32)]
    add x257 -> x1, other arithmetic: 180 us -> 0.52 us  [local(): sum((((jnp.arange(count, dtype=jnp.int32) ^ me) >> b & 1) << bits - 1 - b...]
    all_gather x19 -> x0, blocking collectives: 175 us -> none  [the longest x16 150 us: prefix(): gathered = jax.tree.map(lambda a: lax.all_gather(a, axis), part)]
    pad x252 -> x0, local copies, waits for them, and re-layouts: 172 us -> none  [local_scan(): lax.associative_scan(affine, (decays, drives), axis=1, reverse=backwards)]
  transfers between devices with their start and end apart: 45 -> 54, of which waited for: 15 -> 15; matrix products, arithmetic and copies ran while one was open for 56% -> 3% of each run, Pallas kernels for 0% -> 36%
where the time goes in v1:
time: 660 us; the launch traced here: 651 us
  Pallas kernels  291 us (44%)
  waiting for transfers between devices  222 us (34%)
  starting transfers between devices  83.2 us (13%)
  local copies, waits for them, and re-layouts  34.4 us (5%)
  between operations  14.8 us (2%)
    pallas_call x35, Pallas kernels, launch(): pl.pallas_call(kernel, grid_spec=pltpu.PrefetchScalarGridSpec(num_scalar_...  291 us
    all_gather x1, waiting for transfers between devices, local(): first = lax.all_gather(first, 'seq', axis=0)  96.5 us
    ppermute x29, waiting for transfers between devices, swap(): return lax.ppermute(value, axis, [(i, i ^ 1 << bit) for i in range(size)])  61.1 us
    ppermute x29, starting transfers between devices, swap(): return lax.ppermute(value, axis, [(i, i ^ 1 << bit) for i in range(size)])  31.5 us
    unnamed x93, local copies, waits for them, and re-layouts  18.7 us
    ppermute x3, waiting for transfers between devices, across_direct(): came = [lax.ppermute(pieces[mask], 'batch', pairs) for mask, pairs in ends]  18.1 us
    ppermute x7, waiting for transfers between devices, local(): lax.ppermute(block_totals, 'seq', [(i, i ^ mask) for i in range(count)])  17.9 us
    ppermute x3, waiting for transfers between devices, across_direct(): came = [lax.ppermute(held, 'batch', pairs) for _, pairs in ends]  15.8 us
  transfers between devices with their start and end apart: 54, of which 15 were waited for; matrix products, arithmetic and copies ran while one was open for 3% of the time, Pallas kernels for 36%

profile of v1, /device:TPU:0, one launch (start us, length us, event | category | flops | bytes accessed | tf_op | source)
XLA Modules:
  0.0 651.2 jit_solution(14564650400981314)
XLA Ops:
  9.5 3.3 pack.2.refs_3_
  15.6 2.8 pack.3.refs_2_
  23.0 96.5 %all-gather.5.cloned.1.call-done = bf16[13056,768]{1,0:T(8,128)(2,1)} async-done(((bf16[1632,768]{1,0:T(8,128)(2,1)}), bf16[13056,768]{1,0:T(8,128)(2,1)}) %all-gather.5.cloned.1.call-update) | async-done | bytes 20054032 | tf_op jit(solution)/shard_map/all_gather | solution.py:1537
  120.8 5.7 qkv.1.refs_7_
  127.2 4.4 all-to-all-start
  131.7 17.5 %gates.1 = (f32[3,4096,128]{2,1,0:T(8,128)}, f32[3,4096,128]{2,1,0:T(8,128)}, f32[2,3,8,128]{3,2,1,0:T(8,128)}) custom-call(s32[4]{0:T(128)} %refs_1_.3, s32[4,512,1]{2,1,0:T(8,128)} %copy.51.refs_1_, s32[4,512,1]{2,1,0:T(8,128)} %copy.52.refs_2_, bf16[8,1632,768]{2,1,0:T(8,128)(2,1)} %bitcast.58, bf16[8,1632,768]{2,1,0:T(8,128)(2,1)} %bitcast.59, ...), custom_call_target="tpu_custom_call" | custom-call | flops 6442450944000 | bytes 25165824000 | tf_op jit(solution)/shard_map/gates/pallas_call | solution.py:64
  157.1 2.6 collective-permute-start.5
  159.8 17.9 %collective-permute-done.1.refs_3_ = f32[2,3,8,128]{3,2,1,0:T(8,128)S(1)} collective-permute-done((f32[2,3,8,128]{3,2,1,0:T(8,128)}, f32[2,3,8,128]{3,2,1,0:T(8,128)S(1)}, u32[]{:S(2)}, u32[]{:S(2)}) %collective-permute-start.1) | collective-permute-done | bytes 24608 | tf_op jit(solution)/shard_map/ppermute | solution.py:1555
  178.6 13.9 %attend.1 = (bf16[8,6,64,128]{3,2,1,0:T(8,128)(2,1)}, f32[6,1,1024]{2,1,0:T(1,128)}) custom-call(bf16[8,6,3,64,128]{4,3,2,1,0:T(8,128)(2,1)} %all-to-all-done.refs_0_, f32[2,3,8,128]{3,2,1,0:T(8,128)} %get-tuple-element.126.refs_1_), custom_call_target="tpu_custom_call" | custom-call | flops 6442450944000 | bytes 3145728000 | tf_op jit(solution)/shard_map/attend/pallas_call | solution.py:64
  192.5 4.4 all-to-all-start.1
  198.6 10.8 %states.1 = (f32[3,4096,128]{2,1,0:T(8,128)}, bf16[512,768]{1,0:T(8,128)(2,1)}, f32[512,768]{1,0:T(8,128)}, bf16[512,768]{1,0:T(8,128)(2,1)}) custom-call(s32[1]{0:T(128)} %bitcast.13.refs_0_, f32[3,4096,128]{2,1,0:T(8,128)} %get-tuple-element.128.refs_1_.refs_5_.refs_2_, f32[3,4096,128]{2,1,0:T(8,128)} %get-tuple-element.129.refs_2_.refs_3_, ...), custom_call_target="tpu_custom_call" | custom-call | flops 1006632960000 | bytes 18874368000 | tf_op jit(solution)/shard_map/states/pallas_call | solution.py:64
  209.9 8.3 %all-to-all-done.1.refs_0_ = bf16[8,6,64,128]{3,2,1,0:T(8,128)(2,1)} async-done(((bf16[8,6,64,128]{3,2,1,0:T(8,128)(2,1)}), bf16[8,6,64,128]{3,2,1,0:T(8,128)(2,1)}, u32[]{:S(2)}, u32[]{:S(2)}) %all-to-all-start.1) | async-done | bytes 786464 | tf_op jit(solution)/shard_map/all_to_all | solution.py:1560
  218.2 18.2 %ffn.1 = (bf16[768,512]{1,0:T(8,128)(2,1)}, f32[512,768]{1,0:T(8,128)}, f32[512,1]{1,0:T(8,128)}, bf16[512,768]{1,0:T(8,128)(2,1)}, bf16[512,3072]{1,0:T(8,128)(...) custom-call(bf16[8,6,64,128]{3,2,1,0:T(8,128)(2,1)} %all-to-all-done.1.refs_0_, ...), custom_call_target="tpu_custom_call" | custom-call | flops 5435817984000 | bytes 25165824000 | tf_op jit(solution)/shard_map/ffn/pallas_call | solution.py:64
  239.5 3.0 collective-permute-start.7
  244.3 19.9 %conv.1 = (f32[512,768]{1,0:T(8,128)}, f32[512,768]{1,0:T(8,128)}, f32[512,768]{1,0:T(8,128)}, f32[512,768]{1,0:T(8,128)}, bf16[512,1536]{1,0:T(8,128)(2,1)}, /*...) custom-call(bf16[512,768]{1,0:T(8,128)(2,1)} %get-tuple-element.132., ...), custom_call_target="tpu_custom_call", output_to_operand_aliasing={{8}: (10, {}), {9}: (11, {})} | custom-call | flops 7247757312000 | bytes 29884416000 | tf_op jit(solution)/shard_map/conv/pallas_call | solution.py:64
  264.2 3.7 collective-permute-start.11
  271.2 2.9 collective-permute-start.13
  274.7 17.3 %conv_back.1 = (bf16[512,768]{1,0:T(8,128)(2,1)}, f32[512,768]{1,0:T(8,128)}, f32[2,768]{1,0:T(2,128)}, bf16[4,1,1536]{2,1,0:T(2,128)(2,1)}, bf16[4,1,1536]{2,1,0:T(2,128)(2,1)}) custom-call(bf16[512,1536]{1,0:T(8,128)(2,1)} %get-tuple-element.137.refs_0_.refs_5_, bf16[4,1,1536]{2,1,0:T(2,128)(2,1)} %copy-done.39, ...), custom_call_target="tpu_custom_call", output_to_operand_aliasing={{3}: (9, {}), {4}: (10, {})} | custom-call | flops 7247757312000 | bytes 22020096000 | tf_op jit(solution)/shard_map/conv_back/pallas_call | solution.py:64
  292.0 3.5 collective-permute-start.14
  297.9 3.5 collective-permute-done.15.refs_12_
  302.1 18.4 %conv_weight.1 = (bf16[2,576,768]{2,1,0:T(8,128)(2,1)}, bf16[2,576,768]{2,1,0:T(8,128)(2,1)}, bf16[2,576,768]{2,1,0:T(8,128)(2,1)}, bf16[2,576,768]{2,1,0:T(8,128)(2,1)}) custom-call(s32[8]{0:T(128)} %broadcast_xor_fusion.refs_0_.refs_1_, bf16[512,768]{1,0:T(8,128)(2,1)} %get-tuple-element.132.refs_0_.refs_12_.refs_1_, ...), custom_call_target="tpu_custom_call" | custom-call | flops 7247757312000 | bytes 7077888000 | tf_op jit(solution)/shard_map/conv_weight/pallas_call | solution.py:64
  320.5 2.8 collective-permute-start.20
  323.3 10.6 %states_back.1 = (f32[3,4096,128]{2,1,0:T(8,128)}, f32[3,8,128]{2,1,0:T(8,128)}) custom-call(bf16[512,768]{1,0:T(8,128)(2,1)} %get-tuple-element.149.refs_0_.refs_6_, bf16[8,1632,768]{2,1,0:T(8,128)(2,1)} %bitcast.66, f32[4,128,1]{2,1,0:T(8,128)} %convert_element_type.28.refs_6_.refs_2_, s32[4,1,128]{2,1,0:T(1,128)} %sub.14.refs_3_, s32[4,1,128]{2,1,0:T(1,128)} %bitcast.47, ...), custom_call_target="tpu_custom_call" | custom-call | flops 1006632960000 | bytes 12582912000 | tf_op jit(solution)/shard_map/states_back/pallas_call | solution.py:64
  333.9 25.3 %ffn_back.1 = (bf16[768,768]{1,0:T(8,128)(2,1)}, bf16[768,768]{1,0:T(8,128)(2,1)}, bf16[768,768]{1,0:T(8,128)(2,1)}, bf16[768,768]{1,0:T(8,128)(2,1)}, bf16[4,76...) custom-call(s32[8]{0:T(128)} %shift-left_add_fusion.refs_0_, ...), custom_call_target="tpu_custom_call" | custom-call | flops 10267656192000 | bytes 34603008000 | tf_op jit(solution)/shard_map/ffn_back/pallas_call | solution.py:64
  361.7 4.4 all-to-all-start.2
  367.3 5.6 split.4
  372.9 1.9 collective-permute-start.22
  377.7 6.9 %fold.1 = (bf16[2,384,768]{2,1,0:T(8,128)(2,1)}, bf16[2,384,768]{2,1,0:T(8,128)(2,1)}, bf16[2,384,768]{2,1,0:T(8,128)(2,1)}, bf16[2,384,768]{2,1,0:T(8,128)(2,1)}) custom-call(bf16[4,768,768]{2,1,0:T(8,128)(2,1)} %get-tuple-element.158.refs_0_.refs_1_, bf16[4,768,768]{2,1,0:T(8,128)(2,1)} %get-tuple-element.158.refs_0_.refs_1_, bf16[768,768]{1,0:T(8,128)(2,1)} %copy-done, ...), custom_call_target="tpu_custom_call" | custom-call | flops 2359296000 | bytes 14155776000 | tf_op jit(solution)/shard_map/fold/pallas_call | solution.py:64
  385.5 21.8 %attend_back.1.refs_5_ = bf16[8,6,3,64,128]{4,3,2,1,0:T(8,128)(2,1)} custom-call(bf16[8,6,3,64,128]{4,3,2,1,0:T(8,128)(2,1)} %all-to-all-done.refs_0_, bf16[8,480,128]{2,1,0:T(8,128)(2,1)} %all-to-all-done.2.refs_1_.refs_7_, f32[6,1,1024]{2,1,0:T(1,128)} %get-tuple-element.130.refs_9_.refs_2_, bf16[2,384,768]{2,1,0:T(8,128)(2,1)} %get-tuple-element.167.refs_3_), custom_call_target="tpu_custom_call" | custom-call | flops 16106127360000 | bytes 5505024000 | tf_op jit(solution)/shard_map/attend_back/pallas_call | solution.py:64
  407.3 4.4 all-to-all-start.3
  411.7 4.1 cross.2
  417.3 16.3 %gates_back.1 = (bf16[4,256,1536]{2,1,0:T(8,128)(2,1)}, f32[1,1536]{1,0:T(1,128)}) custom-call(s32[1]{0:T(128)} %bitcast.13.refs_0_, s32[4]{0:T(128)} %refs_1_.3, f32[3,4096,128]{2,1,0:T(8,128)} %get-tuple-element.128.refs_1_.refs_5_.refs_2_, f32[3,4096,128]{2,1,0:T(8,128)} %get-tuple-element.129.refs_2_.refs_3_, ...), custom_call_target="tpu_custom_call" | custom-call | flops 1610612736000 | bytes 25165824000 | tf_op jit(solution)/shard_map/gates_back/pallas_call | solution.py:64
  433.6 4.5 split.5
  441.5 12.5 %rest.1 = (bf16[4,416,768]{2,1,0:T(8,128)(2,1)}, bf16[4,416,768]{2,1,0:T(8,128)(2,1)}) custom-call(s32[8]{0:T(128)} %broadcast_xor_fusion.refs_0_.refs_1_, bf16[8,1632,768]{2,1,0:T(8,128)(2,1)} %bitcast.70, bf16[4,256,1536]{2,1,0:T(8,128)(2,1)} %get-tuple-element.181.refs_2_, bf16[8,1632,768]{2,1,0:T(8,128)(2,1)} %bitcast.71, ...), custom_call_target="tpu_custom_call" | custom-call | flops 4831838208000 | bytes 11796480000 | tf_op jit(solution)/shard_map/rest/pallas_call | solution.py:64
  454.0 2.6 halve.2
  456.6 11.8 %qkv_back.1 = (f32[512,768]{1,0:T(8,128)}, bf16[4,416,768]{2,1,0:T(8,128)(2,1)}, bf16[4,416,768]{2,1,0:T(8,128)(2,1)}) custom-call(s32[8]{0:T(128)} %broadcast_xor_fusion.refs_0_.refs_1_, bf16[8,6,3,64,128]{4,3,2,1,0:T(8,128)(2,1)} %all-to-all-done.3.refs_1_, bf16[512,768]{1,0:T(8,128)(2,1)} %bitcast.80, bf16[8,1632,768]{2,1,0:T(8,128)(2,1)} %bitcast.73, ...), custom_call_target="tpu_custom_call" | custom-call | flops 4831838208000 | bytes 18087936000 | tf_op jit(solution)/shard_map/qkv_back/pallas_call | solution.py:64
  468.4 3.9 cross.3
  472.9 2.4 collective-permute-start.31
  475.3 20.1 %collective-permute-done.31.refs_1_ = bf16[288,768]{1,0:T(8,128)(2,1)S(1)} collective-permute-done((bf16[288,768]{1,0:T(8,128)(2,1)S(1)}, bf16[288,768]{1,0:T(8,128)(2,1)S(1)}, u32[]{:S(2)}, u32[]{:S(2)}) %collective-permute-start.31) | collective-permute-done | bytes 442400 | tf_op jit(solution)/shard_map/ppermute | solution.py:1173
  496.2 2.0 add.27.refs_4_.refs_1_
  499.7 6.7 %split.6 = (bf16[2,416,768]{2,1,0:T(8,128)(2,1)}, bf16[2,416,768]{2,1,0:T(8,128)(2,1)}, bf16[2,416,768]{2,1,0:T(8,128)(2,1)}, bf16[2,416,768]{2,1,0:T(8,128)(2,1)}) custom-call(bf16[4,416,768]{2,1,0:T(8,128)(2,1)} %get-tuple-element.188.refs_3_.refs_0_, bf16[4,416,768]{2,1,0:T(8,128)(2,1)} %get-tuple-element.191.refs_7_.refs_1_, ...), custom_call_target="tpu_custom_call" | custom-call | flops 1277952000 | bytes 15335424000 | tf_op jit(solution)/shard_map/split/pallas_call | solution.py:64
  507.1 3.0 collective-permute-start.34
  510.1 21.3 %collective-permute-done.35.refs_2_ = bf16[384,768]{1,0:T(8,128)(2,1)S(1)} collective-permute-done((bf16[384,768]{1,0:T(8,128)(2,1)S(1)}, bf16[384,768]{1,0:T(8,128)(2,1)S(1)}, u32[]{:S(2)}, u32[]{:S(2)}) %collective-permute-start.35) | collective-permute-done | bytes 589856 | tf_op jit(solution)/shard_map/ppermute | solution.py:1173
  532.2 2.2 halve.3
  535.2 2.1 assemble.2.refs_4_.refs_1_
  538.8 4.1 split.7
  546.1 2.2 collective-permute-start.39
  548.3 14.0 %collective-permute-done.39.refs_1_ = bf16[192,768]{1,0:T(8,128)(2,1)S(1)} collective-permute-done((bf16[192,768]{1,0:T(8,128)(2,1)}, bf16[192,768]{1,0:T(8,128)(2,1)S(1)}, u32[]{:S(2)}, u32[]{:S(2)}) %collective-permute-start.39) | collective-permute-done | bytes 294944 | tf_op jit(solution)/shard_map/ppermute | solution.py:1173
  564.8 3.3 collective-permute-start.43
  569.0 3.6 finish.2.refs_5_
  573.7 3.4 deal.1
  577.0 2.2 collective-permute-start.41
  579.2 2.2 collective-permute-start.42
  582.3 1.9 assemble.3.refs_4_.refs_1_
  584.2 10.1 %collective-permute-done.40.refs_1_ = bf16[208,768]{1,0:T(8,128)(2,1)S(1)} collective-permute-done((bf16[208,768]{1,0:T(8,128)(2,1)}, bf16[208,768]{1,0:T(8,128)(2,1)S(1)}, u32[]{:S(2)}, u32[]{:S(2)}) %collective-permute-start.40) | collective-permute-done | bytes 319520 | tf_op jit(solution)/shard_map/ppermute | solution.py:1447
  594.3 8.0 %collective-permute-done.41.refs_2_ = bf16[208,768]{1,0:T(8,128)(2,1)S(1)} collective-permute-done((bf16[208,768]{1,0:T(8,128)(2,1)}, bf16[208,768]{1,0:T(8,128)(2,1)S(1)}, u32[]{:S(2)}, u32[]{:S(2)}) %collective-permute-start.41) | collective-permute-done | bytes 319520 | tf_op jit(solution)/shard_map/ppermute | solution.py:1447
  603.2 2.1 total.1.refs_3_.refs_1_
  605.3 5.8 collective-permute-start.44
  611.2 2.2 collective-permute-start.46
  613.4 3.6 collective-permute-done.47.refs_2_
  617.8 2.8 finish.3
  620.6 6.5 collective-permute-done.44.refs_2_
  627.1 9.3 %collective-permute-done.45.refs_3_ = bf16[208,768]{1,0:T(8,128)(2,1)S(1)} collective-permute-done((bf16[208,768]{1,0:T(8,128)(2,1)}, bf16[208,768]{1,0:T(8,128)(2,1)S(1)}, u32[]{:S(2)}, u32[]{:S(2)}) %collective-permute-start.45) | collective-permute-done | bytes 319520 | tf_op jit(solution)/shard_map/ppermute | solution.py:1461
  637.2 2.8 spread.1
  (206 shorter events, 68.7 us)
Async XLA Ops:
  7.2 112.3 %all-gather.5.cloned.1.call-start = ((), (), s32[]{:S(2)}) async-start(), calls=%async_computation.4 | async-start | bytes 22560768 | tf_op jit(solution)/shard_map/all_gather | solution.py:1537
  12.9 229.7 %all-gather.7.cloned.1.call-start = ((), (), s32[]{:S(2)}) async-start(), calls=%async_computation.5 | async-start | bytes 15925248 | tf_op jit(solution)/shard_map/all_gather | solution.py:1538
  19.4 101.5 %copy-start.28 = (s32[4,512]{1,0:T(4,128)}, s32[4,512]{1,0:T(4,128)S(1)}, u32[]{:S(2)}) copy-start(s32[4,512]{1,0:T(4,128)S(1)} %rev.4) | copy-start | bytes 24580
  127.2 51.3 %all-to-all-start = ((bf16[8,6,3,64,128]{4,3,2,1,0:T(8,128)(2,1)}), bf16[8,6,3,64,128]{4,3,2,1,0:T(8,128)(2,1)}, u32[]{:S(2)}, u32[]{:S(2)}) async-start(bf16[8,6,3,64,128]{4,3,2,1,0:T(8,128)(2,1)} %qkv.1.refs_7_), calls=%async_computation | async-start | bytes 4718592 | tf_op jit(solution)/shard_map/all_to_all | solution.py:1552
  131.7 19.6 %copy-start.31 = (s32[4,1,128]{2,1,0:T(1,128)S(1)}, s32[4,1,128]{2,1,0:T(1,128)}, u32[]{:S(2)}) copy-start(s32[4,1,128]{2,1,0:T(1,128)} %param.25) | copy-start | bytes 6148
  131.7 19.6 %copy-start.33 = (s32[4,128]{1,0:T(4,128)S(1)}, s32[4,128]{1,0:T(4,128)}, u32[]{:S(2)}) copy-start(s32[4,128]{1,0:T(4,128)} %reduce_window_sum.15) | copy-start | bytes 6148
  149.2 7.9 %collective-permute-start = (f32[2,3,8,128]{3,2,1,0:T(8,128)}, f32[2,3,8,128]{3,2,1,0:T(8,128)S(1)}, u32[]{:S(2)}, u32[]{:S(2)}) collective-permute-start(f32[2,3,8,128]{3,2,1,0:T(8,128)} %get-tuple-element.126.refs_1_), channel_id=1, source_target_pairs={{0,1},{1,0},{2,3},{3,2},{4,5},{5,4},{6,7},{7,6},{8,9},{9,8},{10,11... | collective-permute-start | bytes 73736 | tf_op jit(solution)/shard_map/ppermute | solution.py:1555
  149.6 28.1 %collective-permute-start.1 = (f32[2,3,8,128]{3,2,1,0:T(8,128)}, f32[2,3,8,128]{3,2,1,0:T(8,128)S(1)}, u32[]{:S(2)}, u32[]{:S(2)}) collective-permute-start(f32[2,3,8,128]{3,2,1,0:T(8,128)} %get-tuple-element.126.refs_1_), channel_id=1, source_target_pairs={{0,2},{1,3},{2,0},{3,1},{4,6},{5,7},{6,4},{7,5},{8,10},{9,11},{10,... | collective-permute-start | bytes 73736 | tf_op jit(solution)/shard_map/ppermute | solution.py:1555
  153.9 43.0 %collective-permute-start.2 = (f32[2,3,8,128]{3,2,1,0:T(8,128)}, f32[2,3,8,128]{3,2,1,0:T(8,128)}, u32[]{:S(2)}, u32[]{:S(2)}) collective-permute-start(f32[2,3,8,128]{3,2,1,0:T(8,128)} %get-tuple-element.126.refs_1_), channel_id=1, source_target_pairs={{0,3},{1,2},{2,1},{3,0},{4,7},{5,6},{6,5},{7,4},{8,11},{9,10},{10,... | collective-permute-start | bytes 73736 | tf_op jit(solution)/shard_map/ppermute | solution.py:1555
  153.9 43.0 %collective-permute-start.3 = (f32[2,3,8,128]{3,2,1,0:T(8,128)}, f32[2,3,8,128]{3,2,1,0:T(8,128)}, u32[]{:S(2)}, u32[]{:S(2)}) collective-permute-start(f32[2,3,8,128]{3,2,1,0:T(8,128)} %get-tuple-element.126.refs_1_), channel_id=1, source_target_pairs={{0,4},{1,5},{2,6},{3,7},{4,0},{5,1},{6,2},{7,3},{8,12},{9,13},{10,... | collective-permute-start | bytes 73736 | tf_op jit(solution)/shard_map/ppermute | solution.py:1555
  155.6 41.3 %collective-permute-start.4 = (f32[2,3,8,128]{3,2,1,0:T(8,128)}, f32[2,3,8,128]{3,2,1,0:T(8,128)}, u32[]{:S(2)}, u32[]{:S(2)}) collective-permute-start(f32[2,3,8,128]{3,2,1,0:T(8,128)} %get-tuple-element.126.refs_1_), channel_id=1, source_target_pairs={{0,5},{1,4},{2,7},{3,6},{4,1},{5,0},{6,3},{7,2},{8,13},{9,12},{10,... | collective-permute-start | bytes 73736 | tf_op jit(solution)/shard_map/ppermute | solution.py:1555
  157.1 35.3 %copy-start.35 = (f32[2,3,8,128]{3,2,1,0:T(8,128)}, f32[2,3,8,128]{3,2,1,0:T(8,128)S(1)}, u32[]{:S(2)}) copy-start(f32[2,3,8,128]{3,2,1,0:T(8,128)S(1)} %collective-permute-done.refs_2_) | copy-start | bytes 73732
  157.1 39.8 %collective-permute-start.5 = (f32[2,3,8,128]{3,2,1,0:T(8,128)}, f32[2,3,8,128]{3,2,1,0:T(8,128)}, u32[]{:S(2)}, u32[]{:S(2)}) collective-permute-start(f32[2,3,8,128]{3,2,1,0:T(8,128)} %get-tuple-element.126.refs_1_), channel_id=1, source_target_pairs={{0,6},{1,7},{2,4},{3,5},{4,2},{5,3},{6,0},{7,1},{8,14},{9,15},{10,... | collective-permute-start | bytes 73736 | tf_op jit(solution)/shard_map/ppermute | solution.py:1555
  177.7 14.8 %copy-start.36 = (f32[2,3,8,128]{3,2,1,0:T(8,128)}, f32[2,3,8,128]{3,2,1,0:T(8,128)S(1)}, u32[]{:S(2)}) copy-start(f32[2,3,8,128]{3,2,1,0:T(8,128)S(1)} %collective-permute-done.1.refs_3_) | copy-start | bytes 73732
  177.7 19.3 %collective-permute-start.6 = (f32[2,3,8,128]{3,2,1,0:T(8,128)}, f32[2,3,8,128]{3,2,1,0:T(8,128)}, u32[]{:S(2)}, u32[]{:S(2)}) collective-permute-start(f32[2,3,8,128]{3,2,1,0:T(8,128)} %get-tuple-element.126.refs_1_), channel_id=1, source_target_pairs={{0,7},{1,6},{2,5},{3,4},{4,3},{5,2},{6,1},{7,0},{8,15},{9,14},{10,... | collective-permute-start | bytes 73736 | tf_op jit(solution)/shard_map/ppermute | solution.py:1555
  192.5 25.7 %all-to-all-start.1 = ((bf16[8,6,64,128]{3,2,1,0:T(8,128)(2,1)}), bf16[8,6,64,128]{3,2,1,0:T(8,128)(2,1)}, u32[]{:S(2)}, u32[]{:S(2)}) async-start(bf16[8,6,64,128]{3,2,1,0:T(8,128)(2,1)} %get-tuple-element.127), calls=%async_computation.1 | async-start | bytes 1572864 | tf_op jit(solution)/shard_map/all_to_all | solution.py:1560
  209.4 34.0 %collective-permute-start.10 = (bf16[512,768]{1,0:T(8,128)(2,1)}, bf16[512,768]{1,0:T(8,128)(2,1)}, u32[]{:S(2)}, u32[]{:S(2)}) collective-permute-start(bf16[512,768]{1,0:T(8,128)(2,1)} %get-tuple-element.131.refs_7_.refs_1_.refs_2_), channel_id=1, source_target_pairs={{0,1},{1,0},{2,3},{3,2},{4,5},{5,4},{6,7},{7,6},{8,9},{9,8},{10,11... | collective-permute-start | bytes 2359304 | tf_op jit(solution)/shard_map/ppermute | solution.py:1173
  236.4 7.0 %collective-permute-start.9 = (bf16[512,768]{1,0:T(8,128)(2,1)}, bf16[512,768]{1,0:T(8,128)(2,1)S(1)}, u32[]{:S(2)}, u32[]{:S(2)}) collective-permute-start(bf16[512,768]{1,0:T(8,128)(2,1)} %get-tuple-element.132.refs_0_.refs_12_.refs_1_), channel_id=1, source_target_pairs={{0,1},{1,0},{2,3},{3,2},{4,5},{5,4},{6,7},{7,6},{8,9},{9,8},{10,11... | collective-permute-start | bytes 2359304 | tf_op jit(solution)/shard_map/ppermute | solution.py:1173
  238.2 4.4 collective-permute-start.8
  239.5 3.9 collective-permute-start.7
  244.3 24.9 %copy-start.45 = (s32[8]{0:T(128)S(1)}, s32[8]{0:T(128)}, u32[]{:S(2)}) copy-start(s32[8]{0:T(128)} %constant.58.clone) | copy-start | bytes 100
  264.2 9.9 %collective-permute-start.11 = (bf16[4,1,1536]{2,1,0:T(2,128)(2,1)}, bf16[4,1,1536]{2,1,0:T(2,128)(2,1)S(1)}, u32[]{:S(2)}, u32[]{:S(2)}) collective-permute-start(bf16[4,1,1536]{2,1,0:T(2,128)(2,1)} %get-tuple-element.138.refs_11_), channel_id=1, source_target_pairs={{0,1},{1,2},{2,3},{3,4},{4,5},{5,6},{6,7},{8,9},{9,10},{10,11},{11... | collective-permute-start | bytes 36872 | tf_op jit(solution)/shard_map/ppermute | solution.py:1488
  268.0 6.1 collective-permute-start.12
  271.2 30.3 %collective-permute-start.13 = (bf16[512,1536]{1,0:T(8,128)(2,1)}, bf16[512,1536]{1,0:T(8,128)(2,1)}, u32[]{:S(2)}, u32[]{:S(2)}) collective-permute-start(bf16[512,1536]{1,0:T(8,128)(2,1)} %get-tuple-element.137.refs_0_.refs_5_), channel_id=1, source_target_pairs={{0,1},{1,0},{2,3},{3,2},{4,5},{5,4},{6,7},{7,6},{8,9},{9,8},{10,11... | collective-permute-start | bytes 4718600 | tf_op jit(solution)/shard_map/ppermute | solution.py:1173
  274.7 22.6 %copy-start.32 = (s32[4,1,128]{2,1,0:T(1,128)S(1)}, s32[4,1,128]{2,1,0:T(1,128)}, u32[]{:S(2)}) copy-start(s32[4,1,128]{2,1,0:T(1,128)} %param.25) | copy-start | bytes 6148
  274.7 22.6 %copy-start.34 = (s32[4,128]{1,0:T(4,128)S(1)}, s32[4,128]{1,0:T(4,128)}, u32[]{:S(2)}) copy-start(s32[4,128]{1,0:T(4,128)} %reduce_window_sum.15) | copy-start | bytes 6148
  292.0 5.9 collective-permute-start.14
  295.5 5.9 collective-permute-start.15
  320.5 41.2 %collective-permute-start.20 = (bf16[2,576,768]{2,1,0:T(8,128)(2,1)}, bf16[2,576,768]{2,1,0:T(8,128)(2,1)}, u32[]{:S(2)}, u32[]{:S(2)}) collective-permute-start(bf16[2,576,768]{2,1,0:T(8,128)(2,1)} %get-tuple-element.165), channel_id=1, source_target_pairs={{0,2},{1,3},{2,0},{3,1},{4,6},{5,7},{6,4},{7,5},{8,10},{9,11},{10,... | collective-permute-start | bytes 5308424 | tf_op jit(solution)/shard_map/ppermute | solution.py:1173
  323.3 44.0 %collective-permute-start.21 = (bf16[2,576,768]{2,1,0:T(8,128)(2,1)}, bf16[2,576,768]{2,1,0:T(8,128)(2,1)}, u32[]{:S(2)}, u32[]{:S(2)}) collective-permute-start(bf16[2,576,768]{2,1,0:T(8,128)(2,1)} %get-tuple-element.155.refs_6_), channel_id=1, source_target_pairs={{0,4},{1,5},{2,6},{3,7},{4,0},{5,1},{6,2},{7,3},{8,12},{9,13},{10,... | collective-permute-start | bytes 5308424 | tf_op jit(solution)/shard_map/ppermute | solution.py:1173
  359.2 15.6 %collective-permute-start.16 = (bf16[768,768]{1,0:T(8,128)(2,1)}, bf16[768,768]{1,0:T(8,128)(2,1)S(1)}, u32[]{:S(2)}, u32[]{:S(2)}) collective-permute-start(bf16[768,768]{1,0:T(8,128)(2,1)} %get-tuple-element.159), channel_id=1, source_target_pairs={{0,1},{1,0},{2,3},{3,2},{4,5},{5,4},{6,7},{7,6},{8,9},{9,8},{10,11... | collective-permute-start | bytes 3538952 | tf_op jit(solution)/shard_map/ppermute | solution.py:1173
  359.3 17.0 %collective-permute-start.17 = (bf16[768,768]{1,0:T(8,128)(2,1)}, bf16[768,768]{1,0:T(8,128)(2,1)S(1)}, u32[]{:S(2)}, u32[]{:S(2)}) collective-permute-start(bf16[768,768]{1,0:T(8,128)(2,1)} %get-tuple-element.160), channel_id=1, source_target_pairs={{0,1},{1,0},{2,3},{3,2},{4,5},{5,4},{6,7},{7,6},{8,9},{9,8},{10,11... | collective-permute-start | bytes 3538952 | tf_op jit(solution)/shard_map/ppermute | solution.py:1173
  359.8 16.5 %collective-permute-start.18 = (bf16[768,768]{1,0:T(8,128)(2,1)}, bf16[768,768]{1,0:T(8,128)(2,1)S(1)}, u32[]{:S(2)}, u32[]{:S(2)}) collective-permute-start(bf16[768,768]{1,0:T(8,128)(2,1)} %get-tuple-element.161), channel_id=1, source_target_pairs={{0,1},{1,0},{2,3},{3,2},{4,5},{5,4},{6,7},{7,6},{8,9},{9,8},{10,11... | collective-permute-start | bytes 3538952 | tf_op jit(solution)/shard_map/ppermute | solution.py:1173
  361.7 14.6 %collective-permute-start.19 = (bf16[768,768]{1,0:T(8,128)(2,1)}, bf16[768,768]{1,0:T(8,128)(2,1)}, u32[]{:S(2)}, u32[]{:S(2)}) collective-permute-start(bf16[768,768]{1,0:T(8,128)(2,1)} %get-tuple-element.162), channel_id=1, source_target_pairs={{0,1},{1,0},{2,3},{3,2},{4,5},{5,4},{6,7},{7,6},{8,9},{9,8},{10,11... | collective-permute-start | bytes 3538952 | tf_op jit(solution)/shard_map/ppermute | solution.py:1173
  361.7 23.9 %all-to-all-start.2 = ((bf16[8,480,128]{2,1,0:T(8,128)(2,1)}), bf16[8,480,128]{2,1,0:T(8,128)(2,1)}, u32[]{:S(2)}, u32[]{:S(2)}) async-start(bf16[8,480,128]{2,1,0:T(8,128)(2,1)} %get-tuple-element.157.refs_4_), calls=%async_computation.2 | async-start | bytes 1966080 | tf_op jit(solution)/shard_map/all_to_all | solution.py:1620
  372.9 38.8 %collective-permute-start.22 = (bf16[1,576,768]{2,1,0:T(8,128)(2,1)}, bf16[1,576,768]{2,1,0:T(8,128)(2,1)}, u32[]{:S(2)}, u32[]{:S(2)}) collective-permute-start(bf16[1,576,768]{2,1,0:T(8,128)(2,1)} %get-tuple-element.176), channel_id=1, source_target_pairs={{0,4},{1,5},{2,6},{3,7},{4,0},{5,1},{6,2},{7,3},{8,12},{9,13},{10,... | collective-permute-start | bytes 2654216 | tf_op jit(solution)/shard_map/ppermute | solution.py:1173
  374.8 36.9 %collective-permute-start.23 = (bf16[1,576,768]{2,1,0:T(8,128)(2,1)}, bf16[1,576,768]{2,1,0:T(8,128)(2,1)}, u32[]{:S(2)}, u32[]{:S(2)}) collective-permute-start(bf16[1,576,768]{2,1,0:T(8,128)(2,1)} %get-tuple-element.166.refs_10_), channel_id=1, source_target_pairs={{0,2},{1,3},{2,0},{3,1},{4,6},{5,7},{6,4},{7,5},{8,10},{9,11},{10,... | collective-permute-start | bytes 2654216 | tf_op jit(solution)/shard_map/ppermute | solution.py:1173
  384.6 49.1 %collective-permute-start.25 = (bf16[2,384,768]{2,1,0:T(8,128)(2,1)}, bf16[2,384,768]{2,1,0:T(8,128)(2,1)}, u32[]{:S(2)}, u32[]{:S(2)}) collective-permute-start(bf16[2,384,768]{2,1,0:T(8,128)(2,1)} %get-tuple-element.186), channel_id=1, source_target_pairs={{0,2},{1,3},{2,0},{3,1},{4,6},{5,7},{6,4},{7,5},{8,10},{9,11},{10,... | collective-permute-start | bytes 3538952 | tf_op jit(solution)/shard_map/ppermute | solution.py:1173
  385.2 48.5 %collective-permute-start.26 = (bf16[2,384,768]{2,1,0:T(8,128)(2,1)}, bf16[2,384,768]{2,1,0:T(8,128)(2,1)}, u32[]{:S(2)}, u32[]{:S(2)}) collective-permute-start(bf16[2,384,768]{2,1,0:T(8,128)(2,1)} %get-tuple-element.167.refs_3_), channel_id=1, source_target_pairs={{0,4},{1,5},{2,6},{3,7},{4,0},{5,1},{6,2},{7,3},{8,12},{9,13},{10,... | collective-permute-start | bytes 3538952 | tf_op jit(solution)/shard_map/ppermute | solution.py:1173
  407.3 49.3 %all-to-all-start.3 = ((bf16[8,6,3,64,128]{4,3,2,1,0:T(8,128)(2,1)}), bf16[8,6,3,64,128]{4,3,2,1,0:T(8,128)(2,1)}, u32[]{:S(2)}, u32[]{:S(2)}) async-start(bf16[8,6,3,64,128]{4,3,2,1,0:T(8,128)(2,1)} %attend_back.1.refs_5_), calls=%async_computation.3 | async-start | bytes 4718592 | tf_op jit(solution)/shard_map/all_to_all | solution.py:1626
  415.8 38.2 %collective-permute-start.24 = (bf16[576,768]{1,0:T(8,128)(2,1)}, bf16[576,768]{1,0:T(8,128)(2,1)}, u32[]{:S(2)}, u32[]{:S(2)}) collective-permute-start(bf16[576,768]{1,0:T(8,128)(2,1)} %get-tuple-element.177.refs_10_), channel_id=1, source_target_pairs={{0,8},{8,0},{16,24},{24,16},{1,9},{9,1},{17,25},{25,17},{2,10},{10... | collective-permute-start | bytes 2654216 | tf_op jit(solution)/shard_map/ppermute | solution.py:1173
  438.1 30.3 %collective-permute-start.27 = (bf16[1,384,768]{2,1,0:T(8,128)(2,1)}, bf16[1,384,768]{2,1,0:T(8,128)(2,1)}, u32[]{:S(2)}, u32[]{:S(2)}) collective-permute-start(bf16[1,384,768]{2,1,0:T(8,128)(2,1)} %get-tuple-element.194), channel_id=1, source_target_pairs={{0,4},{1,5},{2,6},{3,7},{4,0},{5,1},{6,2},{7,3},{8,12},{9,13},{10,... | collective-permute-start | bytes 1769480 | tf_op jit(solution)/shard_map/ppermute | solution.py:1173
  440.0 28.4 %collective-permute-start.28 = (bf16[1,384,768]{2,1,0:T(8,128)(2,1)}, bf16[1,384,768]{2,1,0:T(8,128)(2,1)}, u32[]{:S(2)}, u32[]{:S(2)}) collective-permute-start(bf16[1,384,768]{2,1,0:T(8,128)(2,1)} %get-tuple-element.187.refs_7_), channel_id=1, source_target_pairs={{0,2},{1,3},{2,0},{3,1},{4,6},{5,7},{6,4},{7,5},{8,10},{9,11},{10,... | collective-permute-start | bytes 1769480 | tf_op jit(solution)/shard_map/ppermute | solution.py:1173
  472.3 25.9 %collective-permute-start.29 = (bf16[4,416,768]{2,1,0:T(8,128)(2,1)}, bf16[4,416,768]{2,1,0:T(8,128)(2,1)S(1)}, u32[]{:S(2)}, u32[]{:S(2)}) collective-permute-start(bf16[4,416,768]{2,1,0:T(8,128)(2,1)} %get-tuple-element.197), channel_id=1, source_target_pairs={{0,1},{1,0},{2,3},{3,2},{4,5},{5,4},{6,7},{7,6},{8,9},{9,8},{10,11... | collective-permute-start | bytes 7667720 | tf_op jit(solution)/shard_map/ppermute | solution.py:1173
  472.4 25.8 %collective-permute-start.30 = (bf16[4,416,768]{2,1,0:T(8,128)(2,1)}, bf16[4,416,768]{2,1,0:T(8,128)(2,1)}, u32[]{:S(2)}, u32[]{:S(2)}) collective-permute-start(bf16[4,416,768]{2,1,0:T(8,128)(2,1)} %get-tuple-element.198), channel_id=1, source_target_pairs={{0,1},{1,0},{2,3},{3,2},{4,5},{5,4},{6,7},{7,6},{8,9},{9,8},{10,11... | collective-permute-start | bytes 7667720 | tf_op jit(solution)/shard_map/ppermute | solution.py:1173
  472.9 22.5 %collective-permute-start.31 = (bf16[288,768]{1,0:T(8,128)(2,1)S(1)}, bf16[288,768]{1,0:T(8,128)(2,1)S(1)}, u32[]{:S(2)}, u32[]{:S(2)}) collective-permute-start(bf16[288,768]{1,0:T(8,128)(2,1)S(1)} %copy-done.38), channel_id=1, source_target_pairs={{0,16},{8,24},{16,0},{24,8},{1,17},{9,25},{17,1},{25,9},{2,18},{10... | collective-permute-start | bytes 1327112 | tf_op jit(solution)/shard_map/ppermute | solution.py:1173
  498.2 8.9 %copy-start.3 = (bf16[288,768]{1,0:T(8,128)(2,1)S(1)}, bf16[288,768]{1,0:T(8,128)(2,1)}, u32[]{:S(2)}) copy-start(bf16[288,768]{1,0:T(8,128)(2,1)} %add.27.refs_4_.refs_1_) | copy-start | bytes 1327108
  506.4 30.9 %collective-permute-start.32 = (bf16[2,416,768]{2,1,0:T(8,128)(2,1)}, bf16[2,416,768]{2,1,0:T(8,128)(2,1)S(1)}, u32[]{:S(2)}, u32[]{:S(2)}) collective-permute-start(bf16[2,416,768]{2,1,0:T(8,128)(2,1)} %get-tuple-element.203), channel_id=1, source_target_pairs={{0,2},{1,3},{2,0},{3,1},{4,6},{5,7},{6,4},{7,5},{8,10},{9,11},{10,... | collective-permute-start | bytes 3833864 | tf_op jit(solution)/shard_map/ppermute | solution.py:1173
  506.9 30.4 %collective-permute-start.33 = (bf16[2,416,768]{2,1,0:T(8,128)(2,1)}, bf16[2,416,768]{2,1,0:T(8,128)(2,1)S(1)}, u32[]{:S(2)}, u32[]{:S(2)}) collective-permute-start(bf16[2,416,768]{2,1,0:T(8,128)(2,1)} %get-tuple-element.204.refs_3_), channel_id=1, source_target_pairs={{0,4},{1,5},{2,6},{3,7},{4,0},{5,1},{6,2},{7,3},{8,12},{9,13},{10,... | collective-permute-start | bytes 3833864 | tf_op jit(solution)/shard_map/ppermute | solution.py:1173
  507.1 24.3 %collective-permute-start.35 = (bf16[384,768]{1,0:T(8,128)(2,1)S(1)}, bf16[384,768]{1,0:T(8,128)(2,1)S(1)}, u32[]{:S(2)}, u32[]{:S(2)}) collective-permute-start(bf16[384,768]{1,0:T(8,128)(2,1)S(1)} %copy-done.12), channel_id=1, source_target_pairs={{0,8},{8,0},{16,24},{24,16},{1,9},{9,1},{17,25},{25,17},{2,10},{10... | collective-permute-start | bytes 1769480 | tf_op jit(solution)/shard_map/ppermute | solution.py:1173
  507.1 27.3 %collective-permute-start.34 = (bf16[288,768]{1,0:T(8,128)(2,1)S(1)}, bf16[288,768]{1,0:T(8,128)(2,1)S(1)}, u32[]{:S(2)}, u32[]{:S(2)}) collective-permute-start(bf16[288,768]{1,0:T(8,128)(2,1)S(1)} %copy-done.3), channel_id=1, source_target_pairs={{0,16},{8,24},{16,0},{24,8},{1,17},{9,25},{17,1},{25,9},{2,18},{10... | collective-permute-start | bytes 1327112 | tf_op jit(solution)/shard_map/ppermute | solution.py:1173
  537.3 30.8 %collective-permute-start.38 = (bf16[576,768]{1,0:T(8,128)(2,1)}, bf16[576,768]{1,0:T(8,128)(2,1)S(1)}, u32[]{:S(2)}, u32[]{:S(2)}) collective-permute-start(bf16[576,768]{1,0:T(8,128)(2,1)} %assemble.2.refs_4_.refs_1_), channel_id=1, source_target_pairs={{0,8},{8,0},{16,24},{24,16},{1,9},{9,1},{17,25},{25,17},{2,10},{10... | collective-permute-start | bytes 2654216 | tf_op jit(solution)/shard_map/ppermute | solution.py:1173
  542.9 29.7 %collective-permute-start.36 = (bf16[1,416,768]{2,1,0:T(8,128)(2,1)}, bf16[1,416,768]{2,1,0:T(8,128)(2,1)S(1)}, u32[]{:S(2)}, u32[]{:S(2)}) collective-permute-start(bf16[1,416,768]{2,1,0:T(8,128)(2,1)} %get-tuple-element.209), channel_id=1, source_target_pairs={{0,4},{1,5},{2,6},{3,7},{4,0},{5,1},{6,2},{7,3},{8,12},{9,13},{10,... | collective-permute-start | bytes 1916936 | tf_op jit(solution)/shard_map/ppermute | solution.py:1173
  544.6 28.0 %collective-permute-start.37 = (bf16[1,416,768]{2,1,0:T(8,128)(2,1)}, bf16[1,416,768]{2,1,0:T(8,128)(2,1)S(1)}, u32[]{:S(2)}, u32[]{:S(2)}) collective-permute-start(bf16[1,416,768]{2,1,0:T(8,128)(2,1)} %get-tuple-element.210.refs_2_), channel_id=1, source_target_pairs={{0,2},{1,3},{2,0},{3,1},{4,6},{5,7},{6,4},{7,5},{8,10},{9,11},{10,... | collective-permute-start | bytes 1916936 | tf_op jit(solution)/shard_map/ppermute | solution.py:1173
  546.1 16.2 %collective-permute-start.39 = (bf16[192,768]{1,0:T(8,128)(2,1)}, bf16[192,768]{1,0:T(8,128)(2,1)S(1)}, u32[]{:S(2)}, u32[]{:S(2)}) collective-permute-start(bf16[192,768]{1,0:T(8,128)(2,1)} %get-tuple-element.206.refs_3_), channel_id=1, source_target_pairs={{0,16},{8,24},{16,0},{24,8},{1,17},{9,25},{17,1},{25,9},{2,18},{10... | collective-permute-start | bytes 884744 | tf_op jit(solution)/shard_map/ppermute | solution.py:1173
  564.8 16.7 %collective-permute-start.43 = (bf16[192,768]{1,0:T(8,128)(2,1)}, bf16[192,768]{1,0:T(8,128)(2,1)S(1)}, u32[]{:S(2)}, u32[]{:S(2)}) collective-permute-start(bf16[192,768]{1,0:T(8,128)(2,1)} %add.28.refs_3_.refs_1_), channel_id=1, source_target_pairs={{0,16},{8,24},{16,0},{24,8},{1,17},{9,25},{17,1},{25,9},{2,18},{10... | collective-permute-start | bytes 884744 | tf_op jit(solution)/shard_map/ppermute | solution.py:1173
  577.0 17.3 %collective-permute-start.40 = (bf16[208,768]{1,0:T(8,128)(2,1)}, bf16[208,768]{1,0:T(8,128)(2,1)S(1)}, u32[]{:S(2)}, u32[]{:S(2)}) collective-permute-start(bf16[208,768]{1,0:T(8,128)(2,1)} %get-tuple-element.213), channel_id=1, source_target_pairs={{0,8},{8,0},{16,24},{24,16},{1,9},{9,1},{17,25},{25,17},{2,10},{10... | collective-permute-start | bytes 958472 | tf_op jit(solution)/shard_map/ppermute | solution.py:1447
  577.0 25.3 %collective-permute-start.41 = (bf16[208,768]{1,0:T(8,128)(2,1)}, bf16[208,768]{1,0:T(8,128)(2,1)S(1)}, u32[]{:S(2)}, u32[]{:S(2)}) collective-permute-start(bf16[208,768]{1,0:T(8,128)(2,1)} %get-tuple-element.214), channel_id=1, source_target_pairs={{0,16},{8,24},{16,0},{24,8},{1,17},{9,25},{17,1},{25,9},{2,18},{10... | collective-permute-start | bytes 958472 | tf_op jit(solution)/shard_map/ppermute | solution.py:1447
  579.2 23.2 %collective-permute-start.42 = (bf16[208,768]{1,0:T(8,128)(2,1)}, bf16[208,768]{1,0:T(8,128)(2,1)S(1)}, u32[]{:S(2)}, u32[]{:S(2)}) collective-permute-start(bf16[208,768]{1,0:T(8,128)(2,1)} %get-tuple-element.215.refs_3_), channel_id=1, source_target_pairs={{0,24},{8,16},{16,8},{24,0},{1,25},{9,17},{17,9},{25,1},{2,26},{10... | collective-permute-start | bytes 958472 | tf_op jit(solution)/shard_map/ppermute | solution.py:1447
  584.2 32.8 %collective-permute-start.47 = (bf16[384,768]{1,0:T(8,128)(2,1)}, bf16[384,768]{1,0:T(8,128)(2,1)S(1)}, u32[]{:S(2)}, u32[]{:S(2)}) collective-permute-start(bf16[384,768]{1,0:T(8,128)(2,1)} %assemble.3.refs_4_.refs_1_), channel_id=1, source_target_pairs={{0,8},{8,0},{16,24},{24,16},{1,9},{9,1},{17,25},{25,17},{2,10},{10... | collective-permute-start | bytes 1769480 | tf_op jit(solution)/shard_map/ppermute | solution.py:1173
  605.3 21.7 %collective-permute-start.44 = (bf16[208,768]{1,0:T(8,128)(2,1)}, bf16[208,768]{1,0:T(8,128)(2,1)S(1)}, u32[]{:S(2)}, u32[]{:S(2)}) collective-permute-start(bf16[208,768]{1,0:T(8,128)(2,1)} %total.1.refs_3_.refs_1_), channel_id=1, source_target_pairs={{0,8},{8,0},{16,24},{24,16},{1,9},{9,1},{17,25},{25,17},{2,10},{10... | collective-permute-start | bytes 958472 | tf_op jit(solution)/shard_map/ppermute | solution.py:1461
  611.1 25.3 %collective-permute-start.45 = (bf16[208,768]{1,0:T(8,128)(2,1)}, bf16[208,768]{1,0:T(8,128)(2,1)S(1)}, u32[]{:S(2)}, u32[]{:S(2)}) collective-permute-start(bf16[208,768]{1,0:T(8,128)(2,1)} %total.1.refs_3_.refs_1_), channel_id=1, source_target_pairs={{0,16},{8,24},{16,0},{24,8},{1,17},{9,25},{17,1},{25,9},{2,18},{10... | collective-permute-start | bytes 958472 | tf_op jit(solution)/shard_map/ppermute | solution.py:1461
  611.2 25.1 %collective-permute-start.46 = (bf16[208,768]{1,0:T(8,128)(2,1)}, bf16[208,768]{1,0:T(8,128)(2,1)S(1)}, u32[]{:S(2)}, u32[]{:S(2)}) collective-permute-start(bf16[208,768]{1,0:T(8,128)(2,1)} %total.1.refs_3_.refs_1_), channel_id=1, source_target_pairs={{0,24},{8,16},{16,8},{24,0},{1,25},{9,17},{17,9},{25,1},{2,26},{10... | collective-permute-start | bytes 958472 | tf_op jit(solution)/shard_map/ppermute | solution.py:1461
  627.0 9.3 %copy-start.16 = (bf16[208,768]{1,0:T(8,128)(2,1)}, bf16[208,768]{1,0:T(8,128)(2,1)S(1)}, u32[]{:S(2)}) copy-start(bf16[208,768]{1,0:T(8,128)(2,1)S(1)} %collective-permute-done.44.refs_2_) | copy-start | bytes 958468
  (36 other events, 74.1 us)
Sparse Core Ops, SparseCore 0:
  13.0 106.4 all-gather.4
  121.3 114.1 all-gather.6

commit v2 on v1

--- a/solution.py
+++ b/solution.py
@@ -16,7 +16,7 @@
 SCALE = 1000
 F32 = jnp.float32
 BF16 = jnp.bfloat16
-VMEM_BYTES = 60 << 20
+VMEM_BYTES = 40 << 20
 
 
 def dot(left, right, left_dim, right_dim):
@@ -35,6 +35,10 @@
     return jax.ShapeDtypeStruct(dims, dtype)
 
 
+def stored(dims, dtype):
+    return pltpu.HBM(dims, dtype) if PLACED else shape(dims, dtype)
+
+
 def whole(dims):
     return pl.BlockSpec(dims, lambda *_: (0,) * len(dims))
 
@@ -43,13 +47,16 @@
     return pl.CostEstimate(flops=int(flops) * SCALE, bytes_accessed=int(nbytes) * SCALE, transcendentals=0)
 
 
+NEAR = []
 LATEST = []
+PLACED = []
+TOKEN = jax.ShapeDtypeStruct((8, LANES), F32)
 
 
 def launch(
     body, grid, prefetch, inputs, in_specs, out_specs, out_shape, scratch, price, name, carry=()
 ):
-    deps = LATEST[-1:]
+    deps = [pltpu.with_memory_space_constraint(v, pltpu.HBM) for v in LATEST]
     single = not isinstance(out_shape, (list, tuple))
     outs = [out_shape] if single else list(out_shape)
     specs = [out_specs] if single else list(out_specs)
@@ -59,24 +66,31 @@
 
     def kernel(*refs):
         own = refs[lead + extra :]
-        body(*refs[:lead], *own[: len(outs)], *own[len(outs) + len(carry) :])
-
+        body(*refs[:lead], *own[: len(outs)], *own[len(outs) + len(carry) + 1 :])
+
+    inputs = [
+        v
+        if not PLACED or v.size < 1 << 16 or any(v is near for near in NEAR)
+        else pltpu.with_memory_space_constraint(v, pltpu.HBM)
+        for v in inputs
+    ]
     results = pl.pallas_call(
         kernel,
         grid_spec=pltpu.PrefetchScalarGridSpec(
             num_scalar_prefetch=len(prefetch),
             grid=grid,
             in_specs=list(in_specs) + [anywhere] * extra,
-            out_specs=specs + [anywhere] * len(carry),
+            out_specs=specs + [anywhere] * (len(carry) + 1),
             scratch_shapes=scratch,
         ),
-        out_shape=outs + [shape(v.shape, v.dtype) for v in carry],
+        out_shape=outs + [stored(v.shape, v.dtype) for v in (*carry, TOKEN)],
         input_output_aliases={lead + i: len(outs) + i for i in range(len(carry))},
         compiler_params=params(len(grid)),
         cost_estimate=price,
         name=name,
     )(*prefetch, *inputs, *carry, *deps)
-    LATEST[:] = results[len(outs) - 1 : len(outs)]
+    NEAR.extend(v for v, out in zip(results, outs) if isinstance(out, jax.ShapeDtypeStruct))
+    *results, LATEST[:] = *results[:-1], results[-1:]
     return results[0] if len(results) == 1 else results
 
 
@@ -140,7 +154,7 @@
         [rows, packed],
         [ whole(rows.shape), pl.BlockSpec((count, blk, width), lambda j: (0, base + j, 0)), ],
         pl.BlockSpec((count, per, 1, head, toks), lambda j: (0, 0, j, 0, 0)),
-        shape((count, per, 3, head, toks), BF16),
+        stored((count, per, 3, head, toks), BF16),
         [],
         cost(6 * total * width * width, 6 * width * width + 8 * total * width),
         "qkv",
@@ -178,7 +192,7 @@
         [qkv],
         [pl.BlockSpec((count, 1, 3, head, toks), lambda p: (0, p, 0, 0, 0))],
         [ pl.BlockSpec((count, 1, head, toks), lambda p: (0, p, 0, 0)), pl.BlockSpec((1, 1, length), lambda p: (p, 0, 0)), ],
-        [shape((count, per, head, toks), BF16), shape((per, 1, length), F32)],
+        [stored((count, per, head, toks), BF16), shape((per, 1, length), F32)],
         [],
         cost(16 * per * length * length * head, 8 * per * length * head),
         "attend",
@@ -226,7 +240,7 @@
         [qkv, grads, totals],
         [ pl.BlockSpec((count, 1, 3, head, toks), lambda p: (0, p, 0, 0, 0)), pl.BlockSpec((count, head, toks), lambda p: (0, p, 0)), pl.BlockSpec((1, 1, length), lambda p: (p, 0, 0)), ],
         pl.BlockSpec((count, 1, 3, head, toks), lambda p: (0, p, 0, 0, 0)),
-        shape(qkv.shape, BF16),
+        stored(qkv.shape, BF16),
         [],
         cost(40 * per * length * length * head, 14 * per * length * head),
         "attend_back",
@@ -302,7 +316,7 @@
         [mixture, rows, packed, packed, packed, bias, norms],
         [ whole(mixture.shape), whole(rows.shape), pl.BlockSpec((count, blk, width), lambda j: (0, at_out, 0)), pl.BlockSpec((count, blk, width), lambda j: (0, at_up + j, 0)), pl.BlockSpec((owners, hidden // count, width), lambda j: (j, at_down, 0)), pl.BlockSpec((1, width), lambda j: (0, j)), whole(norms.shape), ],
         [ whole((width, total)), whole((total, width)), whole((total, 1)), whole((total, width)), pl.BlockSpec((total, width), lambda j: (0, j)), pl.BlockSpec((total, width), lambda j: (0, j)), whole((total, width)), whole((total, 1)), whole((total, width)), ],
-        [ shape((width, total), BF16), shape((total, width), F32), shape((total, 1), F32), shape((total, width), BF16), shape((total, hidden), BF16), shape((total, hidden), F32), shape((total, width), F32), shape((total, 1), F32), shape((total, width), BF16), ],
+        [ stored((width, total), BF16), stored((total, width), F32), stored((total, 1), F32), stored((total, width), BF16), stored((total, hidden), BF16), stored((total, hidden), F32), shape((total, width), F32), shape((total, 1), F32), shape((total, width), BF16)],
         [pltpu.VMEM((total, width), F32)],
         cost( 2 * total * width * (width + 2 * hidden), 4 * hidden * width + 10 * total * hidden ),
         "ffn",
@@ -324,6 +338,9 @@
     w_up_ref,
     w_down_ref,
     total_ref,
+    mix_ref,
+    pooled_ref,
+    d_proj_ref,
     *refs,
 ):
     j = pl.program_id(0)
@@ -331,8 +348,8 @@
     owners, share, _ = w_down_ref.shape
     half = count // 2
     send_refs, refs = refs[:half], refs[half:]
-    keep_ref, bias_ref, d_attn_ref, d_attended_ref, sums_ref, d_mix_ref = refs[:6]
-    db_ref, at_ref, acc_ref, part_ref = refs[6:]
+    keep_ref, bias_ref, d_attn_ref, sums_ref, d_mix_ref = refs[:5]
+    db_ref, at_ref, acc_ref, part_ref = refs[5:]
 
     @pl.when(j == 0)
     def _():
@@ -376,7 +393,21 @@
         d_sum = norm_backward(normal, rstd_ref[...], norms_ref[0:1], gradient)
         d_attn_ref[...] = d_sum
         low = d_sum.astype(BF16)
-        d_attended_ref[...] = low
+
+        def put(row):
+            for pos in range(count):
+                start = pl.multiple_of(order_ref[pos] * blk, 16)
+                piece = part_ref[pl.ds(start, blk), :].astype(BF16)
+                if pos < half:
+                    keep_ref[pos, row : row + blk, :] = piece
+                else:
+                    send_refs[pos - half][row : row + blk, :] = piece
+
+        base = keep_ref.shape[1] - 2 * blk
+        part_ref[...] = dot(mix_ref[...], low, 1, 0)
+        put(base)
+        part_ref[...] = dot(pooled_ref[...].T, d_proj_ref[...], 1, 0)
+        put(base + blk)
         turned = dot(flat_block(w_out_ref), low, 1, 1).astype(BF16)
         per = seqs * HEADS // count
         head, toks = width // HEADS, d_mix_ref.shape[2]
@@ -398,7 +429,7 @@
 
 
 def ffn_back_call(
-    slot, order, d_ffn, active, slope, normed, normal, rstd, norms, packed, at_out, at_up, at_down, totals, seqs):
+    slot, order, d_ffn, active, slope, normed, normal, rstd, norms, packed, at_out, at_up, at_down, totals, mixture, pooled, d_proj, seqs):
     total, width = d_ffn.shape
     hidden = active.shape[1]
     count = packed.shape[0]
@@ -409,16 +440,16 @@
     per = seqs * HEADS // count
     head = width // HEADS
     toks = total // seqs
-    rows_out = share + chunks * blk
+    rows_out = share + (chunks + 2) * blk
     wide = pl.BlockSpec((total, width), lambda j, *_: (0, j))
     results = launch(
         functools.partial(ffn_back_kernel, seqs),
         (chunks,),
         [slot, order],
-        [d_ffn, active, slope, normed, normal, rstd, norms, packed, packed, packed, totals],
-        [ whole(d_ffn.shape), wide, wide, whole(normed.shape), whole(normal.shape), whole(rstd.shape), whole(norms.shape), pl.BlockSpec((count, blk, width), lambda j, *_: (0, at_out, 0)), pl.BlockSpec((count, blk, width), lambda j, *_: (0, at_up + j, 0)), pl.BlockSpec((owners, share, width), lambda j, *_: (j, at_down, 0)), whole(totals.shape), ],
-        [ *[whole((rows_out, width))] * (count // 2), whole((count // 2, rows_out, width)), pl.BlockSpec((1, width), lambda j, *_: (0, j)), whole((total, width)), whole((total, width)), whole((2, width)), whole((count, per * head + 3 * RIDE, toks)), ],
-        [ *[shape((rows_out, width), BF16)] * (count // 2), shape((count // 2, rows_out, width), BF16), shape((1, hidden), F32), shape((total, width), F32), shape((total, width), BF16), shape((2, width), F32), shape((count, per * head + 3 * RIDE, toks), BF16), ],
+        [d_ffn, active, slope, normed, normal, rstd, norms, packed, packed, packed, totals, mixture, pooled, d_proj],
+        [ whole(d_ffn.shape), wide, wide, whole(normed.shape), whole(normal.shape), whole(rstd.shape), whole(norms.shape), pl.BlockSpec((count, blk, width), lambda j, *_: (0, at_out, 0)), pl.BlockSpec((count, blk, width), lambda j, *_: (0, at_up + j, 0)), pl.BlockSpec((owners, share, width), lambda j, *_: (j, at_down, 0)), whole(totals.shape), whole(mixture.shape), whole(pooled.shape), whole(d_proj.shape), ],
+        [ *[whole((rows_out, width))] * (count // 2), whole((count // 2, rows_out, width)), pl.BlockSpec((1, width), lambda j, *_: (0, j)), whole((total, width)), whole((2, width)), whole((count, per * head + 3 * RIDE, toks)), ],
+        [ *[stored((rows_out, width), BF16)] * (count // 2), stored((count // 2, rows_out, width), BF16), stored((1, hidden), F32), stored((total, width), F32), stored((2, width), F32), stored((count, per * head + 3 * RIDE, toks), BF16), ],
         [ pltpu.VMEM((total, width), BF16), pltpu.VMEM((width, total), BF16), pltpu.VMEM((total, width), F32), pltpu.VMEM((width, width), F32), ],
         cost( 8 * total * width * hidden + 2 * total * width * width, 8 * hidden * width + 10 * total * hidden, ),
         "ffn_back",
@@ -486,7 +517,7 @@
         [ids[..., None], ids[:, ::-1, None], packed, packed, packed, bias],
         [ pl.BlockSpec((1, steps, 1), lambda s, g: (s, 0, 0)), pl.BlockSpec((1, steps, 1), lambda s, g: (s, 0, 0)), pl.BlockSpec((per_group, table_rows, width), lambda s, g: (g[s], at_table, 0)), pl.BlockSpec((count, blk, width), lambda s, g: (0, at_gru, 0)), pl.BlockSpec((count, blk, width), lambda s, g: (0, at_gru + 1, 0)), whole(bias.shape), ],
         [whole(laid), whole(laid), whole((2, chunks, 2 * seqs, LANES))],
-        [shape(laid, F32), shape(laid, F32), shape((2, chunks, 2 * seqs, LANES), F32)],
+        [stored(laid, F32), stored(laid, F32), stored((2, chunks, 2 * seqs, LANES), F32)],
         [],
         cost( 2 * seqs * steps * width * (2 * NCHAR + 2 * width), 16 * seqs * steps * width ),
         "gates",
@@ -608,7 +639,7 @@
         [z, c, gathered, starts, ends, lens, packed],
         [ stream, stream, whole(gathered.shape), whole(starts.shape), whole(ends.shape), whole(lens.shape), pl.BlockSpec((count, blk, width), lambda i, *_: (0, at_char, 0)), ],
         [stream] + [whole((total, width))] * 3,
-        [shape(z.shape, F32), shape((total, width), BF16), shape((total, width), F32), shape((total, width), BF16), ],
+        [stored(z.shape, F32), stored((total, width), BF16), stored((total, width), F32), shape((total, width), BF16), ],
         [ pltpu.VMEM((chunks, span, LANES), F32), pltpu.VMEM((chunks, 2 * seqs, LANES), F32), pltpu.VMEM((total, width), F32), ],
         cost(2 * total * width * (width + length // 8), 12 * chunks * length * LANES),
         "states",
@@ -662,7 +693,7 @@
         [d_proj, packed, lens, starts, ends, z],
         [ whole(d_proj.shape), pl.BlockSpec((count, blk, width), lambda i: (0, at_char, 0)), whole(lens.shape), whole(starts.shape), whole(ends.shape), whole(z.shape), ],
         [whole(z.shape), whole((chunks, 2 * seqs, LANES))],
-        [shape(z.shape, F32), shape((chunks, 2 * seqs, LANES), F32)],
+        [stored(z.shape, F32), shape((chunks, 2 * seqs, LANES), F32)],
         [],
         cost( 2 * d_proj.shape[0] * width * (width + length // 8), 8 * chunks * length * LANES ),
         "states_back",
@@ -830,7 +861,7 @@
         [f_low, proj_low, normal1, proj, norms, low, high, packed, tok_grad, char_grad],
         [ whole(rows), whole(rows), whole(rows), whole(rows), whole(norms.shape), whole(low.shape), whole(high.shape), pl.BlockSpec((count, blk, width), lambda h, k: (0, 2 * k + h, 0)), whole(rows), whole(rows), ],
         [ whole(rows), whole(rows), whole(rows), whole(rows), pl.BlockSpec(rows, lambda h, k: (0, h)), pl.BlockSpec((1, 2, width), lambda h, k: (h, 0, 0)), pl.BlockSpec((seqs, 1, width), lambda h, k: (0, 0, h)), pl.BlockSpec((seqs, 1, width), lambda h, k: (0, 0, h)), ],
-        [ shape(rows, F32), shape(rows, F32), shape(rows, F32), shape(rows, F32), shape((total, 2 * width), BF16), shape((2, 2, width), F32), shape((seqs, 1, 2 * width), BF16), shape((seqs, 1, 2 * width), BF16), ],
+        [ stored(rows, F32), stored(rows, F32), shape(rows, F32), shape(rows, F32), shape((total, 2 * width), BF16), shape((2, 2, width), F32), shape((seqs, 1, 2 * width), BF16), shape((seqs, 1, 2 * width), BF16), ],
         [pltpu.VMEM(rows, F32), pltpu.VMEM((3, total, 2 * width), BF16)],
         cost(24 * total * width * width, 24 * width * width + 40 * total * width),
         "conv",
@@ -850,9 +881,9 @@
 
 
 def conv_weight_kernel(
-    toks, order_ref, f_ref, p_ref, other_f_ref, other_p_ref, dm_ref, low_ref, high_ref,
-    other_dm_ref, begin_ref, end_ref, far_low_ref, far_high_ref, keep_a_ref, sent_a_ref, keep_b_ref, sent_b_ref,
-    turned_ref, whole_ref, shift_ref, part_ref,
+    toks, order_ref, f_ref, p_ref, other_f_ref, other_p_ref, dm_ref, other_dm_ref, low_ref,
+    high_ref, begin_ref, end_ref, far_low_ref, far_high_ref, keep_a_ref, sent_a_ref, keep_b_ref,
+    sent_b_ref, turned_ref, whole_ref, part_ref,
 ):
     k, half = pl.program_id(0), pl.program_id(1)
     total, width = f_ref.shape
@@ -861,14 +892,6 @@
 
     @pl.when((k == 0) & (half == 0))
     def _():
-        for core, pair in enumerate(((f_ref, p_ref), (other_f_ref, other_p_ref))):
-            for part, source in enumerate(pair):
-                whole_ref[part * width : (part + 1) * width, :] = source[...].T
-            for pos in range(pieces):
-                start = pl.multiple_of(order_ref[pos] * blk, 16)
-                turned_ref[pos * blk : (pos + 1) * blk, core * total : (core + 1) * total] = (
-                    whole_ref[pl.ds(start, blk), :]
-                )
         odd = (order_ref[0] & 1) == 1
         edges = (
             (low_ref[...], high_ref[...]),
@@ -877,29 +900,38 @@
                 jnp.where(odd, begin_ref[...], far_high_ref[...]),
             ),
         )
-        for core, (source, (low, high)) in enumerate(zip((dm_ref, other_dm_ref), edges)):
-            rows = slice(core * total, (core + 1) * total)
-            for part in range(2):
+        pairs = ((f_ref, p_ref), (other_f_ref, other_p_ref))
+        for core, (pair, (low, high)) in enumerate(zip(pairs, edges)):
+            for part, source in enumerate(pair):
                 columns = slice(part * width, (part + 1) * width)
-                middle = source[:, columns]
+                middle = source[...]
                 before, after = shifted(
                     middle.astype(F32),
                     toks,
                     low[:, :, columns].astype(F32),
                     high[:, :, columns].astype(F32),
                 )
-                shift_ref[part, rows, :] = after
-                shift_ref[2 + part, rows, :] = middle
-                shift_ref[4 + part, rows, :] = before
-
-    at = 2 * k + half
-    part_ref[...] = dot(turned_ref[...], shift_ref[at], 1, 0)
+                for at, value in enumerate((before, middle, after)):
+                    whole_ref[at, columns, :] = value.T
+            for pos in range(pieces):
+                start = pl.multiple_of(order_ref[pos] * blk, 16)
+                for at in range(3):
+                    turned_ref[
+                        at, pos * blk : (pos + 1) * blk, core * total : (core + 1) * total
+                    ] = whole_ref[at, pl.ds(start, blk), :]
+
+    turned = turned_ref[k]
+    part_ref[...] = dot(turned[:, :total], dm_ref[...], 1, 0) + dot(
+        turned[:, total:], other_dm_ref[...], 1, 0
+    )
 
     def put(keep_ref, sent_ref, kept, sent):
         for index, (one, other) in enumerate(zip(kept, sent)):
             keep_ref[index] = part_ref[one * blk : (one + 1) * blk, :].astype(BF16)
             sent_ref[index] = part_ref[other * blk : (other + 1) * blk, :].astype(BF16)
 
+    at = 2 * k + half
+
     @pl.when(at < 3)
     def _():
         put(keep_a_ref, sent_a_ref, range(pieces // 2), range(pieces // 2, pieces))
@@ -909,28 +941,28 @@
         put(keep_b_ref, sent_b_ref, range(0, pieces, 2), range(1, pieces, 2))
 
 
-def conv_weight_call(order, own, other, dm, low, high, other_dm, begin, end, far_low, far_high, count):
+def conv_weight_call(order, own, other, dm, other_dm, edges, count):
     total, width = own[0].shape
-    toks = total // low.shape[0]
+    toks = total // edges[0].shape[0]
     blk = 2 * width // count
     out = (count // 4, 3 * blk, width)
     first = pl.BlockSpec((count // 4, blk, width), lambda k, h, *_: (0, jnp.minimum(2 * k + h, 2), 0))
     second = pl.BlockSpec(
         (count // 4, blk, width), lambda k, h, *_: (0, jnp.maximum(2 * k + h - 3, 0), 0)
     )
-    inputs = [*own, *other, dm, low, high, other_dm, begin, end, far_low, far_high]
+    columns = pl.BlockSpec((total, width), lambda k, h, *_: (0, h))
+    plain = [*own, *other]
     keep_a, sent_a, keep_b, sent_b = launch(
         functools.partial(conv_weight_kernel, toks),
         (3, 2),
         [order],
-        inputs,
-        [whole(v.shape) for v in inputs],
+        [*plain, dm, other_dm, *edges],
+        [*[whole(v.shape) for v in plain], columns, columns, *[whole(v.shape) for v in edges]],
         [first, first, second, second],
-        [shape(out, BF16)] * 4,
+        [stored(out, BF16)] * 4,
         [
-            pltpu.VMEM((width, 2 * total), BF16),
-            pltpu.VMEM((2 * width, total), BF16),
-            pltpu.VMEM((6, 2 * total, width), BF16),
+            pltpu.VMEM((3, width, 2 * total), BF16),
+            pltpu.VMEM((3, 2 * width, total), BF16),
             pltpu.VMEM((width, width), F32),
         ],
         cost(24 * total * width * width, 12 * width * width),
@@ -981,7 +1013,7 @@
         d_ffn_ref[...] = norm_backward(normal, rstd_ref[...], norms_ref[1:2], gradient)
 
 
-def conv_back_call(d_merged, low, high, packed, d_tok, d_char, normal1, rstd1, norms, seqs, carry):
+def conv_back_call(d_merged, low, high, packed, d_tok, d_char, normal1, rstd1, norms, seqs):
     total, width = d_tok.shape
     count = packed.shape[0]
     blk = 2 * width // count
@@ -997,12 +1029,11 @@
         [ pltpu.VMEM((6, total, width), BF16), pltpu.VMEM((total, 2 * width), F32), ],
         cost(24 * total * width * width, 24 * width * width + 20 * total * width),
         "conv_back",
-        carry,
     )
 
 
 def rest_kernel(
-    order_ref, table_ref, s_ref, w0_ref, w1_ref, mix_ref, d_att_ref, send_ref, keep_ref, part_ref,
+    order_ref, table_ref, s_ref, w0_ref, w1_ref, send_ref, keep_ref, part_ref,
 ):
     count, blk, width = w0_ref.shape
     rows = part_ref.shape[0]
@@ -1015,13 +1046,9 @@
         sums[:, width:], flat_block(w1_ref), 1, 1
     )
     place_blocks(part_ref, order_ref, send_ref, keep_ref, rows // count, 2 * blk)
-    part_ref[0:width, :] = dot(mix_ref[...], d_att_ref[...], 1, 0)
-    place_blocks(
-        part_ref.at[0:width], order_ref, send_ref, keep_ref, blk, 2 * blk + rows // count
-    )
-
-
-def rest_call(order, packed, at_table, at_gru, sums, mixture, d_att, height):
+
+
+def rest_call(order, packed, at_table, at_gru, sums, height):
     count, _, width = packed.shape
     blk = width // count
     rows = sums.shape[0] * sums.shape[1]
@@ -1031,17 +1058,15 @@
         rest_kernel,
         (1,),
         [order],
-        [packed, sums, packed, packed, mixture, d_att],
+        [packed, sums, packed, packed],
         [
             pl.BlockSpec((count, table_rows, width), lambda i, *_: (0, at_table, 0)),
             whole(sums.shape),
             pl.BlockSpec((count, blk, width), lambda i, *_: (0, at_gru, 0)),
             pl.BlockSpec((count, blk, width), lambda i, *_: (0, at_gru + 1, 0)),
-            whole(mixture.shape),
-            whole(d_att.shape),
         ],
         [whole(out), whole(out)],
-        [shape(out, BF16), shape(out, BF16)],
+        [stored(out, BF16), stored(out, BF16)],
         [pltpu.VMEM((rows, width), F32)],
         cost(8 * rows * width * width, 20 * width * width),
         "rest",
@@ -1049,7 +1074,7 @@
 
 
 def qkv_back_kernel(
-    seqs, order_ref, d_ref, x_ref, w_ref, d_attn_ref, pooled_ref, d_proj_ref,
+    seqs, order_ref, d_ref, x_ref, w_ref, d_attn_ref,
     sums0_ref, sums1_ref, sums23_ref, bias_ref, bias_up_ref, out_ref, send_ref, keep_ref, xt_ref,
     dt_ref, part_ref, small_ref,
 ):
@@ -1088,10 +1113,8 @@
             small_ref[10 + part : 11 + part] = bias_up_ref[:, part * width : (part + 1) * width]
         small = small_ref[...].astype(BF16)
         for pos in range(pieces):
-            keep_ref[pos, 4 * blk : 4 * blk + SMALL_ROWS, :] = small
-            send_ref[pos, 4 * blk : 4 * blk + SMALL_ROWS, :] = small
-        part_ref[...] = dot(pooled_ref[...].T, d_proj_ref[...], 1, 0)
-        put(slice(3 * blk, 4 * blk))
+            keep_ref[pos, 3 * blk : 3 * blk + SMALL_ROWS, :] = small
+            send_ref[pos, 3 * blk : 3 * blk + SMALL_ROWS, :] = small
 
     for s in range(seqs):
         for h in range(HEADS):
@@ -1106,13 +1129,13 @@
 
 
 def qkv_back_call(
-    order, d_qkv, rows, packed, base, d_attn, pooled, d_proj, small, seqs, height
+    order, d_qkv, rows, packed, base, d_attn, small, seqs, height
 ):
     count, per, _, head, toks = d_qkv.shape
     total, width = rows.shape
     blk = width // count
     out = (count // 2, height, width)
-    rest = [d_attn, pooled, d_proj, *small]
+    rest = [d_attn, *small]
     return launch(
         functools.partial(qkv_back_kernel, seqs),
         (3,),
@@ -1125,7 +1148,7 @@
             *[whole(v.shape) for v in rest],
         ],
         [whole((total, width)), whole(out), whole(out)],
-        [shape((total, width), F32), shape(out, BF16), shape(out, BF16)],
+        [stored((total, width), F32), stored(out, BF16), stored(out, BF16)],
         [
             pltpu.VMEM((width, total), BF16),
             pltpu.VMEM((width, total), BF16),
@@ -1217,7 +1240,7 @@
         [keep, keep, *arrived, *arrived],
         [top, bottom] + [one_top] * pieces + [one_bottom] * pieces,
         [pl.BlockSpec((pieces // 2, tile, width), lambda i: (0, i, 0))] * 4,
-        [shape((pieces // 2, rows // 2, width), BF16)] * 4,
+        [stored((pieces // 2, rows // 2, width), BF16)] * 4,
         [],
         cost(pieces * rows * width, 6 * pieces * rows * width),
         "fold",
@@ -1244,7 +1267,7 @@
         [state[0][0], state[1][0], state[0][1], state[1][1]],
         [spec] * 4,
         [out] * 4,
-        [shape((pieces // 2, rows, width), BF16)] * 4,
+        [stored((pieces // 2, rows, width), BF16)] * 4,
         [],
         cost(pieces * rows * width, 12 * pieces * rows * width),
         "split",
@@ -1272,7 +1295,7 @@
         [state[0][0], state[1][0], state[0][1], state[1][1]],
         [spec] * 4,
         [pl.BlockSpec((rows // steps, width), lambda i, *_: (i, 0))] * 2,
-        [shape((rows, width), BF16)] * 2,
+        [stored((rows, width), BF16)] * 2,
         [],
         cost(rows * width, 12 * rows * width),
         "cross",
@@ -1298,7 +1321,7 @@
         [kept, came],
         [whole(kept.shape)] * 2,
         [whole((rows // 2, width))] * 2,
-        [shape((rows // 2, width), BF16)] * 2,
+        [stored((rows // 2, width), BF16)] * 2,
         [],
         cost(rows * width, 6 * rows * width),
         "halve",
@@ -1310,7 +1333,7 @@
     out_ref[...] = add_low(kept_ref[...], came_ref[...])
 
 
-def add(kept, came):
+def add(kept, came, carry):
     return launch(
         add_kernel,
         (1,),
@@ -1318,10 +1341,11 @@
         [kept, came],
         [whole(kept.shape)] * 2,
         whole(kept.shape),
-        shape(kept.shape, BF16),
+        stored(kept.shape, BF16),
         [],
         cost(kept.size, 6 * kept.size),
         "add",
+        carry,
     )
 
 
@@ -1342,7 +1366,7 @@
         [held, came],
         [whole(held.shape)] * 2,
         whole((2 * rows, width)),
-        shape((2 * rows, width), BF16),
+        stored((2 * rows, width), BF16),
         [],
         cost(rows * width, 8 * rows * width),
         "assemble",
@@ -1376,7 +1400,7 @@
         [held, came],
         [whole(held.shape)] * 2,
         [whole(dims) for dims in outs],
-        [shape(dims, F32) for dims in outs],
+        [stored(dims, F32) for dims in outs],
         [],
         cost(held.size, 16 * held.size),
         "finish",
@@ -1391,10 +1415,11 @@
         kept, sent, *carry = halve(place, bit, kept, came, carry or ())
         came = swap(sent, "batch", bit)
         carry = yield carry
-    held = add(kept, came)
+    held = add(kept, came, carry or ())
+    held, carry = (held[0], held[1:]) if carry else (held, ())
     for bit in reversed(range(bits)):
         came = swap(held, "batch", bit)
-        yield
+        yield carry
         if bit:
             held = assemble(place, bit, held, came)
     yield finish(place, held, came, layout, outs)
@@ -1417,7 +1442,7 @@
     refs[-1][...] = total.astype(BF16)
 
 
-def spread_kernel(layout, parts, place_ref, *refs):
+def spread_kernel(layout, small_at, parts, place_ref, me_ref, *refs):
     ins, outs, all_ref = refs[:parts], refs[parts:-1], refs[-1]
     rows = ins[0].shape[0]
     for mask, ref in enumerate(ins):
@@ -1425,9 +1450,22 @@
         all_ref[pl.ds(start, rows), :] = ref[...]
     for begin, size, out, index in layout:
         outs[out][index] = all_ref[begin : begin + size].astype(F32)
-
-
-def across_direct(place, state, layout, outs):
+    blk, share = outs[-5].shape[1], outs[-1].shape[1]
+    small = all_ref[small_at : small_at + SMALL_ROWS].astype(F32)
+    width = small.shape[1]
+    me = me_ref[0]
+    mine = pltpu.roll(small, lax.rem(width - me * blk, width), 1)[:, :blk]
+    outs[-5][...] = mine[0:4]
+    outs[-4][...] = mine[4:8]
+    outs[-3][...] = mine[8:9]
+    outs[-2][...] = mine[9:10]
+    spot = me * share
+    turned = pltpu.roll(small, lax.rem(width - lax.rem(spot, width), width), 1)[:, :share]
+    row = lax.broadcasted_iota(jnp.int32, turned.shape, 0)
+    outs[-1][...] = column_sum(jnp.where(row == 10 + lax.div(spot, width), turned, 0.0))
+
+
+def across_direct(place, me, state, layout, small_at, outs):
     parts = lax.axis_size("batch")
     _, rows, width = state[0][0].shape
     part = (2 * rows // parts, width)
@@ -1439,7 +1477,7 @@
         [state[0][0], state[1][0], state[0][1], state[1][1]],
         [whole(state[0][0].shape)] * 4,
         [whole(part)] * parts,
-        [shape(part, BF16)] * parts,
+        [stored(part, BF16)] * parts,
         [pltpu.VMEM((2 * rows, width), BF16)],
         cost(rows * width, 12 * rows * width),
         "deal",
@@ -1453,7 +1491,7 @@
         [pieces[0], *came],
         [whole(part)] * parts,
         whole(part),
-        shape(part, BF16),
+        stored(part, BF16),
         [],
         cost(rows * width, 5 * rows * width),
         "total",
@@ -1461,13 +1499,13 @@
     came = [lax.ppermute(held, "batch", pairs) for _, pairs in ends]
     yield
     yield launch(
-        functools.partial(spread_kernel, layout, parts),
+        functools.partial(spread_kernel, layout, small_at, parts),
         (1,),
-        [place],
+        [place, me],
         [held, *came],
         [whole(part)] * parts,
         [whole(dims) for dims in outs],
-        [shape(dims, F32) for dims in outs],
+        [stored(dims, F32) for dims in outs],
         [pltpu.VMEM((2 * rows, width), BF16)],
         cost(rows * width, 12 * rows * width),
         "spread",
@@ -1512,6 +1550,8 @@
 
     place = lax.axis_index("batch").astype(jnp.int32).reshape(1)
     LATEST.clear()
+    PLACED[:] = [True]
+    NEAR.clear()
 
     table_at = share
     small_at = table_at + table_rows
@@ -1573,7 +1613,11 @@
             jnp.concatenate([v[:, -1:] for v in joined], -1),
         )
 
-    low, high = neighbours(*edges(f_low, proj_low))
+    begin, end = edges(f_low, proj_low)
+    low, high = neighbours(begin, end)
+    far_high = lax.ppermute(begin, "seq", [(i, i - 2) for i in range(2, count)])
+    far_low = lax.ppermute(end, "seq", [(i, i + 2) for i in range(count - 2)])
+    joined_edges = [low, high, begin, end, far_low, far_high]
     other = [swap(v, "seq", 0) for v in (f_low, proj_low)]
     tok_out, char_out, d_tok, d_char, d_merged, sums23, begin, end, *other = conv_call(
         f_low, proj_low, normal1, proj, norms, low, high, third,
@@ -1597,25 +1641,23 @@
 
     everything = (slice(None), slice(None))
     double = 2 * blk
+    batch_bits = lax.axis_size("batch").bit_length() - 1
     unit = 8 * lax.axis_size("batch")
-    height = max(3 * blk + table_rows, 4 * blk + SMALL_ROWS)
+    height = max(2 * blk + table_rows, 3 * blk + SMALL_ROWS)
     height += -height % unit
-    d_proj, d_ffn, sums1, begin, end = conv_back_call(
-        d_merged, low, high, third, d_tok, d_char, normal1, rstd1, norms, seqs, [begin, end]
-    )
-    far_high = lax.ppermute(begin, "seq", [(i, i - 2) for i in range(2, count)])
-    far_low = lax.ppermute(end, "seq", [(i, i + 2) for i in range(count - 2)])
+    d_proj, d_ffn, sums1 = conv_back_call(
+        d_merged, low, high, third, d_tok, d_char, normal1, rstd1, norms, seqs
+    )
     conv_state = conv_weight_call(
-        order, (f_low, proj_low), other, d_merged, low, high, other_dm, begin, end, far_low,
-        far_high, count,
+        order, (f_low, proj_low), other, d_merged, other_dm, joined_edges, count
     )
     conv_state = send_links(conv_state, 1)
     ds, back_totals = states_back_call(
         d_proj, first, at_char, lens, starts[:, None, :], ends[:, None, :], z
     )
-    send, keep, d_bias_up, d_attn, d_attended, sums0, d_mix = ffn_back_call(
+    send, keep, d_bias_up, d_attn, sums0, d_mix = ffn_back_call(
         slot, order, d_ffn, active, slope, normed, normal0, rstd0, norms, first, at_out, at_up,
-        at_down, back_totals, seqs,
+        at_down, back_totals, mix_t, pooled, d_proj, seqs,
     )
     d_mix = lax.all_to_all(d_mix, "seq", 0, 0, tiled=True)
     ffn_came = [swap(piece, "seq", 0) for piece in send]
@@ -1625,7 +1667,7 @@
     d_qkv = attend_back_call(qkv, d_mix, totals, step)
     d_qkv = lax.all_to_all(d_qkv, "seq", 0, 0, tiled=True)
     conv_steps = across_halves(
-        place, *cross(place, conv_state),
+        place, *cross(place, conv_state)[:2],
         [
             (r * double, double, 0, (r // 2, slice(None), slice(r % 2 * width, (r % 2 + 1) * width)))
             for r in range(6)
@@ -1638,54 +1680,55 @@
         count * table_rows // NCHAR, 2,
     )
     ffn_state, _ = onward(ffn_state, 1)
-    rest_send, rest_keep = rest_call(
-        order, first, at_table, at_gru, sums, mix_t, d_attended, height
-    )
-    next(conv_steps)
+    for _ in range(1, batch_bits):
+        next(conv_steps)
+    rest_send, rest_keep = rest_call(order, first, at_table, at_gru, sums, height)
     hidden_grad, qkv_send, qkv_keep = qkv_back_call(
-        order, d_qkv, rows, first, at_qkv, d_attn, pooled, d_proj,
+        order, d_qkv, rows, first, at_qkv, d_attn,
         [sums0, sums1, sums23, d_bias, d_bias_up], seqs, height,
     )
-    kept, sent, *both = cross(place, ffn_state, (rest_send, qkv_send))
+    PLACED.clear()
+    ffn_steps = across_halves(
+        place, *cross(place, ffn_state)[:2],
+        [
+            (0, share, 0, everything),
+            *columns_of(share, 4, 1),
+            (share + 4 * blk, blk, 2, everything),
+            (share + 5 * blk, blk, 3, everything),
+        ],
+        [(share, width), (blk, 4 * width), (blk, width), (blk, width)],
+    )
+    next(ffn_steps)
+    both = conv_steps.send([rest_send, qkv_send])
     rest_came, qkv_came = (swap(send, "seq", 0) for send in both)
-    ffn_steps = across_halves(
-        place, kept, sent,
-        [(0, share, 0, everything), *columns_of(share, 4, 1)],
-        [(share, width), (blk, 4 * width)],
-    )
-    next(ffn_steps)
-    next(conv_steps)
     last_state, _ = split([[rest_keep, rest_came], [qkv_keep, qkv_came]])
     last_state = send_links(last_state, 1)
-    next(ffn_steps)
+    for _ in range(1, batch_bits):
+        next(ffn_steps)
     next(conv_steps)
     last_state, _ = onward(last_state, 1)
-    next(ffn_steps)
     (conv_grad,) = last(conv_steps)
     last_steps = across_direct(
-        place, last_state,
+        place, me_one, last_state,
         [
             *columns_of(0, 2, 0),
             (2 * blk, table_rows, 1, everything),
-            (2 * blk + table_rows, blk, 2, everything),
-            *columns_of(height, 3, 3),
-            (height + 3 * blk, blk, 4, everything),
-            (height + 4 * blk, SMALL_ROWS, 5, everything),
+            *columns_of(height, 3, 2),
         ],
+        height + 3 * blk,
         [
-            (blk, 2 * width), (table_rows, width), (blk, width), (blk, 3 * width), (blk, width),
-            (SMALL_ROWS, width),
+            (blk, 2 * width), (table_rows, width), (blk, 3 * width),
+            (4, blk), (4, blk), (1, blk), (1, blk), (1, share),
         ],
     )
     next(last_steps)
     next(ffn_steps)
+    next(ffn_steps)
     next(last_steps)
-    down_grad, up_grad = last(ffn_steps)
-    gru_grad, table_grad, out_grad, qkv_grad, char_grad_w, small_sum = last(last_steps)
-
-    mine = lax.dynamic_slice(small_sum, (0, me * blk), (10, blk))
-    d_gain, d_shift, d_gate_b, d_cand_b = mine[:4].T, mine[4:8].T, mine[8], mine[9]
-    d_ffn_b = lax.dynamic_slice(small_sum[10:14].reshape(-1), (me * share,), (share,))
+    down_grad, up_grad, out_grad, char_grad_w = last(ffn_steps)
+    gru_grad, table_grad, qkv_grad, *small_grads = last(last_steps)
+    d_gain, d_shift = (v.T for v in small_grads[:2])
+    d_gate_b, d_cand_b, d_ffn_b = (v.reshape(-1) for v in small_grads[2:])
     shape_out = (seqs, toks, width)
     return (
         tok_out.reshape(shape_out),

time: 660 us -> 621 us (0.941)
  Pallas kernels: 291 us -> 252 us
  waiting for transfers between devices: 222 us -> 241 us
  local copies, waits for them, and re-layouts: 34.4 us -> 19.2 us
    pallas_call x35, Pallas kernels: 291 us -> 252 us  [launch(): pl.pallas_call(kernel, grid_spec=pltpu.PrefetchScalarGridSpec(num_scalar_...]
    ppermute x3, waiting for transfers between devices: 18.1 us -> 30.3 us  [across_direct(): came = [lax.ppermute(pieces[mask], 'batch', pairs) for mask, pairs in ends]]
    unnamed x93 -> x108, local copies, waits for them, and re-layouts: 18.7 us -> 13.1 us
  transfers between devices with their start and end apart: 54 -> 54, of which waited for: 15 -> 17; matrix products, arithmetic and copies ran while one was open for 3% -> 1% of each run, Pallas kernels for 36% -> 34%
where the time goes in v2:
time: 621 us; the launch traced here: 613 us
  Pallas kernels  252 us (41%)
  waiting for transfers between devices  241 us (39%)
  starting transfers between devices  82.9 us (13%)
  local copies, waits for them, and re-layouts  19.2 us (3%)
  between operations  15.4 us (2%)
    pallas_call x35, Pallas kernels, launch(): pl.pallas_call(kernel, grid_spec=pltpu.PrefetchScalarGridSpec(num_scalar_...  252 us
    all_gather x1, waiting for transfers between devices, local(): first = lax.all_gather(first, 'seq', axis=0)  99 us
    ppermute x29, waiting for transfers between devices, swap(): return lax.ppermute(value, axis, [(i, i ^ 1 << bit) for i in range(size)])  66.7 us
    ppermute x29, starting transfers between devices, swap(): return lax.ppermute(value, axis, [(i, i ^ 1 << bit) for i in range(size)])  30.7 us
    ppermute x3, waiting for transfers between devices, across_direct(): came = [lax.ppermute(pieces[mask], 'batch', pairs) for mask, pairs in ends]  30.3 us
    ppermute x7, waiting for transfers between devices, local(): lax.ppermute(block_totals, 'seq', [(i, i ^ mask) for i in range(count)])  21.2 us
    ppermute x3, waiting for transfers between devices, across_direct(): came = [lax.ppermute(held, 'batch', pairs) for _, pairs in ends]  13.4 us
    unnamed x108, local copies, waits for them, and re-layouts  13.1 us
  transfers between devices with their start and end apart: 54, of which 17 were waited for; matrix products, arithmetic and copies ran while one was open for 1% of the time, Pallas kernels for 34%

profile of v2, /device:TPU:0, one launch (start us, length us, event | category | flops | bytes accessed | tf_op | source)
XLA Modules:
  0.0 613.3 jit_solution(18341076311135087712)
XLA Ops:
  8.9 3.3 pack.2
  14.9 2.8 pack.3
  19.8 99.0 %all-gather.5.cloned.1.call-done = bf16[13056,768]{1,0:T(8,128)(2,1)} async-done(((bf16[1632,768]{1,0:T(8,128)(2,1)}), bf16[13056,768]{1,0:T(8,128)(2,1)}) %all-gather.5.cloned.1.call-update) | async-done | bytes 20054032 | tf_op jit(solution)/shard_map/all_gather | solution.py:1577
  119.7 5.7 qkv.1
  125.3 4.6 all-to-all-start
  129.9 17.5 %gates.1 = (f32[3,4096,128]{2,1,0:T(8,128)}, f32[3,4096,128]{2,1,0:T(8,128)}, f32[2,3,8,128]{3,2,1,0:T(8,128)}, f32[8,128]{1,0:T(8,128)}) custom-call(s32[4]{0:T(128)S(1)} %copy-done.33, s32[4,512,1]{2,1,0:T(8,128)S(1)} %copy.49.refs_1_, s32[4,512,1]{2,1,0:T(8,128)S(1)} %copy.50.refs_2_, bf16[8,1632,768]{2,1,0:T(8,128)(2,1)} %bitcast.53, ...), custom_call_target="tpu_custom_call" | custom-call | flops 6442450944000 | bytes 25165824000 | tf_op jit(solution)/shard_map/gates/pallas_call | solution.py:77
  147.8 1.7 collective-permute-start.1
  150.1 1.7 collective-permute-start.3
  153.3 2.6 collective-permute-start.5
  155.9 21.1 %collective-permute-done.1.refs_3_ = f32[2,3,8,128]{3,2,1,0:T(8,128)S(1)} collective-permute-done((f32[2,3,8,128]{3,2,1,0:T(8,128)}, f32[2,3,8,128]{3,2,1,0:T(8,128)S(1)}, u32[]{:S(2)}, u32[]{:S(2)}) %collective-permute-start.1) | collective-permute-done | bytes 24608 | tf_op jit(solution)/shard_map/ppermute | solution.py:1595
  178.5 13.9 %attend.1 = (bf16[8,6,64,128]{3,2,1,0:T(8,128)(2,1)}, f32[6,1,1024]{2,1,0:T(1,128)S(1)}, f32[8,128]{1,0:T(8,128)}) custom-call(bf16[8,6,3,64,128]{4,3,2,1,0:T(8,128)(2,1)} %all-to-all-done.refs_0_, f32[8,128]{1,0:T(8,128)} %get-tuple-element.177.refs_1_), custom_call_target="tpu_custom_call" | custom-call | flops 6442450944000 | bytes 3145728000 | tf_op jit(solution)/shard_map/attend/pallas_call | solution.py:77
  192.4 4.7 all-to-all-start.1
  198.1 10.6 %states.1 = (f32[3,4096,128]{2,1,0:T(8,128)}, bf16[512,768]{1,0:T(8,128)(2,1)}, f32[512,768]{1,0:T(8,128)}, bf16[512,768]{1,0:T(8,128)(2,1)}, f32[8,128]{1,0:T(8,128)}) custom-call(s32[1]{0:T(128)} %bitcast.13.refs_0_.refs_1_, f32[3,4096,128]{2,1,0:T(8,128)} %get-tuple-element.179.refs_1_.refs_5_.refs_2_, ...), custom_call_target="tpu_custom_call" | custom-call | flops 1006632960000 | bytes 18874368000 | tf_op jit(solution)/shard_map/states/pallas_call | solution.py:77
  210.9 7.6 %all-to-all-done.1.refs_0_ = bf16[8,6,64,128]{3,2,1,0:T(8,128)(2,1)} async-done(((bf16[8,6,64,128]{3,2,1,0:T(8,128)(2,1)}), bf16[8,6,64,128]{3,2,1,0:T(8,128)(2,1)}, u32[]{:S(2)}, u32[]{:S(2)}) %all-to-all-start.1) | async-done | bytes 786464 | tf_op jit(solution)/shard_map/all_to_all | solution.py:1600
  218.5 17.4 %ffn.1 = (bf16[768,512]{1,0:T(8,128)(2,1)}, f32[512,768]{1,0:T(8,128)}, f32[512,1]{1,0:T(8,128)}, bf16[512,768]{1,0:T(8,128)(2,1)}, bf16[512,3072]{1,0:T(8,128)(...) custom-call(bf16[8,6,64,128]{3,2,1,0:T(8,128)(2,1)} %all-to-all-done, ...), custom_call_target="tpu_custom_call" | custom-call | flops 5435817984000 | bytes 25165824000 | tf_op jit(solution)/shard_map/ffn/pallas_call | solution.py:77
  238.5 3.0 collective-permute-start.7
  244.6 18.2 %conv.1 = (f32[512,768]{1,0:T(8,128)}, f32[512,768]{1,0:T(8,128)}, f32[512,768]{1,0:T(8,128)S(1)}, f32[512,768]{1,0:T(8,128)S(1)}, bf16[512,1536]{1,0:T(8,128)(2...) custom-call(bf16[512,768]{1,0:T(8,128)(2,1)S(1)} %get-tuple-element., ...), custom_call_target="tpu_custom_call", output_to_operand_aliasing={{8}: (10, {}), {9}: (11, {})} | custom-call | flops 7247757312000 | bytes 29884416000 | tf_op jit(solution)/shard_map/conv/pallas_call | solution.py:77
  262.9 3.7 collective-permute-start.11
  269.3 7.9 %collective-permute-start.14 = (bf16[4,1,1536]{2,1,0:T(2,128)(2,1)}, bf16[4,1,1536]{2,1,0:T(2,128)(2,1)}, u32[]{:S(2)}, u32[]{:S(2)}) collective-permute-start(bf16[4,1,1536]{2,1,0:T(2,128)(2,1)} %copy-done.17), channel_id=1, source_target_pairs={{0,2},{1,3},{2,4},{3,5},{4,6},{5,7},{8,10},{9,11},{10,12},{11,13},... | collective-permute-start | bytes 36872 | tf_op jit(solution)/shard_map/ppermute | solution.py:1619
  277.3 14.5 %conv_back.1 = (bf16[512,768]{1,0:T(8,128)(2,1)S(1)}, f32[512,768]{1,0:T(8,128)S(1)}, f32[2,768]{1,0:T(2,128)S(1)}, f32[8,128]{1,0:T(8,128)}) custom-call(bf16[512,1536]{1,0:T(8,128)(2,1)} %get-tuple-element.194.refs_0_.refs_5_, bf16[4,1,1536]{2,1,0:T(2,128)(2,1)S(1)} %collective-permute-done.11.refs_1_, ...), custom_call_target="tpu_custom_call" | custom-call | flops 7247757312000 | bytes 22020096000 | tf_op jit(solution)/shard_map/conv_back/pallas_call | solution.py:77
  291.8 16.9 %conv_weight.1 = (bf16[2,576,768]{2,1,0:T(8,128)(2,1)}, bf16[2,576,768]{2,1,0:T(8,128)(2,1)}, bf16[2,576,768]{2,1,0:T(8,128)(2,1)}, bf16[2,576,768]{2,1,0:T(8,128)(2,1)}, f32[8,128]{1,0:T(8,128)}) custom-call(s32[8]{0:T(128)S(1)} %broadcast_xor_fusion.refs_0_.refs_1_, bf16[512,768]{1,0:T(8,128)(2,1)S(1)} %get-tuple-element.186.refs_0_.refs_1_, ...), custom_call_target="tpu_custom_call" | custom-call | flops 7247757312000 | bytes 7077888000 | tf_op jit(solution)/shard_map/conv_weight/pallas_call | solution.py:77
  308.7 2.3 collective-permute-start.20
  311.3 10.3 %states_back.1 = (f32[3,4096,128]{2,1,0:T(8,128)}, f32[3,8,128]{2,1,0:T(8,128)S(1)}, f32[8,128]{1,0:T(8,128)}) custom-call(bf16[512,768]{1,0:T(8,128)(2,1)S(1)} %get-tuple-element.207.refs_0_.refs_15_, bf16[8,1632,768]{2,1,0:T(8,128)(2,1)} %bitcast.61, f32[4,128,1]{2,1,0:T(8,128)S(1)} %convert_element_type.28.refs_6_.refs_2_, s32[4,1,128]{2,1,0:T(1,128)S(1)} %sub.14.refs_3_, ...), custom_call_target="tpu_custom_call" | custom-call | flops 1006632960000 | bytes 12582912000 | tf_op jit(solution)/shard_map/states_back/pallas_call | solution.py:77
  321.6 27.1 %ffn_back.1 = (bf16[960,768]{1,0:T(8,128)(2,1)}, bf16[960,768]{1,0:T(8,128)(2,1)}, bf16[960,768]{1,0:T(8,128)(2,1)}, bf16[960,768]{1,0:T(8,128)(2,1)}, bf16[4,96...) custom-call(s32[8]{0:T(128)S(1)} %shift-left_add_fusion.refs_0_, ...), custom_call_target="tpu_custom_call" | custom-call | flops 10267656192000 | bytes 34603008000 | tf_op jit(solution)/shard_map/ffn_back/pallas_call | solution.py:77
  350.6 3.6 all-to-all-start.2
  354.3 5.6 split.4
  359.8 1.9 collective-permute-start.22
  361.8 1.5 collective-permute-start.23
  363.3 7.9 %fold.1 = (bf16[2,480,768]{2,1,0:T(8,128)(2,1)}, bf16[2,480,768]{2,1,0:T(8,128)(2,1)}, bf16[2,480,768]{2,1,0:T(8,128)(2,1)}, bf16[2,480,768]{2,1,0:T(8,128)(2,1)}, f32[8,128]{1,0:T(8,128)}) custom-call(bf16[4,960,768]{2,1,0:T(8,128)(2,1)} %get-tuple-element.218.refs_0_.refs_1_, bf16[4,960,768]{2,1,0:T(8,128)(2,1)} %get-tuple-element.218.refs_0_.refs_1_, ...), custom_call_target="tpu_custom_call" | custom-call | flops 2949120000 | bytes 17694720000 | tf_op jit(solution)/shard_map/fold/pallas_call | solution.py:77
  373.8 21.7 %attend_back.1 = (bf16[8,6,3,64,128]{4,3,2,1,0:T(8,128)(2,1)}, f32[8,128]{1,0:T(8,128)}) custom-call(bf16[8,6,3,64,128]{4,3,2,1,0:T(8,128)(2,1)} %all-to-all-done.refs_0_, bf16[8,480,128]{2,1,0:T(8,128)(2,1)} %copy-done.42, f32[6,1,1024]{2,1,0:T(1,128)S(1)} %get-tuple-element.217.refs_2_, f32[8,128]{1,0:T(8,128)} %get-tuple-element.229.refs_3_), custom_call_target="tpu_custom_call" | custom-call | flops 16106127360000 | bytes 5505024000 | tf_op jit(solution)/shard_map/attend_back/pallas_call | solution.py:77
  395.6 4.6 all-to-all-start.3
  400.2 4.1 cross.2
  404.4 1.5 collective-permute-start.24
  405.8 14.5 %gates_back.1 = (bf16[4,256,1536]{2,1,0:T(8,128)(2,1)S(1)}, f32[1,1536]{1,0:T(1,128)S(1)}, f32[8,128]{1,0:T(8,128)}) custom-call(s32[1]{0:T(128)} %bitcast.13.refs_0_.refs_1_, s32[4]{0:T(128)S(1)} %copy-done.33, f32[3,4096,128]{2,1,0:T(8,128)} %get-tuple-element.179.refs_1_.refs_5_.refs_2_, f32[3,4096,128]{2,1,0:T(8,128)} %get-tuple-element.180.refs_2_.refs_3_, ...), custom_call_target="tpu_custom_call" | custom-call | flops 1610612736000 | bytes 25165824000 | tf_op jit(solution)/shard_map/gates_back/pallas_call | solution.py:77
  420.3 5.0 split.5
  425.4 2.0 collective-permute-start.28
  427.3 1.5 collective-permute-start.29
  428.8 2.6 halve.2
  431.4 2.4 collective-permute-start.27
  433.8 9.9 %rest.1 = (bf16[4,320,768]{2,1,0:T(8,128)(2,1)}, bf16[4,320,768]{2,1,0:T(8,128)(2,1)}, f32[8,128]{1,0:T(8,128)}) custom-call(s32[8]{0:T(128)S(1)} %broadcast_xor_fusion.refs_0_.refs_1_, bf16[8,1632,768]{2,1,0:T(8,128)(2,1)} %bitcast.65, bf16[4,256,1536]{2,1,0:T(8,128)(2,1)S(1)} %get-tuple-element.245.refs_2_, bf16[8,1632,768]{2,1,0:T(8,128)(2,1)} %bitcast.66, ...), custom_call_target="tpu_custom_call" | custom-call | flops 4831838208000 | bytes 11796480000 | tf_op jit(solution)/shard_map/rest/pallas_call | solution.py:77
  443.7 1.6 all-to-all-done.3.refs_1_
  445.4 10.2 %qkv_back.1 = (f32[512,768]{1,0:T(8,128)}, bf16[4,320,768]{2,1,0:T(8,128)(2,1)}, bf16[4,320,768]{2,1,0:T(8,128)(2,1)}, f32[8,128]{1,0:T(8,128)}) custom-call(s32[8]{0:T(128)S(1)} %broadcast_xor_fusion.refs_0_.refs_1_, bf16[8,6,3,64,128]{4,3,2,1,0:T(8,128)(2,1)} %all-to-all-done.3.refs_1_, bf16[512,768]{1,0:T(8,128)(2,1)} %bitcast.75, ...), custom_call_target="tpu_custom_call" | custom-call | flops 4831838208000 | bytes 18087936000 | tf_op jit(solution)/shard_map/qkv_back/pallas_call | solution.py:77
  455.5 4.3 collective-permute-done.28.refs_3_
  459.9 2.8 cross.3
  463.2 1.8 copy-done.3
  466.8 1.5 collective-permute-start.35
  468.3 2.0 collective-permute-done.30.refs_2_
  470.2 2.8 collective-permute-done.31.refs_3_
  476.2 2.4 collective-permute-start.34
  478.6 14.5 %collective-permute-done.35.refs_2_ = bf16[480,768]{1,0:T(8,128)(2,1)S(1)} collective-permute-done((bf16[480,768]{1,0:T(8,128)(2,1)S(1)}, bf16[480,768]{1,0:T(8,128)(2,1)S(1)}, u32[]{:S(2)}, u32[]{:S(2)}) %collective-permute-start.35) | collective-permute-done | bytes 737312 | tf_op jit(solution)/shard_map/ppermute | solution.py:1196
  493.9 4.4 collective-permute-done.34.refs_2_
  501.5 3.2 collective-permute-start.42
  504.7 21.9 %collective-permute-done.38.refs_2_ = bf16[576,768]{1,0:T(8,128)(2,1)S(1)} collective-permute-done((bf16[576,768]{1,0:T(8,128)(2,1)S(1)}, bf16[576,768]{1,0:T(8,128)(2,1)S(1)}, u32[]{:S(2)}, u32[]{:S(2)}) %collective-permute-start.38) | collective-permute-done | bytes 884768 | tf_op jit(solution)/shard_map/ppermute | solution.py:1196
  526.6 2.1 finish.2
  532.6 15.7 %collective-permute-done.43.refs_2_ = bf16[240,768]{1,0:T(8,128)(2,1)S(1)} collective-permute-done((bf16[240,768]{1,0:T(8,128)(2,1)S(1)}, bf16[240,768]{1,0:T(8,128)(2,1)S(1)}, u32[]{:S(2)}, u32[]{:S(2)}) %collective-permute-start.43) | collective-permute-done | bytes 368672 | tf_op jit(solution)/shard_map/ppermute | solution.py:1196
  548.4 2.0 collective-permute-start.39
  551.3 1.5 collective-permute-start.41
  552.8 23.7 %collective-permute-done.39.refs_1_ = bf16[160,768]{1,0:T(8,128)(2,1)S(1)} collective-permute-done((bf16[160,768]{1,0:T(8,128)(2,1)S(1)}, bf16[160,768]{1,0:T(8,128)(2,1)S(1)}, u32[]{:S(2)}, u32[]{:S(2)}) %collective-permute-start.39) | collective-permute-done | bytes 245792 | tf_op jit(solution)/shard_map/ppermute | solution.py:1485
  576.6 6.6 %collective-permute-done.41.refs_3_ = bf16[160,768]{1,0:T(8,128)(2,1)S(1)} collective-permute-done((bf16[160,768]{1,0:T(8,128)(2,1)S(1)}, bf16[160,768]{1,0:T(8,128)(2,1)S(1)}, u32[]{:S(2)}, u32[]{:S(2)}) %collective-permute-start.41) | collective-permute-done | bytes 245792 | tf_op jit(solution)/shard_map/ppermute | solution.py:1485
  583.9 2.3 collective-permute-start.45
  586.2 2.1 collective-permute-start.46
  588.3 1.8 finish.3
  590.6 4.3 collective-permute-done.44.refs_3_
  594.9 9.1 %collective-permute-done.45.refs_4_ = bf16[160,768]{1,0:T(8,128)(2,1)S(1)} collective-permute-done((bf16[160,768]{1,0:T(8,128)(2,1)S(1)}, bf16[160,768]{1,0:T(8,128)(2,1)S(1)}, u32[]{:S(2)}, u32[]{:S(2)}) %collective-permute-start.45) | collective-permute-done | bytes 245792 | tf_op jit(solution)/shard_map/ppermute | solution.py:1499
  (217 shorter events, 45.0 us)
Async XLA Ops:
  7.2 111.6 %all-gather.5.cloned.1.call-start = ((), (), s32[]{:S(2)}) async-start(), calls=%async_computation.4 | async-start | bytes 22560768 | tf_op jit(solution)/shard_map/all_gather | solution.py:1577
  12.2 229.4 %all-gather.7.cloned.1.call-start = ((), (), s32[]{:S(2)}) async-start(), calls=%async_computation.5 | async-start | bytes 15925248 | tf_op jit(solution)/shard_map/all_gather | solution.py:1578
  18.1 100.7 %copy-start.45 = (s32[4,512]{1,0:T(4,128)}, s32[4,512]{1,0:T(4,128)S(1)}, u32[]{:S(2)}) copy-start(s32[4,512]{1,0:T(4,128)S(1)} %rev.4) | copy-start | bytes 24580
  125.3 53.2 %all-to-all-start = ((bf16[8,6,3,64,128]{4,3,2,1,0:T(8,128)(2,1)}), bf16[8,6,3,64,128]{4,3,2,1,0:T(8,128)(2,1)}, u32[]{:S(2)}, u32[]{:S(2)}) async-start(bf16[8,6,3,64,128]{4,3,2,1,0:T(8,128)(2,1)} %get-tuple-element.175), calls=%async_computation | async-start | bytes 4718592 | tf_op jit(solution)/shard_map/all_to_all | solution.py:1592
  147.4 5.3 collective-permute-start
  147.8 29.3 %collective-permute-start.1 = (f32[2,3,8,128]{3,2,1,0:T(8,128)}, f32[2,3,8,128]{3,2,1,0:T(8,128)S(1)}, u32[]{:S(2)}, u32[]{:S(2)}) collective-permute-start(f32[2,3,8,128]{3,2,1,0:T(8,128)} %get-tuple-element.181.refs_1_), channel_id=1, source_target_pairs={{0,2},{1,3},{2,0},{3,1},{4,6},{5,7},{6,4},{7,5},{8,10},{9,11},{10,... | collective-permute-start | bytes 73736 | tf_op jit(solution)/shard_map/ppermute | solution.py:1595
  150.0 47.2 %collective-permute-start.2 = (f32[2,3,8,128]{3,2,1,0:T(8,128)}, f32[2,3,8,128]{3,2,1,0:T(8,128)}, u32[]{:S(2)}, u32[]{:S(2)}) collective-permute-start(f32[2,3,8,128]{3,2,1,0:T(8,128)} %get-tuple-element.181.refs_1_), channel_id=1, source_target_pairs={{0,3},{1,2},{2,1},{3,0},{4,7},{5,6},{6,5},{7,4},{8,11},{9,10},{10,... | collective-permute-start | bytes 73736 | tf_op jit(solution)/shard_map/ppermute | solution.py:1595
  150.1 47.1 %collective-permute-start.3 = (f32[2,3,8,128]{3,2,1,0:T(8,128)}, f32[2,3,8,128]{3,2,1,0:T(8,128)}, u32[]{:S(2)}, u32[]{:S(2)}) collective-permute-start(f32[2,3,8,128]{3,2,1,0:T(8,128)} %get-tuple-element.181.refs_1_), channel_id=1, source_target_pairs={{0,4},{1,5},{2,6},{3,7},{4,0},{5,1},{6,2},{7,3},{8,12},{9,13},{10,... | collective-permute-start | bytes 73736 | tf_op jit(solution)/shard_map/ppermute | solution.py:1595
  151.7 45.5 %collective-permute-start.4 = (f32[2,3,8,128]{3,2,1,0:T(8,128)}, f32[2,3,8,128]{3,2,1,0:T(8,128)}, u32[]{:S(2)}, u32[]{:S(2)}) collective-permute-start(f32[2,3,8,128]{3,2,1,0:T(8,128)} %get-tuple-element.181.refs_1_), channel_id=1, source_target_pairs={{0,5},{1,4},{2,7},{3,6},{4,1},{5,0},{6,3},{7,2},{8,13},{9,12},{10,... | collective-permute-start | bytes 73736 | tf_op jit(solution)/shard_map/ppermute | solution.py:1595
  153.3 43.9 %collective-permute-start.5 = (f32[2,3,8,128]{3,2,1,0:T(8,128)}, f32[2,3,8,128]{3,2,1,0:T(8,128)}, u32[]{:S(2)}, u32[]{:S(2)}) collective-permute-start(f32[2,3,8,128]{3,2,1,0:T(8,128)} %get-tuple-element.181.refs_1_), channel_id=1, source_target_pairs={{0,6},{1,7},{2,4},{3,5},{4,2},{5,3},{6,0},{7,1},{8,14},{9,15},{10,... | collective-permute-start | bytes 73736 | tf_op jit(solution)/shard_map/ppermute | solution.py:1595
  177.7 19.6 %collective-permute-start.6 = (f32[2,3,8,128]{3,2,1,0:T(8,128)}, f32[2,3,8,128]{3,2,1,0:T(8,128)}, u32[]{:S(2)}, u32[]{:S(2)}) collective-permute-start(f32[2,3,8,128]{3,2,1,0:T(8,128)} %get-tuple-element.181.refs_1_), channel_id=1, source_target_pairs={{0,7},{1,6},{2,5},{3,4},{4,3},{5,2},{6,1},{7,0},{8,15},{9,14},{10,... | collective-permute-start | bytes 73736 | tf_op jit(solution)/shard_map/ppermute | solution.py:1595
  192.4 26.1 %all-to-all-start.1 = ((bf16[8,6,64,128]{3,2,1,0:T(8,128)(2,1)}), bf16[8,6,64,128]{3,2,1,0:T(8,128)(2,1)}, u32[]{:S(2)}, u32[]{:S(2)}) async-start(bf16[8,6,64,128]{3,2,1,0:T(8,128)(2,1)} %get-tuple-element.178), calls=%async_computation.1 | async-start | bytes 1572864 | tf_op jit(solution)/shard_map/all_to_all | solution.py:1600
  208.7 33.7 %collective-permute-start.10 = (bf16[512,768]{1,0:T(8,128)(2,1)}, bf16[512,768]{1,0:T(8,128)(2,1)}, u32[]{:S(2)}, u32[]{:S(2)}) collective-permute-start(bf16[512,768]{1,0:T(8,128)(2,1)} %get-tuple-element.187.refs_1_.refs_2_), channel_id=1, source_target_pairs={{0,1},{1,0},{2,3},{3,2},{4,5},{5,4},{6,7},{7,6},{8,9},{9,8},{10,11... | collective-permute-start | bytes 2359304 | tf_op jit(solution)/shard_map/ppermute | solution.py:1196
  218.5 19.9 %copy-start.47 = (bf16[4,1,768]{2,1,0:T(2,128)(2,1)S(1)}, bf16[4,1,768]{2,1,0:T(2,128)(2,1)}, u32[]{:S(2)}) copy-start(bf16[4,1,768]{2,1,0:T(2,128)(2,1)} %get-tuple-element.322) | copy-start | bytes 18436
  218.5 23.0 %copy-start.53 = (s32[8]{0:T(128)S(1)}, s32[8]{0:T(128)}, u32[]{:S(2)}) copy-start(s32[8]{0:T(128)} %constant.50.clone) | copy-start | bytes 100
  237.0 5.3 collective-permute-start.9
  237.1 25.7 %copy-start.15 = (bf16[4,1,1536]{2,1,0:T(2,128)(2,1)}, bf16[4,1,1536]{2,1,0:T(2,128)(2,1)S(1)}, u32[]{:S(2)}) copy-start(bf16[4,1,1536]{2,1,0:T(2,128)(2,1)S(1)} %pad_maximum_fusion.1.refs_9_) | copy-start | bytes 36868
  237.1 4.5 collective-permute-start.8
  238.5 24.4 %copy-start.17 = (bf16[4,1,1536]{2,1,0:T(2,128)(2,1)}, bf16[4,1,1536]{2,1,0:T(2,128)(2,1)S(1)}, u32[]{:S(2)}) copy-start(bf16[4,1,1536]{2,1,0:T(2,128)(2,1)S(1)} %pad_maximum_fusion.refs_10_) | copy-start | bytes 36868
  238.5 3.9 collective-permute-start.7
  244.6 23.3 %copy-start.8 = (s32[4,128]{1,0:T(4,128)S(1)}, s32[4,128]{1,0:T(4,128)}, u32[]{:S(2)}) copy-start(s32[4,128]{1,0:T(4,128)} %reduce_window_sum.15) | copy-start | bytes 6148
  244.6 23.3 %copy-start.51 = (s32[4,1,128]{2,1,0:T(1,128)S(1)}, s32[4,1,128]{2,1,0:T(1,128)}, u32[]{:S(2)}) copy-start(s32[4,1,128]{2,1,0:T(1,128)} %param.25) | copy-start | bytes 6148
  244.6 32.6 %copy-start.36 = (f32[512,768]{1,0:T(8,128)S(1)}, f32[512,768]{1,0:T(8,128)}, u32[]{:S(2)}) copy-start(f32[512,768]{1,0:T(8,128)} %copy-done.34) | copy-start | bytes 4718596
  262.9 14.3 %collective-permute-start.11 = (bf16[4,1,1536]{2,1,0:T(2,128)(2,1)S(1)}, bf16[4,1,1536]{2,1,0:T(2,128)(2,1)S(1)}, u32[]{:S(2)}, u32[]{:S(2)}) collective-permute-start(bf16[4,1,1536]{2,1,0:T(2,128)(2,1)S(1)} %get-tuple-element.195), channel_id=1, source_target_pairs={{0,1},{1,2},{2,3},{3,4},{4,5},{5,6},{6,7},{8,9},{9,10},{10,11},{11... | collective-permute-start | bytes 36872 | tf_op jit(solution)/shard_map/ppermute | solution.py:1526
  266.6 10.6 %collective-permute-start.12 = (bf16[4,1,1536]{2,1,0:T(2,128)(2,1)S(1)}, bf16[4,1,1536]{2,1,0:T(2,128)(2,1)S(1)}, u32[]{:S(2)}, u32[]{:S(2)}) collective-permute-start(bf16[4,1,1536]{2,1,0:T(2,128)(2,1)S(1)} %get-tuple-element.196), channel_id=1, source_target_pairs={{1,0},{2,1},{3,2},{4,3},{5,4},{6,5},{7,6},{9,8},{10,9},{11,10},{12... | collective-permute-start | bytes 36872 | tf_op jit(solution)/shard_map/ppermute | solution.py:1526
  268.0 23.8 %collective-permute-start.15 = (bf16[4,1,1536]{2,1,0:T(2,128)(2,1)}, bf16[4,1,1536]{2,1,0:T(2,128)(2,1)}, u32[]{:S(2)}, u32[]{:S(2)}) collective-permute-start(bf16[4,1,1536]{2,1,0:T(2,128)(2,1)} %copy-done.15), channel_id=1, source_target_pairs={{2,0},{3,1},{4,2},{5,3},{6,4},{7,5},{10,8},{11,9},{12,10},{13,11},... | collective-permute-start | bytes 36872 | tf_op jit(solution)/shard_map/ppermute | solution.py:1618
  269.3 22.5 %collective-permute-start.14 = (bf16[4,1,1536]{2,1,0:T(2,128)(2,1)}, bf16[4,1,1536]{2,1,0:T(2,128)(2,1)}, u32[]{:S(2)}, u32[]{:S(2)}) collective-permute-start(bf16[4,1,1536]{2,1,0:T(2,128)(2,1)} %copy-done.17), channel_id=1, source_target_pairs={{0,2},{1,3},{2,4},{3,5},{4,6},{5,7},{8,10},{9,11},{10,12},{11,13},... | collective-permute-start | bytes 36872 | tf_op jit(solution)/shard_map/ppermute | solution.py:1619
  277.1 14.6 %collective-permute-start.13 = (bf16[512,1536]{1,0:T(8,128)(2,1)}, bf16[512,1536]{1,0:T(8,128)(2,1)}, u32[]{:S(2)}, u32[]{:S(2)}) collective-permute-start(bf16[512,1536]{1,0:T(8,128)(2,1)} %get-tuple-element.194.refs_0_.refs_5_), channel_id=1, source_target_pairs={{0,1},{1,0},{2,3},{3,2},{4,5},{5,4},{6,7},{7,6},{8,9},{9,8},{10,11... | collective-permute-start | bytes 4718600 | tf_op jit(solution)/shard_map/ppermute | solution.py:1196
  308.7 41.9 %collective-permute-start.20 = (bf16[2,576,768]{2,1,0:T(8,128)(2,1)}, bf16[2,576,768]{2,1,0:T(8,128)(2,1)}, u32[]{:S(2)}, u32[]{:S(2)}) collective-permute-start(bf16[2,576,768]{2,1,0:T(8,128)(2,1)} %get-tuple-element.225), channel_id=1, source_target_pairs={{0,2},{1,3},{2,0},{3,1},{4,6},{5,7},{6,4},{7,5},{8,10},{9,11},{10,... | collective-permute-start | bytes 5308424 | tf_op jit(solution)/shard_map/ppermute | solution.py:1196
  311.1 43.2 %collective-permute-start.21 = (bf16[2,576,768]{2,1,0:T(8,128)(2,1)}, bf16[2,576,768]{2,1,0:T(8,128)(2,1)}, u32[]{:S(2)}, u32[]{:S(2)}) collective-permute-start(bf16[2,576,768]{2,1,0:T(8,128)(2,1)} %get-tuple-element.226), channel_id=1, source_target_pairs={{0,4},{1,5},{2,6},{3,7},{4,0},{5,1},{6,2},{7,3},{8,12},{9,13},{10,... | collective-permute-start | bytes 5308424 | tf_op jit(solution)/shard_map/ppermute | solution.py:1196
  348.7 13.1 %collective-permute-start.16 = (bf16[960,768]{1,0:T(8,128)(2,1)}, bf16[960,768]{1,0:T(8,128)(2,1)S(1)}, u32[]{:S(2)}, u32[]{:S(2)}) collective-permute-start(bf16[960,768]{1,0:T(8,128)(2,1)} %get-tuple-element.219), channel_id=1, source_target_pairs={{0,1},{1,0},{2,3},{3,2},{4,5},{5,4},{6,7},{7,6},{8,9},{9,8},{10,11... | collective-permute-start | bytes 4423688 | tf_op jit(solution)/shard_map/ppermute | solution.py:1196
  349.0 14.3 %collective-permute-start.17 = (bf16[960,768]{1,0:T(8,128)(2,1)}, bf16[960,768]{1,0:T(8,128)(2,1)}, u32[]{:S(2)}, u32[]{:S(2)}) collective-permute-start(bf16[960,768]{1,0:T(8,128)(2,1)} %get-tuple-element.220), channel_id=1, source_target_pairs={{0,1},{1,0},{2,3},{3,2},{4,5},{5,4},{6,7},{7,6},{8,9},{9,8},{10,11... | collective-permute-start | bytes 4423688 | tf_op jit(solution)/shard_map/ppermute | solution.py:1196
  349.3 14.0 %collective-permute-start.18 = (bf16[960,768]{1,0:T(8,128)(2,1)}, bf16[960,768]{1,0:T(8,128)(2,1)}, u32[]{:S(2)}, u32[]{:S(2)}) collective-permute-start(bf16[960,768]{1,0:T(8,128)(2,1)} %get-tuple-element.221), channel_id=1, source_target_pairs={{0,1},{1,0},{2,3},{3,2},{4,5},{5,4},{6,7},{7,6},{8,9},{9,8},{10,11... | collective-permute-start | bytes 4423688 | tf_op jit(solution)/shard_map/ppermute | solution.py:1196
  350.6 12.6 %collective-permute-start.19 = (bf16[960,768]{1,0:T(8,128)(2,1)}, bf16[960,768]{1,0:T(8,128)(2,1)}, u32[]{:S(2)}, u32[]{:S(2)}) collective-permute-start(bf16[960,768]{1,0:T(8,128)(2,1)} %get-tuple-element.222), channel_id=1, source_target_pairs={{0,1},{1,0},{2,3},{3,2},{4,5},{5,4},{6,7},{7,6},{8,9},{9,8},{10,11... | collective-permute-start | bytes 4423688 | tf_op jit(solution)/shard_map/ppermute | solution.py:1196
  350.6 22.2 %all-to-all-start.2 = ((bf16[8,480,128]{2,1,0:T(8,128)(2,1)}), bf16[8,480,128]{2,1,0:T(8,128)(2,1)S(1)}, u32[]{:S(2)}, u32[]{:S(2)}) async-start(bf16[8,480,128]{2,1,0:T(8,128)(2,1)} %get-tuple-element.216), calls=%async_computation.2 | async-start | bytes 1966080 | tf_op jit(solution)/shard_map/all_to_all | solution.py:1662
  359.8 40.4 %collective-permute-start.22 = (bf16[1,576,768]{2,1,0:T(8,128)(2,1)}, bf16[1,576,768]{2,1,0:T(8,128)(2,1)}, u32[]{:S(2)}, u32[]{:S(2)}) collective-permute-start(bf16[1,576,768]{2,1,0:T(8,128)(2,1)} %get-tuple-element.239), channel_id=1, source_target_pairs={{0,4},{1,5},{2,6},{3,7},{4,0},{5,1},{6,2},{7,3},{8,12},{9,13},{10,... | collective-permute-start | bytes 2654216 | tf_op jit(solution)/shard_map/ppermute | solution.py:1196
  361.8 38.5 %collective-permute-start.23 = (bf16[1,576,768]{2,1,0:T(8,128)(2,1)}, bf16[1,576,768]{2,1,0:T(8,128)(2,1)}, u32[]{:S(2)}, u32[]{:S(2)}) collective-permute-start(bf16[1,576,768]{2,1,0:T(8,128)(2,1)} %get-tuple-element.240), channel_id=1, source_target_pairs={{0,2},{1,3},{2,0},{3,1},{4,6},{5,7},{6,4},{7,5},{8,10},{9,11},{10,... | collective-permute-start | bytes 2654216 | tf_op jit(solution)/shard_map/ppermute | solution.py:1196
  371.2 49.1 %collective-permute-start.25 = (bf16[2,480,768]{2,1,0:T(8,128)(2,1)}, bf16[2,480,768]{2,1,0:T(8,128)(2,1)}, u32[]{:S(2)}, u32[]{:S(2)}) collective-permute-start(bf16[2,480,768]{2,1,0:T(8,128)(2,1)} %get-tuple-element.250), channel_id=1, source_target_pairs={{0,2},{1,3},{2,0},{3,1},{4,6},{5,7},{6,4},{7,5},{8,10},{9,11},{10,... | collective-permute-start | bytes 4423688 | tf_op jit(solution)/shard_map/ppermute | solution.py:1196
  372.3 48.0 %collective-permute-start.26 = (bf16[2,480,768]{2,1,0:T(8,128)(2,1)}, bf16[2,480,768]{2,1,0:T(8,128)(2,1)}, u32[]{:S(2)}, u32[]{:S(2)}) collective-permute-start(bf16[2,480,768]{2,1,0:T(8,128)(2,1)} %get-tuple-element.251), channel_id=1, source_target_pairs={{0,4},{1,5},{2,6},{3,7},{4,0},{5,1},{6,2},{7,3},{8,12},{9,13},{10,... | collective-permute-start | bytes 4423688 | tf_op jit(solution)/shard_map/ppermute | solution.py:1196
  395.6 49.8 %all-to-all-start.3 = ((bf16[8,6,3,64,128]{4,3,2,1,0:T(8,128)(2,1)}), bf16[8,6,3,64,128]{4,3,2,1,0:T(8,128)(2,1)}, u32[]{:S(2)}, u32[]{:S(2)}) async-start(bf16[8,6,3,64,128]{4,3,2,1,0:T(8,128)(2,1)} %get-tuple-element.230), calls=%async_computation.3 | async-start | bytes 4718592 | tf_op jit(solution)/shard_map/all_to_all | solution.py:1668
  404.4 24.5 %collective-permute-start.24 = (bf16[576,768]{1,0:T(8,128)(2,1)}, bf16[576,768]{1,0:T(8,128)(2,1)}, u32[]{:S(2)}, u32[]{:S(2)}) collective-permute-start(bf16[576,768]{1,0:T(8,128)(2,1)} %get-tuple-element.247), channel_id=1, source_target_pairs={{0,8},{8,0},{16,24},{24,16},{1,9},{9,1},{17,25},{25,17},{2,10},{10... | collective-permute-start | bytes 2654216 | tf_op jit(solution)/shard_map/ppermute | solution.py:1196
  425.4 34.5 %collective-permute-start.28 = (bf16[1,480,768]{2,1,0:T(8,128)(2,1)}, bf16[1,480,768]{2,1,0:T(8,128)(2,1)}, u32[]{:S(2)}, u32[]{:S(2)}) collective-permute-start(bf16[1,480,768]{2,1,0:T(8,128)(2,1)} %get-tuple-element.265), channel_id=1, source_target_pairs={{0,4},{1,5},{2,6},{3,7},{4,0},{5,1},{6,2},{7,3},{8,12},{9,13},{10,... | collective-permute-start | bytes 2211848 | tf_op jit(solution)/shard_map/ppermute | solution.py:1196
  427.3 32.5 %collective-permute-start.29 = (bf16[1,480,768]{2,1,0:T(8,128)(2,1)}, bf16[1,480,768]{2,1,0:T(8,128)(2,1)}, u32[]{:S(2)}, u32[]{:S(2)}) collective-permute-start(bf16[1,480,768]{2,1,0:T(8,128)(2,1)} %get-tuple-element.266), channel_id=1, source_target_pairs={{0,2},{1,3},{2,0},{3,1},{4,6},{5,7},{6,4},{7,5},{8,10},{9,11},{10,... | collective-permute-start | bytes 2211848 | tf_op jit(solution)/shard_map/ppermute | solution.py:1196
  431.4 31.3 %collective-permute-start.27 = (bf16[288,768]{1,0:T(8,128)(2,1)}, bf16[288,768]{1,0:T(8,128)(2,1)}, u32[]{:S(2)}, u32[]{:S(2)}) collective-permute-start(bf16[288,768]{1,0:T(8,128)(2,1)} %get-tuple-element.260), channel_id=1, source_target_pairs={{0,16},{8,24},{16,0},{24,8},{1,17},{9,25},{17,1},{25,9},{2,18},{10... | collective-permute-start | bytes 1327112 | tf_op jit(solution)/shard_map/ppermute | solution.py:1196
  466.2 4.0 collective-permute-start.30
  466.3 6.8 %collective-permute-start.31 = (bf16[4,320,768]{2,1,0:T(8,128)(2,1)S(1)}, bf16[4,320,768]{2,1,0:T(8,128)(2,1)S(1)}, u32[]{:S(2)}, u32[]{:S(2)}) collective-permute-start(bf16[4,320,768]{2,1,0:T(8,128)(2,1)S(1)} %get-tuple-element.270), channel_id=1, source_target_pairs={{0,1},{1,0},{2,3},{3,2},{4,5},{5,4},{6,7},{7,6},{8,9},{9,8},{10,11... | collective-permute-start | bytes 5898248 | tf_op jit(solution)/shard_map/ppermute | solution.py:1196
  466.8 26.3 %collective-permute-start.35 = (bf16[480,768]{1,0:T(8,128)(2,1)S(1)}, bf16[480,768]{1,0:T(8,128)(2,1)S(1)}, u32[]{:S(2)}, u32[]{:S(2)}) collective-permute-start(bf16[480,768]{1,0:T(8,128)(2,1)S(1)} %get-tuple-element.278), channel_id=1, source_target_pairs={{0,8},{8,0},{16,24},{24,16},{1,9},{9,1},{17,25},{25,17},{2,10},{10... | collective-permute-start | bytes 2211848 | tf_op jit(solution)/shard_map/ppermute | solution.py:1196
  474.0 25.0 %collective-permute-start.32 = (bf16[2,320,768]{2,1,0:T(8,128)(2,1)S(1)}, bf16[2,320,768]{2,1,0:T(8,128)(2,1)S(1)}, u32[]{:S(2)}, u32[]{:S(2)}) collective-permute-start(bf16[2,320,768]{2,1,0:T(8,128)(2,1)S(1)} %get-tuple-element.274), channel_id=1, source_target_pairs={{0,2},{1,3},{2,0},{3,1},{4,6},{5,7},{6,4},{7,5},{8,10},{9,11},{10,... | collective-permute-start | bytes 2949128 | tf_op jit(solution)/shard_map/ppermute | solution.py:1196
  475.3 23.7 %collective-permute-start.33 = (bf16[2,320,768]{2,1,0:T(8,128)(2,1)S(1)}, bf16[2,320,768]{2,1,0:T(8,128)(2,1)S(1)}, u32[]{:S(2)}, u32[]{:S(2)}) collective-permute-start(bf16[2,320,768]{2,1,0:T(8,128)(2,1)S(1)} %get-tuple-element.275), channel_id=1, source_target_pairs={{0,4},{1,5},{2,6},{3,7},{4,0},{5,1},{6,2},{7,3},{8,12},{9,13},{10,... | collective-permute-start | bytes 2949128 | tf_op jit(solution)/shard_map/ppermute | solution.py:1196
  476.2 22.1 %collective-permute-start.34 = (bf16[288,768]{1,0:T(8,128)(2,1)S(1)}, bf16[288,768]{1,0:T(8,128)(2,1)S(1)}, u32[]{:S(2)}, u32[]{:S(2)}) collective-permute-start(bf16[288,768]{1,0:T(8,128)(2,1)S(1)} %get-tuple-element.276.refs_1_), channel_id=1, source_target_pairs={{0,16},{8,24},{16,0},{24,8},{1,17},{9,25},{17,1},{25,9},{2,18},{10... | collective-permute-start | bytes 1327112 | tf_op jit(solution)/shard_map/ppermute | solution.py:1196
  498.4 28.2 %collective-permute-start.38 = (bf16[576,768]{1,0:T(8,128)(2,1)S(1)}, bf16[576,768]{1,0:T(8,128)(2,1)S(1)}, u32[]{:S(2)}, u32[]{:S(2)}) collective-permute-start(bf16[576,768]{1,0:T(8,128)(2,1)S(1)} %get-tuple-element.286.refs_1_), channel_id=1, source_target_pairs={{0,8},{8,0},{16,24},{24,16},{1,9},{9,1},{17,25},{25,17},{2,10},{10... | collective-permute-start | bytes 2654216 | tf_op jit(solution)/shard_map/ppermute | solution.py:1196
  499.4 27.2 %copy-start.23 = (f32[8,128]{1,0:T(8,128)}, f32[8,128]{1,0:T(8,128)S(1)}, u32[]{:S(2)}) copy-start(f32[8,128]{1,0:T(8,128)S(1)} %get-tuple-element.287.refs_3_) | copy-start | bytes 12292
  499.4 29.3 %collective-permute-start.36 = (bf16[1,320,768]{2,1,0:T(8,128)(2,1)S(1)}, bf16[1,320,768]{2,1,0:T(8,128)(2,1)S(1)}, u32[]{:S(2)}, u32[]{:S(2)}) collective-permute-start(bf16[1,320,768]{2,1,0:T(8,128)(2,1)S(1)} %get-tuple-element.284), channel_id=1, source_target_pairs={{0,4},{1,5},{2,6},{3,7},{4,0},{5,1},{6,2},{7,3},{8,12},{9,13},{10,... | collective-permute-start | bytes 1474568 | tf_op jit(solution)/shard_map/ppermute | solution.py:1196
  500.6 28.2 %collective-permute-start.37 = (bf16[1,320,768]{2,1,0:T(8,128)(2,1)S(1)}, bf16[1,320,768]{2,1,0:T(8,128)(2,1)S(1)}, u32[]{:S(2)}, u32[]{:S(2)}) collective-permute-start(bf16[1,320,768]{2,1,0:T(8,128)(2,1)S(1)} %get-tuple-element.285), channel_id=1, source_target_pairs={{0,2},{1,3},{2,0},{3,1},{4,6},{5,7},{6,4},{7,5},{8,10},{9,11},{10,... | collective-permute-start | bytes 1474568 | tf_op jit(solution)/shard_map/ppermute | solution.py:1196
  501.5 29.0 %collective-permute-start.42 = (bf16[240,768]{1,0:T(8,128)(2,1)S(1)}, bf16[240,768]{1,0:T(8,128)(2,1)S(1)}, u32[]{:S(2)}, u32[]{:S(2)}) collective-permute-start(bf16[240,768]{1,0:T(8,128)(2,1)S(1)} %get-tuple-element.294), channel_id=1, source_target_pairs={{0,16},{8,24},{16,0},{24,8},{1,17},{9,25},{17,1},{25,9},{2,18},{10... | collective-permute-start | bytes 1105928 | tf_op jit(solution)/shard_map/ppermute | solution.py:1196
  531.1 17.1 %collective-permute-start.43 = (bf16[240,768]{1,0:T(8,128)(2,1)S(1)}, bf16[240,768]{1,0:T(8,128)(2,1)S(1)}, u32[]{:S(2)}, u32[]{:S(2)}) collective-permute-start(bf16[240,768]{1,0:T(8,128)(2,1)S(1)} %get-tuple-element.296.refs_1_), channel_id=1, source_target_pairs={{0,16},{8,24},{16,0},{24,8},{1,17},{9,25},{17,1},{25,9},{2,18},{10... | collective-permute-start | bytes 1105928 | tf_op jit(solution)/shard_map/ppermute | solution.py:1196
  548.3 34.9 %copy-start.20 = (f32[8,128]{1,0:T(8,128)}, f32[8,128]{1,0:T(8,128)S(1)}, u32[]{:S(2)}) copy-start(f32[8,128]{1,0:T(8,128)S(1)} %get-tuple-element.298.refs_4_) | copy-start | bytes 12292
  548.3 40.0 %collective-permute-start.47 = (bf16[480,768]{1,0:T(8,128)(2,1)S(1)}, bf16[480,768]{1,0:T(8,128)(2,1)S(1)}, u32[]{:S(2)}, u32[]{:S(2)}) collective-permute-start(bf16[480,768]{1,0:T(8,128)(2,1)S(1)} %get-tuple-element.300.refs_1_), channel_id=1, source_target_pairs={{0,8},{8,0},{16,24},{24,16},{1,9},{9,1},{17,25},{25,17},{2,10},{10... | collective-permute-start | bytes 2211848 | tf_op jit(solution)/shard_map/ppermute | solution.py:1196
  548.4 28.2 %collective-permute-start.39 = (bf16[160,768]{1,0:T(8,128)(2,1)S(1)}, bf16[160,768]{1,0:T(8,128)(2,1)S(1)}, u32[]{:S(2)}, u32[]{:S(2)}) collective-permute-start(bf16[160,768]{1,0:T(8,128)(2,1)S(1)} %get-tuple-element.290), channel_id=1, source_target_pairs={{0,8},{8,0},{16,24},{24,16},{1,9},{9,1},{17,25},{25,17},{2,10},{10... | collective-permute-start | bytes 737288 | tf_op jit(solution)/shard_map/ppermute | solution.py:1485
  550.4 26.2 %collective-permute-start.40 = (bf16[160,768]{1,0:T(8,128)(2,1)S(1)}, bf16[160,768]{1,0:T(8,128)(2,1)S(1)}, u32[]{:S(2)}, u32[]{:S(2)}) collective-permute-start(bf16[160,768]{1,0:T(8,128)(2,1)S(1)} %get-tuple-element.291), channel_id=1, source_target_pairs={{0,16},{8,24},{16,0},{24,8},{1,17},{9,25},{17,1},{25,9},{2,18},{10... | collective-permute-start | bytes 737288 | tf_op jit(solution)/shard_map/ppermute | solution.py:1485
  551.3 31.8 %collective-permute-start.41 = (bf16[160,768]{1,0:T(8,128)(2,1)S(1)}, bf16[160,768]{1,0:T(8,128)(2,1)S(1)}, u32[]{:S(2)}, u32[]{:S(2)}) collective-permute-start(bf16[160,768]{1,0:T(8,128)(2,1)S(1)} %get-tuple-element.292), channel_id=1, source_target_pairs={{0,24},{8,16},{16,8},{24,0},{1,25},{9,17},{17,9},{25,1},{2,26},{10... | collective-permute-start | bytes 737288 | tf_op jit(solution)/shard_map/ppermute | solution.py:1485
  583.9 11.1 %collective-permute-start.44 = (bf16[160,768]{1,0:T(8,128)(2,1)S(1)}, bf16[160,768]{1,0:T(8,128)(2,1)S(1)}, u32[]{:S(2)}, u32[]{:S(2)}) collective-permute-start(bf16[160,768]{1,0:T(8,128)(2,1)S(1)} %get-tuple-element.299.refs_2_), channel_id=1, source_target_pairs={{0,8},{8,0},{16,24},{24,16},{1,9},{9,1},{17,25},{25,17},{2,10},{10... | collective-permute-start | bytes 737288 | tf_op jit(solution)/shard_map/ppermute | solution.py:1499
  583.9 20.2 %collective-permute-start.45 = (bf16[160,768]{1,0:T(8,128)(2,1)S(1)}, bf16[160,768]{1,0:T(8,128)(2,1)S(1)}, u32[]{:S(2)}, u32[]{:S(2)}) collective-permute-start(bf16[160,768]{1,0:T(8,128)(2,1)S(1)} %get-tuple-element.299.refs_2_), channel_id=1, source_target_pairs={{0,16},{8,24},{16,0},{24,8},{1,17},{9,25},{17,1},{25,9},{2,18},{10... | collective-permute-start | bytes 737288 | tf_op jit(solution)/shard_map/ppermute | solution.py:1499
  586.2 17.9 %collective-permute-start.46 = (bf16[160,768]{1,0:T(8,128)(2,1)S(1)}, bf16[160,768]{1,0:T(8,128)(2,1)S(1)}, u32[]{:S(2)}, u32[]{:S(2)}) collective-permute-start(bf16[160,768]{1,0:T(8,128)(2,1)S(1)} %get-tuple-element.299.refs_2_), channel_id=1, source_target_pairs={{0,24},{8,16},{16,8},{24,0},{1,25},{9,17},{17,9},{25,1},{2,26},{10... | collective-permute-start | bytes 737288 | tf_op jit(solution)/shard_map/ppermute | solution.py:1499
  (44 other events, 338.1 us)
Sparse Core Ops, SparseCore 0:
  12.3 106.4 all-gather.4
  120.7 114.0 all-gather.6

commit v3 on v2

--- a/solution.py
+++ b/solution.py
@@ -1,4 +1,5 @@
 import functools
+import math
 
 import jax
 import jax.numpy as jnp
@@ -16,7 +17,8 @@
 SCALE = 1000
 F32 = jnp.float32
 BF16 = jnp.bfloat16
-VMEM_BYTES = 40 << 20
+VMEM_BYTES = 44 << 20
+VMEM_MARGIN = 9 << 20
 
 
 def dot(left, right, left_dim, right_dim):
@@ -25,9 +27,20 @@
     )
 
 
-def params(grid_rank):
+def padded_bytes(dims, dtype):
+    size = jnp.dtype(dtype).itemsize
+    dims = (1, 1, *dims)
+    rows = -(-dims[-2] * size // 32) * 32
+    lanes = -(-dims[-1] // LANES) * LANES
+    return math.prod(dims[:-2]) * rows * lanes
+
+
+def params(grid_rank, blocks, scratch):
+    need = sum(2 * padded_bytes(spec.block_shape, value.dtype) for spec, value in blocks)
+    need += sum(padded_bytes(ref.shape, ref.dtype) for ref in scratch)
     return pltpu.CompilerParams(
-        dimension_semantics=("arbitrary",) * grid_rank, vmem_limit_bytes=VMEM_BYTES
+        dimension_semantics=("arbitrary",) * grid_rank,
+        vmem_limit_bytes=min(VMEM_BYTES, need + VMEM_MARGIN),
     )
 
 
@@ -85,13 +98,75 @@
         ),
         out_shape=outs + [stored(v.shape, v.dtype) for v in (*carry, TOKEN)],
         input_output_aliases={lead + i: len(outs) + i for i in range(len(carry))},
-        compiler_params=params(len(grid)),
+        compiler_params=params(
+            len(grid), [*zip(in_specs, inputs), *zip(specs, outs)], scratch
+        ),
         cost_estimate=price,
         name=name,
     )(*prefetch, *inputs, *carry, *deps)
     NEAR.extend(v for v, out in zip(results, outs) if isinstance(out, jax.ShapeDtypeStruct))
     *results, LATEST[:] = *results[:-1], results[-1:]
     return results[0] if len(results) == 1 else results
+
+
+def plan(body, grid, prefetch, inputs, in_specs, out_specs, out_shape, scratch, price, name):
+    listed = isinstance(out_shape, (list, tuple))
+    outs = (list(out_specs), list(out_shape)) if listed else ([out_specs], [out_shape])
+    return body, grid, prefetch, inputs, in_specs, *outs, scratch, price, name
+
+
+def together(plans, carry=()):
+    bodies, grids, prefetch, inputs, in_specs, out_specs, outs, scratch, prices, names = zip(*plans)
+    assert len(set(grids)) == 1
+    groups = (prefetch, inputs, outs, scratch)
+
+    def body(*refs):
+        own = [[] for _ in plans]
+        for group in groups:
+            for refs_of, part in zip(own, group):
+                refs_of.extend(refs[: len(part)])
+                refs = refs[len(part) :]
+        for one, refs_of in zip(bodies, own):
+            one(*refs_of)
+
+    def flat(parts):
+        return [v for part in parts for v in part]
+
+    price = pl.CostEstimate(
+        flops=sum(v.flops for v in prices),
+        bytes_accessed=sum(v.bytes_accessed for v in prices),
+        transcendentals=0,
+    )
+    results = launch(
+        body, grids[0], flat(prefetch), flat(inputs), flat(in_specs), flat(out_specs), flat(outs),
+        flat(scratch), price, "_".join(names), carry,
+    )
+    results = list(results) if isinstance(results, (list, tuple)) else [results]
+    found = []
+    for part in outs:
+        found.append(results[: len(part)])
+        results = results[len(part) :]
+    return found, results
+
+
+class Steps:
+    def __init__(self, plans):
+        self.plans, self.result = plans, None
+        self.plan = next(plans)
+
+    def resume(self, values):
+        try:
+            self.plan = self.plans.send(values)
+        except StopIteration as end:
+            self.plan, self.result = None, end.value
+
+
+def advance(*runs, carry=()):
+    live = [run for run in runs if run.plan]
+    found, carried = together([run.plan for run in live], carry)
+    for run, values in zip(live, found):
+        run.resume(values)
+    return carried
 
 
 def flat_block(ref):
@@ -349,7 +424,7 @@
     half = count // 2
     send_refs, refs = refs[:half], refs[half:]
     keep_ref, bias_ref, d_attn_ref, sums_ref, d_mix_ref = refs[:5]
-    db_ref, at_ref, acc_ref, part_ref = refs[5:]
+    db_ref, at_ref, acc_ref, part_ref, down_ref = refs[5:]
 
     @pl.when(j == 0)
     def _():
@@ -360,17 +435,7 @@
     part_ref[...] = dot(g_ref[...].T, db_ref[...], 1, 0)
     for i in range(owners):
         slot = slot_ref[j * owners + i]
-        piece = part_ref[i * share : (i + 1) * share, :].astype(BF16)
-
-        @pl.when(slot < half)
-        def _():
-            keep_ref[slot, 0:share, :] = piece
-
-        for at, send_ref in enumerate(send_refs):
-
-            @pl.when(slot == half + at)
-            def _():
-                send_ref[0:share, :] = piece
+        down_ref[slot] = part_ref[i * share : (i + 1) * share, :].astype(BF16)
 
     d_up = (dot(db_ref[...], flat_block(w_down_ref), 1, 1) * slope_ref[...]).astype(BF16)
     bias_ref[...] = column_sum(d_up.astype(F32))
@@ -386,6 +451,9 @@
 
     @pl.when(j == pl.num_programs(0) - 1)
     def _():
+        for pos in range(half):
+            keep_ref[pos, 0:share, :] = down_ref[pos]
+            send_refs[pos][0:share, :] = down_ref[half + pos]
         gradient = acc_ref[...]
         normal = normal_ref[...]
         sums_ref[0:1, :] = column_sum(gradient * normal)
@@ -450,7 +518,7 @@
         [ whole(d_ffn.shape), wide, wide, whole(normed.shape), whole(normal.shape), whole(rstd.shape), whole(norms.shape), pl.BlockSpec((count, blk, width), lambda j, *_: (0, at_out, 0)), pl.BlockSpec((count, blk, width), lambda j, *_: (0, at_up + j, 0)), pl.BlockSpec((owners, share, width), lambda j, *_: (j, at_down, 0)), whole(totals.shape), whole(mixture.shape), whole(pooled.shape), whole(d_proj.shape), ],
         [ *[whole((rows_out, width))] * (count // 2), whole((count // 2, rows_out, width)), pl.BlockSpec((1, width), lambda j, *_: (0, j)), whole((total, width)), whole((2, width)), whole((count, per * head + 3 * RIDE, toks)), ],
         [ *[stored((rows_out, width), BF16)] * (count // 2), stored((count // 2, rows_out, width), BF16), stored((1, hidden), F32), stored((total, width), F32), stored((2, width), F32), stored((count, per * head + 3 * RIDE, toks), BF16), ],
-        [ pltpu.VMEM((total, width), BF16), pltpu.VMEM((width, total), BF16), pltpu.VMEM((total, width), F32), pltpu.VMEM((width, width), F32), ],
+        [ pltpu.VMEM((total, width), BF16), pltpu.VMEM((width, total), BF16), pltpu.VMEM((total, width), F32), pltpu.VMEM((width, width), F32), pltpu.VMEM((count, share, width), BF16), ],
         cost( 8 * total * width * hidden + 2 * total * width * width, 8 * hidden * width + 10 * total * hidden, ),
         "ffn_back",
     )
@@ -882,8 +950,8 @@
 
 def conv_weight_kernel(
     toks, order_ref, f_ref, p_ref, other_f_ref, other_p_ref, dm_ref, other_dm_ref, low_ref,
-    high_ref, begin_ref, end_ref, far_low_ref, far_high_ref, keep_a_ref, sent_a_ref, keep_b_ref,
-    sent_b_ref, turned_ref, whole_ref, part_ref,
+    high_ref, other_low_ref, other_high_ref, keep_a_ref, sent_a_ref, keep_b_ref, sent_b_ref,
+    turned_ref, whole_ref, part_ref,
 ):
     k, half = pl.program_id(0), pl.program_id(1)
     total, width = f_ref.shape
@@ -892,14 +960,7 @@
 
     @pl.when((k == 0) & (half == 0))
     def _():
-        odd = (order_ref[0] & 1) == 1
-        edges = (
-            (low_ref[...], high_ref[...]),
-            (
-                jnp.where(odd, far_low_ref[...], end_ref[...]),
-                jnp.where(odd, begin_ref[...], far_high_ref[...]),
-            ),
-        )
+        edges = ((low_ref[...], high_ref[...]), (other_low_ref[...], other_high_ref[...]))
         pairs = ((f_ref, p_ref), (other_f_ref, other_p_ref))
         for core, (pair, (low, high)) in enumerate(zip(pairs, edges)):
             for part, source in enumerate(pair):
@@ -1210,7 +1271,7 @@
 
 
 def tiles(rows):
-    return 3 if rows % 48 == 0 else 1
+    return 3 if PLACED and rows % 48 == 0 else 1
 
 
 def fold_pieces_kernel(keep_top, keep_bottom, *refs):
@@ -1255,12 +1316,12 @@
     ]
 
 
-def split(state, carry=()):
+def split(state):
     pieces, rows, width = state[0][0].shape
     steps = tiles(rows)
-    spec = pl.BlockSpec((pieces, rows // steps, width), lambda i: (0, i, 0))
-    out = pl.BlockSpec((pieces // 2, rows // steps, width), lambda i: (0, i, 0))
-    ka, sa, kb, sb, *carried = launch(
+    spec = pl.BlockSpec((pieces, rows // steps, width), lambda i, *_: (0, i, 0))
+    out = pl.BlockSpec((pieces // 2, rows // steps, width), lambda i, *_: (0, i, 0))
+    return plan(
         fold_kernel,
         (steps,),
         [],
@@ -1271,9 +1332,12 @@
         [],
         cost(pieces * rows * width, 12 * pieces * rows * width),
         "split",
-        carry,
-    )
-    return [[ka, sa], [kb, sb]], carried
+    )
+
+
+def paired(values):
+    ka, sa, kb, sb = values
+    return [[ka, sa], [kb, sb]]
 
 
 def cross_kernel(place_ref, ka_ref, kb_ref, ca_ref, cb_ref, kept_ref, sent_ref):
@@ -1284,11 +1348,11 @@
     sent_ref[...] = jnp.where(high, first, second)
 
 
-def cross(place, state, carry=()):
+def cross(place, state):
     _, rows, width = state[0][0].shape
     steps = tiles(rows)
     spec = pl.BlockSpec((1, rows // steps, width), lambda i, *_: (0, i, 0))
-    return launch(
+    return plan(
         cross_kernel,
         (steps,),
         [place],
@@ -1299,7 +1363,6 @@
         [],
         cost(rows * width, 12 * rows * width),
         "cross",
-        carry,
     )
 
 
@@ -1312,9 +1375,9 @@
     sent_ref[...] = jnp.where(high, first, second)
 
 
-def halve(place, bit, kept, came, carry):
+def halve(place, bit, kept, came):
     rows, width = kept.shape
-    return launch(
+    return plan(
         functools.partial(halve_kernel, bit),
         (1,),
         [place],
@@ -1325,7 +1388,6 @@
         [],
         cost(rows * width, 6 * rows * width),
         "halve",
-        carry,
     )
 
 
@@ -1333,8 +1395,8 @@
     out_ref[...] = add_low(kept_ref[...], came_ref[...])
 
 
-def add(kept, came, carry):
-    return launch(
+def add(kept, came):
+    return plan(
         add_kernel,
         (1,),
         [],
@@ -1345,7 +1407,6 @@
         [],
         cost(kept.size, 6 * kept.size),
         "add",
-        carry,
     )
 
 
@@ -1359,7 +1420,7 @@
 
 def assemble(place, bit, held, came):
     rows, width = held.shape
-    return launch(
+    return plan(
         functools.partial(assemble_kernel, bit),
         (1,),
         [place],
@@ -1393,7 +1454,7 @@
 
 def finish(place, held, came, layout, outs):
     layout = list(cut(layout, held.shape[0]))
-    return launch(
+    return plan(
         functools.partial(finish_kernel, layout),
         (1,),
         [place],
@@ -1410,19 +1471,15 @@
 def across_halves(place, kept, sent, layout, outs):
     bits = lax.axis_size("batch").bit_length() - 1
     came = swap(sent, "batch", 0)
-    carry = yield
     for bit in range(1, bits):
-        kept, sent, *carry = halve(place, bit, kept, came, carry or ())
+        kept, sent = yield halve(place, bit, kept, came)
         came = swap(sent, "batch", bit)
-        carry = yield carry
-    held = add(kept, came, carry or ())
-    held, carry = (held[0], held[1:]) if carry else (held, ())
+    (held,) = yield add(kept, came)
     for bit in reversed(range(bits)):
         came = swap(held, "batch", bit)
-        yield carry
         if bit:
-            held = assemble(place, bit, held, came)
-    yield finish(place, held, came, layout, outs)
+            (held,) = yield assemble(place, bit, held, came)
+    return (yield finish(place, held, came, layout, outs))
 
 
 def deal_kernel(place_ref, ka_ref, kb_ref, ca_ref, cb_ref, *refs):
@@ -1466,11 +1523,13 @@
 
 
 def across_direct(place, me, state, layout, small_at, outs):
+    for link in range(2, lax.axis_size("seq").bit_length() - 1):
+        state = send_links(paired((yield split(state))), link)
     parts = lax.axis_size("batch")
     _, rows, width = state[0][0].shape
     part = (2 * rows // parts, width)
     ends = [(mask, [(i, i ^ mask) for i in range(parts)]) for mask in range(1, parts)]
-    pieces = launch(
+    pieces = yield plan(
         deal_kernel,
         (1,),
         [place],
@@ -1483,40 +1542,33 @@
         "deal",
     )
     came = [lax.ppermute(pieces[mask], "batch", pairs) for mask, pairs in ends]
-    yield
-    held = launch(
+    (held,) = yield plan(
         total_kernel,
         (1,),
         [],
         [pieces[0], *came],
         [whole(part)] * parts,
-        whole(part),
-        stored(part, BF16),
+        [whole(part)],
+        [stored(part, BF16)],
         [],
         cost(rows * width, 5 * rows * width),
         "total",
     )
     came = [lax.ppermute(held, "batch", pairs) for _, pairs in ends]
-    yield
-    yield launch(
-        functools.partial(spread_kernel, layout, small_at, parts),
-        (1,),
-        [place, me],
-        [held, *came],
-        [whole(part)] * parts,
-        [whole(dims) for dims in outs],
-        [stored(dims, F32) for dims in outs],
-        [pltpu.VMEM((2 * rows, width), BF16)],
-        cost(rows * width, 12 * rows * width),
-        "spread",
-    )
-
-
-def last(steps):
-    result = None
-    for result in steps:
-        pass
-    return result if isinstance(result, (list, tuple)) else [result]
+    return (
+        yield plan(
+            functools.partial(spread_kernel, layout, small_at, parts),
+            (1,),
+            [place, me],
+            [held, *came],
+            [whole(part)] * parts,
+            [whole(dims) for dims in outs],
+            [stored(dims, F32) for dims in outs],
+            [pltpu.VMEM((2 * rows, width), BF16)],
+            cost(rows * width, 12 * rows * width),
+            "spread",
+        )
+    )
 
 
 def neighbours(first, last):
@@ -1595,8 +1647,8 @@
         lax.ppermute(block_totals, "seq", [(i, i ^ mask) for i in range(count)])
         for mask in range(1, count)
     ]
-    step = 512
-    mixture, totals = attend_call(qkv, step)
+    step = (1 << 19) // (count * toks)
+    mixture, totals = attend_call(qkv, 2 * step)
     mixture = lax.all_to_all(mixture, "seq", 0, 0, tiled=True)
     gathered = collect(me_one, gathered)
     prior, pooled, proj, proj_low = states_call(
@@ -1615,23 +1667,21 @@
 
     begin, end = edges(f_low, proj_low)
     low, high = neighbours(begin, end)
-    far_high = lax.ppermute(begin, "seq", [(i, i - 2) for i in range(2, count)])
-    far_low = lax.ppermute(end, "seq", [(i, i + 2) for i in range(count - 2)])
-    joined_edges = [low, high, begin, end, far_low, far_high]
     other = [swap(v, "seq", 0) for v in (f_low, proj_low)]
     tok_out, char_out, d_tok, d_char, d_merged, sums23, begin, end, *other = conv_call(
         f_low, proj_low, normal1, proj, norms, low, high, third,
         tok_grad.reshape(total, width), char_grad.reshape(total, width), seqs, other,
     )
 
+    joined_edges = [low, high, swap(low, "seq", 0), swap(high, "seq", 0)]
     low, high = neighbours(begin, end)
     other_dm = swap(d_merged, "seq", 0)
 
-    def onward(state, first_link, carry=()):
+    def onward(state, first_link):
         for link in range(first_link + 1, bits):
-            state, carry = split(state, carry)
-            state = send_links(state, link)
-        return state, carry
+            ((values,), _) = together([split(state)])
+            state = send_links(paired(values), link)
+        return state
 
     def columns_of(begin, blocks, out):
         return [
@@ -1661,72 +1711,79 @@
     )
     d_mix = lax.all_to_all(d_mix, "seq", 0, 0, tiled=True)
     ffn_came = [swap(piece, "seq", 0) for piece in send]
-    conv_state, _ = onward(conv_state, 1)
+    conv_state = onward(conv_state, 1)
     ffn_state = fold(keep, ffn_came)
     ffn_state = send_links(ffn_state, 1)
     d_qkv = attend_back_call(qkv, d_mix, totals, step)
+    PLACED.clear()
     d_qkv = lax.all_to_all(d_qkv, "seq", 0, 0, tiled=True)
-    conv_steps = across_halves(
-        place, *cross(place, conv_state)[:2],
-        [
-            (r * double, double, 0, (r // 2, slice(None), slice(r % 2 * width, (r % 2 + 1) * width)))
-            for r in range(6)
-        ],
-        [(3, double, 2 * width)],
-    )
-    next(conv_steps)
+    ((halves,), _) = together([cross(place, conv_state)])
+    conv_run = Steps(
+        across_halves(
+            place, *halves,
+            [
+                (
+                    r * double, double, 0,
+                    (r // 2, slice(None), slice(r % 2 * width, (r % 2 + 1) * width)),
+                )
+                for r in range(6)
+            ],
+            [(3, double, 2 * width)],
+        )
+    )
     sums, d_bias = gates_back_call(
         me_one, group_ids, z, c, prior, ds, gathered, d_mix, char_ids,
         count * table_rows // NCHAR, 2,
     )
-    ffn_state, _ = onward(ffn_state, 1)
+    ffn_state = onward(ffn_state, 1)
     for _ in range(1, batch_bits):
-        next(conv_steps)
+        advance(conv_run)
     rest_send, rest_keep = rest_call(order, first, at_table, at_gru, sums, height)
     hidden_grad, qkv_send, qkv_keep = qkv_back_call(
         order, d_qkv, rows, first, at_qkv, d_attn,
         [sums0, sums1, sums23, d_bias, d_bias_up], seqs, height,
     )
     PLACED.clear()
-    ffn_steps = across_halves(
-        place, *cross(place, ffn_state)[:2],
-        [
-            (0, share, 0, everything),
-            *columns_of(share, 4, 1),
-            (share + 4 * blk, blk, 2, everything),
-            (share + 5 * blk, blk, 3, everything),
-        ],
-        [(share, width), (blk, 4 * width), (blk, width), (blk, width)],
-    )
-    next(ffn_steps)
-    both = conv_steps.send([rest_send, qkv_send])
-    rest_came, qkv_came = (swap(send, "seq", 0) for send in both)
-    last_state, _ = split([[rest_keep, rest_came], [qkv_keep, qkv_came]])
-    last_state = send_links(last_state, 1)
-    for _ in range(1, batch_bits):
-        next(ffn_steps)
-    next(conv_steps)
-    last_state, _ = onward(last_state, 1)
-    (conv_grad,) = last(conv_steps)
-    last_steps = across_direct(
-        place, me_one, last_state,
-        [
-            *columns_of(0, 2, 0),
-            (2 * blk, table_rows, 1, everything),
-            *columns_of(height, 3, 2),
-        ],
-        height + 3 * blk,
-        [
-            (blk, 2 * width), (table_rows, width), (blk, 3 * width),
-            (4, blk), (4, blk), (1, blk), (1, blk), (1, share),
-        ],
-    )
-    next(last_steps)
-    next(ffn_steps)
-    next(ffn_steps)
-    next(last_steps)
-    down_grad, up_grad, out_grad, char_grad_w = last(ffn_steps)
-    gru_grad, table_grad, qkv_grad, *small_grads = last(last_steps)
+    (halves, (held,)), (rest_send, qkv_send) = together(
+        [cross(place, ffn_state), conv_run.plan], [rest_send, qkv_send]
+    )
+    conv_run.resume([held])
+    ffn_run = Steps(
+        across_halves(
+            place, *halves,
+            [
+                (0, share, 0, everything),
+                *columns_of(share, 4, 1),
+                (share + 4 * blk, blk, 2, everything),
+                (share + 5 * blk, blk, 3, everything),
+            ],
+            [(share, width), (blk, 4 * width), (blk, width), (blk, width)],
+        )
+    )
+    rest_came, qkv_came = (swap(send, "seq", 0) for send in (rest_send, qkv_send))
+    ((values,), _) = together([split([[rest_keep, rest_came], [qkv_keep, qkv_came]])])
+    last_run = Steps(
+        across_direct(
+            place, me_one, send_links(paired(values), 1),
+            [
+                *columns_of(0, 2, 0),
+                (2 * blk, table_rows, 1, everything),
+                *columns_of(height, 3, 2),
+            ],
+            height + 3 * blk,
+            [
+                (blk, 2 * width), (table_rows, width), (blk, 3 * width),
+                (4, blk), (4, blk), (1, blk), (1, blk), (1, share),
+            ],
+        )
+    )
+    advance(conv_run, ffn_run, last_run)
+    advance(ffn_run, last_run)
+    while conv_run.plan or ffn_run.plan or last_run.plan:
+        advance(conv_run, ffn_run, last_run)
+    (conv_grad,) = conv_run.result
+    down_grad, up_grad, out_grad, char_grad_w = ffn_run.result
+    gru_grad, table_grad, qkv_grad, *small_grads = last_run.result
     d_gain, d_shift = (v.T for v in small_grads[:2])
     d_gate_b, d_cand_b, d_ffn_b = (v.reshape(-1) for v in small_grads[2:])
     shape_out = (seqs, toks, width)

time: 621 us -> 614 us (0.989)
  Pallas kernels: 252 us -> 240 us
    ppermute x3, waiting for transfers between devices: 13.4 us -> 28.3 us  [across_direct(): came = [lax.ppermute(held, 'batch', pairs) for _, pairs in ends]]
    pallas_call x35 -> x28, Pallas kernels: 252 us -> 240 us  [launch(): pl.pallas_call(kernel, grid_spec=pltpu.PrefetchScalarGridSpec(num_scalar_...]
    ppermute x29 -> x31, starting transfers between devices: 30.7 us -> 42.6 us  [swap(): return lax.ppermute(value, axis, [(i, i ^ 1 << bit) for i in range(size)])]
    ppermute x29 -> x31, waiting for transfers between devices: 66.7 us -> 57 us  [swap(): return lax.ppermute(value, axis, [(i, i ^ 1 << bit) for i in range(size)])]
    ppermute x2 -> x0, starting transfers between devices: 9.15 us -> none  [the longest x1 7.86 us: local(): far_low = lax.ppermute(end, 'seq', [(i, i + 2) for i in range(count - 2)])]
  transfers between devices with their start and end apart: 54 -> 54, of which waited for: 17 -> 19; matrix products, arithmetic and copies ran while one was open for 1% -> 1% of each run, Pallas kernels for 34% -> 32%
where the time goes in v3:
time: 614 us; the launch traced here: 607 us
  waiting for transfers between devices  244 us (40%)
  Pallas kernels  240 us (39%)
  starting transfers between devices  86.6 us (14%)
  local copies, waits for them, and re-layouts  19.5 us (3%)
  between operations  15 us (2%)
    pallas_call x28, Pallas kernels, launch(): pl.pallas_call(kernel, grid_spec=pltpu.PrefetchScalarGridSpec(num_scalar_...  240 us
    all_gather x1, waiting for transfers between devices, local(): first = lax.all_gather(first, 'seq', axis=0)  99.1 us
    ppermute x31, waiting for transfers between devices, swap(): return lax.ppermute(value, axis, [(i, i ^ 1 << bit) for i in range(size)])  57 us
    ppermute x31, starting transfers between devices, swap(): return lax.ppermute(value, axis, [(i, i ^ 1 << bit) for i in range(size)])  42.6 us
    ppermute x3, waiting for transfers between devices, across_direct(): came = [lax.ppermute(held, 'batch', pairs) for _, pairs in ends]  28.3 us
    ppermute x3, waiting for transfers between devices, across_direct(): came = [lax.ppermute(pieces[mask], 'batch', pairs) for mask, pairs in ends]  26.5 us
    ppermute x7, waiting for transfers between devices, local(): lax.ppermute(block_totals, 'seq', [(i, i ^ mask) for i in range(count)])  21.1 us
    unnamed x108, local copies, waits for them, and re-layouts  13.4 us
  transfers between devices with their start and end apart: 54, of which 19 were waited for; matrix products, arithmetic and copies ran while one was open for 1% of the time, Pallas kernels for 32%

profile of v3, /device:TPU:0, one launch (start us, length us, event | category | flops | bytes accessed | tf_op | source)
XLA Modules:
  0.0 607.3 jit_solution(11151114740919087288)
XLA Ops:
  8.9 3.3 pack.2
  14.9 2.7 pack.3
  19.7 99.1 %all-gather.5.cloned.1.call-done = bf16[13056,768]{1,0:T(8,128)(2,1)} async-done(((bf16[1632,768]{1,0:T(8,128)(2,1)}), bf16[13056,768]{1,0:T(8,128)(2,1)}) %all-gather.5.cloned.1.call-update) | async-done | bytes 20054032 | tf_op jit(solution)/shard_map/all_gather | solution.py:1629
  119.7 5.7 qkv.1
  125.3 4.6 all-to-all-start
  129.9 17.5 %gates.1 = (f32[3,4096,128]{2,1,0:T(8,128)}, f32[3,4096,128]{2,1,0:T(8,128)}, f32[2,3,8,128]{3,2,1,0:T(8,128)}, f32[8,128]{1,0:T(8,128)}) custom-call(s32[4]{0:T(128)S(1)} %copy-done.31, s32[4,512,1]{2,1,0:T(8,128)S(1)} %copy.49.refs_1_, s32[4,512,1]{2,1,0:T(8,128)S(1)} %copy.50.refs_2_, bf16[8,1632,768]{2,1,0:T(8,128)(2,1)} %bitcast.56, ...), custom_call_target="tpu_custom_call" | custom-call | flops 6442450944000 | bytes 25165824000 | tf_op jit(solution)/shard_map/gates/pallas_call | solution.py:90
  147.8 1.7 collective-permute-start.1
  150.1 1.7 collective-permute-start.3
  153.3 2.6 collective-permute-start.5
  155.9 21.1 %collective-permute-done.1.refs_3_ = f32[2,3,8,128]{3,2,1,0:T(8,128)S(1)} collective-permute-done((f32[2,3,8,128]{3,2,1,0:T(8,128)}, f32[2,3,8,128]{3,2,1,0:T(8,128)S(1)}, u32[]{:S(2)}, u32[]{:S(2)}) %collective-permute-start.1) | collective-permute-done | bytes 24608 | tf_op jit(solution)/shard_map/ppermute | solution.py:1647
  178.5 12.3 %attend.1 = (bf16[8,6,64,128]{3,2,1,0:T(8,128)(2,1)}, f32[6,1,1024]{2,1,0:T(1,128)S(1)}, f32[8,128]{1,0:T(8,128)}) custom-call(bf16[8,6,3,64,128]{4,3,2,1,0:T(8,128)(2,1)} %all-to-all-done.refs_0_, f32[8,128]{1,0:T(8,128)} %get-tuple-element.170.refs_1_), custom_call_target="tpu_custom_call" | custom-call | flops 6442450944000 | bytes 3145728000 | tf_op jit(solution)/shard_map/attend/pallas_call | solution.py:90
  190.8 4.7 all-to-all-start.1
  196.5 10.6 %states.1 = (f32[3,4096,128]{2,1,0:T(8,128)}, bf16[512,768]{1,0:T(8,128)(2,1)}, f32[512,768]{1,0:T(8,128)}, bf16[512,768]{1,0:T(8,128)(2,1)}, f32[8,128]{1,0:T(8,128)}) custom-call(s32[1]{0:T(128)} %bitcast.13.refs_0_.refs_2_, f32[3,4096,128]{2,1,0:T(8,128)} %get-tuple-element.172.refs_1_.refs_5_.refs_2_, ...), custom_call_target="tpu_custom_call" | custom-call | flops 1006632960000 | bytes 18874368000 | tf_op jit(solution)/shard_map/states/pallas_call | solution.py:90
  209.3 7.6 %all-to-all-done.1.refs_0_ = bf16[8,6,64,128]{3,2,1,0:T(8,128)(2,1)} async-done(((bf16[8,6,64,128]{3,2,1,0:T(8,128)(2,1)}), bf16[8,6,64,128]{3,2,1,0:T(8,128)(2,1)}, u32[]{:S(2)}, u32[]{:S(2)}) %all-to-all-start.1) | async-done | bytes 786464 | tf_op jit(solution)/shard_map/all_to_all | solution.py:1652
  216.9 17.4 %ffn.1 = (bf16[768,512]{1,0:T(8,128)(2,1)}, f32[512,768]{1,0:T(8,128)}, f32[512,1]{1,0:T(8,128)}, bf16[512,768]{1,0:T(8,128)(2,1)}, bf16[512,3072]{1,0:T(8,128)(...) custom-call(bf16[8,6,64,128]{3,2,1,0:T(8,128)(2,1)} %all-to-all-done, ...), custom_call_target="tpu_custom_call" | custom-call | flops 5435817984000 | bytes 25165824000 | tf_op jit(solution)/shard_map/ffn/pallas_call | solution.py:90
  236.9 3.6 collective-permute-start.7
  243.2 18.3 %conv.1 = (f32[512,768]{1,0:T(8,128)}, f32[512,768]{1,0:T(8,128)}, f32[512,768]{1,0:T(8,128)S(1)}, f32[512,768]{1,0:T(8,128)S(1)}, bf16[512,1536]{1,0:T(8,128)(2...) custom-call(bf16[512,768]{1,0:T(8,128)(2,1)S(1)} %get-tuple-element., ...), custom_call_target="tpu_custom_call", output_to_operand_aliasing={{8}: (10, {}), {9}: (11, {})} | custom-call | flops 7247757312000 | bytes 29884416000 | tf_op jit(solution)/shard_map/conv/pallas_call | solution.py:90
  261.5 3.6 collective-permute-start.11
  266.6 3.1 collective-permute-start.15
  270.2 14.4 %conv_back.1 = (bf16[512,768]{1,0:T(8,128)(2,1)S(1)}, f32[512,768]{1,0:T(8,128)S(1)}, f32[2,768]{1,0:T(2,128)S(1)}, f32[8,128]{1,0:T(8,128)}) custom-call(bf16[512,1536]{1,0:T(8,128)(2,1)} %get-tuple-element.187.refs_0_.refs_5_, bf16[4,1,1536]{2,1,0:T(2,128)(2,1)S(1)} %collective-permute-done.11.refs_1_, ...), custom_call_target="tpu_custom_call" | custom-call | flops 7247757312000 | bytes 22020096000 | tf_op jit(solution)/shard_map/conv_back/pallas_call | solution.py:90
  284.7 16.9 %conv_weight.1 = (bf16[2,576,768]{2,1,0:T(8,128)(2,1)}, bf16[2,576,768]{2,1,0:T(8,128)(2,1)}, bf16[2,576,768]{2,1,0:T(8,128)(2,1)}, bf16[2,576,768]{2,1,0:T(8,128)(2,1)}, f32[8,128]{1,0:T(8,128)}) custom-call(s32[8]{0:T(128)S(1)} %broadcast_xor_fusion.refs_0_.refs_1_, bf16[512,768]{1,0:T(8,128)(2,1)S(1)} %get-tuple-element.179.refs_0_.refs_1_, ...), custom_call_target="tpu_custom_call" | custom-call | flops 7247757312000 | bytes 7077888000 | tf_op jit(solution)/shard_map/conv_weight/pallas_call | solution.py:90
  301.6 2.3 collective-permute-start.20
  304.5 10.2 %states_back.1 = (f32[3,4096,128]{2,1,0:T(8,128)}, f32[3,8,128]{2,1,0:T(8,128)S(1)}, f32[8,128]{1,0:T(8,128)}) custom-call(bf16[512,768]{1,0:T(8,128)(2,1)S(1)} %get-tuple-element.200.refs_0_.refs_15_, bf16[8,1632,768]{2,1,0:T(8,128)(2,1)} %bitcast.64, f32[4,128,1]{2,1,0:T(8,128)S(1)} %convert_element_type.28.refs_6_.refs_2_, s32[4,1,128]{2,1,0:T(1,128)S(1)} %sub.14.refs_3_, ...), custom_call_target="tpu_custom_call" | custom-call | flops 1006632960000 | bytes 12582912000 | tf_op jit(solution)/shard_map/states_back/pallas_call | solution.py:90
  314.7 25.4 %ffn_back.1 = (bf16[960,768]{1,0:T(8,128)(2,1)}, bf16[960,768]{1,0:T(8,128)(2,1)}, bf16[960,768]{1,0:T(8,128)(2,1)}, bf16[960,768]{1,0:T(8,128)(2,1)}, bf16[4,96...) custom-call(s32[8]{0:T(128)S(1)} %shift-left_add_fusion.refs_0_, ...), custom_call_target="tpu_custom_call" | custom-call | flops 10267656192000 | bytes 34603008000 | tf_op jit(solution)/shard_map/ffn_back/pallas_call | solution.py:90
  342.2 1.6 collective-permute-start.19
  343.8 3.6 all-to-all-start.2
  347.4 5.6 split.3
  353.0 1.9 collective-permute-start.22
  354.9 1.5 collective-permute-start.23
  356.4 7.9 %fold.1 = (bf16[2,480,768]{2,1,0:T(8,128)(2,1)}, bf16[2,480,768]{2,1,0:T(8,128)(2,1)}, bf16[2,480,768]{2,1,0:T(8,128)(2,1)}, bf16[2,480,768]{2,1,0:T(8,128)(2,1)}, f32[8,128]{1,0:T(8,128)}) custom-call(bf16[4,960,768]{2,1,0:T(8,128)(2,1)} %get-tuple-element.211.refs_0_.refs_1_, bf16[4,960,768]{2,1,0:T(8,128)(2,1)} %get-tuple-element.211.refs_0_.refs_1_, ...), custom_call_target="tpu_custom_call" | custom-call | flops 2949120000 | bytes 17694720000 | tf_op jit(solution)/shard_map/fold/pallas_call | solution.py:90
  366.1 21.7 %attend_back.1 = (bf16[8,6,3,64,128]{4,3,2,1,0:T(8,128)(2,1)}, f32[8,128]{1,0:T(8,128)}) custom-call(bf16[8,6,3,64,128]{4,3,2,1,0:T(8,128)(2,1)} %all-to-all-done.refs_0_, bf16[8,480,128]{2,1,0:T(8,128)(2,1)} %copy-done.4, f32[6,1,1024]{2,1,0:T(1,128)S(1)} %get-tuple-element.210.refs_2_, f32[8,128]{1,0:T(8,128)} %get-tuple-element.222.refs_3_), custom_call_target="tpu_custom_call" | custom-call | flops 16106127360000 | bytes 5505024000 | tf_op jit(solution)/shard_map/attend_back/pallas_call | solution.py:90
  387.8 4.9 all-to-all-start.3
  392.8 2.9 cross.1
  395.7 1.5 collective-permute-start.24
  397.2 14.8 %gates_back.1 = (bf16[4,256,1536]{2,1,0:T(8,128)(2,1)S(1)}, f32[1,1536]{1,0:T(1,128)S(1)}, f32[8,128]{1,0:T(8,128)S(1)}) custom-call(s32[1]{0:T(128)} %bitcast.13.refs_0_.refs_2_, s32[4]{0:T(128)S(1)} %copy-done.31, f32[3,4096,128]{2,1,0:T(8,128)} %get-tuple-element.172.refs_1_.refs_5_.refs_2_, f32[3,4096,128]{2,1,0:T(8,128)} %get-tuple-element.173.refs_2_.refs_3_, ...), custom_call_target="tpu_custom_call" | custom-call | flops 1610612736000 | bytes 25165824000 | tf_op jit(solution)/shard_map/gates_back/pallas_call | solution.py:90
  412.6 3.1 split.4
  415.7 2.0 collective-permute-start.27
  419.1 2.2 halve.1
  422.7 2.4 collective-permute-start.29
  425.1 8.0 %rest.1 = (bf16[4,320,768]{2,1,0:T(8,128)(2,1)S(1)}, bf16[4,320,768]{2,1,0:T(8,128)(2,1)S(1)}, f32[8,128]{1,0:T(8,128)S(1)}) custom-call(s32[8]{0:T(128)S(1)} %copy-done.33, bf16[8,1632,768]{2,1,0:T(8,128)(2,1)} %bitcast.68, bf16[4,256,1536]{2,1,0:T(8,128)(2,1)S(1)} %get-tuple-element.238.refs_2_, bf16[8,1632,768]{2,1,0:T(8,128)(2,1)} %bitcast.69, ...), custom_call_target="tpu_custom_call" | custom-call | flops 4831838208000 | bytes 11796480000 | tf_op jit(solution)/shard_map/rest/pallas_call | solution.py:90
  435.0 3.5 all-to-all-done.3.refs_1_
  441.1 8.8 %qkv_back.1 = (f32[512,768]{1,0:T(8,128)}, bf16[4,320,768]{2,1,0:T(8,128)(2,1)S(1)}, bf16[4,320,768]{2,1,0:T(8,128)(2,1)S(1)}, f32[8,128]{1,0:T(8,128)S(1)}) custom-call(s32[8]{0:T(128)S(1)} %copy-done.33, bf16[8,6,3,64,128]{4,3,2,1,0:T(8,128)(2,1)} %all-to-all-done.3.refs_1_, bf16[512,768]{1,0:T(8,128)(2,1)S(1)} %bitcast.43, ...), custom_call_target="tpu_custom_call" | custom-call | flops 4831838208000 | bytes 18087936000 | tf_op jit(solution)/shard_map/qkv_back/pallas_call | solution.py:90
  449.9 2.9 collective-permute-done.27.refs_3_
  452.9 2.0 cross_add.1
  455.5 3.5 collective-permute-done.32.refs_2_
  459.0 2.8 collective-permute-done.33.refs_3_
  464.9 1.5 collective-permute-start.31
  466.4 2.4 collective-permute-start.30
  468.8 22.6 %collective-permute-done.30.refs_3_ = bf16[288,768]{1,0:T(8,128)(2,1)S(1)} collective-permute-done((bf16[288,768]{1,0:T(8,128)(2,1)S(1)}, bf16[288,768]{1,0:T(8,128)(2,1)S(1)}, u32[]{:S(2)}, u32[]{:S(2)}) %collective-permute-start.30) | collective-permute-done | bytes 442400 | tf_op jit(solution)/shard_map/ppermute | solution.py:1257
  495.2 2.4 collective-permute-start.36
  497.7 1.5 collective-permute-start.37
  499.1 23.6 %collective-permute-done.37.refs_2_ = bf16[240,768]{1,0:T(8,128)(2,1)S(1)} collective-permute-done((bf16[240,768]{1,0:T(8,128)(2,1)S(1)}, bf16[240,768]{1,0:T(8,128)(2,1)S(1)}, u32[]{:S(2)}, u32[]{:S(2)}) %collective-permute-start.37) | collective-permute-done | bytes 368672 | tf_op jit(solution)/shard_map/ppermute | solution.py:1257
  523.5 3.5 collective-permute-start.40
  527.0 2.0 collective-permute-start.42
  528.9 2.4 collective-permute-start.43
  531.4 9.9 %collective-permute-done.41.refs_7_ = bf16[160,768]{1,0:T(8,128)(2,1)S(1)} collective-permute-done((bf16[160,768]{1,0:T(8,128)(2,1)S(1)}, bf16[160,768]{1,0:T(8,128)(2,1)S(1)}, u32[]{:S(2)}, u32[]{:S(2)}) %collective-permute-start.41) | collective-permute-done | bytes 245792 | tf_op jit(solution)/shard_map/ppermute | solution.py:1544
  541.3 16.6 %collective-permute-done.42.refs_8_ = bf16[160,768]{1,0:T(8,128)(2,1)S(1)} collective-permute-done((bf16[160,768]{1,0:T(8,128)(2,1)S(1)}, bf16[160,768]{1,0:T(8,128)(2,1)S(1)}, u32[]{:S(2)}, u32[]{:S(2)}) %collective-permute-start.42) | collective-permute-done | bytes 245792 | tf_op jit(solution)/shard_map/ppermute | solution.py:1544
  557.9 2.2 finish_assemble_total.1
  560.1 4.5 collective-permute-start.44
  564.6 2.6 collective-permute-start.46
  567.2 1.8 collective-permute-start.47
  568.9 22.7 %collective-permute-done.45.refs_6_ = bf16[160,768]{1,0:T(8,128)(2,1)S(1)} collective-permute-done((bf16[160,768]{1,0:T(8,128)(2,1)S(1)}, bf16[160,768]{1,0:T(8,128)(2,1)S(1)}, u32[]{:S(2)}, u32[]{:S(2)}) %collective-permute-start.45) | collective-permute-done | bytes 245792 | tf_op jit(solution)/shard_map/ppermute | solution.py:1557
  592.0 5.2 collective-permute-done.47.refs_8_
  597.2 2.5 finish_spread.1
  (210 shorter events, 43.2 us)
Async XLA Ops:
  7.2 111.6 %all-gather.5.cloned.1.call-start = ((), (), s32[]{:S(2)}) async-start(), calls=%async_computation.4 | async-start | bytes 22560768 | tf_op jit(solution)/shard_map/all_gather | solution.py:1629
  12.2 228.3 %all-gather.7.cloned.1.call-start = ((), (), s32[]{:S(2)}) async-start(), calls=%async_computation.5 | async-start | bytes 15925248 | tf_op jit(solution)/shard_map/all_gather | solution.py:1630
  18.1 100.7 %copy-start.45 = (s32[4,512]{1,0:T(4,128)}, s32[4,512]{1,0:T(4,128)S(1)}, u32[]{:S(2)}) copy-start(s32[4,512]{1,0:T(4,128)S(1)} %rev.4) | copy-start | bytes 24580
  125.3 53.2 %all-to-all-start = ((bf16[8,6,3,64,128]{4,3,2,1,0:T(8,128)(2,1)}), bf16[8,6,3,64,128]{4,3,2,1,0:T(8,128)(2,1)}, u32[]{:S(2)}, u32[]{:S(2)}) async-start(bf16[8,6,3,64,128]{4,3,2,1,0:T(8,128)(2,1)} %get-tuple-element.168), calls=%async_computation | async-start | bytes 4718592 | tf_op jit(solution)/shard_map/all_to_all | solution.py:1644
  147.4 5.3 collective-permute-start
  147.8 29.3 %collective-permute-start.1 = (f32[2,3,8,128]{3,2,1,0:T(8,128)}, f32[2,3,8,128]{3,2,1,0:T(8,128)S(1)}, u32[]{:S(2)}, u32[]{:S(2)}) collective-permute-start(f32[2,3,8,128]{3,2,1,0:T(8,128)} %get-tuple-element.174.refs_1_), channel_id=1, source_target_pairs={{0,2},{1,3},{2,0},{3,1},{4,6},{5,7},{6,4},{7,5},{8,10},{9,11},{10,... | collective-permute-start | bytes 73736 | tf_op jit(solution)/shard_map/ppermute | solution.py:1647
  150.0 45.6 %collective-permute-start.2 = (f32[2,3,8,128]{3,2,1,0:T(8,128)}, f32[2,3,8,128]{3,2,1,0:T(8,128)}, u32[]{:S(2)}, u32[]{:S(2)}) collective-permute-start(f32[2,3,8,128]{3,2,1,0:T(8,128)} %get-tuple-element.174.refs_1_), channel_id=1, source_target_pairs={{0,3},{1,2},{2,1},{3,0},{4,7},{5,6},{6,5},{7,4},{8,11},{9,10},{10,... | collective-permute-start | bytes 73736 | tf_op jit(solution)/shard_map/ppermute | solution.py:1647
  150.1 45.5 %collective-permute-start.3 = (f32[2,3,8,128]{3,2,1,0:T(8,128)}, f32[2,3,8,128]{3,2,1,0:T(8,128)}, u32[]{:S(2)}, u32[]{:S(2)}) collective-permute-start(f32[2,3,8,128]{3,2,1,0:T(8,128)} %get-tuple-element.174.refs_1_), channel_id=1, source_target_pairs={{0,4},{1,5},{2,6},{3,7},{4,0},{5,1},{6,2},{7,3},{8,12},{9,13},{10,... | collective-permute-start | bytes 73736 | tf_op jit(solution)/shard_map/ppermute | solution.py:1647
  151.8 43.8 %collective-permute-start.4 = (f32[2,3,8,128]{3,2,1,0:T(8,128)}, f32[2,3,8,128]{3,2,1,0:T(8,128)}, u32[]{:S(2)}, u32[]{:S(2)}) collective-permute-start(f32[2,3,8,128]{3,2,1,0:T(8,128)} %get-tuple-element.174.refs_1_), channel_id=1, source_target_pairs={{0,5},{1,4},{2,7},{3,6},{4,1},{5,0},{6,3},{7,2},{8,13},{9,12},{10,... | collective-permute-start | bytes 73736 | tf_op jit(solution)/shard_map/ppermute | solution.py:1647
  153.3 42.3 %collective-permute-start.5 = (f32[2,3,8,128]{3,2,1,0:T(8,128)}, f32[2,3,8,128]{3,2,1,0:T(8,128)}, u32[]{:S(2)}, u32[]{:S(2)}) collective-permute-start(f32[2,3,8,128]{3,2,1,0:T(8,128)} %get-tuple-element.174.refs_1_), channel_id=1, source_target_pairs={{0,6},{1,7},{2,4},{3,5},{4,2},{5,3},{6,0},{7,1},{8,14},{9,15},{10,... | collective-permute-start | bytes 73736 | tf_op jit(solution)/shard_map/ppermute | solution.py:1647
  177.7 18.0 %collective-permute-start.6 = (f32[2,3,8,128]{3,2,1,0:T(8,128)}, f32[2,3,8,128]{3,2,1,0:T(8,128)}, u32[]{:S(2)}, u32[]{:S(2)}) collective-permute-start(f32[2,3,8,128]{3,2,1,0:T(8,128)} %get-tuple-element.174.refs_1_), channel_id=1, source_target_pairs={{0,7},{1,6},{2,5},{3,4},{4,3},{5,2},{6,1},{7,0},{8,15},{9,14},{10,... | collective-permute-start | bytes 73736 | tf_op jit(solution)/shard_map/ppermute | solution.py:1647
  190.8 26.1 %all-to-all-start.1 = ((bf16[8,6,64,128]{3,2,1,0:T(8,128)(2,1)}), bf16[8,6,64,128]{3,2,1,0:T(8,128)(2,1)}, u32[]{:S(2)}, u32[]{:S(2)}) async-start(bf16[8,6,64,128]{3,2,1,0:T(8,128)(2,1)} %get-tuple-element.171), calls=%async_computation.1 | async-start | bytes 1572864 | tf_op jit(solution)/shard_map/all_to_all | solution.py:1652
  207.1 33.8 %collective-permute-start.10 = (bf16[512,768]{1,0:T(8,128)(2,1)}, bf16[512,768]{1,0:T(8,128)(2,1)}, u32[]{:S(2)}, u32[]{:S(2)}) collective-permute-start(bf16[512,768]{1,0:T(8,128)(2,1)} %get-tuple-element.180.refs_1_.refs_2_), channel_id=1, source_target_pairs={{0,1},{1,0},{2,3},{3,2},{4,5},{5,4},{6,7},{7,6},{8,9},{9,8},{10,11... | collective-permute-start | bytes 2359304 | tf_op jit(solution)/shard_map/ppermute | solution.py:1257
  216.9 23.6 %copy-start.53 = (s32[8]{0:T(128)S(1)}, s32[8]{0:T(128)}, u32[]{:S(2)}) copy-start(s32[8]{0:T(128)} %constant.50.clone) | copy-start | bytes 100
  235.5 5.4 collective-permute-start.9
  235.5 5.0 collective-permute-start.8
  236.9 4.0 collective-permute-start.7
  240.5 74.2 %copy-start.32 = (s32[8]{0:T(128)}, s32[8]{0:T(128)S(1)}, u32[]{:S(2)}) copy-start(s32[8]{0:T(128)S(1)} %broadcast_xor_fusion.refs_0_.refs_1_) | copy-start | bytes 100
  243.2 23.4 %copy-start.11 = (s32[4,128]{1,0:T(4,128)S(1)}, s32[4,128]{1,0:T(4,128)}, u32[]{:S(2)}) copy-start(s32[4,128]{1,0:T(4,128)} %reduce_window_sum.15) | copy-start | bytes 6148
  243.2 23.4 %copy-start.51 = (s32[4,1,128]{2,1,0:T(1,128)S(1)}, s32[4,1,128]{2,1,0:T(1,128)}, u32[]{:S(2)}) copy-start(s32[4,1,128]{2,1,0:T(1,128)} %param.25) | copy-start | bytes 6148
  243.2 27.0 %copy-start.37 = (f32[512,768]{1,0:T(8,128)S(1)}, f32[512,768]{1,0:T(8,128)}, u32[]{:S(2)}) copy-start(f32[512,768]{1,0:T(8,128)} %copy-done.35) | copy-start | bytes 4718596
  261.5 8.7 %collective-permute-start.11 = (bf16[4,1,1536]{2,1,0:T(2,128)(2,1)S(1)}, bf16[4,1,1536]{2,1,0:T(2,128)(2,1)S(1)}, u32[]{:S(2)}, u32[]{:S(2)}) collective-permute-start(bf16[4,1,1536]{2,1,0:T(2,128)(2,1)S(1)} %get-tuple-element.188), channel_id=1, source_target_pairs={{0,1},{1,2},{2,3},{3,4},{4,5},{5,6},{6,7},{8,9},{9,10},{10,11},{11... | collective-permute-start | bytes 36872 | tf_op jit(solution)/shard_map/ppermute | solution.py:1578
  265.1 5.1 collective-permute-start.12
  266.6 18.1 %collective-permute-start.15 = (bf16[4,1,1536]{2,1,0:T(2,128)(2,1)}, bf16[4,1,1536]{2,1,0:T(2,128)(2,1)}, u32[]{:S(2)}, u32[]{:S(2)}) collective-permute-start(bf16[4,1,1536]{2,1,0:T(2,128)(2,1)} %collective-permute-done.8.refs_6_.refs_8_), channel_id=1, source_target_pairs={{0,1},{1,0},{2,3},{3,2},{4,5},{5,4},{6,7},{7,6},{8,9},{9,8},{10,11... | collective-permute-start | bytes 36872 | tf_op jit(solution)/shard_map/ppermute | solution.py:1257
  269.7 15.0 %collective-permute-start.14 = (bf16[4,1,1536]{2,1,0:T(2,128)(2,1)}, bf16[4,1,1536]{2,1,0:T(2,128)(2,1)}, u32[]{:S(2)}, u32[]{:S(2)}) collective-permute-start(bf16[4,1,1536]{2,1,0:T(2,128)(2,1)} %collective-permute-done.7.refs_5_.refs_7_), channel_id=1, source_target_pairs={{0,1},{1,0},{2,3},{3,2},{4,5},{5,4},{6,7},{7,6},{8,9},{9,8},{10,11... | collective-permute-start | bytes 36872 | tf_op jit(solution)/shard_map/ppermute | solution.py:1257
  269.8 14.9 %collective-permute-start.13 = (bf16[512,1536]{1,0:T(8,128)(2,1)}, bf16[512,1536]{1,0:T(8,128)(2,1)}, u32[]{:S(2)}, u32[]{:S(2)}) collective-permute-start(bf16[512,1536]{1,0:T(8,128)(2,1)} %get-tuple-element.187.refs_0_.refs_5_), channel_id=1, source_target_pairs={{0,1},{1,0},{2,3},{3,2},{4,5},{5,4},{6,7},{7,6},{8,9},{9,8},{10,11... | collective-permute-start | bytes 4718600 | tf_op jit(solution)/shard_map/ppermute | solution.py:1257
  301.6 40.6 %collective-permute-start.20 = (bf16[2,576,768]{2,1,0:T(8,128)(2,1)}, bf16[2,576,768]{2,1,0:T(8,128)(2,1)}, u32[]{:S(2)}, u32[]{:S(2)}) collective-permute-start(bf16[2,576,768]{2,1,0:T(8,128)(2,1)} %get-tuple-element.218), channel_id=1, source_target_pairs={{0,2},{1,3},{2,0},{3,1},{4,6},{5,7},{6,4},{7,5},{8,10},{9,11},{10,... | collective-permute-start | bytes 5308424 | tf_op jit(solution)/shard_map/ppermute | solution.py:1257
  303.9 43.5 %collective-permute-start.21 = (bf16[2,576,768]{2,1,0:T(8,128)(2,1)}, bf16[2,576,768]{2,1,0:T(8,128)(2,1)}, u32[]{:S(2)}, u32[]{:S(2)}) collective-permute-start(bf16[2,576,768]{2,1,0:T(8,128)(2,1)} %get-tuple-element.219), channel_id=1, source_target_pairs={{0,4},{1,5},{2,6},{3,7},{4,0},{5,1},{6,2},{7,3},{8,12},{9,13},{10,... | collective-permute-start | bytes 5308424 | tf_op jit(solution)/shard_map/ppermute | solution.py:1257
  340.2 14.7 %collective-permute-start.16 = (bf16[960,768]{1,0:T(8,128)(2,1)}, bf16[960,768]{1,0:T(8,128)(2,1)}, u32[]{:S(2)}, u32[]{:S(2)}) collective-permute-start(bf16[960,768]{1,0:T(8,128)(2,1)} %get-tuple-element.212), channel_id=1, source_target_pairs={{0,1},{1,0},{2,3},{3,2},{4,5},{5,4},{6,7},{7,6},{8,9},{9,8},{10,11... | collective-permute-start | bytes 4423688 | tf_op jit(solution)/shard_map/ppermute | solution.py:1257
  341.5 14.9 %collective-permute-start.17 = (bf16[960,768]{1,0:T(8,128)(2,1)}, bf16[960,768]{1,0:T(8,128)(2,1)}, u32[]{:S(2)}, u32[]{:S(2)}) collective-permute-start(bf16[960,768]{1,0:T(8,128)(2,1)} %get-tuple-element.213), channel_id=1, source_target_pairs={{0,1},{1,0},{2,3},{3,2},{4,5},{5,4},{6,7},{7,6},{8,9},{9,8},{10,11... | collective-permute-start | bytes 4423688 | tf_op jit(solution)/shard_map/ppermute | solution.py:1257
  341.6 14.9 %collective-permute-start.18 = (bf16[960,768]{1,0:T(8,128)(2,1)}, bf16[960,768]{1,0:T(8,128)(2,1)}, u32[]{:S(2)}, u32[]{:S(2)}) collective-permute-start(bf16[960,768]{1,0:T(8,128)(2,1)} %get-tuple-element.214), channel_id=1, source_target_pairs={{0,1},{1,0},{2,3},{3,2},{4,5},{5,4},{6,7},{7,6},{8,9},{9,8},{10,11... | collective-permute-start | bytes 4423688 | tf_op jit(solution)/shard_map/ppermute | solution.py:1257
  342.2 14.2 %collective-permute-start.19 = (bf16[960,768]{1,0:T(8,128)(2,1)}, bf16[960,768]{1,0:T(8,128)(2,1)}, u32[]{:S(2)}, u32[]{:S(2)}) collective-permute-start(bf16[960,768]{1,0:T(8,128)(2,1)} %get-tuple-element.215), channel_id=1, source_target_pairs={{0,1},{1,0},{2,3},{3,2},{4,5},{5,4},{6,7},{7,6},{8,9},{9,8},{10,11... | collective-permute-start | bytes 4423688 | tf_op jit(solution)/shard_map/ppermute | solution.py:1257
  343.8 21.3 %all-to-all-start.2 = ((bf16[8,480,128]{2,1,0:T(8,128)(2,1)}), bf16[8,480,128]{2,1,0:T(8,128)(2,1)S(1)}, u32[]{:S(2)}, u32[]{:S(2)}) async-start(bf16[8,480,128]{2,1,0:T(8,128)(2,1)} %get-tuple-element.209), calls=%async_computation.2 | async-start | bytes 1966080 | tf_op jit(solution)/shard_map/all_to_all | solution.py:1712
  353.0 39.7 %collective-permute-start.22 = (bf16[1,576,768]{2,1,0:T(8,128)(2,1)}, bf16[1,576,768]{2,1,0:T(8,128)(2,1)}, u32[]{:S(2)}, u32[]{:S(2)}) collective-permute-start(bf16[1,576,768]{2,1,0:T(8,128)(2,1)} %get-tuple-element.232), channel_id=1, source_target_pairs={{0,4},{1,5},{2,6},{3,7},{4,0},{5,1},{6,2},{7,3},{8,12},{9,13},{10,... | collective-permute-start | bytes 2654216 | tf_op jit(solution)/shard_map/ppermute | solution.py:1257
  354.9 37.8 %collective-permute-start.23 = (bf16[1,576,768]{2,1,0:T(8,128)(2,1)}, bf16[1,576,768]{2,1,0:T(8,128)(2,1)}, u32[]{:S(2)}, u32[]{:S(2)}) collective-permute-start(bf16[1,576,768]{2,1,0:T(8,128)(2,1)} %get-tuple-element.233), channel_id=1, source_target_pairs={{0,2},{1,3},{2,0},{3,1},{4,6},{5,7},{6,4},{7,5},{8,10},{9,11},{10,... | collective-permute-start | bytes 2654216 | tf_op jit(solution)/shard_map/ppermute | solution.py:1257
  364.4 47.9 %collective-permute-start.25 = (bf16[2,480,768]{2,1,0:T(8,128)(2,1)}, bf16[2,480,768]{2,1,0:T(8,128)(2,1)}, u32[]{:S(2)}, u32[]{:S(2)}) collective-permute-start(bf16[2,480,768]{2,1,0:T(8,128)(2,1)} %get-tuple-element.243), channel_id=1, source_target_pairs={{0,2},{1,3},{2,0},{3,1},{4,6},{5,7},{6,4},{7,5},{8,10},{9,11},{10,... | collective-permute-start | bytes 4423688 | tf_op jit(solution)/shard_map/ppermute | solution.py:1257
  365.0 47.3 %collective-permute-start.26 = (bf16[2,480,768]{2,1,0:T(8,128)(2,1)}, bf16[2,480,768]{2,1,0:T(8,128)(2,1)}, u32[]{:S(2)}, u32[]{:S(2)}) collective-permute-start(bf16[2,480,768]{2,1,0:T(8,128)(2,1)} %get-tuple-element.244), channel_id=1, source_target_pairs={{0,4},{1,5},{2,6},{3,7},{4,0},{5,1},{6,2},{7,3},{8,12},{9,13},{10,... | collective-permute-start | bytes 4423688 | tf_op jit(solution)/shard_map/ppermute | solution.py:1257
  387.8 50.7 %all-to-all-start.3 = ((bf16[8,6,3,64,128]{4,3,2,1,0:T(8,128)(2,1)}), bf16[8,6,3,64,128]{4,3,2,1,0:T(8,128)(2,1)}, u32[]{:S(2)}, u32[]{:S(2)}) async-start(bf16[8,6,3,64,128]{4,3,2,1,0:T(8,128)(2,1)} %get-tuple-element.223), calls=%async_computation.3 | async-start | bytes 4718592 | tf_op jit(solution)/shard_map/all_to_all | solution.py:1719
  395.7 23.5 %collective-permute-start.24 = (bf16[576,768]{1,0:T(8,128)(2,1)}, bf16[576,768]{1,0:T(8,128)(2,1)}, u32[]{:S(2)}, u32[]{:S(2)}) collective-permute-start(bf16[576,768]{1,0:T(8,128)(2,1)} %get-tuple-element.240), channel_id=1, source_target_pairs={{0,8},{8,0},{16,24},{24,16},{1,9},{9,1},{17,25},{25,17},{2,10},{10... | collective-permute-start | bytes 2654216 | tf_op jit(solution)/shard_map/ppermute | solution.py:1257
  415.7 37.1 %collective-permute-start.27 = (bf16[1,480,768]{2,1,0:T(8,128)(2,1)}, bf16[1,480,768]{2,1,0:T(8,128)(2,1)}, u32[]{:S(2)}, u32[]{:S(2)}) collective-permute-start(bf16[1,480,768]{2,1,0:T(8,128)(2,1)} %get-tuple-element.252), channel_id=1, source_target_pairs={{0,4},{1,5},{2,6},{3,7},{4,0},{5,1},{6,2},{7,3},{8,12},{9,13},{10,... | collective-permute-start | bytes 2211848 | tf_op jit(solution)/shard_map/ppermute | solution.py:1257
  417.7 35.3 %collective-permute-start.28 = (bf16[1,480,768]{2,1,0:T(8,128)(2,1)}, bf16[1,480,768]{2,1,0:T(8,128)(2,1)}, u32[]{:S(2)}, u32[]{:S(2)}) collective-permute-start(bf16[1,480,768]{2,1,0:T(8,128)(2,1)} %get-tuple-element.253), channel_id=1, source_target_pairs={{0,2},{1,3},{2,0},{3,1},{4,6},{5,7},{6,4},{7,5},{8,10},{9,11},{10,... | collective-permute-start | bytes 2211848 | tf_op jit(solution)/shard_map/ppermute | solution.py:1257
  422.7 27.2 %collective-permute-start.29 = (bf16[288,768]{1,0:T(8,128)(2,1)}, bf16[288,768]{1,0:T(8,128)(2,1)}, u32[]{:S(2)}, u32[]{:S(2)}) collective-permute-start(bf16[288,768]{1,0:T(8,128)(2,1)} %get-tuple-element.255), channel_id=1, source_target_pairs={{0,16},{8,24},{16,0},{24,8},{1,17},{9,25},{17,1},{25,9},{2,18},{10... | collective-permute-start | bytes 1327112 | tf_op jit(solution)/shard_map/ppermute | solution.py:1257
  455.0 4.0 collective-permute-start.32
  455.0 6.8 %collective-permute-start.33 = (bf16[4,320,768]{2,1,0:T(8,128)(2,1)S(1)}, bf16[4,320,768]{2,1,0:T(8,128)(2,1)S(1)}, u32[]{:S(2)}, u32[]{:S(2)}) collective-permute-start(bf16[4,320,768]{2,1,0:T(8,128)(2,1)S(1)} %get-tuple-element.265), channel_id=1, source_target_pairs={{0,1},{1,0},{2,3},{3,2},{4,5},{5,4},{6,7},{7,6},{8,9},{9,8},{10,11... | collective-permute-start | bytes 5898248 | tf_op jit(solution)/shard_map/ppermute | solution.py:1257
  462.8 29.6 %copy-start.21 = (f32[8,128]{1,0:T(8,128)}, f32[8,128]{1,0:T(8,128)S(1)}, u32[]{:S(2)}) copy-start(f32[8,128]{1,0:T(8,128)S(1)} %get-tuple-element.271.refs_10_) | copy-start | bytes 12292
  462.8 29.6 %collective-permute-start.34 = (bf16[2,320,768]{2,1,0:T(8,128)(2,1)S(1)}, bf16[2,320,768]{2,1,0:T(8,128)(2,1)S(1)}, u32[]{:S(2)}, u32[]{:S(2)}) collective-permute-start(bf16[2,320,768]{2,1,0:T(8,128)(2,1)S(1)} %get-tuple-element.269), channel_id=1, source_target_pairs={{0,2},{1,3},{2,0},{3,1},{4,6},{5,7},{6,4},{7,5},{8,10},{9,11},{10,... | collective-permute-start | bytes 2949128 | tf_op jit(solution)/shard_map/ppermute | solution.py:1257
  464.2 28.2 %collective-permute-start.35 = (bf16[2,320,768]{2,1,0:T(8,128)(2,1)S(1)}, bf16[2,320,768]{2,1,0:T(8,128)(2,1)S(1)}, u32[]{:S(2)}, u32[]{:S(2)}) collective-permute-start(bf16[2,320,768]{2,1,0:T(8,128)(2,1)S(1)} %get-tuple-element.270), channel_id=1, source_target_pairs={{0,4},{1,5},{2,6},{3,7},{4,0},{5,1},{6,2},{7,3},{8,12},{9,13},{10,... | collective-permute-start | bytes 2949128 | tf_op jit(solution)/shard_map/ppermute | solution.py:1257
  464.9 27.4 %collective-permute-start.31 = (bf16[480,768]{1,0:T(8,128)(2,1)S(1)}, bf16[480,768]{1,0:T(8,128)(2,1)S(1)}, u32[]{:S(2)}, u32[]{:S(2)}) collective-permute-start(bf16[480,768]{1,0:T(8,128)(2,1)S(1)} %get-tuple-element.261), channel_id=1, source_target_pairs={{0,8},{8,0},{16,24},{24,16},{1,9},{9,1},{17,25},{25,17},{2,10},{10... | collective-permute-start | bytes 2211848 | tf_op jit(solution)/shard_map/ppermute | solution.py:1257
  466.4 25.0 %collective-permute-start.30 = (bf16[288,768]{1,0:T(8,128)(2,1)S(1)}, bf16[288,768]{1,0:T(8,128)(2,1)S(1)}, u32[]{:S(2)}, u32[]{:S(2)}) collective-permute-start(bf16[288,768]{1,0:T(8,128)(2,1)S(1)} %get-tuple-element.259.refs_2_), channel_id=1, source_target_pairs={{0,16},{8,24},{16,0},{24,8},{1,17},{9,25},{17,1},{25,9},{2,18},{10... | collective-permute-start | bytes 1327112 | tf_op jit(solution)/shard_map/ppermute | solution.py:1257
  493.2 29.6 %copy-start.23 = (f32[8,128]{1,0:T(8,128)}, f32[8,128]{1,0:T(8,128)S(1)}, u32[]{:S(2)}) copy-start(f32[8,128]{1,0:T(8,128)S(1)} %get-tuple-element.279.refs_7_) | copy-start | bytes 12292
  493.2 29.6 %collective-permute-start.38 = (bf16[1,320,768]{2,1,0:T(8,128)(2,1)S(1)}, bf16[1,320,768]{2,1,0:T(8,128)(2,1)S(1)}, u32[]{:S(2)}, u32[]{:S(2)}) collective-permute-start(bf16[1,320,768]{2,1,0:T(8,128)(2,1)S(1)} %get-tuple-element.277), channel_id=1, source_target_pairs={{0,4},{1,5},{2,6},{3,7},{4,0},{5,1},{6,2},{7,3},{8,12},{9,13},{10,... | collective-permute-start | bytes 1474568 | tf_op jit(solution)/shard_map/ppermute | solution.py:1257
  494.5 28.2 %collective-permute-start.39 = (bf16[1,320,768]{2,1,0:T(8,128)(2,1)S(1)}, bf16[1,320,768]{2,1,0:T(8,128)(2,1)S(1)}, u32[]{:S(2)}, u32[]{:S(2)}) collective-permute-start(bf16[1,320,768]{2,1,0:T(8,128)(2,1)S(1)} %get-tuple-element.278), channel_id=1, source_target_pairs={{0,2},{1,3},{2,0},{3,1},{4,6},{5,7},{6,4},{7,5},{8,10},{9,11},{10,... | collective-permute-start | bytes 1474568 | tf_op jit(solution)/shard_map/ppermute | solution.py:1257
  495.2 62.7 %collective-permute-start.36 = (bf16[576,768]{1,0:T(8,128)(2,1)S(1)}, bf16[576,768]{1,0:T(8,128)(2,1)S(1)}, u32[]{:S(2)}, u32[]{:S(2)}) collective-permute-start(bf16[576,768]{1,0:T(8,128)(2,1)S(1)} %get-tuple-element.272.refs_2_), channel_id=1, source_target_pairs={{0,8},{8,0},{16,24},{24,16},{1,9},{9,1},{17,25},{25,17},{2,10},{10... | collective-permute-start | bytes 2654216 | tf_op jit(solution)/shard_map/ppermute | solution.py:1257
  497.7 25.1 %collective-permute-start.37 = (bf16[240,768]{1,0:T(8,128)(2,1)S(1)}, bf16[240,768]{1,0:T(8,128)(2,1)S(1)}, u32[]{:S(2)}, u32[]{:S(2)}) collective-permute-start(bf16[240,768]{1,0:T(8,128)(2,1)S(1)} %get-tuple-element.274), channel_id=1, source_target_pairs={{0,16},{8,24},{16,0},{24,8},{1,17},{9,25},{17,1},{25,9},{2,18},{10... | collective-permute-start | bytes 1105928 | tf_op jit(solution)/shard_map/ppermute | solution.py:1257
  523.5 34.4 %copy-start.22 = (f32[8,128]{1,0:T(8,128)}, f32[8,128]{1,0:T(8,128)S(1)}, u32[]{:S(2)}) copy-start(f32[8,128]{1,0:T(8,128)S(1)} %get-tuple-element.285.refs_10_) | copy-start | bytes 12292
  523.5 34.4 %collective-permute-start.40 = (bf16[240,768]{1,0:T(8,128)(2,1)S(1)}, bf16[240,768]{1,0:T(8,128)(2,1)S(1)}, u32[]{:S(2)}, u32[]{:S(2)}) collective-permute-start(bf16[240,768]{1,0:T(8,128)(2,1)S(1)} %get-tuple-element.280.refs_4_), channel_id=1, source_target_pairs={{0,16},{8,24},{16,0},{24,8},{1,17},{9,25},{17,1},{25,9},{2,18},{10... | collective-permute-start | bytes 1105928 | tf_op jit(solution)/shard_map/ppermute | solution.py:1257
  527.0 14.3 %collective-permute-start.41 = (bf16[160,768]{1,0:T(8,128)(2,1)S(1)}, bf16[160,768]{1,0:T(8,128)(2,1)S(1)}, u32[]{:S(2)}, u32[]{:S(2)}) collective-permute-start(bf16[160,768]{1,0:T(8,128)(2,1)S(1)} %get-tuple-element.282), channel_id=1, source_target_pairs={{0,8},{8,0},{16,24},{24,16},{1,9},{9,1},{17,25},{25,17},{2,10},{10... | collective-permute-start | bytes 737288 | tf_op jit(solution)/shard_map/ppermute | solution.py:1544
  527.0 30.9 %collective-permute-start.42 = (bf16[160,768]{1,0:T(8,128)(2,1)S(1)}, bf16[160,768]{1,0:T(8,128)(2,1)S(1)}, u32[]{:S(2)}, u32[]{:S(2)}) collective-permute-start(bf16[160,768]{1,0:T(8,128)(2,1)S(1)} %get-tuple-element.283), channel_id=1, source_target_pairs={{0,16},{8,24},{16,0},{24,8},{1,17},{9,25},{17,1},{25,9},{2,18},{10... | collective-permute-start | bytes 737288 | tf_op jit(solution)/shard_map/ppermute | solution.py:1544
  528.9 28.9 %collective-permute-start.43 = (bf16[160,768]{1,0:T(8,128)(2,1)S(1)}, bf16[160,768]{1,0:T(8,128)(2,1)S(1)}, u32[]{:S(2)}, u32[]{:S(2)}) collective-permute-start(bf16[160,768]{1,0:T(8,128)(2,1)S(1)} %get-tuple-element.284), channel_id=1, source_target_pairs={{0,24},{8,16},{16,8},{24,0},{1,25},{9,17},{17,9},{25,1},{2,26},{10... | collective-permute-start | bytes 737288 | tf_op jit(solution)/shard_map/ppermute | solution.py:1544
  560.1 37.2 %copy-start.20 = (f32[8,128]{1,0:T(8,128)}, f32[8,128]{1,0:T(8,128)S(1)}, u32[]{:S(2)}) copy-start(f32[8,128]{1,0:T(8,128)S(1)} %get-tuple-element.288.refs_9_) | copy-start | bytes 12292
  560.1 37.2 %collective-permute-start.44 = (bf16[480,768]{1,0:T(8,128)(2,1)S(1)}, bf16[480,768]{1,0:T(8,128)(2,1)S(1)}, u32[]{:S(2)}, u32[]{:S(2)}) collective-permute-start(bf16[480,768]{1,0:T(8,128)(2,1)S(1)} %get-tuple-element.286.refs_3_), channel_id=1, source_target_pairs={{0,8},{8,0},{16,24},{24,16},{1,9},{9,1},{17,25},{25,17},{2,10},{10... | collective-permute-start | bytes 2211848 | tf_op jit(solution)/shard_map/ppermute | solution.py:1257
  564.6 27.1 %collective-permute-start.45 = (bf16[160,768]{1,0:T(8,128)(2,1)S(1)}, bf16[160,768]{1,0:T(8,128)(2,1)S(1)}, u32[]{:S(2)}, u32[]{:S(2)}) collective-permute-start(bf16[160,768]{1,0:T(8,128)(2,1)S(1)} %get-tuple-element.287.refs_5_), channel_id=1, source_target_pairs={{0,8},{8,0},{16,24},{24,16},{1,9},{9,1},{17,25},{25,17},{2,10},{10... | collective-permute-start | bytes 737288 | tf_op jit(solution)/shard_map/ppermute | solution.py:1557
  564.6 27.4 %collective-permute-start.46 = (bf16[160,768]{1,0:T(8,128)(2,1)S(1)}, bf16[160,768]{1,0:T(8,128)(2,1)S(1)}, u32[]{:S(2)}, u32[]{:S(2)}) collective-permute-start(bf16[160,768]{1,0:T(8,128)(2,1)S(1)} %get-tuple-element.287.refs_5_), channel_id=1, source_target_pairs={{0,16},{8,24},{16,0},{24,8},{1,17},{9,25},{17,1},{25,9},{2,18},{10... | collective-permute-start | bytes 737288 | tf_op jit(solution)/shard_map/ppermute | solution.py:1557
  567.2 30.1 %collective-permute-start.47 = (bf16[160,768]{1,0:T(8,128)(2,1)S(1)}, bf16[160,768]{1,0:T(8,128)(2,1)S(1)}, u32[]{:S(2)}, u32[]{:S(2)}) collective-permute-start(bf16[160,768]{1,0:T(8,128)(2,1)S(1)} %get-tuple-element.287.refs_5_), channel_id=1, source_target_pairs={{0,24},{8,16},{16,8},{24,0},{1,25},{9,17},{17,9},{25,1},{2,26},{10... | collective-permute-start | bytes 737288 | tf_op jit(solution)/shard_map/ppermute | solution.py:1557
  (44 other events, 330.8 us)
Sparse Core Ops, SparseCore 0:
  12.3 106.4 all-gather.4
  120.7 114.0 all-gather.6

commit v4 on v3

--- a/solution.py
+++ b/solution.py
@@ -1468,14 +1468,17 @@
     )
 
 
-def across_halves(place, kept, sent, layout, outs):
+def across_halves(place, kept, sent, layout, outs, merged=False):
     bits = lax.axis_size("batch").bit_length() - 1
     came = swap(sent, "batch", 0)
-    for bit in range(1, bits):
+    halved = bits - 1 if merged else bits
+    for bit in range(1, halved):
         kept, sent = yield halve(place, bit, kept, came)
         came = swap(sent, "batch", bit)
     (held,) = yield add(kept, came)
-    for bit in reversed(range(bits)):
+    for bit in range(halved, bits):
+        (held,) = yield add(held, swap(held, "batch", bit))
+    for bit in reversed(range(halved)):
         came = swap(held, "batch", bit)
         if bit:
             (held,) = yield assemble(place, bit, held, came)
@@ -1757,7 +1760,7 @@
                 (share + 4 * blk, blk, 2, everything),
                 (share + 5 * blk, blk, 3, everything),
             ],
-            [(share, width), (blk, 4 * width), (blk, width), (blk, width)],
+            [(share, width), (blk, 4 * width), (blk, width), (blk, width)], True,
         )
     )
     rest_came, qkv_came = (swap(send, "seq", 0) for send in (rest_send, qkv_send))
@@ -1778,7 +1781,7 @@
         )
     )
     advance(conv_run, ffn_run, last_run)
-    advance(ffn_run, last_run)
+    advance(last_run)
     while conv_run.plan or ffn_run.plan or last_run.plan:
         advance(conv_run, ffn_run, last_run)
     (conv_grad,) = conv_run.result

time: 614 us -> 601 us (0.979)
  waiting for transfers between devices: 244 us -> 236 us
    ppermute x31 -> x30, waiting for transfers between devices: 57 us -> 42.4 us  [swap(): return lax.ppermute(value, axis, [(i, i ^ 1 << bit) for i in range(size)])]
    ppermute x3, waiting for transfers between devices: 26.5 us -> 35.9 us  [across_direct(): came = [lax.ppermute(pieces[mask], 'batch', pairs) for mask, pairs in ends]]
    ppermute x31 -> x30, starting transfers between devices: 42.6 us -> 37.9 us  [swap(): return lax.ppermute(value, axis, [(i, i ^ 1 << bit) for i in range(size)])]
  transfers between devices with their start and end apart: 54 -> 53, of which waited for: 19 -> 19; matrix products, arithmetic and copies ran while one was open for 1% -> 1% of each run, Pallas kernels for 32% -> 32%
where the time goes in v4:
time: 601 us; the launch traced here: 595 us
  Pallas kernels  239 us (40%)
  waiting for transfers between devices  236 us (39%)
  starting transfers between devices  81.9 us (14%)
  local copies, waits for them, and re-layouts  19.5 us (3%)
  between operations  15 us (2%)
    pallas_call x28, Pallas kernels, launch(): pl.pallas_call(kernel, grid_spec=pltpu.PrefetchScalarGridSpec(num_scalar_...  239 us
    all_gather x1, waiting for transfers between devices, local(): first = lax.all_gather(first, 'seq', axis=0)  99.1 us
    ppermute x30, waiting for transfers between devices, swap(): return lax.ppermute(value, axis, [(i, i ^ 1 << bit) for i in range(size)])  42.4 us
    ppermute x30, starting transfers between devices, swap(): return lax.ppermute(value, axis, [(i, i ^ 1 << bit) for i in range(size)])  37.9 us
    ppermute x3, waiting for transfers between devices, across_direct(): came = [lax.ppermute(pieces[mask], 'batch', pairs) for mask, pairs in ends]  35.9 us
    ppermute x3, waiting for transfers between devices, across_direct(): came = [lax.ppermute(held, 'batch', pairs) for _, pairs in ends]  25.9 us
    ppermute x7, waiting for transfers between devices, local(): lax.ppermute(block_totals, 'seq', [(i, i ^ mask) for i in range(count)])  21.1 us
    unnamed x108, local copies, waits for them, and re-layouts  13.4 us
  transfers between devices with their start and end apart: 53, of which 19 were waited for; matrix products, arithmetic and copies ran while one was open for 1% of the time, Pallas kernels for 32%

profile of v4, /device:TPU:0, one launch (start us, length us, event | category | flops | bytes accessed | tf_op | source)
XLA Modules:
  0.0 594.7 jit_solution(9810533112710576511)
XLA Ops:
  8.9 3.3 pack.2
  14.9 2.7 pack.3
  19.7 99.1 %all-gather.5.cloned.1.call-done = bf16[13056,768]{1,0:T(8,128)(2,1)} async-done(((bf16[1632,768]{1,0:T(8,128)(2,1)}), bf16[13056,768]{1,0:T(8,128)(2,1)}) %all-gather.5.cloned.1.call-update) | async-done | bytes 20054032 | tf_op jit(solution)/shard_map/all_gather | solution.py:1632
  119.7 5.7 qkv.1
  125.3 4.6 all-to-all-start
  129.9 17.5 %gates.1 = (f32[3,4096,128]{2,1,0:T(8,128)}, f32[3,4096,128]{2,1,0:T(8,128)}, f32[2,3,8,128]{3,2,1,0:T(8,128)}, f32[8,128]{1,0:T(8,128)}) custom-call(s32[4]{0:T(128)S(1)} %copy-done.31, s32[4,512,1]{2,1,0:T(8,128)S(1)} %copy.49.refs_1_, s32[4,512,1]{2,1,0:T(8,128)S(1)} %copy.50.refs_2_, bf16[8,1632,768]{2,1,0:T(8,128)(2,1)} %bitcast.56, ...), custom_call_target="tpu_custom_call" | custom-call | flops 6442450944000 | bytes 25165824000 | tf_op jit(solution)/shard_map/gates/pallas_call | solution.py:90
  147.8 1.7 collective-permute-start.1
  150.1 1.7 collective-permute-start.3
  153.3 2.6 collective-permute-start.5
  155.9 21.1 %collective-permute-done.1.refs_3_ = f32[2,3,8,128]{3,2,1,0:T(8,128)S(1)} collective-permute-done((f32[2,3,8,128]{3,2,1,0:T(8,128)}, f32[2,3,8,128]{3,2,1,0:T(8,128)S(1)}, u32[]{:S(2)}, u32[]{:S(2)}) %collective-permute-start.1) | collective-permute-done | bytes 24608 | tf_op jit(solution)/shard_map/ppermute | solution.py:1650
  178.5 12.3 %attend.1 = (bf16[8,6,64,128]{3,2,1,0:T(8,128)(2,1)}, f32[6,1,1024]{2,1,0:T(1,128)S(1)}, f32[8,128]{1,0:T(8,128)}) custom-call(bf16[8,6,3,64,128]{4,3,2,1,0:T(8,128)(2,1)} %all-to-all-done.refs_0_, f32[8,128]{1,0:T(8,128)} %get-tuple-element.168.refs_1_), custom_call_target="tpu_custom_call" | custom-call | flops 6442450944000 | bytes 3145728000 | tf_op jit(solution)/shard_map/attend/pallas_call | solution.py:90
  190.8 4.7 all-to-all-start.1
  196.5 10.6 %states.1 = (f32[3,4096,128]{2,1,0:T(8,128)}, bf16[512,768]{1,0:T(8,128)(2,1)}, f32[512,768]{1,0:T(8,128)}, bf16[512,768]{1,0:T(8,128)(2,1)}, f32[8,128]{1,0:T(8,128)}) custom-call(s32[1]{0:T(128)} %bitcast.13.refs_0_.refs_2_, f32[3,4096,128]{2,1,0:T(8,128)} %get-tuple-element.170.refs_1_.refs_5_.refs_2_, ...), custom_call_target="tpu_custom_call" | custom-call | flops 1006632960000 | bytes 18874368000 | tf_op jit(solution)/shard_map/states/pallas_call | solution.py:90
  209.3 7.6 %all-to-all-done.1.refs_0_ = bf16[8,6,64,128]{3,2,1,0:T(8,128)(2,1)} async-done(((bf16[8,6,64,128]{3,2,1,0:T(8,128)(2,1)}), bf16[8,6,64,128]{3,2,1,0:T(8,128)(2,1)}, u32[]{:S(2)}, u32[]{:S(2)}) %all-to-all-start.1) | async-done | bytes 786464 | tf_op jit(solution)/shard_map/all_to_all | solution.py:1655
  216.9 17.3 %ffn.1 = (bf16[768,512]{1,0:T(8,128)(2,1)}, f32[512,768]{1,0:T(8,128)}, f32[512,1]{1,0:T(8,128)}, bf16[512,768]{1,0:T(8,128)(2,1)}, bf16[512,3072]{1,0:T(8,128)(...) custom-call(bf16[8,6,64,128]{3,2,1,0:T(8,128)(2,1)} %all-to-all-done, ...), custom_call_target="tpu_custom_call" | custom-call | flops 5435817984000 | bytes 25165824000 | tf_op jit(solution)/shard_map/ffn/pallas_call | solution.py:90
  236.8 3.6 collective-permute-start.7
  243.2 18.3 %conv.1 = (f32[512,768]{1,0:T(8,128)}, f32[512,768]{1,0:T(8,128)}, f32[512,768]{1,0:T(8,128)S(1)}, f32[512,768]{1,0:T(8,128)S(1)}, bf16[512,1536]{1,0:T(8,128)(2...) custom-call(bf16[512,768]{1,0:T(8,128)(2,1)S(1)} %get-tuple-element., ...), custom_call_target="tpu_custom_call", output_to_operand_aliasing={{8}: (10, {}), {9}: (11, {})} | custom-call | flops 7247757312000 | bytes 29884416000 | tf_op jit(solution)/shard_map/conv/pallas_call | solution.py:90
  261.4 3.6 collective-permute-start.11
  266.5 3.1 collective-permute-start.15
  270.2 14.4 %conv_back.1 = (bf16[512,768]{1,0:T(8,128)(2,1)S(1)}, f32[512,768]{1,0:T(8,128)S(1)}, f32[2,768]{1,0:T(2,128)S(1)}, f32[8,128]{1,0:T(8,128)}) custom-call(bf16[512,1536]{1,0:T(8,128)(2,1)} %get-tuple-element.185.refs_0_.refs_5_, bf16[4,1,1536]{2,1,0:T(2,128)(2,1)S(1)} %collective-permute-done.11.refs_1_, ...), custom_call_target="tpu_custom_call" | custom-call | flops 7247757312000 | bytes 22020096000 | tf_op jit(solution)/shard_map/conv_back/pallas_call | solution.py:90
  284.7 16.9 %conv_weight.1 = (bf16[2,576,768]{2,1,0:T(8,128)(2,1)}, bf16[2,576,768]{2,1,0:T(8,128)(2,1)}, bf16[2,576,768]{2,1,0:T(8,128)(2,1)}, bf16[2,576,768]{2,1,0:T(8,128)(2,1)}, f32[8,128]{1,0:T(8,128)}) custom-call(s32[8]{0:T(128)S(1)} %broadcast_xor_fusion.refs_0_.refs_1_, bf16[512,768]{1,0:T(8,128)(2,1)S(1)} %get-tuple-element.177.refs_0_.refs_1_, ...), custom_call_target="tpu_custom_call" | custom-call | flops 7247757312000 | bytes 7077888000 | tf_op jit(solution)/shard_map/conv_weight/pallas_call | solution.py:90
  301.5 2.3 collective-permute-start.20
  304.4 10.2 %states_back.1 = (f32[3,4096,128]{2,1,0:T(8,128)}, f32[3,8,128]{2,1,0:T(8,128)S(1)}, f32[8,128]{1,0:T(8,128)}) custom-call(bf16[512,768]{1,0:T(8,128)(2,1)S(1)} %get-tuple-element.198.refs_0_.refs_15_, bf16[8,1632,768]{2,1,0:T(8,128)(2,1)} %bitcast.64, f32[4,128,1]{2,1,0:T(8,128)S(1)} %convert_element_type.28.refs_6_.refs_2_, s32[4,1,128]{2,1,0:T(1,128)S(1)} %sub.14.refs_3_, ...), custom_call_target="tpu_custom_call" | custom-call | flops 1006632960000 | bytes 12582912000 | tf_op jit(solution)/shard_map/states_back/pallas_call | solution.py:90
  314.7 25.4 %ffn_back.1 = (bf16[960,768]{1,0:T(8,128)(2,1)}, bf16[960,768]{1,0:T(8,128)(2,1)}, bf16[960,768]{1,0:T(8,128)(2,1)}, bf16[960,768]{1,0:T(8,128)(2,1)}, bf16[4,96...) custom-call(s32[8]{0:T(128)S(1)} %shift-left_add_fusion.refs_0_, ...), custom_call_target="tpu_custom_call" | custom-call | flops 10267656192000 | bytes 34603008000 | tf_op jit(solution)/shard_map/ffn_back/pallas_call | solution.py:90
  342.1 1.6 collective-permute-start.19
  343.7 3.6 all-to-all-start.2
  347.3 5.6 split.3
  352.9 1.9 collective-permute-start.22
  354.9 1.5 collective-permute-start.23
  356.4 7.9 %fold.1 = (bf16[2,480,768]{2,1,0:T(8,128)(2,1)}, bf16[2,480,768]{2,1,0:T(8,128)(2,1)}, bf16[2,480,768]{2,1,0:T(8,128)(2,1)}, bf16[2,480,768]{2,1,0:T(8,128)(2,1)}, f32[8,128]{1,0:T(8,128)}) custom-call(bf16[4,960,768]{2,1,0:T(8,128)(2,1)} %get-tuple-element.209.refs_0_.refs_1_, bf16[4,960,768]{2,1,0:T(8,128)(2,1)} %get-tuple-element.209.refs_0_.refs_1_, ...), custom_call_target="tpu_custom_call" | custom-call | flops 2949120000 | bytes 17694720000 | tf_op jit(solution)/shard_map/fold/pallas_call | solution.py:90
  366.0 21.7 %attend_back.1 = (bf16[8,6,3,64,128]{4,3,2,1,0:T(8,128)(2,1)}, f32[8,128]{1,0:T(8,128)}) custom-call(bf16[8,6,3,64,128]{4,3,2,1,0:T(8,128)(2,1)} %all-to-all-done.refs_0_, bf16[8,480,128]{2,1,0:T(8,128)(2,1)} %copy-done.4, f32[6,1,1024]{2,1,0:T(1,128)S(1)} %get-tuple-element.208.refs_2_, f32[8,128]{1,0:T(8,128)} %get-tuple-element.220.refs_3_), custom_call_target="tpu_custom_call" | custom-call | flops 16106127360000 | bytes 5505024000 | tf_op jit(solution)/shard_map/attend_back/pallas_call | solution.py:90
  387.7 4.9 all-to-all-start.3
  392.7 2.9 cross.1
  395.6 1.5 collective-permute-start.24
  397.1 14.8 %gates_back.1 = (bf16[4,256,1536]{2,1,0:T(8,128)(2,1)S(1)}, f32[1,1536]{1,0:T(1,128)S(1)}, f32[8,128]{1,0:T(8,128)S(1)}) custom-call(s32[1]{0:T(128)} %bitcast.13.refs_0_.refs_2_, s32[4]{0:T(128)S(1)} %copy-done.31, f32[3,4096,128]{2,1,0:T(8,128)} %get-tuple-element.170.refs_1_.refs_5_.refs_2_, f32[3,4096,128]{2,1,0:T(8,128)} %get-tuple-element.171.refs_2_.refs_3_, ...), custom_call_target="tpu_custom_call" | custom-call | flops 1610612736000 | bytes 25165824000 | tf_op jit(solution)/shard_map/gates_back/pallas_call | solution.py:90
  412.5 3.1 split.4
  415.6 2.0 collective-permute-start.27
  417.6 1.5 collective-permute-start.28
  419.1 2.2 halve.1
  422.6 2.4 collective-permute-start.29
  425.0 8.0 %rest.1 = (bf16[4,320,768]{2,1,0:T(8,128)(2,1)S(1)}, bf16[4,320,768]{2,1,0:T(8,128)(2,1)S(1)}, f32[8,128]{1,0:T(8,128)S(1)}) custom-call(s32[8]{0:T(128)S(1)} %copy-done.33, bf16[8,1632,768]{2,1,0:T(8,128)(2,1)} %bitcast.68, bf16[4,256,1536]{2,1,0:T(8,128)(2,1)S(1)} %get-tuple-element.236.refs_2_, bf16[8,1632,768]{2,1,0:T(8,128)(2,1)} %bitcast.69, ...), custom_call_target="tpu_custom_call" | custom-call | flops 4831838208000 | bytes 11796480000 | tf_op jit(solution)/shard_map/rest/pallas_call | solution.py:90
  435.0 3.5 all-to-all-done.3.refs_1_
  441.0 8.8 %qkv_back.1 = (f32[512,768]{1,0:T(8,128)}, bf16[4,320,768]{2,1,0:T(8,128)(2,1)S(1)}, bf16[4,320,768]{2,1,0:T(8,128)(2,1)S(1)}, f32[8,128]{1,0:T(8,128)S(1)}) custom-call(s32[8]{0:T(128)S(1)} %copy-done.33, bf16[8,6,3,64,128]{4,3,2,1,0:T(8,128)(2,1)} %all-to-all-done.3.refs_1_, bf16[512,768]{1,0:T(8,128)(2,1)S(1)} %bitcast.43, ...), custom_call_target="tpu_custom_call" | custom-call | flops 4831838208000 | bytes 18087936000 | tf_op jit(solution)/shard_map/qkv_back/pallas_call | solution.py:90
  449.8 2.9 collective-permute-done.27.refs_3_
  452.9 2.0 cross_add.1
  455.5 3.5 collective-permute-done.32.refs_2_
  458.9 2.8 collective-permute-done.33.refs_3_
  464.9 1.5 collective-permute-start.31
  466.4 2.4 collective-permute-start.30
  468.8 22.6 %collective-permute-done.30.refs_2_ = bf16[288,768]{1,0:T(8,128)(2,1)S(1)} collective-permute-done((bf16[288,768]{1,0:T(8,128)(2,1)S(1)}, bf16[288,768]{1,0:T(8,128)(2,1)S(1)}, u32[]{:S(2)}, u32[]{:S(2)}) %collective-permute-start.30) | collective-permute-done | bytes 442400 | tf_op jit(solution)/shard_map/ppermute | solution.py:1257
  493.1 2.5 collective-permute-start.36
  497.6 1.5 collective-permute-start.37
  499.1 8.0 %collective-permute-done.38.refs_3_ = bf16[1,320,768]{2,1,0:T(8,128)(2,1)S(1)} collective-permute-done((bf16[1,320,768]{2,1,0:T(8,128)(2,1)S(1)}, bf16[1,320,768]{2,1,0:T(8,128)(2,1)S(1)}, u32[]{:S(2)}, u32[]{:S(2)}) %collective-permute-start.38) | collective-permute-done | bytes 491552 | tf_op jit(solution)/shard_map/ppermute | solution.py:1257
  509.1 1.7 collective-permute-start.41
  510.7 2.4 collective-permute-start.42
  513.1 26.0 %collective-permute-done.40.refs_6_ = bf16[160,768]{1,0:T(8,128)(2,1)S(1)} collective-permute-done((bf16[160,768]{1,0:T(8,128)(2,1)S(1)}, bf16[160,768]{1,0:T(8,128)(2,1)S(1)}, u32[]{:S(2)}, u32[]{:S(2)}) %collective-permute-start.40) | collective-permute-done | bytes 245792 | tf_op jit(solution)/shard_map/ppermute | solution.py:1547
  539.1 9.9 %collective-permute-done.41.refs_7_ = bf16[160,768]{1,0:T(8,128)(2,1)S(1)} collective-permute-done((bf16[160,768]{1,0:T(8,128)(2,1)S(1)}, bf16[160,768]{1,0:T(8,128)(2,1)S(1)}, u32[]{:S(2)}, u32[]{:S(2)}) %collective-permute-start.41) | collective-permute-done | bytes 245792 | tf_op jit(solution)/shard_map/ppermute | solution.py:1547
  549.0 2.1 finish_add_total.1
  551.1 3.2 collective-permute-start.43
  554.4 2.0 collective-permute-start.45
  556.3 2.4 collective-permute-start.46
  558.7 22.1 %collective-permute-done.44.refs_6_ = bf16[160,768]{1,0:T(8,128)(2,1)S(1)} collective-permute-done((bf16[160,768]{1,0:T(8,128)(2,1)S(1)}, bf16[160,768]{1,0:T(8,128)(2,1)S(1)}, u32[]{:S(2)}, u32[]{:S(2)}) %collective-permute-start.44) | collective-permute-done | bytes 245792 | tf_op jit(solution)/shard_map/ppermute | solution.py:1560
  580.8 3.8 collective-permute-done.46.refs_8_
  584.6 2.5 finish_spread.1
  (208 shorter events, 42.5 us)
Async XLA Ops:
  7.2 111.6 %all-gather.5.cloned.1.call-start = ((), (), s32[]{:S(2)}) async-start(), calls=%async_computation.4 | async-start | bytes 22560768 | tf_op jit(solution)/shard_map/all_gather | solution.py:1632
  12.2 228.3 %all-gather.7.cloned.1.call-start = ((), (), s32[]{:S(2)}) async-start(), calls=%async_computation.5 | async-start | bytes 15925248 | tf_op jit(solution)/shard_map/all_gather | solution.py:1633
  18.1 100.7 %copy-start.45 = (s32[4,512]{1,0:T(4,128)}, s32[4,512]{1,0:T(4,128)S(1)}, u32[]{:S(2)}) copy-start(s32[4,512]{1,0:T(4,128)S(1)} %rev.4) | copy-start | bytes 24580
  125.3 53.2 %all-to-all-start = ((bf16[8,6,3,64,128]{4,3,2,1,0:T(8,128)(2,1)}), bf16[8,6,3,64,128]{4,3,2,1,0:T(8,128)(2,1)}, u32[]{:S(2)}, u32[]{:S(2)}) async-start(bf16[8,6,3,64,128]{4,3,2,1,0:T(8,128)(2,1)} %get-tuple-element.166), calls=%async_computation | async-start | bytes 4718592 | tf_op jit(solution)/shard_map/all_to_all | solution.py:1647
  147.5 5.3 collective-permute-start
  147.8 29.3 %collective-permute-start.1 = (f32[2,3,8,128]{3,2,1,0:T(8,128)}, f32[2,3,8,128]{3,2,1,0:T(8,128)S(1)}, u32[]{:S(2)}, u32[]{:S(2)}) collective-permute-start(f32[2,3,8,128]{3,2,1,0:T(8,128)} %get-tuple-element.172.refs_1_), channel_id=1, source_target_pairs={{0,2},{1,3},{2,0},{3,1},{4,6},{5,7},{6,4},{7,5},{8,10},{9,11},{10,... | collective-permute-start | bytes 73736 | tf_op jit(solution)/shard_map/ppermute | solution.py:1650
  150.0 45.6 %collective-permute-start.2 = (f32[2,3,8,128]{3,2,1,0:T(8,128)}, f32[2,3,8,128]{3,2,1,0:T(8,128)}, u32[]{:S(2)}, u32[]{:S(2)}) collective-permute-start(f32[2,3,8,128]{3,2,1,0:T(8,128)} %get-tuple-element.172.refs_1_), channel_id=1, source_target_pairs={{0,3},{1,2},{2,1},{3,0},{4,7},{5,6},{6,5},{7,4},{8,11},{9,10},{10,... | collective-permute-start | bytes 73736 | tf_op jit(solution)/shard_map/ppermute | solution.py:1650
  150.1 45.5 %collective-permute-start.3 = (f32[2,3,8,128]{3,2,1,0:T(8,128)}, f32[2,3,8,128]{3,2,1,0:T(8,128)}, u32[]{:S(2)}, u32[]{:S(2)}) collective-permute-start(f32[2,3,8,128]{3,2,1,0:T(8,128)} %get-tuple-element.172.refs_1_), channel_id=1, source_target_pairs={{0,4},{1,5},{2,6},{3,7},{4,0},{5,1},{6,2},{7,3},{8,12},{9,13},{10,... | collective-permute-start | bytes 73736 | tf_op jit(solution)/shard_map/ppermute | solution.py:1650
  151.8 43.8 %collective-permute-start.4 = (f32[2,3,8,128]{3,2,1,0:T(8,128)}, f32[2,3,8,128]{3,2,1,0:T(8,128)}, u32[]{:S(2)}, u32[]{:S(2)}) collective-permute-start(f32[2,3,8,128]{3,2,1,0:T(8,128)} %get-tuple-element.172.refs_1_), channel_id=1, source_target_pairs={{0,5},{1,4},{2,7},{3,6},{4,1},{5,0},{6,3},{7,2},{8,13},{9,12},{10,... | collective-permute-start | bytes 73736 | tf_op jit(solution)/shard_map/ppermute | solution.py:1650
  153.3 42.3 %collective-permute-start.5 = (f32[2,3,8,128]{3,2,1,0:T(8,128)}, f32[2,3,8,128]{3,2,1,0:T(8,128)}, u32[]{:S(2)}, u32[]{:S(2)}) collective-permute-start(f32[2,3,8,128]{3,2,1,0:T(8,128)} %get-tuple-element.172.refs_1_), channel_id=1, source_target_pairs={{0,6},{1,7},{2,4},{3,5},{4,2},{5,3},{6,0},{7,1},{8,14},{9,15},{10,... | collective-permute-start | bytes 73736 | tf_op jit(solution)/shard_map/ppermute | solution.py:1650
  177.7 18.0 %collective-permute-start.6 = (f32[2,3,8,128]{3,2,1,0:T(8,128)}, f32[2,3,8,128]{3,2,1,0:T(8,128)}, u32[]{:S(2)}, u32[]{:S(2)}) collective-permute-start(f32[2,3,8,128]{3,2,1,0:T(8,128)} %get-tuple-element.172.refs_1_), channel_id=1, source_target_pairs={{0,7},{1,6},{2,5},{3,4},{4,3},{5,2},{6,1},{7,0},{8,15},{9,14},{10,... | collective-permute-start | bytes 73736 | tf_op jit(solution)/shard_map/ppermute | solution.py:1650
  190.8 26.1 %all-to-all-start.1 = ((bf16[8,6,64,128]{3,2,1,0:T(8,128)(2,1)}), bf16[8,6,64,128]{3,2,1,0:T(8,128)(2,1)}, u32[]{:S(2)}, u32[]{:S(2)}) async-start(bf16[8,6,64,128]{3,2,1,0:T(8,128)(2,1)} %get-tuple-element.169), calls=%async_computation.1 | async-start | bytes 1572864 | tf_op jit(solution)/shard_map/all_to_all | solution.py:1655
  207.1 33.7 %collective-permute-start.10 = (bf16[512,768]{1,0:T(8,128)(2,1)}, bf16[512,768]{1,0:T(8,128)(2,1)}, u32[]{:S(2)}, u32[]{:S(2)}) collective-permute-start(bf16[512,768]{1,0:T(8,128)(2,1)} %get-tuple-element.178.refs_1_.refs_2_), channel_id=1, source_target_pairs={{0,1},{1,0},{2,3},{3,2},{4,5},{5,4},{6,7},{7,6},{8,9},{9,8},{10,11... | collective-permute-start | bytes 2359304 | tf_op jit(solution)/shard_map/ppermute | solution.py:1257
  216.9 19.9 %copy-start.47 = (bf16[4,1,768]{2,1,0:T(2,128)(2,1)S(1)}, bf16[4,1,768]{2,1,0:T(2,128)(2,1)}, u32[]{:S(2)}) copy-start(bf16[4,1,768]{2,1,0:T(2,128)(2,1)} %get-tuple-element.304) | copy-start | bytes 18436
  216.9 23.6 %copy-start.53 = (s32[8]{0:T(128)S(1)}, s32[8]{0:T(128)}, u32[]{:S(2)}) copy-start(s32[8]{0:T(128)} %constant.50.clone) | copy-start | bytes 100
  235.4 5.4 collective-permute-start.9
  235.5 5.0 collective-permute-start.8
  236.8 4.0 collective-permute-start.7
  240.5 74.2 %copy-start.32 = (s32[8]{0:T(128)}, s32[8]{0:T(128)S(1)}, u32[]{:S(2)}) copy-start(s32[8]{0:T(128)S(1)} %broadcast_xor_fusion.refs_0_.refs_1_) | copy-start | bytes 100
  243.1 23.4 %copy-start.11 = (s32[4,128]{1,0:T(4,128)S(1)}, s32[4,128]{1,0:T(4,128)}, u32[]{:S(2)}) copy-start(s32[4,128]{1,0:T(4,128)} %reduce_window_sum.15) | copy-start | bytes 6148
  243.2 23.4 %copy-start.51 = (s32[4,1,128]{2,1,0:T(1,128)S(1)}, s32[4,1,128]{2,1,0:T(1,128)}, u32[]{:S(2)}) copy-start(s32[4,1,128]{2,1,0:T(1,128)} %param.25) | copy-start | bytes 6148
  243.2 27.0 %copy-start.37 = (f32[512,768]{1,0:T(8,128)S(1)}, f32[512,768]{1,0:T(8,128)}, u32[]{:S(2)}) copy-start(f32[512,768]{1,0:T(8,128)} %copy-done.35) | copy-start | bytes 4718596
  261.4 8.7 %collective-permute-start.11 = (bf16[4,1,1536]{2,1,0:T(2,128)(2,1)S(1)}, bf16[4,1,1536]{2,1,0:T(2,128)(2,1)S(1)}, u32[]{:S(2)}, u32[]{:S(2)}) collective-permute-start(bf16[4,1,1536]{2,1,0:T(2,128)(2,1)S(1)} %get-tuple-element.186), channel_id=1, source_target_pairs={{0,1},{1,2},{2,3},{3,4},{4,5},{5,6},{6,7},{8,9},{9,10},{10,11},{11... | collective-permute-start | bytes 36872 | tf_op jit(solution)/shard_map/ppermute | solution.py:1581
  265.0 5.1 collective-permute-start.12
  266.5 18.1 %collective-permute-start.15 = (bf16[4,1,1536]{2,1,0:T(2,128)(2,1)}, bf16[4,1,1536]{2,1,0:T(2,128)(2,1)}, u32[]{:S(2)}, u32[]{:S(2)}) collective-permute-start(bf16[4,1,1536]{2,1,0:T(2,128)(2,1)} %collective-permute-done.8.refs_6_.refs_8_), channel_id=1, source_target_pairs={{0,1},{1,0},{2,3},{3,2},{4,5},{5,4},{6,7},{7,6},{8,9},{9,8},{10,11... | collective-permute-start | bytes 36872 | tf_op jit(solution)/shard_map/ppermute | solution.py:1257
  269.6 15.0 %collective-permute-start.14 = (bf16[4,1,1536]{2,1,0:T(2,128)(2,1)}, bf16[4,1,1536]{2,1,0:T(2,128)(2,1)}, u32[]{:S(2)}, u32[]{:S(2)}) collective-permute-start(bf16[4,1,1536]{2,1,0:T(2,128)(2,1)} %collective-permute-done.7.refs_5_.refs_7_), channel_id=1, source_target_pairs={{0,1},{1,0},{2,3},{3,2},{4,5},{5,4},{6,7},{7,6},{8,9},{9,8},{10,11... | collective-permute-start | bytes 36872 | tf_op jit(solution)/shard_map/ppermute | solution.py:1257
  269.7 14.9 %collective-permute-start.13 = (bf16[512,1536]{1,0:T(8,128)(2,1)}, bf16[512,1536]{1,0:T(8,128)(2,1)}, u32[]{:S(2)}, u32[]{:S(2)}) collective-permute-start(bf16[512,1536]{1,0:T(8,128)(2,1)} %get-tuple-element.185.refs_0_.refs_5_), channel_id=1, source_target_pairs={{0,1},{1,0},{2,3},{3,2},{4,5},{5,4},{6,7},{7,6},{8,9},{9,8},{10,11... | collective-permute-start | bytes 4718600 | tf_op jit(solution)/shard_map/ppermute | solution.py:1257
  284.6 19.8 %copy-start.12 = (s32[4,128]{1,0:T(4,128)S(1)}, s32[4,128]{1,0:T(4,128)}, u32[]{:S(2)}) copy-start(s32[4,128]{1,0:T(4,128)} %reduce_window_sum.15) | copy-start | bytes 6148
  301.5 40.6 %collective-permute-start.20 = (bf16[2,576,768]{2,1,0:T(8,128)(2,1)}, bf16[2,576,768]{2,1,0:T(8,128)(2,1)}, u32[]{:S(2)}, u32[]{:S(2)}) collective-permute-start(bf16[2,576,768]{2,1,0:T(8,128)(2,1)} %get-tuple-element.216), channel_id=1, source_target_pairs={{0,2},{1,3},{2,0},{3,1},{4,6},{5,7},{6,4},{7,5},{8,10},{9,11},{10,... | collective-permute-start | bytes 5308424 | tf_op jit(solution)/shard_map/ppermute | solution.py:1257
  303.8 43.5 %collective-permute-start.21 = (bf16[2,576,768]{2,1,0:T(8,128)(2,1)}, bf16[2,576,768]{2,1,0:T(8,128)(2,1)}, u32[]{:S(2)}, u32[]{:S(2)}) collective-permute-start(bf16[2,576,768]{2,1,0:T(8,128)(2,1)} %get-tuple-element.217), channel_id=1, source_target_pairs={{0,4},{1,5},{2,6},{3,7},{4,0},{5,1},{6,2},{7,3},{8,12},{9,13},{10,... | collective-permute-start | bytes 5308424 | tf_op jit(solution)/shard_map/ppermute | solution.py:1257
  340.1 14.7 %collective-permute-start.16 = (bf16[960,768]{1,0:T(8,128)(2,1)}, bf16[960,768]{1,0:T(8,128)(2,1)}, u32[]{:S(2)}, u32[]{:S(2)}) collective-permute-start(bf16[960,768]{1,0:T(8,128)(2,1)} %get-tuple-element.210), channel_id=1, source_target_pairs={{0,1},{1,0},{2,3},{3,2},{4,5},{5,4},{6,7},{7,6},{8,9},{9,8},{10,11... | collective-permute-start | bytes 4423688 | tf_op jit(solution)/shard_map/ppermute | solution.py:1257
  341.4 14.9 %collective-permute-start.17 = (bf16[960,768]{1,0:T(8,128)(2,1)}, bf16[960,768]{1,0:T(8,128)(2,1)}, u32[]{:S(2)}, u32[]{:S(2)}) collective-permute-start(bf16[960,768]{1,0:T(8,128)(2,1)} %get-tuple-element.211), channel_id=1, source_target_pairs={{0,1},{1,0},{2,3},{3,2},{4,5},{5,4},{6,7},{7,6},{8,9},{9,8},{10,11... | collective-permute-start | bytes 4423688 | tf_op jit(solution)/shard_map/ppermute | solution.py:1257
  341.5 14.9 %collective-permute-start.18 = (bf16[960,768]{1,0:T(8,128)(2,1)}, bf16[960,768]{1,0:T(8,128)(2,1)}, u32[]{:S(2)}, u32[]{:S(2)}) collective-permute-start(bf16[960,768]{1,0:T(8,128)(2,1)} %get-tuple-element.212), channel_id=1, source_target_pairs={{0,1},{1,0},{2,3},{3,2},{4,5},{5,4},{6,7},{7,6},{8,9},{9,8},{10,11... | collective-permute-start | bytes 4423688 | tf_op jit(solution)/shard_map/ppermute | solution.py:1257
  342.1 14.2 %collective-permute-start.19 = (bf16[960,768]{1,0:T(8,128)(2,1)}, bf16[960,768]{1,0:T(8,128)(2,1)}, u32[]{:S(2)}, u32[]{:S(2)}) collective-permute-start(bf16[960,768]{1,0:T(8,128)(2,1)} %get-tuple-element.213), channel_id=1, source_target_pairs={{0,1},{1,0},{2,3},{3,2},{4,5},{5,4},{6,7},{7,6},{8,9},{9,8},{10,11... | collective-permute-start | bytes 4423688 | tf_op jit(solution)/shard_map/ppermute | solution.py:1257
  343.7 21.3 %all-to-all-start.2 = ((bf16[8,480,128]{2,1,0:T(8,128)(2,1)}), bf16[8,480,128]{2,1,0:T(8,128)(2,1)S(1)}, u32[]{:S(2)}, u32[]{:S(2)}) async-start(bf16[8,480,128]{2,1,0:T(8,128)(2,1)} %get-tuple-element.207), calls=%async_computation.2 | async-start | bytes 1966080 | tf_op jit(solution)/shard_map/all_to_all | solution.py:1715
  352.9 39.7 %collective-permute-start.22 = (bf16[1,576,768]{2,1,0:T(8,128)(2,1)}, bf16[1,576,768]{2,1,0:T(8,128)(2,1)}, u32[]{:S(2)}, u32[]{:S(2)}) collective-permute-start(bf16[1,576,768]{2,1,0:T(8,128)(2,1)} %get-tuple-element.230), channel_id=1, source_target_pairs={{0,4},{1,5},{2,6},{3,7},{4,0},{5,1},{6,2},{7,3},{8,12},{9,13},{10,... | collective-permute-start | bytes 2654216 | tf_op jit(solution)/shard_map/ppermute | solution.py:1257
  354.9 37.8 %collective-permute-start.23 = (bf16[1,576,768]{2,1,0:T(8,128)(2,1)}, bf16[1,576,768]{2,1,0:T(8,128)(2,1)}, u32[]{:S(2)}, u32[]{:S(2)}) collective-permute-start(bf16[1,576,768]{2,1,0:T(8,128)(2,1)} %get-tuple-element.231), channel_id=1, source_target_pairs={{0,2},{1,3},{2,0},{3,1},{4,6},{5,7},{6,4},{7,5},{8,10},{9,11},{10,... | collective-permute-start | bytes 2654216 | tf_op jit(solution)/shard_map/ppermute | solution.py:1257
  364.3 47.9 %collective-permute-start.25 = (bf16[2,480,768]{2,1,0:T(8,128)(2,1)}, bf16[2,480,768]{2,1,0:T(8,128)(2,1)}, u32[]{:S(2)}, u32[]{:S(2)}) collective-permute-start(bf16[2,480,768]{2,1,0:T(8,128)(2,1)} %get-tuple-element.241), channel_id=1, source_target_pairs={{0,2},{1,3},{2,0},{3,1},{4,6},{5,7},{6,4},{7,5},{8,10},{9,11},{10,... | collective-permute-start | bytes 4423688 | tf_op jit(solution)/shard_map/ppermute | solution.py:1257
  364.9 47.3 %collective-permute-start.26 = (bf16[2,480,768]{2,1,0:T(8,128)(2,1)}, bf16[2,480,768]{2,1,0:T(8,128)(2,1)}, u32[]{:S(2)}, u32[]{:S(2)}) collective-permute-start(bf16[2,480,768]{2,1,0:T(8,128)(2,1)} %get-tuple-element.242), channel_id=1, source_target_pairs={{0,4},{1,5},{2,6},{3,7},{4,0},{5,1},{6,2},{7,3},{8,12},{9,13},{10,... | collective-permute-start | bytes 4423688 | tf_op jit(solution)/shard_map/ppermute | solution.py:1257
  387.7 50.7 %all-to-all-start.3 = ((bf16[8,6,3,64,128]{4,3,2,1,0:T(8,128)(2,1)}), bf16[8,6,3,64,128]{4,3,2,1,0:T(8,128)(2,1)}, u32[]{:S(2)}, u32[]{:S(2)}) async-start(bf16[8,6,3,64,128]{4,3,2,1,0:T(8,128)(2,1)} %get-tuple-element.221), calls=%async_computation.3 | async-start | bytes 4718592 | tf_op jit(solution)/shard_map/all_to_all | solution.py:1722
  395.6 23.5 %collective-permute-start.24 = (bf16[576,768]{1,0:T(8,128)(2,1)}, bf16[576,768]{1,0:T(8,128)(2,1)}, u32[]{:S(2)}, u32[]{:S(2)}) collective-permute-start(bf16[576,768]{1,0:T(8,128)(2,1)} %get-tuple-element.238), channel_id=1, source_target_pairs={{0,8},{8,0},{16,24},{24,16},{1,9},{9,1},{17,25},{25,17},{2,10},{10... | collective-permute-start | bytes 2654216 | tf_op jit(solution)/shard_map/ppermute | solution.py:1257
  415.6 37.1 %collective-permute-start.27 = (bf16[1,480,768]{2,1,0:T(8,128)(2,1)}, bf16[1,480,768]{2,1,0:T(8,128)(2,1)}, u32[]{:S(2)}, u32[]{:S(2)}) collective-permute-start(bf16[1,480,768]{2,1,0:T(8,128)(2,1)} %get-tuple-element.250), channel_id=1, source_target_pairs={{0,4},{1,5},{2,6},{3,7},{4,0},{5,1},{6,2},{7,3},{8,12},{9,13},{10,... | collective-permute-start | bytes 2211848 | tf_op jit(solution)/shard_map/ppermute | solution.py:1257
  417.6 35.3 %collective-permute-start.28 = (bf16[1,480,768]{2,1,0:T(8,128)(2,1)}, bf16[1,480,768]{2,1,0:T(8,128)(2,1)}, u32[]{:S(2)}, u32[]{:S(2)}) collective-permute-start(bf16[1,480,768]{2,1,0:T(8,128)(2,1)} %get-tuple-element.251), channel_id=1, source_target_pairs={{0,2},{1,3},{2,0},{3,1},{4,6},{5,7},{6,4},{7,5},{8,10},{9,11},{10,... | collective-permute-start | bytes 2211848 | tf_op jit(solution)/shard_map/ppermute | solution.py:1257
  422.6 27.2 %collective-permute-start.29 = (bf16[288,768]{1,0:T(8,128)(2,1)}, bf16[288,768]{1,0:T(8,128)(2,1)}, u32[]{:S(2)}, u32[]{:S(2)}) collective-permute-start(bf16[288,768]{1,0:T(8,128)(2,1)} %get-tuple-element.253), channel_id=1, source_target_pairs={{0,16},{8,24},{16,0},{24,8},{1,17},{9,25},{17,1},{25,9},{2,18},{10... | collective-permute-start | bytes 1327112 | tf_op jit(solution)/shard_map/ppermute | solution.py:1257
  454.9 4.0 collective-permute-start.32
  455.0 6.8 %collective-permute-start.33 = (bf16[4,320,768]{2,1,0:T(8,128)(2,1)S(1)}, bf16[4,320,768]{2,1,0:T(8,128)(2,1)S(1)}, u32[]{:S(2)}, u32[]{:S(2)}) collective-permute-start(bf16[4,320,768]{2,1,0:T(8,128)(2,1)S(1)} %get-tuple-element.263), channel_id=1, source_target_pairs={{0,1},{1,0},{2,3},{3,2},{4,5},{5,4},{6,7},{7,6},{8,9},{9,8},{10,11... | collective-permute-start | bytes 5898248 | tf_op jit(solution)/shard_map/ppermute | solution.py:1257
  462.8 29.6 %copy-start.25 = (f32[8,128]{1,0:T(8,128)}, f32[8,128]{1,0:T(8,128)S(1)}, u32[]{:S(2)}) copy-start(f32[8,128]{1,0:T(8,128)S(1)} %get-tuple-element.269.refs_9_) | copy-start | bytes 12292
  462.8 29.6 %collective-permute-start.34 = (bf16[2,320,768]{2,1,0:T(8,128)(2,1)S(1)}, bf16[2,320,768]{2,1,0:T(8,128)(2,1)S(1)}, u32[]{:S(2)}, u32[]{:S(2)}) collective-permute-start(bf16[2,320,768]{2,1,0:T(8,128)(2,1)S(1)} %get-tuple-element.267), channel_id=1, source_target_pairs={{0,2},{1,3},{2,0},{3,1},{4,6},{5,7},{6,4},{7,5},{8,10},{9,11},{10,... | collective-permute-start | bytes 2949128 | tf_op jit(solution)/shard_map/ppermute | solution.py:1257
  464.2 28.2 %collective-permute-start.35 = (bf16[2,320,768]{2,1,0:T(8,128)(2,1)S(1)}, bf16[2,320,768]{2,1,0:T(8,128)(2,1)S(1)}, u32[]{:S(2)}, u32[]{:S(2)}) collective-permute-start(bf16[2,320,768]{2,1,0:T(8,128)(2,1)S(1)} %get-tuple-element.268), channel_id=1, source_target_pairs={{0,4},{1,5},{2,6},{3,7},{4,0},{5,1},{6,2},{7,3},{8,12},{9,13},{10,... | collective-permute-start | bytes 2949128 | tf_op jit(solution)/shard_map/ppermute | solution.py:1257
  464.9 27.4 %collective-permute-start.31 = (bf16[480,768]{1,0:T(8,128)(2,1)S(1)}, bf16[480,768]{1,0:T(8,128)(2,1)S(1)}, u32[]{:S(2)}, u32[]{:S(2)}) collective-permute-start(bf16[480,768]{1,0:T(8,128)(2,1)S(1)} %get-tuple-element.259), channel_id=1, source_target_pairs={{0,8},{8,0},{16,24},{24,16},{1,9},{9,1},{17,25},{25,17},{2,10},{10... | collective-permute-start | bytes 2211848 | tf_op jit(solution)/shard_map/ppermute | solution.py:1257
  466.4 25.0 %collective-permute-start.30 = (bf16[288,768]{1,0:T(8,128)(2,1)S(1)}, bf16[288,768]{1,0:T(8,128)(2,1)S(1)}, u32[]{:S(2)}, u32[]{:S(2)}) collective-permute-start(bf16[288,768]{1,0:T(8,128)(2,1)S(1)} %get-tuple-element.257.refs_1_), channel_id=1, source_target_pairs={{0,16},{8,24},{16,0},{24,8},{1,17},{9,25},{17,1},{25,9},{2,18},{10... | collective-permute-start | bytes 1327112 | tf_op jit(solution)/shard_map/ppermute | solution.py:1257
  493.1 55.9 %collective-permute-start.36 = (bf16[576,768]{1,0:T(8,128)(2,1)S(1)}, bf16[576,768]{1,0:T(8,128)(2,1)S(1)}, u32[]{:S(2)}, u32[]{:S(2)}) collective-permute-start(bf16[576,768]{1,0:T(8,128)(2,1)S(1)} %get-tuple-element.270.refs_1_), channel_id=1, source_target_pairs={{0,8},{8,0},{16,24},{24,16},{1,9},{9,1},{17,25},{25,17},{2,10},{10... | collective-permute-start | bytes 2654216 | tf_op jit(solution)/shard_map/ppermute | solution.py:1257
  495.6 11.5 %collective-permute-start.38 = (bf16[1,320,768]{2,1,0:T(8,128)(2,1)S(1)}, bf16[1,320,768]{2,1,0:T(8,128)(2,1)S(1)}, u32[]{:S(2)}, u32[]{:S(2)}) collective-permute-start(bf16[1,320,768]{2,1,0:T(8,128)(2,1)S(1)} %get-tuple-element.274), channel_id=1, source_target_pairs={{0,4},{1,5},{2,6},{3,7},{4,0},{5,1},{6,2},{7,3},{8,12},{9,13},{10,... | collective-permute-start | bytes 1474568 | tf_op jit(solution)/shard_map/ppermute | solution.py:1257
  496.9 11.2 %collective-permute-start.39 = (bf16[1,320,768]{2,1,0:T(8,128)(2,1)S(1)}, bf16[1,320,768]{2,1,0:T(8,128)(2,1)S(1)}, u32[]{:S(2)}, u32[]{:S(2)}) collective-permute-start(bf16[1,320,768]{2,1,0:T(8,128)(2,1)S(1)} %get-tuple-element.275), channel_id=1, source_target_pairs={{0,2},{1,3},{2,0},{3,1},{4,6},{5,7},{6,4},{7,5},{8,10},{9,11},{10,... | collective-permute-start | bytes 1474568 | tf_op jit(solution)/shard_map/ppermute | solution.py:1257
  497.6 51.4 %collective-permute-start.37 = (bf16[480,768]{1,0:T(8,128)(2,1)S(1)}, bf16[480,768]{1,0:T(8,128)(2,1)S(1)}, u32[]{:S(2)}, u32[]{:S(2)}) collective-permute-start(bf16[480,768]{1,0:T(8,128)(2,1)S(1)} %get-tuple-element.271.refs_3_), channel_id=1, source_target_pairs={{0,16},{8,24},{16,0},{24,8},{1,17},{9,25},{17,1},{25,9},{2,18},{10... | collective-permute-start | bytes 2211848 | tf_op jit(solution)/shard_map/ppermute | solution.py:1257
  508.6 40.3 %copy-start.21 = (f32[8,128]{1,0:T(8,128)}, f32[8,128]{1,0:T(8,128)S(1)}, u32[]{:S(2)}) copy-start(f32[8,128]{1,0:T(8,128)S(1)} %get-tuple-element.281.refs_9_) | copy-start | bytes 12292
  508.6 30.4 %collective-permute-start.40 = (bf16[160,768]{1,0:T(8,128)(2,1)S(1)}, bf16[160,768]{1,0:T(8,128)(2,1)S(1)}, u32[]{:S(2)}, u32[]{:S(2)}) collective-permute-start(bf16[160,768]{1,0:T(8,128)(2,1)S(1)} %get-tuple-element.278), channel_id=1, source_target_pairs={{0,8},{8,0},{16,24},{24,16},{1,9},{9,1},{17,25},{25,17},{2,10},{10... | collective-permute-start | bytes 737288 | tf_op jit(solution)/shard_map/ppermute | solution.py:1547
  509.1 39.9 %collective-permute-start.41 = (bf16[160,768]{1,0:T(8,128)(2,1)S(1)}, bf16[160,768]{1,0:T(8,128)(2,1)S(1)}, u32[]{:S(2)}, u32[]{:S(2)}) collective-permute-start(bf16[160,768]{1,0:T(8,128)(2,1)S(1)} %get-tuple-element.279), channel_id=1, source_target_pairs={{0,16},{8,24},{16,0},{24,8},{1,17},{9,25},{17,1},{25,9},{2,18},{10... | collective-permute-start | bytes 737288 | tf_op jit(solution)/shard_map/ppermute | solution.py:1547
  510.7 38.2 %collective-permute-start.42 = (bf16[160,768]{1,0:T(8,128)(2,1)S(1)}, bf16[160,768]{1,0:T(8,128)(2,1)S(1)}, u32[]{:S(2)}, u32[]{:S(2)}) collective-permute-start(bf16[160,768]{1,0:T(8,128)(2,1)S(1)} %get-tuple-element.280), channel_id=1, source_target_pairs={{0,24},{8,16},{16,8},{24,0},{1,25},{9,17},{17,9},{25,1},{2,26},{10... | collective-permute-start | bytes 737288 | tf_op jit(solution)/shard_map/ppermute | solution.py:1547
  551.1 33.5 %copy-start.20 = (f32[8,128]{1,0:T(8,128)}, f32[8,128]{1,0:T(8,128)S(1)}, u32[]{:S(2)}) copy-start(f32[8,128]{1,0:T(8,128)S(1)} %get-tuple-element.284.refs_9_) | copy-start | bytes 12292
  551.1 33.5 %collective-permute-start.43 = (bf16[480,768]{1,0:T(8,128)(2,1)S(1)}, bf16[480,768]{1,0:T(8,128)(2,1)S(1)}, u32[]{:S(2)}, u32[]{:S(2)}) collective-permute-start(bf16[480,768]{1,0:T(8,128)(2,1)S(1)} %get-tuple-element.282.refs_3_), channel_id=1, source_target_pairs={{0,8},{8,0},{16,24},{24,16},{1,9},{9,1},{17,25},{25,17},{2,10},{10... | collective-permute-start | bytes 2211848 | tf_op jit(solution)/shard_map/ppermute | solution.py:1257
  554.3 26.5 %collective-permute-start.44 = (bf16[160,768]{1,0:T(8,128)(2,1)S(1)}, bf16[160,768]{1,0:T(8,128)(2,1)S(1)}, u32[]{:S(2)}, u32[]{:S(2)}) collective-permute-start(bf16[160,768]{1,0:T(8,128)(2,1)S(1)} %get-tuple-element.283.refs_5_), channel_id=1, source_target_pairs={{0,8},{8,0},{16,24},{24,16},{1,9},{9,1},{17,25},{25,17},{2,10},{10... | collective-permute-start | bytes 737288 | tf_op jit(solution)/shard_map/ppermute | solution.py:1560
  554.4 26.4 %collective-permute-start.45 = (bf16[160,768]{1,0:T(8,128)(2,1)S(1)}, bf16[160,768]{1,0:T(8,128)(2,1)S(1)}, u32[]{:S(2)}, u32[]{:S(2)}) collective-permute-start(bf16[160,768]{1,0:T(8,128)(2,1)S(1)} %get-tuple-element.283.refs_5_), channel_id=1, source_target_pairs={{0,16},{8,24},{16,0},{24,8},{1,17},{9,25},{17,1},{25,9},{2,18},{10... | collective-permute-start | bytes 737288 | tf_op jit(solution)/shard_map/ppermute | solution.py:1560
  556.3 28.3 %collective-permute-start.46 = (bf16[160,768]{1,0:T(8,128)(2,1)S(1)}, bf16[160,768]{1,0:T(8,128)(2,1)S(1)}, u32[]{:S(2)}, u32[]{:S(2)}) collective-permute-start(bf16[160,768]{1,0:T(8,128)(2,1)S(1)} %get-tuple-element.283.refs_5_), channel_id=1, source_target_pairs={{0,24},{8,16},{16,8},{24,0},{1,25},{9,17},{17,9},{25,1},{2,26},{10... | collective-permute-start | bytes 737288 | tf_op jit(solution)/shard_map/ppermute | solution.py:1560
  (43 other events, 306.1 us)
Sparse Core Ops, SparseCore 0:
  12.3 106.4 all-gather.4
  120.7 114.0 all-gather.6

commit v5 on v4

--- a/solution.py
+++ b/solution.py
@@ -366,7 +366,7 @@
     active, slope = gelu_parts(up)
     active = active.astype(BF16)
     g_ref[...] = active
-    slope_ref[...] = slope
+    slope_ref[...] = slope.astype(BF16)
     acc_ref[...] += dot(active, flat_block(w_down_ref), 1, 0)
 
     @pl.when(j == pl.num_programs(0) - 1)
@@ -391,7 +391,7 @@
         [mixture, rows, packed, packed, packed, bias, norms],
         [ whole(mixture.shape), whole(rows.shape), pl.BlockSpec((count, blk, width), lambda j: (0, at_out, 0)), pl.BlockSpec((count, blk, width), lambda j: (0, at_up + j, 0)), pl.BlockSpec((owners, hidden // count, width), lambda j: (j, at_down, 0)), pl.BlockSpec((1, width), lambda j: (0, j)), whole(norms.shape), ],
         [ whole((width, total)), whole((total, width)), whole((total, 1)), whole((total, width)), pl.BlockSpec((total, width), lambda j: (0, j)), pl.BlockSpec((total, width), lambda j: (0, j)), whole((total, width)), whole((total, 1)), whole((total, width)), ],
-        [ stored((width, total), BF16), stored((total, width), F32), stored((total, 1), F32), stored((total, width), BF16), stored((total, hidden), BF16), stored((total, hidden), F32), shape((total, width), F32), shape((total, 1), F32), shape((total, width), BF16)],
+        [ stored((width, total), BF16), stored((total, width), F32), stored((total, 1), F32), stored((total, width), BF16), stored((total, hidden), BF16), stored((total, hidden), BF16), shape((total, width), F32), shape((total, 1), F32), shape((total, width), BF16)],
         [pltpu.VMEM((total, width), F32)],
         cost( 2 * total * width * (width + 2 * hidden), 4 * hidden * width + 10 * total * hidden ),
         "ffn",
@@ -437,7 +437,7 @@
         slot = slot_ref[j * owners + i]
         down_ref[slot] = part_ref[i * share : (i + 1) * share, :].astype(BF16)
 
-    d_up = (dot(db_ref[...], flat_block(w_down_ref), 1, 1) * slope_ref[...]).astype(BF16)
+    d_up = (dot(db_ref[...], flat_block(w_down_ref), 1, 1) * slope_ref[...].astype(F32)).astype(BF16)
     bias_ref[...] = column_sum(d_up.astype(F32))
     part_ref[...] = dot(at_ref[...], d_up, 1, 0)
     place = pl.ds(pl.multiple_of(share + j * blk, 16), blk)

time: 601 us -> 601 us (level)
  no operation moved by 1% of the time
where the time goes in v5:
time: 601 us; the launch traced here: 595 us
  Pallas kernels  239 us (40%)
  waiting for transfers between devices  236 us (39%)
  starting transfers between devices  81.9 us (14%)
  local copies, waits for them, and re-layouts  19.4 us (3%)
  between operations  15 us (2%)
    pallas_call x28, Pallas kernels, launch(): pl.pallas_call(kernel, grid_spec=pltpu.PrefetchScalarGridSpec(num_scalar_...  239 us
    all_gather x1, waiting for transfers between devices, local(): first = lax.all_gather(first, 'seq', axis=0)  99.1 us
    ppermute x30, waiting for transfers between devices, swap(): return lax.ppermute(value, axis, [(i, i ^ 1 << bit) for i in range(size)])  42.5 us
    ppermute x30, starting transfers between devices, swap(): return lax.ppermute(value, axis, [(i, i ^ 1 << bit) for i in range(size)])  37.9 us
    ppermute x3, waiting for transfers between devices, across_direct(): came = [lax.ppermute(pieces[mask], 'batch', pairs) for mask, pairs in ends]  35.9 us
    ppermute x3, waiting for transfers between devices, across_direct(): came = [lax.ppermute(held, 'batch', pairs) for _, pairs in ends]  25.9 us
    ppermute x7, waiting for transfers between devices, local(): lax.ppermute(block_totals, 'seq', [(i, i ^ mask) for i in range(count)])  21.1 us
    unnamed x108, local copies, waits for them, and re-layouts  13.3 us
  transfers between devices with their start and end apart: 53, of which 19 were waited for; matrix products, arithmetic and copies ran while one was open for 1% of the time, Pallas kernels for 32%

profile of v5, /device:TPU:0, one launch (start us, length us, event | category | flops | bytes accessed | tf_op | source)
XLA Modules:
  0.0 594.6 jit_solution(1936137455613348)
XLA Ops:
  8.9 3.3 pack.2
  14.9 2.7 pack.3
  19.7 99.1 %all-gather.5.cloned.1.call-done = bf16[13056,768]{1,0:T(8,128)(2,1)} async-done(((bf16[1632,768]{1,0:T(8,128)(2,1)}), bf16[13056,768]{1,0:T(8,128)(2,1)}) %all-gather.5.cloned.1.call-update) | async-done | bytes 20054032 | tf_op jit(solution)/shard_map/all_gather | solution.py:1632
  119.7 5.7 qkv.1
  125.3 4.6 all-to-all-start
  130.0 17.5 %gates.1 = (f32[3,4096,128]{2,1,0:T(8,128)}, f32[3,4096,128]{2,1,0:T(8,128)}, f32[2,3,8,128]{3,2,1,0:T(8,128)}, f32[8,128]{1,0:T(8,128)}) custom-call(s32[4]{0:T(128)S(1)} %copy-done.31, s32[4,512,1]{2,1,0:T(8,128)S(1)} %copy.49.refs_1_, s32[4,512,1]{2,1,0:T(8,128)S(1)} %copy.50.refs_2_, bf16[8,1632,768]{2,1,0:T(8,128)(2,1)} %bitcast.56, ...), custom_call_target="tpu_custom_call" | custom-call | flops 6442450944000 | bytes 25165824000 | tf_op jit(solution)/shard_map/gates/pallas_call | solution.py:90
  147.8 1.7 collective-permute-start.1
  150.1 1.7 collective-permute-start.3
  153.3 2.6 collective-permute-start.5
  155.9 21.1 %collective-permute-done.1.refs_3_ = f32[2,3,8,128]{3,2,1,0:T(8,128)S(1)} collective-permute-done((f32[2,3,8,128]{3,2,1,0:T(8,128)}, f32[2,3,8,128]{3,2,1,0:T(8,128)S(1)}, u32[]{:S(2)}, u32[]{:S(2)}) %collective-permute-start.1) | collective-permute-done | bytes 24608 | tf_op jit(solution)/shard_map/ppermute | solution.py:1650
  178.5 12.3 %attend.1 = (bf16[8,6,64,128]{3,2,1,0:T(8,128)(2,1)}, f32[6,1,1024]{2,1,0:T(1,128)S(1)}, f32[8,128]{1,0:T(8,128)}) custom-call(bf16[8,6,3,64,128]{4,3,2,1,0:T(8,128)(2,1)} %all-to-all-done.refs_0_, f32[8,128]{1,0:T(8,128)} %get-tuple-element.168.refs_1_), custom_call_target="tpu_custom_call" | custom-call | flops 6442450944000 | bytes 3145728000 | tf_op jit(solution)/shard_map/attend/pallas_call | solution.py:90
  190.8 4.7 all-to-all-start.1
  196.5 10.6 %states.1 = (f32[3,4096,128]{2,1,0:T(8,128)}, bf16[512,768]{1,0:T(8,128)(2,1)}, f32[512,768]{1,0:T(8,128)}, bf16[512,768]{1,0:T(8,128)(2,1)}, f32[8,128]{1,0:T(8,128)}) custom-call(s32[1]{0:T(128)} %bitcast.13.refs_0_.refs_2_, f32[3,4096,128]{2,1,0:T(8,128)} %get-tuple-element.170.refs_1_.refs_5_.refs_2_, ...), custom_call_target="tpu_custom_call" | custom-call | flops 1006632960000 | bytes 18874368000 | tf_op jit(solution)/shard_map/states/pallas_call | solution.py:90
  209.3 7.6 %all-to-all-done.1.refs_0_ = bf16[8,6,64,128]{3,2,1,0:T(8,128)(2,1)} async-done(((bf16[8,6,64,128]{3,2,1,0:T(8,128)(2,1)}), bf16[8,6,64,128]{3,2,1,0:T(8,128)(2,1)}, u32[]{:S(2)}, u32[]{:S(2)}) %all-to-all-start.1) | async-done | bytes 786464 | tf_op jit(solution)/shard_map/all_to_all | solution.py:1655
  216.9 17.2 %ffn.1 = (bf16[768,512]{1,0:T(8,128)(2,1)}, f32[512,768]{1,0:T(8,128)}, f32[512,1]{1,0:T(8,128)}, bf16[512,768]{1,0:T(8,128)(2,1)}, bf16[512,3072]{1,0:T(8,128)(...) custom-call(bf16[8,6,64,128]{3,2,1,0:T(8,128)(2,1)} %all-to-all-done, ...), custom_call_target="tpu_custom_call" | custom-call | flops 5435817984000 | bytes 25165824000 | tf_op jit(solution)/shard_map/ffn/pallas_call | solution.py:90
  236.7 3.6 collective-permute-start.7
  243.0 18.3 %conv.1 = (f32[512,768]{1,0:T(8,128)}, f32[512,768]{1,0:T(8,128)}, f32[512,768]{1,0:T(8,128)S(1)}, f32[512,768]{1,0:T(8,128)S(1)}, bf16[512,1536]{1,0:T(8,128)(2...) custom-call(bf16[512,768]{1,0:T(8,128)(2,1)S(1)} %get-tuple-element., ...), custom_call_target="tpu_custom_call", output_to_operand_aliasing={{8}: (10, {}), {9}: (11, {})} | custom-call | flops 7247757312000 | bytes 29884416000 | tf_op jit(solution)/shard_map/conv/pallas_call | solution.py:90
  261.3 3.6 collective-permute-start.11
  266.5 3.1 collective-permute-start.15
  270.1 14.4 %conv_back.1 = (bf16[512,768]{1,0:T(8,128)(2,1)S(1)}, f32[512,768]{1,0:T(8,128)S(1)}, f32[2,768]{1,0:T(2,128)S(1)}, f32[8,128]{1,0:T(8,128)}) custom-call(bf16[512,1536]{1,0:T(8,128)(2,1)} %get-tuple-element.185.refs_0_.refs_5_, bf16[4,1,1536]{2,1,0:T(2,128)(2,1)S(1)} %collective-permute-done.11.refs_1_, ...), custom_call_target="tpu_custom_call" | custom-call | flops 7247757312000 | bytes 22020096000 | tf_op jit(solution)/shard_map/conv_back/pallas_call | solution.py:90
  284.6 16.9 %conv_weight.1 = (bf16[2,576,768]{2,1,0:T(8,128)(2,1)}, bf16[2,576,768]{2,1,0:T(8,128)(2,1)}, bf16[2,576,768]{2,1,0:T(8,128)(2,1)}, bf16[2,576,768]{2,1,0:T(8,128)(2,1)}, f32[8,128]{1,0:T(8,128)}) custom-call(s32[8]{0:T(128)S(1)} %broadcast_xor_fusion.refs_0_.refs_1_, bf16[512,768]{1,0:T(8,128)(2,1)S(1)} %get-tuple-element.177.refs_0_.refs_1_, ...), custom_call_target="tpu_custom_call" | custom-call | flops 7247757312000 | bytes 7077888000 | tf_op jit(solution)/shard_map/conv_weight/pallas_call | solution.py:90
  301.5 2.3 collective-permute-start.20
  304.4 10.3 %states_back.1 = (f32[3,4096,128]{2,1,0:T(8,128)}, f32[3,8,128]{2,1,0:T(8,128)S(1)}, f32[8,128]{1,0:T(8,128)}) custom-call(bf16[512,768]{1,0:T(8,128)(2,1)S(1)} %get-tuple-element.198.refs_0_.refs_15_, bf16[8,1632,768]{2,1,0:T(8,128)(2,1)} %bitcast.64, f32[4,128,1]{2,1,0:T(8,128)S(1)} %convert_element_type.28.refs_6_.refs_2_, s32[4,1,128]{2,1,0:T(1,128)S(1)} %sub.14.refs_3_, ...), custom_call_target="tpu_custom_call" | custom-call | flops 1006632960000 | bytes 12582912000 | tf_op jit(solution)/shard_map/states_back/pallas_call | solution.py:90
  314.7 25.4 %ffn_back.1 = (bf16[960,768]{1,0:T(8,128)(2,1)}, bf16[960,768]{1,0:T(8,128)(2,1)}, bf16[960,768]{1,0:T(8,128)(2,1)}, bf16[960,768]{1,0:T(8,128)(2,1)}, bf16[4,96...) custom-call(s32[8]{0:T(128)S(1)} %shift-left_add_fusion.refs_0_, ...), custom_call_target="tpu_custom_call" | custom-call | flops 10267656192000 | bytes 34603008000 | tf_op jit(solution)/shard_map/ffn_back/pallas_call | solution.py:90
  342.1 1.6 collective-permute-start.19
  343.7 3.6 all-to-all-start.2
  347.3 5.6 split.3
  352.9 1.9 collective-permute-start.22
  354.8 1.5 collective-permute-start.23
  356.3 7.9 %fold.1 = (bf16[2,480,768]{2,1,0:T(8,128)(2,1)}, bf16[2,480,768]{2,1,0:T(8,128)(2,1)}, bf16[2,480,768]{2,1,0:T(8,128)(2,1)}, bf16[2,480,768]{2,1,0:T(8,128)(2,1)}, f32[8,128]{1,0:T(8,128)}) custom-call(bf16[4,960,768]{2,1,0:T(8,128)(2,1)} %get-tuple-element.209.refs_0_.refs_1_, bf16[4,960,768]{2,1,0:T(8,128)(2,1)} %get-tuple-element.209.refs_0_.refs_1_, ...), custom_call_target="tpu_custom_call" | custom-call | flops 2949120000 | bytes 17694720000 | tf_op jit(solution)/shard_map/fold/pallas_call | solution.py:90
  365.9 21.7 %attend_back.1 = (bf16[8,6,3,64,128]{4,3,2,1,0:T(8,128)(2,1)}, f32[8,128]{1,0:T(8,128)}) custom-call(bf16[8,6,3,64,128]{4,3,2,1,0:T(8,128)(2,1)} %all-to-all-done.refs_0_, bf16[8,480,128]{2,1,0:T(8,128)(2,1)} %copy-done.4, f32[6,1,1024]{2,1,0:T(1,128)S(1)} %get-tuple-element.208.refs_2_, f32[8,128]{1,0:T(8,128)} %get-tuple-element.220.refs_3_), custom_call_target="tpu_custom_call" | custom-call | flops 16106127360000 | bytes 5505024000 | tf_op jit(solution)/shard_map/attend_back/pallas_call | solution.py:90
  387.7 4.9 all-to-all-start.3
  392.6 2.9 cross.1
  395.5 1.5 collective-permute-start.24
  397.0 14.8 %gates_back.1 = (bf16[4,256,1536]{2,1,0:T(8,128)(2,1)S(1)}, f32[1,1536]{1,0:T(1,128)S(1)}, f32[8,128]{1,0:T(8,128)S(1)}) custom-call(s32[1]{0:T(128)} %bitcast.13.refs_0_.refs_2_, s32[4]{0:T(128)S(1)} %copy-done.31, f32[3,4096,128]{2,1,0:T(8,128)} %get-tuple-element.170.refs_1_.refs_5_.refs_2_, f32[3,4096,128]{2,1,0:T(8,128)} %get-tuple-element.171.refs_2_.refs_3_, ...), custom_call_target="tpu_custom_call" | custom-call | flops 1610612736000 | bytes 25165824000 | tf_op jit(solution)/shard_map/gates_back/pallas_call | solution.py:90
  412.4 3.1 split.4
  415.5 2.0 collective-permute-start.27
  417.5 1.5 collective-permute-start.28
  419.0 2.2 halve.1
  422.5 2.4 collective-permute-start.29
  424.9 8.0 %rest.1 = (bf16[4,320,768]{2,1,0:T(8,128)(2,1)S(1)}, bf16[4,320,768]{2,1,0:T(8,128)(2,1)S(1)}, f32[8,128]{1,0:T(8,128)S(1)}) custom-call(s32[8]{0:T(128)S(1)} %copy-done.33, bf16[8,1632,768]{2,1,0:T(8,128)(2,1)} %bitcast.68, bf16[4,256,1536]{2,1,0:T(8,128)(2,1)S(1)} %get-tuple-element.236.refs_2_, bf16[8,1632,768]{2,1,0:T(8,128)(2,1)} %bitcast.69, ...), custom_call_target="tpu_custom_call" | custom-call | flops 4831838208000 | bytes 11796480000 | tf_op jit(solution)/shard_map/rest/pallas_call | solution.py:90
  434.8 3.6 all-to-all-done.3.refs_1_
  441.0 8.8 %qkv_back.1 = (f32[512,768]{1,0:T(8,128)}, bf16[4,320,768]{2,1,0:T(8,128)(2,1)S(1)}, bf16[4,320,768]{2,1,0:T(8,128)(2,1)S(1)}, f32[8,128]{1,0:T(8,128)S(1)}) custom-call(s32[8]{0:T(128)S(1)} %copy-done.33, bf16[8,6,3,64,128]{4,3,2,1,0:T(8,128)(2,1)} %all-to-all-done.3.refs_1_, bf16[512,768]{1,0:T(8,128)(2,1)S(1)} %bitcast.43, ...), custom_call_target="tpu_custom_call" | custom-call | flops 4831838208000 | bytes 18087936000 | tf_op jit(solution)/shard_map/qkv_back/pallas_call | solution.py:90
  449.8 2.9 collective-permute-done.27.refs_3_
  452.8 2.0 cross_add.1
  455.4 3.5 collective-permute-done.32.refs_2_
  458.9 2.8 collective-permute-done.33.refs_3_
  464.8 1.5 collective-permute-start.31
  466.3 2.4 collective-permute-start.30
  468.7 22.6 %collective-permute-done.30.refs_2_ = bf16[288,768]{1,0:T(8,128)(2,1)S(1)} collective-permute-done((bf16[288,768]{1,0:T(8,128)(2,1)S(1)}, bf16[288,768]{1,0:T(8,128)(2,1)S(1)}, u32[]{:S(2)}, u32[]{:S(2)}) %collective-permute-start.30) | collective-permute-done | bytes 442400 | tf_op jit(solution)/shard_map/ppermute | solution.py:1257
  493.0 2.5 collective-permute-start.36
  497.5 1.5 collective-permute-start.37
  499.0 8.0 %collective-permute-done.38.refs_3_ = bf16[1,320,768]{2,1,0:T(8,128)(2,1)S(1)} collective-permute-done((bf16[1,320,768]{2,1,0:T(8,128)(2,1)S(1)}, bf16[1,320,768]{2,1,0:T(8,128)(2,1)S(1)}, u32[]{:S(2)}, u32[]{:S(2)}) %collective-permute-start.38) | collective-permute-done | bytes 491552 | tf_op jit(solution)/shard_map/ppermute | solution.py:1257
  509.0 1.7 collective-permute-start.41
  510.7 2.4 collective-permute-start.42
  513.1 26.0 %collective-permute-done.40.refs_6_ = bf16[160,768]{1,0:T(8,128)(2,1)S(1)} collective-permute-done((bf16[160,768]{1,0:T(8,128)(2,1)S(1)}, bf16[160,768]{1,0:T(8,128)(2,1)S(1)}, u32[]{:S(2)}, u32[]{:S(2)}) %collective-permute-start.40) | collective-permute-done | bytes 245792 | tf_op jit(solution)/shard_map/ppermute | solution.py:1547
  539.1 9.9 %collective-permute-done.41.refs_7_ = bf16[160,768]{1,0:T(8,128)(2,1)S(1)} collective-permute-done((bf16[160,768]{1,0:T(8,128)(2,1)S(1)}, bf16[160,768]{1,0:T(8,128)(2,1)S(1)}, u32[]{:S(2)}, u32[]{:S(2)}) %collective-permute-start.41) | collective-permute-done | bytes 245792 | tf_op jit(solution)/shard_map/ppermute | solution.py:1547
  549.0 2.1 finish_add_total.1
  551.1 3.2 collective-permute-start.43
  554.3 2.0 collective-permute-start.45
  556.3 2.4 collective-permute-start.46
  558.7 22.1 %collective-permute-done.44.refs_6_ = bf16[160,768]{1,0:T(8,128)(2,1)S(1)} collective-permute-done((bf16[160,768]{1,0:T(8,128)(2,1)S(1)}, bf16[160,768]{1,0:T(8,128)(2,1)S(1)}, u32[]{:S(2)}, u32[]{:S(2)}) %collective-permute-start.44) | collective-permute-done | bytes 245792 | tf_op jit(solution)/shard_map/ppermute | solution.py:1560
  580.8 3.8 collective-permute-done.46.refs_8_
  584.6 2.5 finish_spread.1
  (208 shorter events, 42.5 us)
Async XLA Ops:
  7.2 111.6 %all-gather.5.cloned.1.call-start = ((), (), s32[]{:S(2)}) async-start(), calls=%async_computation.4 | async-start | bytes 22560768 | tf_op jit(solution)/shard_map/all_gather | solution.py:1632
  12.2 228.1 %all-gather.7.cloned.1.call-start = ((), (), s32[]{:S(2)}) async-start(), calls=%async_computation.5 | async-start | bytes 15925248 | tf_op jit(solution)/shard_map/all_gather | solution.py:1633
  18.1 100.7 %copy-start.45 = (s32[4,512]{1,0:T(4,128)}, s32[4,512]{1,0:T(4,128)S(1)}, u32[]{:S(2)}) copy-start(s32[4,512]{1,0:T(4,128)S(1)} %rev.4) | copy-start | bytes 24580
  125.3 53.2 %all-to-all-start = ((bf16[8,6,3,64,128]{4,3,2,1,0:T(8,128)(2,1)}), bf16[8,6,3,64,128]{4,3,2,1,0:T(8,128)(2,1)}, u32[]{:S(2)}, u32[]{:S(2)}) async-start(bf16[8,6,3,64,128]{4,3,2,1,0:T(8,128)(2,1)} %get-tuple-element.166), calls=%async_computation | async-start | bytes 4718592 | tf_op jit(solution)/shard_map/all_to_all | solution.py:1647
  147.5 5.3 collective-permute-start
  147.8 29.3 %collective-permute-start.1 = (f32[2,3,8,128]{3,2,1,0:T(8,128)}, f32[2,3,8,128]{3,2,1,0:T(8,128)S(1)}, u32[]{:S(2)}, u32[]{:S(2)}) collective-permute-start(f32[2,3,8,128]{3,2,1,0:T(8,128)} %get-tuple-element.172.refs_1_), channel_id=1, source_target_pairs={{0,2},{1,3},{2,0},{3,1},{4,6},{5,7},{6,4},{7,5},{8,10},{9,11},{10,... | collective-permute-start | bytes 73736 | tf_op jit(solution)/shard_map/ppermute | solution.py:1650
  150.0 45.6 %collective-permute-start.2 = (f32[2,3,8,128]{3,2,1,0:T(8,128)}, f32[2,3,8,128]{3,2,1,0:T(8,128)}, u32[]{:S(2)}, u32[]{:S(2)}) collective-permute-start(f32[2,3,8,128]{3,2,1,0:T(8,128)} %get-tuple-element.172.refs_1_), channel_id=1, source_target_pairs={{0,3},{1,2},{2,1},{3,0},{4,7},{5,6},{6,5},{7,4},{8,11},{9,10},{10,... | collective-permute-start | bytes 73736 | tf_op jit(solution)/shard_map/ppermute | solution.py:1650
  150.1 45.5 %collective-permute-start.3 = (f32[2,3,8,128]{3,2,1,0:T(8,128)}, f32[2,3,8,128]{3,2,1,0:T(8,128)}, u32[]{:S(2)}, u32[]{:S(2)}) collective-permute-start(f32[2,3,8,128]{3,2,1,0:T(8,128)} %get-tuple-element.172.refs_1_), channel_id=1, source_target_pairs={{0,4},{1,5},{2,6},{3,7},{4,0},{5,1},{6,2},{7,3},{8,12},{9,13},{10,... | collective-permute-start | bytes 73736 | tf_op jit(solution)/shard_map/ppermute | solution.py:1650
  151.8 43.8 %collective-permute-start.4 = (f32[2,3,8,128]{3,2,1,0:T(8,128)}, f32[2,3,8,128]{3,2,1,0:T(8,128)}, u32[]{:S(2)}, u32[]{:S(2)}) collective-permute-start(f32[2,3,8,128]{3,2,1,0:T(8,128)} %get-tuple-element.172.refs_1_), channel_id=1, source_target_pairs={{0,5},{1,4},{2,7},{3,6},{4,1},{5,0},{6,3},{7,2},{8,13},{9,12},{10,... | collective-permute-start | bytes 73736 | tf_op jit(solution)/shard_map/ppermute | solution.py:1650
  153.3 42.3 %collective-permute-start.5 = (f32[2,3,8,128]{3,2,1,0:T(8,128)}, f32[2,3,8,128]{3,2,1,0:T(8,128)}, u32[]{:S(2)}, u32[]{:S(2)}) collective-permute-start(f32[2,3,8,128]{3,2,1,0:T(8,128)} %get-tuple-element.172.refs_1_), channel_id=1, source_target_pairs={{0,6},{1,7},{2,4},{3,5},{4,2},{5,3},{6,0},{7,1},{8,14},{9,15},{10,... | collective-permute-start | bytes 73736 | tf_op jit(solution)/shard_map/ppermute | solution.py:1650
  177.7 18.0 %collective-permute-start.6 = (f32[2,3,8,128]{3,2,1,0:T(8,128)}, f32[2,3,8,128]{3,2,1,0:T(8,128)}, u32[]{:S(2)}, u32[]{:S(2)}) collective-permute-start(f32[2,3,8,128]{3,2,1,0:T(8,128)} %get-tuple-element.172.refs_1_), channel_id=1, source_target_pairs={{0,7},{1,6},{2,5},{3,4},{4,3},{5,2},{6,1},{7,0},{8,15},{9,14},{10,... | collective-permute-start | bytes 73736 | tf_op jit(solution)/shard_map/ppermute | solution.py:1650
  190.8 26.1 %all-to-all-start.1 = ((bf16[8,6,64,128]{3,2,1,0:T(8,128)(2,1)}), bf16[8,6,64,128]{3,2,1,0:T(8,128)(2,1)}, u32[]{:S(2)}, u32[]{:S(2)}) async-start(bf16[8,6,64,128]{3,2,1,0:T(8,128)(2,1)} %get-tuple-element.169), calls=%async_computation.1 | async-start | bytes 1572864 | tf_op jit(solution)/shard_map/all_to_all | solution.py:1655
  207.1 33.6 %collective-permute-start.10 = (bf16[512,768]{1,0:T(8,128)(2,1)}, bf16[512,768]{1,0:T(8,128)(2,1)}, u32[]{:S(2)}, u32[]{:S(2)}) collective-permute-start(bf16[512,768]{1,0:T(8,128)(2,1)} %get-tuple-element.178.refs_1_.refs_2_), channel_id=1, source_target_pairs={{0,1},{1,0},{2,3},{3,2},{4,5},{5,4},{6,7},{7,6},{8,9},{9,8},{10,11... | collective-permute-start | bytes 2359304 | tf_op jit(solution)/shard_map/ppermute | solution.py:1257
  216.9 19.8 %copy-start.47 = (bf16[4,1,768]{2,1,0:T(2,128)(2,1)S(1)}, bf16[4,1,768]{2,1,0:T(2,128)(2,1)}, u32[]{:S(2)}) copy-start(bf16[4,1,768]{2,1,0:T(2,128)(2,1)} %get-tuple-element.304) | copy-start | bytes 18436
  216.9 23.5 %copy-start.53 = (s32[8]{0:T(128)S(1)}, s32[8]{0:T(128)}, u32[]{:S(2)}) copy-start(s32[8]{0:T(128)} %constant.50.clone) | copy-start | bytes 100
  235.3 5.4 collective-permute-start.9
  235.4 5.0 collective-permute-start.8
  236.7 4.0 collective-permute-start.7
  240.4 74.4 %copy-start.32 = (s32[8]{0:T(128)}, s32[8]{0:T(128)S(1)}, u32[]{:S(2)}) copy-start(s32[8]{0:T(128)S(1)} %broadcast_xor_fusion.refs_0_.refs_1_) | copy-start | bytes 100
  243.0 23.4 %copy-start.11 = (s32[4,128]{1,0:T(4,128)S(1)}, s32[4,128]{1,0:T(4,128)}, u32[]{:S(2)}) copy-start(s32[4,128]{1,0:T(4,128)} %reduce_window_sum.15) | copy-start | bytes 6148
  243.0 23.4 %copy-start.51 = (s32[4,1,128]{2,1,0:T(1,128)S(1)}, s32[4,1,128]{2,1,0:T(1,128)}, u32[]{:S(2)}) copy-start(s32[4,1,128]{2,1,0:T(1,128)} %param.25) | copy-start | bytes 6148
  243.0 27.1 %copy-start.37 = (f32[512,768]{1,0:T(8,128)S(1)}, f32[512,768]{1,0:T(8,128)}, u32[]{:S(2)}) copy-start(f32[512,768]{1,0:T(8,128)} %copy-done.35) | copy-start | bytes 4718596
  261.3 8.7 %collective-permute-start.11 = (bf16[4,1,1536]{2,1,0:T(2,128)(2,1)S(1)}, bf16[4,1,1536]{2,1,0:T(2,128)(2,1)S(1)}, u32[]{:S(2)}, u32[]{:S(2)}) collective-permute-start(bf16[4,1,1536]{2,1,0:T(2,128)(2,1)S(1)} %get-tuple-element.186), channel_id=1, source_target_pairs={{0,1},{1,2},{2,3},{3,4},{4,5},{5,6},{6,7},{8,9},{9,10},{10,11},{11... | collective-permute-start | bytes 36872 | tf_op jit(solution)/shard_map/ppermute | solution.py:1581
  264.9 5.1 collective-permute-start.12
  266.5 18.1 %collective-permute-start.15 = (bf16[4,1,1536]{2,1,0:T(2,128)(2,1)}, bf16[4,1,1536]{2,1,0:T(2,128)(2,1)}, u32[]{:S(2)}, u32[]{:S(2)}) collective-permute-start(bf16[4,1,1536]{2,1,0:T(2,128)(2,1)} %collective-permute-done.8.refs_6_.refs_8_), channel_id=1, source_target_pairs={{0,1},{1,0},{2,3},{3,2},{4,5},{5,4},{6,7},{7,6},{8,9},{9,8},{10,11... | collective-permute-start | bytes 36872 | tf_op jit(solution)/shard_map/ppermute | solution.py:1257
  269.6 15.0 %collective-permute-start.14 = (bf16[4,1,1536]{2,1,0:T(2,128)(2,1)}, bf16[4,1,1536]{2,1,0:T(2,128)(2,1)}, u32[]{:S(2)}, u32[]{:S(2)}) collective-permute-start(bf16[4,1,1536]{2,1,0:T(2,128)(2,1)} %collective-permute-done.7.refs_5_.refs_7_), channel_id=1, source_target_pairs={{0,1},{1,0},{2,3},{3,2},{4,5},{5,4},{6,7},{7,6},{8,9},{9,8},{10,11... | collective-permute-start | bytes 36872 | tf_op jit(solution)/shard_map/ppermute | solution.py:1257
  269.6 14.9 %collective-permute-start.13 = (bf16[512,1536]{1,0:T(8,128)(2,1)}, bf16[512,1536]{1,0:T(8,128)(2,1)}, u32[]{:S(2)}, u32[]{:S(2)}) collective-permute-start(bf16[512,1536]{1,0:T(8,128)(2,1)} %get-tuple-element.185.refs_0_.refs_5_), channel_id=1, source_target_pairs={{0,1},{1,0},{2,3},{3,2},{4,5},{5,4},{6,7},{7,6},{8,9},{9,8},{10,11... | collective-permute-start | bytes 4718600 | tf_op jit(solution)/shard_map/ppermute | solution.py:1257
  284.6 19.9 %copy-start.12 = (s32[4,128]{1,0:T(4,128)S(1)}, s32[4,128]{1,0:T(4,128)}, u32[]{:S(2)}) copy-start(s32[4,128]{1,0:T(4,128)} %reduce_window_sum.15) | copy-start | bytes 6148
  301.5 40.6 %collective-permute-start.20 = (bf16[2,576,768]{2,1,0:T(8,128)(2,1)}, bf16[2,576,768]{2,1,0:T(8,128)(2,1)}, u32[]{:S(2)}, u32[]{:S(2)}) collective-permute-start(bf16[2,576,768]{2,1,0:T(8,128)(2,1)} %get-tuple-element.216), channel_id=1, source_target_pairs={{0,2},{1,3},{2,0},{3,1},{4,6},{5,7},{6,4},{7,5},{8,10},{9,11},{10,... | collective-permute-start | bytes 5308424 | tf_op jit(solution)/shard_map/ppermute | solution.py:1257
  303.8 43.5 %collective-permute-start.21 = (bf16[2,576,768]{2,1,0:T(8,128)(2,1)}, bf16[2,576,768]{2,1,0:T(8,128)(2,1)}, u32[]{:S(2)}, u32[]{:S(2)}) collective-permute-start(bf16[2,576,768]{2,1,0:T(8,128)(2,1)} %get-tuple-element.217), channel_id=1, source_target_pairs={{0,4},{1,5},{2,6},{3,7},{4,0},{5,1},{6,2},{7,3},{8,12},{9,13},{10,... | collective-permute-start | bytes 5308424 | tf_op jit(solution)/shard_map/ppermute | solution.py:1257
  340.1 14.7 %collective-permute-start.16 = (bf16[960,768]{1,0:T(8,128)(2,1)}, bf16[960,768]{1,0:T(8,128)(2,1)}, u32[]{:S(2)}, u32[]{:S(2)}) collective-permute-start(bf16[960,768]{1,0:T(8,128)(2,1)} %get-tuple-element.210), channel_id=1, source_target_pairs={{0,1},{1,0},{2,3},{3,2},{4,5},{5,4},{6,7},{7,6},{8,9},{9,8},{10,11... | collective-permute-start | bytes 4423688 | tf_op jit(solution)/shard_map/ppermute | solution.py:1257
  341.4 14.9 %collective-permute-start.17 = (bf16[960,768]{1,0:T(8,128)(2,1)}, bf16[960,768]{1,0:T(8,128)(2,1)}, u32[]{:S(2)}, u32[]{:S(2)}) collective-permute-start(bf16[960,768]{1,0:T(8,128)(2,1)} %get-tuple-element.211), channel_id=1, source_target_pairs={{0,1},{1,0},{2,3},{3,2},{4,5},{5,4},{6,7},{7,6},{8,9},{9,8},{10,11... | collective-permute-start | bytes 4423688 | tf_op jit(solution)/shard_map/ppermute | solution.py:1257
  341.4 14.9 %collective-permute-start.18 = (bf16[960,768]{1,0:T(8,128)(2,1)}, bf16[960,768]{1,0:T(8,128)(2,1)}, u32[]{:S(2)}, u32[]{:S(2)}) collective-permute-start(bf16[960,768]{1,0:T(8,128)(2,1)} %get-tuple-element.212), channel_id=1, source_target_pairs={{0,1},{1,0},{2,3},{3,2},{4,5},{5,4},{6,7},{7,6},{8,9},{9,8},{10,11... | collective-permute-start | bytes 4423688 | tf_op jit(solution)/shard_map/ppermute | solution.py:1257
  342.1 14.2 %collective-permute-start.19 = (bf16[960,768]{1,0:T(8,128)(2,1)}, bf16[960,768]{1,0:T(8,128)(2,1)}, u32[]{:S(2)}, u32[]{:S(2)}) collective-permute-start(bf16[960,768]{1,0:T(8,128)(2,1)} %get-tuple-element.213), channel_id=1, source_target_pairs={{0,1},{1,0},{2,3},{3,2},{4,5},{5,4},{6,7},{7,6},{8,9},{9,8},{10,11... | collective-permute-start | bytes 4423688 | tf_op jit(solution)/shard_map/ppermute | solution.py:1257
  343.7 21.3 %all-to-all-start.2 = ((bf16[8,480,128]{2,1,0:T(8,128)(2,1)}), bf16[8,480,128]{2,1,0:T(8,128)(2,1)S(1)}, u32[]{:S(2)}, u32[]{:S(2)}) async-start(bf16[8,480,128]{2,1,0:T(8,128)(2,1)} %get-tuple-element.207), calls=%async_computation.2 | async-start | bytes 1966080 | tf_op jit(solution)/shard_map/all_to_all | solution.py:1715
  352.9 39.7 %collective-permute-start.22 = (bf16[1,576,768]{2,1,0:T(8,128)(2,1)}, bf16[1,576,768]{2,1,0:T(8,128)(2,1)}, u32[]{:S(2)}, u32[]{:S(2)}) collective-permute-start(bf16[1,576,768]{2,1,0:T(8,128)(2,1)} %get-tuple-element.230), channel_id=1, source_target_pairs={{0,4},{1,5},{2,6},{3,7},{4,0},{5,1},{6,2},{7,3},{8,12},{9,13},{10,... | collective-permute-start | bytes 2654216 | tf_op jit(solution)/shard_map/ppermute | solution.py:1257
  354.8 37.8 %collective-permute-start.23 = (bf16[1,576,768]{2,1,0:T(8,128)(2,1)}, bf16[1,576,768]{2,1,0:T(8,128)(2,1)}, u32[]{:S(2)}, u32[]{:S(2)}) collective-permute-start(bf16[1,576,768]{2,1,0:T(8,128)(2,1)} %get-tuple-element.231), channel_id=1, source_target_pairs={{0,2},{1,3},{2,0},{3,1},{4,6},{5,7},{6,4},{7,5},{8,10},{9,11},{10,... | collective-permute-start | bytes 2654216 | tf_op jit(solution)/shard_map/ppermute | solution.py:1257
  364.2 47.9 %collective-permute-start.25 = (bf16[2,480,768]{2,1,0:T(8,128)(2,1)}, bf16[2,480,768]{2,1,0:T(8,128)(2,1)}, u32[]{:S(2)}, u32[]{:S(2)}) collective-permute-start(bf16[2,480,768]{2,1,0:T(8,128)(2,1)} %get-tuple-element.241), channel_id=1, source_target_pairs={{0,2},{1,3},{2,0},{3,1},{4,6},{5,7},{6,4},{7,5},{8,10},{9,11},{10,... | collective-permute-start | bytes 4423688 | tf_op jit(solution)/shard_map/ppermute | solution.py:1257
  364.8 47.3 %collective-permute-start.26 = (bf16[2,480,768]{2,1,0:T(8,128)(2,1)}, bf16[2,480,768]{2,1,0:T(8,128)(2,1)}, u32[]{:S(2)}, u32[]{:S(2)}) collective-permute-start(bf16[2,480,768]{2,1,0:T(8,128)(2,1)} %get-tuple-element.242), channel_id=1, source_target_pairs={{0,4},{1,5},{2,6},{3,7},{4,0},{5,1},{6,2},{7,3},{8,12},{9,13},{10,... | collective-permute-start | bytes 4423688 | tf_op jit(solution)/shard_map/ppermute | solution.py:1257
  387.7 50.8 %all-to-all-start.3 = ((bf16[8,6,3,64,128]{4,3,2,1,0:T(8,128)(2,1)}), bf16[8,6,3,64,128]{4,3,2,1,0:T(8,128)(2,1)}, u32[]{:S(2)}, u32[]{:S(2)}) async-start(bf16[8,6,3,64,128]{4,3,2,1,0:T(8,128)(2,1)} %get-tuple-element.221), calls=%async_computation.3 | async-start | bytes 4718592 | tf_op jit(solution)/shard_map/all_to_all | solution.py:1722
  395.5 23.5 %collective-permute-start.24 = (bf16[576,768]{1,0:T(8,128)(2,1)}, bf16[576,768]{1,0:T(8,128)(2,1)}, u32[]{:S(2)}, u32[]{:S(2)}) collective-permute-start(bf16[576,768]{1,0:T(8,128)(2,1)} %get-tuple-element.238), channel_id=1, source_target_pairs={{0,8},{8,0},{16,24},{24,16},{1,9},{9,1},{17,25},{25,17},{2,10},{10... | collective-permute-start | bytes 2654216 | tf_op jit(solution)/shard_map/ppermute | solution.py:1257
  415.5 37.1 %collective-permute-start.27 = (bf16[1,480,768]{2,1,0:T(8,128)(2,1)}, bf16[1,480,768]{2,1,0:T(8,128)(2,1)}, u32[]{:S(2)}, u32[]{:S(2)}) collective-permute-start(bf16[1,480,768]{2,1,0:T(8,128)(2,1)} %get-tuple-element.250), channel_id=1, source_target_pairs={{0,4},{1,5},{2,6},{3,7},{4,0},{5,1},{6,2},{7,3},{8,12},{9,13},{10,... | collective-permute-start | bytes 2211848 | tf_op jit(solution)/shard_map/ppermute | solution.py:1257
  417.5 35.3 %collective-permute-start.28 = (bf16[1,480,768]{2,1,0:T(8,128)(2,1)}, bf16[1,480,768]{2,1,0:T(8,128)(2,1)}, u32[]{:S(2)}, u32[]{:S(2)}) collective-permute-start(bf16[1,480,768]{2,1,0:T(8,128)(2,1)} %get-tuple-element.251), channel_id=1, source_target_pairs={{0,2},{1,3},{2,0},{3,1},{4,6},{5,7},{6,4},{7,5},{8,10},{9,11},{10,... | collective-permute-start | bytes 2211848 | tf_op jit(solution)/shard_map/ppermute | solution.py:1257
  422.5 27.3 %collective-permute-start.29 = (bf16[288,768]{1,0:T(8,128)(2,1)}, bf16[288,768]{1,0:T(8,128)(2,1)}, u32[]{:S(2)}, u32[]{:S(2)}) collective-permute-start(bf16[288,768]{1,0:T(8,128)(2,1)} %get-tuple-element.253), channel_id=1, source_target_pairs={{0,16},{8,24},{16,0},{24,8},{1,17},{9,25},{17,1},{25,9},{2,18},{10... | collective-permute-start | bytes 1327112 | tf_op jit(solution)/shard_map/ppermute | solution.py:1257
  454.9 4.0 collective-permute-start.32
  454.9 6.8 %collective-permute-start.33 = (bf16[4,320,768]{2,1,0:T(8,128)(2,1)S(1)}, bf16[4,320,768]{2,1,0:T(8,128)(2,1)S(1)}, u32[]{:S(2)}, u32[]{:S(2)}) collective-permute-start(bf16[4,320,768]{2,1,0:T(8,128)(2,1)S(1)} %get-tuple-element.263), channel_id=1, source_target_pairs={{0,1},{1,0},{2,3},{3,2},{4,5},{5,4},{6,7},{7,6},{8,9},{9,8},{10,11... | collective-permute-start | bytes 5898248 | tf_op jit(solution)/shard_map/ppermute | solution.py:1257
  462.7 29.6 %copy-start.25 = (f32[8,128]{1,0:T(8,128)}, f32[8,128]{1,0:T(8,128)S(1)}, u32[]{:S(2)}) copy-start(f32[8,128]{1,0:T(8,128)S(1)} %get-tuple-element.269.refs_9_) | copy-start | bytes 12292
  462.7 29.6 %collective-permute-start.34 = (bf16[2,320,768]{2,1,0:T(8,128)(2,1)S(1)}, bf16[2,320,768]{2,1,0:T(8,128)(2,1)S(1)}, u32[]{:S(2)}, u32[]{:S(2)}) collective-permute-start(bf16[2,320,768]{2,1,0:T(8,128)(2,1)S(1)} %get-tuple-element.267), channel_id=1, source_target_pairs={{0,2},{1,3},{2,0},{3,1},{4,6},{5,7},{6,4},{7,5},{8,10},{9,11},{10,... | collective-permute-start | bytes 2949128 | tf_op jit(solution)/shard_map/ppermute | solution.py:1257
  464.1 28.2 %collective-permute-start.35 = (bf16[2,320,768]{2,1,0:T(8,128)(2,1)S(1)}, bf16[2,320,768]{2,1,0:T(8,128)(2,1)S(1)}, u32[]{:S(2)}, u32[]{:S(2)}) collective-permute-start(bf16[2,320,768]{2,1,0:T(8,128)(2,1)S(1)} %get-tuple-element.268), channel_id=1, source_target_pairs={{0,4},{1,5},{2,6},{3,7},{4,0},{5,1},{6,2},{7,3},{8,12},{9,13},{10,... | collective-permute-start | bytes 2949128 | tf_op jit(solution)/shard_map/ppermute | solution.py:1257
  464.8 27.4 %collective-permute-start.31 = (bf16[480,768]{1,0:T(8,128)(2,1)S(1)}, bf16[480,768]{1,0:T(8,128)(2,1)S(1)}, u32[]{:S(2)}, u32[]{:S(2)}) collective-permute-start(bf16[480,768]{1,0:T(8,128)(2,1)S(1)} %get-tuple-element.259), channel_id=1, source_target_pairs={{0,8},{8,0},{16,24},{24,16},{1,9},{9,1},{17,25},{25,17},{2,10},{10... | collective-permute-start | bytes 2211848 | tf_op jit(solution)/shard_map/ppermute | solution.py:1257
  466.3 25.0 %collective-permute-start.30 = (bf16[288,768]{1,0:T(8,128)(2,1)S(1)}, bf16[288,768]{1,0:T(8,128)(2,1)S(1)}, u32[]{:S(2)}, u32[]{:S(2)}) collective-permute-start(bf16[288,768]{1,0:T(8,128)(2,1)S(1)} %get-tuple-element.257.refs_1_), channel_id=1, source_target_pairs={{0,16},{8,24},{16,0},{24,8},{1,17},{9,25},{17,1},{25,9},{2,18},{10... | collective-permute-start | bytes 1327112 | tf_op jit(solution)/shard_map/ppermute | solution.py:1257
  493.0 55.9 %collective-permute-start.36 = (bf16[576,768]{1,0:T(8,128)(2,1)S(1)}, bf16[576,768]{1,0:T(8,128)(2,1)S(1)}, u32[]{:S(2)}, u32[]{:S(2)}) collective-permute-start(bf16[576,768]{1,0:T(8,128)(2,1)S(1)} %get-tuple-element.270.refs_1_), channel_id=1, source_target_pairs={{0,8},{8,0},{16,24},{24,16},{1,9},{9,1},{17,25},{25,17},{2,10},{10... | collective-permute-start | bytes 2654216 | tf_op jit(solution)/shard_map/ppermute | solution.py:1257
  495.5 11.5 %collective-permute-start.38 = (bf16[1,320,768]{2,1,0:T(8,128)(2,1)S(1)}, bf16[1,320,768]{2,1,0:T(8,128)(2,1)S(1)}, u32[]{:S(2)}, u32[]{:S(2)}) collective-permute-start(bf16[1,320,768]{2,1,0:T(8,128)(2,1)S(1)} %get-tuple-element.274), channel_id=1, source_target_pairs={{0,4},{1,5},{2,6},{3,7},{4,0},{5,1},{6,2},{7,3},{8,12},{9,13},{10,... | collective-permute-start | bytes 1474568 | tf_op jit(solution)/shard_map/ppermute | solution.py:1257
  496.8 11.2 %collective-permute-start.39 = (bf16[1,320,768]{2,1,0:T(8,128)(2,1)S(1)}, bf16[1,320,768]{2,1,0:T(8,128)(2,1)S(1)}, u32[]{:S(2)}, u32[]{:S(2)}) collective-permute-start(bf16[1,320,768]{2,1,0:T(8,128)(2,1)S(1)} %get-tuple-element.275), channel_id=1, source_target_pairs={{0,2},{1,3},{2,0},{3,1},{4,6},{5,7},{6,4},{7,5},{8,10},{9,11},{10,... | collective-permute-start | bytes 1474568 | tf_op jit(solution)/shard_map/ppermute | solution.py:1257
  497.5 51.4 %collective-permute-start.37 = (bf16[480,768]{1,0:T(8,128)(2,1)S(1)}, bf16[480,768]{1,0:T(8,128)(2,1)S(1)}, u32[]{:S(2)}, u32[]{:S(2)}) collective-permute-start(bf16[480,768]{1,0:T(8,128)(2,1)S(1)} %get-tuple-element.271.refs_3_), channel_id=1, source_target_pairs={{0,16},{8,24},{16,0},{24,8},{1,17},{9,25},{17,1},{25,9},{2,18},{10... | collective-permute-start | bytes 2211848 | tf_op jit(solution)/shard_map/ppermute | solution.py:1257
  508.6 40.3 %copy-start.21 = (f32[8,128]{1,0:T(8,128)}, f32[8,128]{1,0:T(8,128)S(1)}, u32[]{:S(2)}) copy-start(f32[8,128]{1,0:T(8,128)S(1)} %get-tuple-element.281.refs_9_) | copy-start | bytes 12292
  508.6 30.4 %collective-permute-start.40 = (bf16[160,768]{1,0:T(8,128)(2,1)S(1)}, bf16[160,768]{1,0:T(8,128)(2,1)S(1)}, u32[]{:S(2)}, u32[]{:S(2)}) collective-permute-start(bf16[160,768]{1,0:T(8,128)(2,1)S(1)} %get-tuple-element.278), channel_id=1, source_target_pairs={{0,8},{8,0},{16,24},{24,16},{1,9},{9,1},{17,25},{25,17},{2,10},{10... | collective-permute-start | bytes 737288 | tf_op jit(solution)/shard_map/ppermute | solution.py:1547
  509.0 39.9 %collective-permute-start.41 = (bf16[160,768]{1,0:T(8,128)(2,1)S(1)}, bf16[160,768]{1,0:T(8,128)(2,1)S(1)}, u32[]{:S(2)}, u32[]{:S(2)}) collective-permute-start(bf16[160,768]{1,0:T(8,128)(2,1)S(1)} %get-tuple-element.279), channel_id=1, source_target_pairs={{0,16},{8,24},{16,0},{24,8},{1,17},{9,25},{17,1},{25,9},{2,18},{10... | collective-permute-start | bytes 737288 | tf_op jit(solution)/shard_map/ppermute | solution.py:1547
  510.7 38.2 %collective-permute-start.42 = (bf16[160,768]{1,0:T(8,128)(2,1)S(1)}, bf16[160,768]{1,0:T(8,128)(2,1)S(1)}, u32[]{:S(2)}, u32[]{:S(2)}) collective-permute-start(bf16[160,768]{1,0:T(8,128)(2,1)S(1)} %get-tuple-element.280), channel_id=1, source_target_pairs={{0,24},{8,16},{16,8},{24,0},{1,25},{9,17},{17,9},{25,1},{2,26},{10... | collective-permute-start | bytes 737288 | tf_op jit(solution)/shard_map/ppermute | solution.py:1547
  551.1 33.5 %copy-start.20 = (f32[8,128]{1,0:T(8,128)}, f32[8,128]{1,0:T(8,128)S(1)}, u32[]{:S(2)}) copy-start(f32[8,128]{1,0:T(8,128)S(1)} %get-tuple-element.284.refs_9_) | copy-start | bytes 12292
  551.1 33.5 %collective-permute-start.43 = (bf16[480,768]{1,0:T(8,128)(2,1)S(1)}, bf16[480,768]{1,0:T(8,128)(2,1)S(1)}, u32[]{:S(2)}, u32[]{:S(2)}) collective-permute-start(bf16[480,768]{1,0:T(8,128)(2,1)S(1)} %get-tuple-element.282.refs_3_), channel_id=1, source_target_pairs={{0,8},{8,0},{16,24},{24,16},{1,9},{9,1},{17,25},{25,17},{2,10},{10... | collective-permute-start | bytes 2211848 | tf_op jit(solution)/shard_map/ppermute | solution.py:1257
  554.3 26.5 %collective-permute-start.44 = (bf16[160,768]{1,0:T(8,128)(2,1)S(1)}, bf16[160,768]{1,0:T(8,128)(2,1)S(1)}, u32[]{:S(2)}, u32[]{:S(2)}) collective-permute-start(bf16[160,768]{1,0:T(8,128)(2,1)S(1)} %get-tuple-element.283.refs_5_), channel_id=1, source_target_pairs={{0,8},{8,0},{16,24},{24,16},{1,9},{9,1},{17,25},{25,17},{2,10},{10... | collective-permute-start | bytes 737288 | tf_op jit(solution)/shard_map/ppermute | solution.py:1560
  554.3 26.4 %collective-permute-start.45 = (bf16[160,768]{1,0:T(8,128)(2,1)S(1)}, bf16[160,768]{1,0:T(8,128)(2,1)S(1)}, u32[]{:S(2)}, u32[]{:S(2)}) collective-permute-start(bf16[160,768]{1,0:T(8,128)(2,1)S(1)} %get-tuple-element.283.refs_5_), channel_id=1, source_target_pairs={{0,16},{8,24},{16,0},{24,8},{1,17},{9,25},{17,1},{25,9},{2,18},{10... | collective-permute-start | bytes 737288 | tf_op jit(solution)/shard_map/ppermute | solution.py:1560
  556.3 28.3 %collective-permute-start.46 = (bf16[160,768]{1,0:T(8,128)(2,1)S(1)}, bf16[160,768]{1,0:T(8,128)(2,1)S(1)}, u32[]{:S(2)}, u32[]{:S(2)}) collective-permute-start(bf16[160,768]{1,0:T(8,128)(2,1)S(1)} %get-tuple-element.283.refs_5_), channel_id=1, source_target_pairs={{0,24},{8,16},{16,8},{24,0},{1,25},{9,17},{17,9},{25,1},{2,26},{10... | collective-permute-start | bytes 737288 | tf_op jit(solution)/shard_map/ppermute | solution.py:1560
  (43 other events, 306.0 us)
Sparse Core Ops, SparseCore 0:
  12.3 106.4 all-gather.4
  120.7 114.0 all-gather.6
